TPU v7x, 32 devices: a whole 2x2x4 slice. The times are simulated.
32 devices in a mesh: section: 2 (over x), dp: 4 (over z), seq: 4 (over y, core).
Axes of the slice: x: 2, y: 2, z: 4, core: 2. Of those that a mesh axis runs over, the one named last changes fastest.
Arguments:
- hidden_in: bfloat16 [2, 4, 1024, 1536], P(None, 'dp', 'seq'), may hold values from -6 to 6
- out_grad: bfloat16 [2, 4, 1024, 1536], P(None, 'dp', 'seq'), may hold values from -6 to 6
- attn_gain: bfloat16 [2, 1536], P('section', ('dp', 'seq')), may hold values from 0.5 to 1.5
- ffn_gain: bfloat16 [2, 1536], P('section', ('dp', 'seq')), may hold values from 0.5 to 1.5
- query_matrix: bfloat16 [2, 1536, 1536], P('section', ('dp', 'seq')), may hold values from -0.15625 to 0.15625
- key_matrix: bfloat16 [2, 1536, 512], P('section', ('dp', 'seq')), may hold values from -0.15625 to 0.15625
- value_matrix: bfloat16 [2, 1536, 512], P('section', ('dp', 'seq')), may hold values from -0.15625 to 0.15625
- output_matrix: bfloat16 [2, 1536, 1536], P('section', ('dp', 'seq')), may hold values from -2.5 to 2.5
- router_matrix: bfloat16 [2, 1536, 32], P('section', ('dp', 'seq')), may hold values from -0.079589844 to 0.079589844
- w_gate: bfloat16 [2, 32, 1536, 512], P('section', 'dp'), may hold values from -0.15625 to 0.15625
- w_up: bfloat16 [2, 32, 1536, 512], P('section', 'dp'), may hold values from -0.15625 to 0.15625
- w_down: bfloat16 [2, 32, 512, 1536], P('section', 'dp'), may hold values from -1 to 1
- routes: int32 [2, 2, 4, 1024, 8], P('section', None, 'dp', 'seq'), may hold values from 0 to 31, all different within a row; in each aligned block of 256 rows (0 to 255, 256 to 511, ..., all dimensions but the last counted through in order) at most 80 rows name the same one
Outputs:
- layer_outs: float32 [2, 2, 4, 1024, 1536], P('section', None, 'dp', 'seq')
- section_grads: float32 [2, 2, 4, 1024, 1536], P('section', None, 'dp', 'seq')
- grad_attn_gain: float32 [2, 1536], P('section', ('dp', 'seq'))
- grad_ffn_gain: float32 [2, 1536], P('section', ('dp', 'seq'))
- grad_query: float32 [2, 1536, 1536], P('section', ('dp', 'seq'))
- grad_key: float32 [2, 1536, 512], P('section', ('dp', 'seq'))
- grad_value: float32 [2, 1536, 512], P('section', ('dp', 'seq'))
- grad_out: float32 [2, 1536, 1536], P('section', ('dp', 'seq'))
- grad_router: float32 [2, 1536, 32], P('section', ('dp', 'seq'))
- grad_gate: float32 [2, 32, 1536, 512], P('section', 'dp', 'seq')
- grad_up: float32 [2, 32, 1536, 512], P('section', 'dp', 'seq')
- grad_down: float32 [2, 32, 512, 1536], P('section', 'dp', 'seq')
Inputs may be any that keep to these rules, and one draw needn't show every extreme that they name: `routes`: each token names 8 different experts. In each aligned block of 256 rows (one block of positions of one sequence) no expert is named by more than 80 rows, a bound that some block reaches.
All inputs are finite; a program needn't handle non-finite values.
Results may differ from a plain program's by a relative error of at most 0.024.
Values may be sent and summed in bfloat16 or wider, within the bound.
A program may use at most 960 MiB of HBM per device.

v0:
```python
from functools import partial

import jax
import jax.numpy as jnp
from jax import lax
from jax.sharding import PartitionSpec as P

HEADS = 24
KV_HEADS = 8
HEAD_DIM = 64
TOP_K = 8
EXPERTS = 32
CAP = 80


epsilon = 1e-06


def as_sent(shard):

    def short(part):
        return part.astype(jnp.bfloat16) if part.dtype == jnp.float32 else part

    return jax.tree.map(short, shard)


def passed_along(block, axis, distance):
    devices = range(lax.axis_size(axis))
    route = [(i - distance, i) for i in devices if i - distance in devices]
    return lax.ppermute(block, axis, route)


def rms_norm(values, norm_gain):
    return (
        values * lax.rsqrt(jnp.mean(values * values, axis=-1, keepdims=True) + epsilon) * norm_gain
    )


def rotary_tables(length):
    half_dim = HEAD_DIM // 2
    frequency = 10000.0 ** (-jnp.arange(half_dim, dtype=jnp.float32) * 2.0 / HEAD_DIM)
    angles = jnp.arange(length, dtype=jnp.float32)[:, None] * frequency[None, :]
    return (jnp.cos(angles)[:, None, :], jnp.sin(angles)[:, None, :])


def rotate(values, cos_table, sin_table):
    length = values.shape[0]
    split_heads = values.reshape(length, -1, HEAD_DIM)
    first_half = split_heads[..., : HEAD_DIM // 2]
    second_half = split_heads[..., HEAD_DIM // 2 :]
    turned = jnp.concatenate(
        [
            first_half * cos_table - second_half * sin_table,
            second_half * cos_table + first_half * sin_table,
        ],
        axis=-1,
    )
    return turned.reshape(length, -1)


def slot_index(route):
    flat_route = route.reshape(-1)
    one_hot = (flat_route[:, None] == jnp.arange(EXPERTS, dtype=jnp.int32)[None, :]).astype(
        jnp.int32
    )
    position = jnp.sum((jnp.cumsum(one_hot, axis=0) - 1) * one_hot, axis=1)
    return flat_route * CAP + position


def dispatch(normed_feedforward, slots):
    width = normed_feedforward.shape[1]
    copies = jnp.repeat(normed_feedforward, TOP_K, axis=0)
    buffer = jnp.zeros((EXPERTS * CAP, width), jnp.bfloat16).at[slots].set(copies)
    return buffer.reshape(EXPERTS, CAP, width)


def to_owners(buffer):
    return lax.all_to_all(buffer, "dp", split_axis=0, concat_axis=1, tiled=True)


def to_sources(buffer):
    return lax.all_to_all(buffer, "dp", split_axis=1, concat_axis=0, tiled=True)


def expert_forward(slot_rows, gate_w, up_w, down_w):
    gate_pre = jnp.einsum("ecd,edf->ecf", slot_rows, gate_w, preferred_element_type=jnp.float32)
    up_pre = jnp.einsum("ecd,edf->ecf", slot_rows, up_w, preferred_element_type=jnp.float32)
    hidden_act = (jax.nn.silu(gate_pre) * up_pre).astype(jnp.bfloat16)
    result = jnp.einsum(
        "ecf,efd->ecd", hidden_act, down_w, preferred_element_type=jnp.float32
    ).astype(jnp.bfloat16)
    return (result, gate_pre, up_pre)


def expert_skip(slot_rows, gate_w, up_w, down_w):
    inner_shape = slot_rows.shape[:2] + (gate_w.shape[2],)
    return (
        jnp.zeros(slot_rows.shape, jnp.bfloat16),
        jnp.zeros(inner_shape, jnp.float32),
        jnp.zeros(inner_shape, jnp.float32),
    )


def expert_backward(slot_rows, row_grads, gate_pre, up_pre, gate_w, up_w, down_w):
    activated = jax.nn.silu(gate_pre)
    hidden_act = (activated * up_pre).astype(jnp.bfloat16)
    down_grad = jnp.einsum(
        "ecf,ecd->efd", hidden_act, row_grads, preferred_element_type=jnp.float32
    )
    hidden_grad = jnp.einsum("ecd,efd->ecf", row_grads, down_w, preferred_element_type=jnp.float32)
    sigmoid = jax.nn.sigmoid(gate_pre)
    gate_low = (hidden_grad * up_pre * sigmoid * (1.0 + gate_pre * (1.0 - sigmoid))).astype(
        jnp.bfloat16
    )
    up_low = (hidden_grad * activated).astype(jnp.bfloat16)
    gate_grad = jnp.einsum("ecd,ecf->edf", slot_rows, gate_low, preferred_element_type=jnp.float32)
    up_grad = jnp.einsum("ecd,ecf->edf", slot_rows, up_low, preferred_element_type=jnp.float32)
    input_grad = jnp.einsum("ecf,edf->ecd", gate_low, gate_w, preferred_element_type=jnp.float32)
    input_grad = input_grad + jnp.einsum(
        "ecf,edf->ecd", up_low, up_w, preferred_element_type=jnp.float32
    )
    return (input_grad.astype(jnp.bfloat16), gate_grad, up_grad, down_grad)


def expert_rest(slot_rows, row_grads, gate_pre, up_pre, gate_w, up_w, down_w):
    return (
        jnp.zeros(slot_rows.shape, jnp.bfloat16),
        jnp.zeros(gate_w.shape, jnp.float32),
        jnp.zeros(up_w.shape, jnp.float32),
        jnp.zeros(down_w.shape, jnp.float32),
    )


def attention_blocks(q_rot, k_rot, values):
    length = q_rot.shape[0]
    block_rows = min(512, length)
    block_count = length // block_rows
    outputs = []
    totals_list = []
    for block_number in range(block_count):
        first_row = block_number * block_rows
        key_end = first_row + block_rows
        q_block = q_rot[first_row:key_end]
        scores = (
            jnp.einsum(
                "qhgd,khd->hgqk", q_block, k_rot[:key_end], preferred_element_type=jnp.float32
            )
            * 0.125
        )
        causal = (first_row + jnp.arange(block_rows, dtype=jnp.int32))[:, None] >= jnp.arange(
            key_end, dtype=jnp.int32
        )[None, :]
        scores = jnp.where(causal, scores, -jnp.inf)
        row_peak = jnp.max(scores, axis=-1, keepdims=True)
        exponents = jnp.exp(scores - row_peak)
        totals = jnp.sum(exponents, axis=-1, keepdims=True)
        weights_low = (exponents / totals).astype(jnp.bfloat16)
        attended = jnp.einsum(
            "hgqk,khd->qhgd", weights_low, values[:key_end], preferred_element_type=jnp.float32
        )
        outputs.append(attended.astype(jnp.bfloat16).reshape(block_rows, -1))
        totals_list.append((row_peak + jnp.log(totals))[..., 0])
    return (jnp.concatenate(outputs, axis=0), jnp.stack(totals_list))


def attention_spare(q_rot, k_rot, values):
    length = q_rot.shape[0]
    block_rows = min(512, length)
    block_count = length // block_rows
    return (
        jnp.zeros((length, q_rot.shape[1] * q_rot.shape[2] * HEAD_DIM), jnp.bfloat16),
        jnp.zeros((block_count, q_rot.shape[1], q_rot.shape[2], block_rows), jnp.float32),
    )


def attention_forward(q_heads, k_heads, v_heads, active):
    length = q_heads.shape[0]
    local_kv = k_heads.shape[1] // HEAD_DIM
    group_size = HEADS // KV_HEADS
    cos_table, sin_table = rotary_tables(length)
    q_rot = (
        rotate(q_heads.astype(jnp.float32), cos_table, sin_table)
        .astype(jnp.bfloat16)
        .reshape(length, local_kv, group_size, HEAD_DIM)
    )
    k_rot = (
        rotate(k_heads.astype(jnp.float32), cos_table, sin_table)
        .astype(jnp.bfloat16)
        .reshape(length, local_kv, HEAD_DIM)
    )
    values = v_heads.reshape(length, local_kv, HEAD_DIM)
    attended, log_total = lax.cond(active, attention_blocks, attention_spare, q_rot, k_rot, values)
    return (attended, log_total, q_rot, k_rot)


def attention_grads(head_grad, q_rot, k_rot, v_heads, log_total):
    length = q_rot.shape[0]
    local_kv = q_rot.shape[1]
    group_size = q_rot.shape[2]
    cos_table, sin_table = rotary_tables(length)
    values = v_heads.reshape(length, local_kv, HEAD_DIM)
    block_rows = min(512, length)
    block_count = length // block_rows
    grad_rows = head_grad.reshape(length, local_kv, group_size, HEAD_DIM)
    key_acc = jnp.zeros((length, local_kv, HEAD_DIM), jnp.float32)
    value_acc = jnp.zeros((length, local_kv, HEAD_DIM), jnp.float32)
    query_parts = []
    for block_number in range(block_count):
        first_row = block_number * block_rows
        key_end = first_row + block_rows
        q_block = q_rot[first_row:key_end]
        grad_block = grad_rows[first_row:key_end]
        key_part = k_rot[:key_end]
        scores = (
            jnp.einsum("qhgd,khd->hgqk", q_block, key_part, preferred_element_type=jnp.float32)
            * 0.125
        )
        causal = (first_row + jnp.arange(block_rows, dtype=jnp.int32))[:, None] >= jnp.arange(
            key_end, dtype=jnp.int32
        )[None, :]
        scores = jnp.where(causal, scores, -jnp.inf)
        probs_full = jnp.exp(scores - log_total[block_number][..., None])
        prob_grad = jnp.einsum(
            "qhgd,khd->hgqk", grad_block, values[:key_end], preferred_element_type=jnp.float32
        )
        score_grad = probs_full * (
            prob_grad - jnp.sum(probs_full * prob_grad, axis=-1, keepdims=True)
        )
        score_low = score_grad.astype(jnp.bfloat16)
        query_parts.append(
            jnp.einsum("hgqk,khd->qhgd", score_low, key_part, preferred_element_type=jnp.float32)
            * 0.125
        )
        key_acc = key_acc.at[:key_end].add(
            jnp.einsum("hgqk,qhgd->khd", score_low, q_block, preferred_element_type=jnp.float32)
            * 0.125
        )
        value_acc = value_acc.at[:key_end].add(
            jnp.einsum(
                "hgqk,qhgd->khd",
                probs_full.astype(jnp.bfloat16),
                grad_block,
                preferred_element_type=jnp.float32,
            )
        )
    query_all = jnp.concatenate(query_parts, axis=0)
    unrotate = partial(rotate, cos_table=cos_table, sin_table=sin_table)
    query_grad = jax.vjp(
        unrotate, jnp.zeros((length, local_kv * group_size * HEAD_DIM), jnp.float32)
    )[1](query_all.reshape(length, -1))[0]
    key_grad = jax.vjp(unrotate, jnp.zeros((length, local_kv * HEAD_DIM), jnp.float32))[1](
        key_acc.reshape(length, -1)
    )[0]
    return (
        query_grad.astype(jnp.bfloat16),
        key_grad.astype(jnp.bfloat16),
        value_acc.reshape(length, -1).astype(jnp.bfloat16),
    )


def attention_grads_spare(head_grad, q_rot, k_rot, v_heads, log_total):
    length = q_rot.shape[0]
    query_width = q_rot.shape[1] * q_rot.shape[2] * HEAD_DIM
    kv_width = q_rot.shape[1] * HEAD_DIM
    return (
        jnp.zeros((length, query_width), jnp.bfloat16),
        jnp.zeros((length, kv_width), jnp.bfloat16),
        jnp.zeros((length, kv_width), jnp.bfloat16),
    )


def attention_backward(head_grad, q_rot, k_rot, v_heads, log_total, active):
    return lax.cond(
        active, attention_grads, attention_grads_spare, head_grad, q_rot, k_rot, v_heads, log_total
    )


def forward_layer(layer_in, route, active, weights, experts):
    attn_scale, ffn_scale, query_w, key_w, value_w, out_w, router_w = weights
    gate_w, up_w, down_w = experts
    normed_input = rms_norm(layer_in, attn_scale).astype(jnp.bfloat16)
    query_rows = jnp.dot(normed_input, query_w, preferred_element_type=jnp.float32).astype(
        jnp.bfloat16
    )
    key_proj = jnp.dot(normed_input, key_w, preferred_element_type=jnp.float32).astype(jnp.bfloat16)
    value_proj = jnp.dot(normed_input, value_w, preferred_element_type=jnp.float32).astype(
        jnp.bfloat16
    )
    q_heads, k_heads, v_heads = (
        lax.all_to_all(query_rows, "seq", split_axis=1, concat_axis=0, tiled=True),
        lax.all_to_all(key_proj, "seq", split_axis=1, concat_axis=0, tiled=True),
        lax.all_to_all(value_proj, "seq", split_axis=1, concat_axis=0, tiled=True),
    )
    mixed_output, log_total, q_rot, k_rot = attention_forward(q_heads, k_heads, v_heads, active)
    mixed_tokens = lax.all_to_all(
        as_sent(mixed_output), "seq", split_axis=0, concat_axis=1, tiled=True
    ).astype(mixed_output.dtype)
    after_update = layer_in + jnp.dot(mixed_tokens, out_w, preferred_element_type=jnp.float32)
    normed_feedforward = rms_norm(after_update, ffn_scale).astype(jnp.bfloat16)
    router_logits = jnp.dot(normed_feedforward, router_w, preferred_element_type=jnp.float32)
    gates = jax.nn.softmax(jnp.take_along_axis(router_logits, route, axis=-1), axis=-1)
    slots = slot_index(route)
    slot_rows = to_owners(dispatch(normed_feedforward, slots))
    results, gate_pre, up_pre = lax.cond(
        active, expert_forward, expert_skip, slot_rows, gate_w, up_w, down_w
    )
    returned = to_sources(results)
    width = returned.shape[2]
    picked = returned.reshape(EXPERTS * CAP, width)[slots].reshape(-1, TOP_K, width)
    layer_out = after_update + jnp.sum(gates[:, :, None] * picked.astype(jnp.float32), axis=1)
    saved = {
        "layer_in": layer_in,
        "after": after_update,
        "q_rot": q_rot,
        "k_rot": k_rot,
        "v_heads": v_heads,
        "log_total": log_total,
        "mixed_tokens": mixed_tokens,
        "normed_ffn": normed_feedforward,
        "gates": gates,
        "picked": picked,
        "gate_pre": gate_pre,
        "up_pre": up_pre,
    }
    return (layer_out, saved)


def backward_layer(layer_grad, saved, route, active, weights, experts):
    attn_scale, ffn_scale, query_w, key_w, value_w, out_w, router_w = weights
    gate_w, up_w, down_w = experts
    width = layer_grad.shape[1]
    slots = slot_index(route)
    gates = saved["gates"]
    gate_term = jnp.sum(layer_grad[:, None, :] * saved["picked"].astype(jnp.float32), axis=-1)
    chosen_grad = gates * (gate_term - jnp.sum(gates * gate_term, axis=-1, keepdims=True))
    selector = (route[:, :, None] == jnp.arange(EXPERTS, dtype=jnp.int32)[None, None, :]).astype(
        jnp.float32
    )
    logit_grad = jnp.sum(selector * chosen_grad[:, :, None], axis=1).astype(jnp.bfloat16)
    router_grad = jnp.einsum(
        "td,te->de", saved["normed_ffn"], logit_grad, preferred_element_type=jnp.float32
    )
    normed_grad = jnp.einsum("te,de->td", logit_grad, router_w, preferred_element_type=jnp.float32)
    slot_grads = (
        (gates[:, :, None] * layer_grad[:, None, :]).astype(jnp.bfloat16).reshape(-1, width)
    )
    grad_buffer = (
        jnp.zeros((EXPERTS * CAP, width), jnp.bfloat16)
        .at[slots]
        .set(slot_grads)
        .reshape(EXPERTS, CAP, width)
    )
    grad_rows = to_owners(grad_buffer)
    slot_rows = to_owners(dispatch(saved["normed_ffn"], slots))
    input_rows, gate_grad, up_grad, down_grad = lax.cond(
        active,
        expert_backward,
        expert_rest,
        slot_rows,
        grad_rows,
        saved["gate_pre"],
        saved["up_pre"],
        gate_w,
        up_w,
        down_w,
    )
    returned = to_sources(input_rows)
    normed_grad = normed_grad + jnp.sum(
        returned.reshape(EXPERTS * CAP, width)[slots].reshape(-1, TOP_K, width).astype(jnp.float32),
        axis=1,
    )
    after_part, ffn_gain_grad = jax.vjp(rms_norm, saved["after"], ffn_scale)[1](normed_grad)
    after_grad = after_part + layer_grad
    branch_grad = after_grad.astype(jnp.bfloat16)
    out_weight_grad = jnp.einsum(
        "tf,td->fd", saved["mixed_tokens"], branch_grad, preferred_element_type=jnp.float32
    )
    mixed_grad = jnp.einsum(
        "td,fd->tf", branch_grad, out_w, preferred_element_type=jnp.float32
    ).astype(jnp.bfloat16)
    head_grad = lax.all_to_all(mixed_grad, "seq", split_axis=1, concat_axis=0, tiled=True)
    query_grad, key_grad, value_grad = attention_backward(
        head_grad, saved["q_rot"], saved["k_rot"], saved["v_heads"], saved["log_total"], active
    )
    token_query, token_key, token_value = (
        lax.all_to_all(query_grad, "seq", split_axis=0, concat_axis=1, tiled=True),
        lax.all_to_all(key_grad, "seq", split_axis=0, concat_axis=1, tiled=True),
        lax.all_to_all(value_grad, "seq", split_axis=0, concat_axis=1, tiled=True),
    )
    normed_input = rms_norm(saved["layer_in"], attn_scale).astype(jnp.bfloat16)
    query_weight_grad = jnp.einsum(
        "td,tf->df", normed_input, token_query, preferred_element_type=jnp.float32
    )
    key_weight_grad = jnp.einsum(
        "td,tf->df", normed_input, token_key, preferred_element_type=jnp.float32
    )
    value_weight_grad = jnp.einsum(
        "td,tf->df", normed_input, token_value, preferred_element_type=jnp.float32
    )
    normed_attn_grad = jnp.einsum(
        "tf,df->td", token_query, query_w, preferred_element_type=jnp.float32
    )
    normed_attn_grad = normed_attn_grad + jnp.einsum(
        "tf,df->td", token_key, key_w, preferred_element_type=jnp.float32
    )
    normed_attn_grad = normed_attn_grad + jnp.einsum(
        "tf,df->td", token_value, value_w, preferred_element_type=jnp.float32
    )
    input_part, attn_gain_grad = jax.vjp(rms_norm, saved["layer_in"], attn_scale)[1](
        normed_attn_grad
    )
    dense_grads = (
        attn_gain_grad,
        ffn_gain_grad,
        query_weight_grad,
        key_weight_grad,
        value_weight_grad,
        out_weight_grad,
        router_grad,
    )
    return (input_part + after_grad, dense_grads, (gate_grad, up_grad, down_grad))


def body(
    hidden_in,
    out_grad,
    attn_gain,
    ffn_gain,
    query_matrix,
    key_matrix,
    value_matrix,
    output_matrix,
    router_matrix,
    w_gate,
    w_up,
    w_down,
    routes,
):
    sections = lax.axis_size("section")
    section = lax.axis_index("section")
    micro = hidden_in.shape[0]
    slice_len = hidden_in.shape[2]
    width = hidden_in.shape[3]
    ticks = micro + sections - 1
    gathered = (
        lax.all_gather(attn_gain, ("dp", "seq"), axis=1, tiled=True),
        lax.all_gather(ffn_gain, ("dp", "seq"), axis=1, tiled=True),
        lax.all_gather(query_matrix, ("dp", "seq"), axis=1, tiled=True),
        lax.all_gather(key_matrix, ("dp", "seq"), axis=1, tiled=True),
        lax.all_gather(value_matrix, ("dp", "seq"), axis=1, tiled=True),
        lax.all_gather(output_matrix, ("dp", "seq"), axis=1, tiled=True),
        lax.all_gather(router_matrix, ("dp", "seq"), axis=1, tiled=True),
    )
    weights = (
        gathered[0][0].astype(jnp.float32),
        gathered[1][0].astype(jnp.float32),
        gathered[2][0],
        gathered[3][0],
        gathered[4][0],
        gathered[5][0],
        gathered[6][0],
    )
    experts = (w_gate[0], w_up[0], w_down[0])
    section_routes = routes[0]
    incoming = jnp.zeros((slice_len, width), jnp.float32)
    saved_list = []
    result_list = []
    for tick_index in range(ticks):
        micro_index = tick_index - section
        active = (micro_index >= 0) & (micro_index < micro)
        clipped = jnp.clip(micro_index, 0, micro - 1)
        route = lax.dynamic_index_in_dim(section_routes, clipped, 0, keepdims=False)[0]
        first_in = hidden_in[min(tick_index, micro - 1), 0].astype(jnp.float32)
        layer_in = jnp.where(section == 0, first_in, incoming)
        layer_out, saved = forward_layer(layer_in, route, active, weights, experts)
        saved_list.append(saved)
        result_list.append(layer_out)
        if tick_index + 1 < ticks:
            incoming = passed_along(layer_out, "section", 1)
    saved_stack = jax.tree.map(lambda *pieces: jnp.stack(pieces), *saved_list)
    result_stack = jnp.stack(result_list)
    layer_outs = jnp.stack(
        [
            lax.dynamic_index_in_dim(result_stack, number + section, 0, keepdims=False)
            for number in range(micro)
        ]
    )
    dense_acc = tuple((jnp.zeros(weight.shape, jnp.float32) for weight in weights))
    expert_acc = tuple((jnp.zeros(weight.shape, jnp.float32) for weight in experts))
    grad_incoming = jnp.zeros((slice_len, width), jnp.float32)
    grad_list = []
    for tick_index in range(ticks):
        micro_index = tick_index - (sections - 1 - section)
        active = (micro_index >= 0) & (micro_index < micro)
        clipped = jnp.clip(micro_index, 0, micro - 1)
        route = lax.dynamic_index_in_dim(section_routes, clipped, 0, keepdims=False)[0]
        saved = jax.tree.map(
            lambda stacked: lax.dynamic_index_in_dim(stacked, clipped + section, 0, keepdims=False),
            saved_stack,
        )
        last_grad = out_grad[min(tick_index, micro - 1), 0].astype(jnp.float32)
        layer_grad = jnp.where(section == sections - 1, last_grad, grad_incoming)
        layer_grad = jnp.where(active, layer_grad, 0.0)
        input_grad, dense_grads, expert_grads = backward_layer(
            layer_grad, saved, route, active, weights, experts
        )
        dense_acc = tuple((total + term for total, term in zip(dense_acc, dense_grads)))
        expert_acc = tuple((total + term for total, term in zip(expert_acc, expert_grads)))
        grad_list.append(input_grad)
        if tick_index + 1 < ticks:
            grad_incoming = passed_along(input_grad.astype(jnp.bfloat16), "section", -1).astype(
                input_grad.dtype
            )
    grad_stack = jnp.stack(grad_list)
    section_grads = jnp.stack(
        [
            lax.dynamic_index_in_dim(grad_stack, number + sections - 1 - section, 0, keepdims=False)
            for number in range(micro)
        ]
    )
    dense_sums = (
        lax.psum_scatter(dense_acc[0][None], ("dp", "seq"), scatter_dimension=1, tiled=True),
        lax.psum_scatter(dense_acc[1][None], ("dp", "seq"), scatter_dimension=1, tiled=True),
        lax.psum_scatter(dense_acc[2][None], ("dp", "seq"), scatter_dimension=1, tiled=True),
        lax.psum_scatter(dense_acc[3][None], ("dp", "seq"), scatter_dimension=1, tiled=True),
        lax.psum_scatter(dense_acc[4][None], ("dp", "seq"), scatter_dimension=1, tiled=True),
        lax.psum_scatter(dense_acc[5][None], ("dp", "seq"), scatter_dimension=1, tiled=True),
        lax.psum_scatter(dense_acc[6][None], ("dp", "seq"), scatter_dimension=1, tiled=True),
    )
    expert_sums = (
        lax.psum_scatter(
            expert_acc[0][None].astype(jnp.bfloat16), "seq", scatter_dimension=2, tiled=True
        ).astype(jnp.float32),
        lax.psum_scatter(
            expert_acc[1][None].astype(jnp.bfloat16), "seq", scatter_dimension=2, tiled=True
        ).astype(jnp.float32),
        lax.psum_scatter(
            expert_acc[2][None].astype(jnp.bfloat16), "seq", scatter_dimension=2, tiled=True
        ).astype(jnp.float32),
    )
    return (
        layer_outs[None, :, None],
        section_grads[None, :, None],
        dense_sums[0],
        dense_sums[1],
        dense_sums[2],
        dense_sums[3],
        dense_sums[4],
        dense_sums[5],
        dense_sums[6],
        expert_sums[0],
        expert_sums[1],
        expert_sums[2],
    )


def solution(mesh):
    return jax.shard_map(
        body,
        mesh=mesh,
        in_specs=(
            P(None, "dp", "seq", None),
            P(None, "dp", "seq", None),
            P("section", ("dp", "seq")),
            P("section", ("dp", "seq")),
            P("section", ("dp", "seq"), None),
            P("section", ("dp", "seq"), None),
            P("section", ("dp", "seq"), None),
            P("section", ("dp", "seq"), None),
            P("section", ("dp", "seq"), None),
            P("section", "dp", None, None),
            P("section", "dp", None, None),
            P("section", "dp", None, None),
            P("section", None, "dp", "seq", None),
        ),
        out_specs=(
            P("section", None, "dp", "seq", None),
            P("section", None, "dp", "seq", None),
            P("section", ("dp", "seq")),
            P("section", ("dp", "seq")),
            P("section", ("dp", "seq"), None),
            P("section", ("dp", "seq"), None),
            P("section", ("dp", "seq"), None),
            P("section", ("dp", "seq"), None),
            P("section", ("dp", "seq"), None),
            P("section", "dp", "seq", None),
            P("section", "dp", "seq", None),
            P("section", "dp", "seq", None),
        ),
        check_vma=False,
    )
```

profile of v0, /device:TPU:16, one launch (start us, length us, event | category | flops | bytes accessed | tf_op | source)
XLA Modules:
  0.0 4999.5 jit_solution(3065411672528064342)
XLA Ops:
  57.7 32.4 all-gather.5.cloned.1.call-done
  96.4 49.6 all-gather.7.cloned.1.call-done
  241.0 168.6 %all-to-all-done.4 = bf16[32,80,1536]{2,1,0:T(8,128)(2,1)} async-done(((bf16[32,80,1536]{2,1,0:T(8,128)(2,1)}), bf16[32,80,1536]{2,1,0:T(8,128)(2,1)}, u32[]{:S(2)}, u32[]{:S(2)}) %all-to-all-start.4) | async-done | bytes 7864352 | tf_op jit(solution)/shard_map/all_to_all | solution.py:78
  409.6 45.6 conditional.13
  475.2 182.7 %all_gather.27 = bf16[1,1536,32]{2,0,1:T(2,128)(2,1)S(1)} all-gather(bf16[1,96,32]{2,0,1:T(2,128)(2,1)S(1)} %copy.841), channel_id=1, replica_groups=mesh['section'=2,'dp'=4,'seq'=4] {'dp','seq'}, dimensions={1}, use_global_device_ids=true | all-gather | bytes 104448 | tf_op jit(solution)/shard_map/all_gather | solution.py:452
  862.3 168.8 %all-to-all-done.10 = bf16[32,80,1536]{2,1,0:T(8,128)(2,1)} async-done(((bf16[32,80,1536]{2,1,0:T(8,128)(2,1)}), bf16[32,80,1536]{2,1,0:T(8,128)(2,1)}, u32[]{:S(2)}, u32[]{:S(2)}) %all-to-all-start.10) | async-done | bytes 7864352 | tf_op jit(solution)/shard_map/all_to_all | solution.py:78
  1031.1 45.3 conditional.15
  1114.2 151.1 %all-to-all-done.11 = bf16[8,320,1536]{2,0,1:T(8,128)(2,1)} async-done(((bf16[8,320,1536]{2,0,1:T(8,128)(2,1)}), bf16[8,320,1536]{2,0,1:T(8,128)(2,1)}, u32[]{:S(2)}, u32[]{:S(2)}) %all-to-all-start.11) | async-done | bytes 7864352 | tf_op jit(solution)/shard_map/all_to_all | solution.py:82
  1490.0 121.3 %all-to-all-done.16 = bf16[32,80,1536]{2,1,0:T(8,128)(2,1)} async-done(((bf16[32,80,1536]{2,1,0:T(8,128)(2,1)}), bf16[32,80,1536]{2,1,0:T(8,128)(2,1)}, u32[]{:S(2)}, u32[]{:S(2)}) %all-to-all-start.16) | async-done | bytes 7864352 | tf_op jit(solution)/shard_map/all_to_all | solution.py:78
  1638.9 149.7 %all-to-all-done.18 = bf16[32,80,1536]{2,1,0:T(8,128)(2,1)} async-done(((bf16[32,80,1536]{2,1,0:T(8,128)(2,1)}), bf16[32,80,1536]{2,1,0:T(8,128)(2,1)}, u32[]{:S(2)}, u32[]{:S(2)}) %all-to-all-start.18) | async-done | bytes 7864352 | tf_op jit(solution)/shard_map/all_to_all | solution.py:78
  1824.9 140.6 %all-to-all-done.19 = bf16[32,80,1536]{2,1,0:T(8,128)(2,1)} async-done(((bf16[32,80,1536]{2,1,0:T(8,128)(2,1)}), bf16[32,80,1536]{2,1,0:T(8,128)(2,1)}, u32[]{:S(2)}, u32[]{:S(2)}) %all-to-all-start.19) | async-done | bytes 7864352 | tf_op jit(solution)/shard_map/all_to_all | solution.py:78
  2005.4 42.6 conditional.18
  2058.7 83.7 %all-to-all-done.17 = bf16[8,320,1536]{2,0,1:T(8,128)(2,1)} async-done(((bf16[8,320,1536]{2,0,1:T(8,128)(2,1)}), bf16[8,320,1536]{2,0,1:T(8,128)(2,1)}, u32[]{:S(2)}, u32[]{:S(2)}) %all-to-all-start.17) | async-done | bytes 7864352 | tf_op jit(solution)/shard_map/all_to_all | solution.py:82
  2211.5 108.3 %all-to-all-done.20 = bf16[8,320,1536]{2,0,1:T(8,128)(2,1)} async-done(((bf16[8,320,1536]{2,0,1:T(8,128)(2,1)}), bf16[8,320,1536]{2,0,1:T(8,128)(2,1)}, u32[]{:S(2)}, u32[]{:S(2)}) %all-to-all-start.20) | async-done | bytes 7864352 | tf_op jit(solution)/shard_map/all_to_all | solution.py:82
  2458.7 115.7 %collective-permute-done.2 = bf16[256,1536]{1,0:T(8,128)(2,1)S(1)} collective-permute-done((bf16[256,1536]{1,0:T(8,128)(2,1)S(1)}, bf16[256,1536]{1,0:T(8,128)(2,1)S(1)}, u32[]{:S(2)}, u32[]{:S(2)}) %collective-permute-start.2) | collective-permute-done | bytes 786464 | tf_op jit(solution)/shard_map/ppermute | solution.py:30
  2622.9 168.6 %all-to-all-done.25 = bf16[32,80,1536]{2,1,0:T(8,128)(2,1)} async-done(((bf16[32,80,1536]{2,1,0:T(8,128)(2,1)}), bf16[32,80,1536]{2,1,0:T(8,128)(2,1)}, u32[]{:S(2)}, u32[]{:S(2)}) %all-to-all-start.25) | async-done | bytes 7864352 | tf_op jit(solution)/shard_map/all_to_all | solution.py:78
  2791.6 156.3 %conditional.20 = (bf16[8,320,1536]{2,1,0:T(8,128)(2,1)}, f32[8,512,1536]{2,1,0:T(8,128)}, f32[8,1536,512]{2,1,0:T(8,128)}, f32[8,1536,512]{2,1,0:T(8,128)}) conditional(s32[]{:T(128)} %convert_element_type.775, () %tuple.230, (bf16[8,4,80,1536]{3,2,0,1:T(8,128)(2,1)}, bf16[8,512,1536]{2,1,0:T(8,128)(2,1)}, f32[3,8,320,512]{3,2,1,0:T(8,128)}, ...), branch_computations={%region_78.80_spmd, %region_79.81_spmd} | conditional | flops 24191959040 | bytes 352846368 | solution.py:355
  2972.4 163.5 %all-to-all-done.27 = bf16[8,320,1536]{2,0,1:T(8,128)(2,1)} async-done(((bf16[8,320,1536]{2,0,1:T(8,128)(2,1)}), bf16[8,320,1536]{2,0,1:T(8,128)(2,1)}, u32[]{:S(2)}, u32[]{:S(2)}) %all-to-all-start.27) | async-done | bytes 7864352 | tf_op jit(solution)/shard_map/all_to_all | solution.py:82
  3192.8 53.0 %conditional.21 = (bf16[1024,384]{0,1:T(8,128)(2,1)}, bf16[1024,128]{0,1:T(8,128)(2,1)}, bf16[1024,128]{0,1:T(8,128)(2,1)}) conditional(s32[]{:T(128)} %convert_element_type.775, () %tuple.229, (bf16[3,1024,2,64]{1,3,2,0:T(8,128)(2,1)}, s32[]{:T(128)}, bf16[3,1024,2,3,64]{1,4,3,2,0:T(8,128)(2,1)}, f32[3,2,2,3,512]{4,3,2,1,0:T(4,128)}, ...), branch_computations={%region_83.85_spmd, %region_84.88_spmd} | conditional | flops 3095751168 | bytes 181453344 | solution.py:273
  3318.7 115.4 %collective-permute-done.3 = bf16[256,1536]{1,0:T(8,128)(2,1)S(1)} collective-permute-done((bf16[256,1536]{1,0:T(8,128)(2,1)S(1)}, bf16[256,1536]{1,0:T(8,128)(2,1)S(1)}, u32[]{:S(2)}, u32[]{:S(2)}) %collective-permute-start.3) | collective-permute-done | bytes 786464 | tf_op jit(solution)/shard_map/ppermute | solution.py:30
  3482.6 168.6 %all-to-all-done.32 = bf16[32,80,1536]{2,1,0:T(8,128)(2,1)} async-done(((bf16[32,80,1536]{2,1,0:T(8,128)(2,1)}), bf16[32,80,1536]{2,1,0:T(8,128)(2,1)}, u32[]{:S(2)}, u32[]{:S(2)}) %all-to-all-start.32) | async-done | bytes 7864352 | tf_op jit(solution)/shard_map/all_to_all | solution.py:78
  3651.2 164.4 %conditional.22 = (bf16[8,320,1536]{2,1,0:T(8,128)(2,1)}, f32[8,512,1536]{2,1,0:T(8,128)}, f32[8,1536,512]{2,1,0:T(8,128)}, f32[8,1536,512]{2,1,0:T(8,128)}) conditional(s32[]{:T(128)} %convert_element_type.789, () %tuple.234, (bf16[8,4,80,1536]{3,2,0,1:T(8,128)(2,1)}, bf16[8,512,1536]{2,1,0:T(8,128)(2,1)}, f32[3,8,320,512]{3,2,1,0:T(8,128)}, ...), branch_computations={%region_97.99_spmd, %region_98.100_spmd} | conditional | flops 24191959040 | bytes 352846368 | solution.py:355
  3839.8 163.5 %all-to-all-done.34 = bf16[8,320,1536]{2,0,1:T(8,128)(2,1)} async-done(((bf16[8,320,1536]{2,0,1:T(8,128)(2,1)}), bf16[8,320,1536]{2,0,1:T(8,128)(2,1)}, u32[]{:S(2)}, u32[]{:S(2)}) %all-to-all-start.34) | async-done | bytes 7864352 | tf_op jit(solution)/shard_map/all_to_all | solution.py:82
  4060.5 50.9 %conditional.23 = (bf16[1024,384]{0,1:T(8,128)(2,1)}, bf16[1024,128]{0,1:T(8,128)(2,1)}, bf16[1024,128]{0,1:T(8,128)(2,1)}) conditional(s32[]{:T(128)} %convert_element_type.789, () %tuple.233, (bf16[3,1024,2,64]{1,3,2,0:T(8,128)(2,1)}, s32[]{:T(128)}, bf16[3,1024,2,3,64]{1,4,3,2,0:T(8,128)(2,1)}, f32[3,2,2,3,512]{4,3,2,1,0:T(4,128)}, ...), branch_computations={%region_102.104_spmd, %region_103.107_spmd} | conditional | flops 3095751168 | bytes 178831872 | solution.py:273
  4157.6 29.6 fusion.266
  4316.7 100.4 %reduce-scatter.29.cloned.1.call-done = bf16[1,8,128,1536]{3,2,1,0:T(8,128)(2,1)} async-done(((bf16[1,8,512,1536]{3,2,1,0:T(8,128)(2,1)}), bf16[1,8,128,1536]{3,2,1,0:T(8,128)(2,1)}) %reduce-scatter.29.cloned.1.call-update) | async-done | bytes 3145744 | tf_op jit(solution)/shard_map/reduce_scatter | solution.py:537
  4422.6 96.4 %reduce-scatter.27.cloned.1.call-done = bf16[1,8,384,512]{3,2,1,0:T(8,128)(2,1)} async-done(((bf16[1,8,1536,512]{3,2,1,0:T(8,128)(2,1)}), bf16[1,8,384,512]{3,2,1,0:T(8,128)(2,1)}) %reduce-scatter.27.cloned.1.call-update) | async-done | bytes 3145744 | tf_op jit(solution)/shard_map/reduce_scatter | solution.py:534
  4524.5 96.2 %reduce-scatter.25.cloned.1.call-done = bf16[1,8,384,512]{3,2,1,0:T(8,128)(2,1)} async-done(((bf16[1,8,1536,512]{3,2,1,0:T(8,128)(2,1)}), bf16[1,8,384,512]{3,2,1,0:T(8,128)(2,1)}) %reduce-scatter.25.cloned.1.call-update) | async-done | bytes 3145744 | tf_op jit(solution)/shard_map/reduce_scatter | solution.py:531
  4626.2 64.5 %reduce-scatter.19.cloned.1.call-done = f32[1,96,512]{2,1,0:T(8,128)} async-done(((f32[1,1536,512]{2,1,0:T(8,128)}), f32[1,96,512]{2,1,0:T(8,128)}) %reduce-scatter.19.cloned.1.call-update) | async-done | bytes 196624 | tf_op jit(solution)/shard_map/reduce_scatter | solution.py:525
  4690.7 70.0 %reduce-scatter.21.cloned.1.call-done = f32[1,96,512]{2,1,0:T(8,128)} async-done(((f32[1,1536,512]{2,1,0:T(8,128)}), f32[1,96,512]{2,1,0:T(8,128)}) %reduce-scatter.21.cloned.1.call-update) | async-done | bytes 196624 | tf_op jit(solution)/shard_map/reduce_scatter | solution.py:526
  4760.6 116.4 %reduce-scatter.23.cloned.1.call-done = f32[1,96,1536]{2,1,0:T(8,128)} async-done(((f32[1,1536,1536]{2,1,0:T(8,128)}), f32[1,96,1536]{2,1,0:T(8,128)}) %reduce-scatter.23.cloned.1.call-update) | async-done | bytes 589840 | tf_op jit(solution)/shard_map/reduce_scatter | solution.py:527
  4877.1 115.7 %reduce-scatter.17.cloned.1.call-done = f32[1,96,1536]{2,1,0:T(8,128)} async-done(((f32[1,1536,1536]{2,1,0:T(8,128)}), f32[1,96,1536]{2,1,0:T(8,128)}) %reduce-scatter.17.cloned.1.call-update) | async-done | bytes 589840 | tf_op jit(solution)/shard_map/reduce_scatter | solution.py:524
  (1038 shorter events, 2072.1 us)
Async XLA Ops:
  7.2 43.9 all-gather.9.cloned.1.call-start
  7.9 82.2 %all-gather.5.cloned.1.call-start = ((), (), s32[]{:S(2)}) async-start(), calls=%async_computation.49 | async-start | bytes 1671168 | tf_op jit(solution)/shard_map/all_gather | solution.py:449
  8.7 137.3 %all-gather.7.cloned.1.call-start = ((), (), s32[]{:S(2)}) async-start(), calls=%async_computation.50 | async-start | bytes 5013504 | tf_op jit(solution)/shard_map/all_gather | solution.py:448
  9.4 204.6 %all-gather.11.cloned.1.call-start = ((), (), s32[]{:S(2)}) async-start(), calls=%async_computation.52 | async-start | bytes 5013504 | tf_op jit(solution)/shard_map/all_gather | solution.py:451
  93.0 57.8 %all-to-all-start = ((bf16[256,4,128]{2,0,1:T(8,128)(2,1)}), bf16[256,4,128]{2,0,1:T(8,128)(2,1)S(1)}, u32[]{:S(2)}, u32[]{:S(2)}) async-start(bf16[256,4,128]{2,0,1:T(8,128)(2,1)} %bitcast.1627), calls=%async_computation | async-start | bytes 524288 | tf_op jit(solution)/shard_map/all_to_all | solution.py:291
  234.1 175.5 %all-to-all-start.4 = ((bf16[32,80,1536]{2,1,0:T(8,128)(2,1)}), bf16[32,80,1536]{2,1,0:T(8,128)(2,1)}, u32[]{:S(2)}, u32[]{:S(2)}) async-start(bf16[32,80,1536]{2,1,0:T(8,128)(2,1)} %bitcast.1696), calls=%async_computation.4 | async-start | bytes 15728640 | tf_op jit(solution)/shard_map/all_to_all | solution.py:78
  465.9 210.4 %all-to-all-start.5 = ((bf16[8,320,1536]{2,0,1:T(8,128)(2,1)}), bf16[8,320,1536]{2,0,1:T(8,128)(2,1)}, u32[]{:S(2)}, u32[]{:S(2)}) async-start(bf16[8,320,1536]{2,0,1:T(8,128)(2,1)} %copy.849), calls=%async_computation.5 | async-start | bytes 15728640 | tf_op jit(solution)/shard_map/all_to_all | solution.py:82
  856.4 174.7 %all-to-all-start.10 = ((bf16[32,80,1536]{2,1,0:T(8,128)(2,1)}), bf16[32,80,1536]{2,1,0:T(8,128)(2,1)}, u32[]{:S(2)}, u32[]{:S(2)}) async-start(bf16[32,80,1536]{2,1,0:T(8,128)(2,1)} %bitcast.1697), calls=%async_computation.10 | async-start | bytes 15728640 | tf_op jit(solution)/shard_map/all_to_all | solution.py:78
  1087.1 178.1 %all-to-all-start.11 = ((bf16[8,320,1536]{2,0,1:T(8,128)(2,1)}), bf16[8,320,1536]{2,0,1:T(8,128)(2,1)}, u32[]{:S(2)}, u32[]{:S(2)}) async-start(bf16[8,320,1536]{2,0,1:T(8,128)(2,1)} %copy.867), calls=%async_computation.11 | async-start | bytes 15728640 | tf_op jit(solution)/shard_map/all_to_all | solution.py:82
  1433.4 177.9 %all-to-all-start.16 = ((bf16[32,80,1536]{2,1,0:T(8,128)(2,1)}), bf16[32,80,1536]{2,1,0:T(8,128)(2,1)}, u32[]{:S(2)}, u32[]{:S(2)}) async-start(bf16[32,80,1536]{2,1,0:T(8,128)(2,1)} %bitcast.1689), calls=%async_computation.16 | async-start | bytes 15728640 | tf_op jit(solution)/shard_map/all_to_all | solution.py:78
  1611.3 177.3 %all-to-all-start.18 = ((bf16[32,80,1536]{2,1,0:T(8,128)(2,1)}), bf16[32,80,1536]{2,1,0:T(8,128)(2,1)}, u32[]{:S(2)}, u32[]{:S(2)}) async-start(bf16[32,80,1536]{2,1,0:T(8,128)(2,1)} %bitcast.1693), calls=%async_computation.18 | async-start | bytes 15728640 | tf_op jit(solution)/shard_map/all_to_all | solution.py:78
  1788.6 176.9 %all-to-all-start.19 = ((bf16[32,80,1536]{2,1,0:T(8,128)(2,1)}), bf16[32,80,1536]{2,1,0:T(8,128)(2,1)}, u32[]{:S(2)}, u32[]{:S(2)}) async-start(bf16[32,80,1536]{2,1,0:T(8,128)(2,1)} %bitcast.1692), calls=%async_computation.19 | async-start | bytes 15728640 | tf_op jit(solution)/shard_map/all_to_all | solution.py:78
  1965.5 176.9 %all-to-all-start.17 = ((bf16[8,320,1536]{2,0,1:T(8,128)(2,1)}), bf16[8,320,1536]{2,0,1:T(8,128)(2,1)}, u32[]{:S(2)}, u32[]{:S(2)}) async-start(bf16[8,320,1536]{2,0,1:T(8,128)(2,1)} %copy.887), calls=%async_computation.17 | async-start | bytes 15728640 | tf_op jit(solution)/shard_map/all_to_all | solution.py:82
  2142.3 177.4 %all-to-all-start.20 = ((bf16[8,320,1536]{2,0,1:T(8,128)(2,1)}), bf16[8,320,1536]{2,0,1:T(8,128)(2,1)}, u32[]{:S(2)}, u32[]{:S(2)}) async-start(bf16[8,320,1536]{2,0,1:T(8,128)(2,1)} %copy.901), calls=%async_computation.20 | async-start | bytes 15728640 | tf_op jit(solution)/shard_map/all_to_all | solution.py:82
  2435.3 178.5 %all-to-all-start.26 = ((bf16[32,80,1536]{2,1,0:T(8,128)(2,1)}), bf16[32,80,1536]{2,1,0:T(8,128)(2,1)}, u32[]{:S(2)}, u32[]{:S(2)}) async-start(bf16[32,80,1536]{2,1,0:T(8,128)(2,1)} %bitcast.1691), calls=%async_computation.26 | async-start | bytes 15728640 | tf_op jit(solution)/shard_map/all_to_all | solution.py:78
  2457.1 117.2 %collective-permute-start.2 = (bf16[256,1536]{1,0:T(8,128)(2,1)S(1)}, bf16[256,1536]{1,0:T(8,128)(2,1)S(1)}, u32[]{:S(2)}, u32[]{:S(2)}) collective-permute-start(bf16[256,1536]{1,0:T(8,128)(2,1)S(1)} %get-tuple-element.1204), channel_id=1, source_target_pairs={{16,0},{17,1},{18,2},{19,3},{20,4},{21,5},{22,6},{23,7},{24,8},{25... | collective-permute-start | bytes 2359304 | tf_op jit(solution)/shard_map/ppermute | solution.py:30
  2613.9 177.7 %all-to-all-start.25 = ((bf16[32,80,1536]{2,1,0:T(8,128)(2,1)}), bf16[32,80,1536]{2,1,0:T(8,128)(2,1)}, u32[]{:S(2)}, u32[]{:S(2)}) async-start(bf16[32,80,1536]{2,1,0:T(8,128)(2,1)} %bitcast.1695), calls=%async_computation.25 | async-start | bytes 15728640 | tf_op jit(solution)/shard_map/all_to_all | solution.py:78
  2958.5 177.3 %all-to-all-start.27 = ((bf16[8,320,1536]{2,0,1:T(8,128)(2,1)}), bf16[8,320,1536]{2,0,1:T(8,128)(2,1)}, u32[]{:S(2)}, u32[]{:S(2)}) async-start(bf16[8,320,1536]{2,0,1:T(8,128)(2,1)} %copy.922), calls=%async_computation.27 | async-start | bytes 15728640 | tf_op jit(solution)/shard_map/all_to_all | solution.py:82
  3295.4 178.3 %all-to-all-start.33 = ((bf16[32,80,1536]{2,1,0:T(8,128)(2,1)}), bf16[32,80,1536]{2,1,0:T(8,128)(2,1)}, u32[]{:S(2)}, u32[]{:S(2)}) async-start(bf16[32,80,1536]{2,1,0:T(8,128)(2,1)} %bitcast.1690), calls=%async_computation.33 | async-start | bytes 15728640 | tf_op jit(solution)/shard_map/all_to_all | solution.py:78
  3316.9 117.2 %collective-permute-start.3 = (bf16[256,1536]{1,0:T(8,128)(2,1)S(1)}, bf16[256,1536]{1,0:T(8,128)(2,1)S(1)}, u32[]{:S(2)}, u32[]{:S(2)}) collective-permute-start(bf16[256,1536]{1,0:T(8,128)(2,1)S(1)} %get-tuple-element.1200), channel_id=1, source_target_pairs={{16,0},{17,1},{18,2},{19,3},{20,4},{21,5},{22,6},{23,7},{24,8},{25... | collective-permute-start | bytes 2359304 | tf_op jit(solution)/shard_map/ppermute | solution.py:30
  3473.7 177.5 %all-to-all-start.32 = ((bf16[32,80,1536]{2,1,0:T(8,128)(2,1)}), bf16[32,80,1536]{2,1,0:T(8,128)(2,1)}, u32[]{:S(2)}, u32[]{:S(2)}) async-start(bf16[32,80,1536]{2,1,0:T(8,128)(2,1)} %bitcast.1694), calls=%async_computation.32 | async-start | bytes 15728640 | tf_op jit(solution)/shard_map/all_to_all | solution.py:78
  3826.3 177.1 %all-to-all-start.34 = ((bf16[8,320,1536]{2,0,1:T(8,128)(2,1)}), bf16[8,320,1536]{2,0,1:T(8,128)(2,1)}, u32[]{:S(2)}, u32[]{:S(2)}) async-start(bf16[8,320,1536]{2,0,1:T(8,128)(2,1)} %copy.943), calls=%async_computation.34 | async-start | bytes 15728640 | tf_op jit(solution)/shard_map/all_to_all | solution.py:82
  4135.6 155.3 %reduce-scatter.35.cloned.1.call-start = ((), (), s32[]{:S(2)}) async-start(), calls=%async_computation.62 | async-start | bytes 835584
  4137.7 154.7 %reduce-scatter.33.cloned.1.call-start = ((), (), s32[]{:S(2)}) async-start(), calls=%async_computation.61 | async-start | bytes 835584
  4139.0 176.4 %reduce-scatter.31.cloned.1.call-start = ((), (), s32[]{:S(2)}) async-start(), calls=%async_computation.60 | async-start | bytes 835584
  4157.5 259.6 %reduce-scatter.29.cloned.1.call-start = ((), (), s32[]{:S(2)}) async-start(), calls=%async_computation.59 | async-start | bytes 15728640 | tf_op jit(solution)/shard_map/reduce_scatter | solution.py:537
  4187.2 331.8 %reduce-scatter.27.cloned.1.call-start = ((), (), s32[]{:S(2)}) async-start(), calls=%async_computation.58 | async-start | bytes 15728640 | tf_op jit(solution)/shard_map/reduce_scatter | solution.py:534
  4216.9 403.8 %reduce-scatter.25.cloned.1.call-start = ((), (), s32[]{:S(2)}) async-start(), calls=%async_computation.57 | async-start | bytes 15728640 | tf_op jit(solution)/shard_map/reduce_scatter | solution.py:531
  4246.4 444.3 %reduce-scatter.19.cloned.1.call-start = ((), (), s32[]{:S(2)}) async-start(), calls=%async_computation.54 | async-start | bytes 3342336 | tf_op jit(solution)/shard_map/reduce_scatter | solution.py:525
  4253.4 507.2 %reduce-scatter.21.cloned.1.call-start = ((), (), s32[]{:S(2)}) async-start(), calls=%async_computation.55 | async-start | bytes 3342336 | tf_op jit(solution)/shard_map/reduce_scatter | solution.py:526
  4257.4 619.7 %reduce-scatter.23.cloned.1.call-start = ((), (), s32[]{:S(2)}) async-start(), calls=%async_computation.56 | async-start | bytes 10027008 | tf_op jit(solution)/shard_map/reduce_scatter | solution.py:527
  4267.1 725.6 %reduce-scatter.17.cloned.1.call-start = ((), (), s32[]{:S(2)}) async-start(), calls=%async_computation.53 | async-start | bytes 10027008 | tf_op jit(solution)/shard_map/reduce_scatter | solution.py:524
  (230 other events, 4754.1 us)
Sparse Core Ops, SparseCore 0:
  10.3 39.1 all-gather.8
  51.8 38.3 all-gather.4
  92.5 53.4 all-gather.6
  148.1 54.5 all-gather.10
  4139.7 57.0 reduce-scatter.34
  4200.6 55.5 reduce-scatter.32
  4259.8 55.5 reduce-scatter.30
  4318.1 99.0 reduce-scatter.28
  4419.9 99.0 reduce-scatter.26
  4521.6 99.0 reduce-scatter.24
  4625.6 65.0 reduce-scatter.18
  4695.4 65.1 reduce-scatter.20
  4765.9 111.1 reduce-scatter.22
  4881.6 111.1 reduce-scatter.16
where the time goes:
time: 5020 us; the launch traced here: 5000 us
  waiting for transfers between devices  2940 us (59%)
  local copies, waits for them, and re-layouts  719 us (14%)
  matrix products  446 us (9%)
  other arithmetic  400 us (8%)
  starting transfers between devices  231 us (5%)
  blocking collectives  207 us (4%)
    all_to_all x9, waiting for transfers between devices, to_owners(): return lax.all_to_all(buffer, 'dp', split_axis=0, concat_axis=1, tiled=True)  1130 us
    all_to_all x6, waiting for transfers between devices, to_sources(): return lax.all_to_all(buffer, 'dp', split_axis=1, concat_axis=0, tiled=True)  670 us
    ppermute x4, waiting for transfers between devices, passed_along(): return lax.ppermute(block, axis, route)  274 us
    all_gather x1, blocking collectives, body(): lax.all_gather(router_matrix, ('dp', 'seq'), axis=1, tiled=True)  183 us
    cond x7, local copies, waits for them, and re-layouts, backward_layer(): lax.cond(active, expert_backward, expert_rest, slot_rows, grad_rows, save...  131 us
    reduce_scatter x1, waiting for transfers between devices, body(): lax.psum_scatter(dense_acc[5][None], ('dp', 'seq'), scatter_dimension=1,...  116 us
    reduce_scatter x1, waiting for transfers between devices, body(): lax.psum_scatter(dense_acc[2][None], ('dp', 'seq'), scatter_dimension=1,...  116 us
    reduce_scatter x1, waiting for transfers between devices, body(): lax.psum_scatter(expert_acc[2][None].astype(jnp.bfloat16), 'seq', scatter...  100 us
  transfers between devices with their start and end apart: 57, of which 46 were waited for; matrix products, arithmetic and copies ran while one was open for 14% of the time, Pallas kernels for 0%

commit v1 on v0

v1 whole, which is shorter than its diff:
```python
from functools import partial

import jax
import jax.numpy as jnp
from jax import lax
from jax.sharding import PartitionSpec as P

HEADS = 24
KV_HEADS = 8
HEAD_DIM = 64
TOP_K = 8
EXPERTS = 32
CAP = 80
GROUP = HEADS // KV_HEADS
TOKENS = ("dp", "seq")

epsilon = 1e-06


def dot(a, b):
    return jnp.dot(a, b, preferred_element_type=jnp.float32)


def dot_t(a, b):
    return lax.dot_general(a, b, (((1,), (1,)), ((), ())), preferred_element_type=jnp.float32)


def t_dot(a, b):
    return lax.dot_general(a, b, (((0,), (0,)), ((), ())), preferred_element_type=jnp.float32)


def low(v):
    return v.astype(jnp.bfloat16)


def swap(block):
    return lax.ppermute(block, "section", [(0, 1), (1, 0)])


def pass_to(block, section):
    return lax.ppermute(block, "section", [(1 - section, section)])


def rms_norm(values, norm_gain):
    return (
        values * lax.rsqrt(jnp.mean(values * values, axis=-1, keepdims=True) + epsilon) * norm_gain
    )


def rotary_tables(length):
    half_dim = HEAD_DIM // 2
    frequency = 10000.0 ** (-jnp.arange(half_dim, dtype=jnp.float32) * 2.0 / HEAD_DIM)
    angles = jnp.arange(length, dtype=jnp.float32)[:, None] * frequency[None, :]
    return (jnp.cos(angles)[:, None, :], jnp.sin(angles)[:, None, :])


def rotate(values, cos_table, sin_table):
    length = values.shape[0]
    split_heads = values.reshape(length, -1, HEAD_DIM)
    first_half = split_heads[..., : HEAD_DIM // 2]
    second_half = split_heads[..., HEAD_DIM // 2 :]
    turned = jnp.concatenate(
        [
            first_half * cos_table - second_half * sin_table,
            second_half * cos_table + first_half * sin_table,
        ],
        axis=-1,
    )
    return turned.reshape(length, -1)


def attention_forward(q_heads, k_heads, v_heads):
    length = q_heads.shape[0]
    local_kv = k_heads.shape[1] // HEAD_DIM
    cos_table, sin_table = rotary_tables(length)
    q_rot = low(rotate(q_heads.astype(jnp.float32), cos_table, sin_table)).reshape(
        length, local_kv, GROUP, HEAD_DIM
    )
    k_rot = low(rotate(k_heads.astype(jnp.float32), cos_table, sin_table)).reshape(
        length, local_kv, HEAD_DIM
    )
    values = v_heads.reshape(length, local_kv, HEAD_DIM)
    block_rows = min(512, length)
    outputs = []
    totals_list = []
    for first_row in range(0, length, block_rows):
        key_end = first_row + block_rows
        scores = (
            jnp.einsum(
                "qhgd,khd->hgqk",
                q_rot[first_row:key_end],
                k_rot[:key_end],
                preferred_element_type=jnp.float32,
            )
            * 0.125
        )
        causal = (first_row + jnp.arange(block_rows, dtype=jnp.int32))[:, None] >= jnp.arange(
            key_end, dtype=jnp.int32
        )[None, :]
        scores = jnp.where(causal, scores, -jnp.inf)
        row_peak = jnp.max(scores, axis=-1, keepdims=True)
        exponents = jnp.exp(scores - row_peak)
        totals = jnp.sum(exponents, axis=-1, keepdims=True)
        attended = jnp.einsum(
            "hgqk,khd->qhgd",
            low(exponents / totals),
            values[:key_end],
            preferred_element_type=jnp.float32,
        )
        outputs.append(low(attended).reshape(block_rows, -1))
        totals_list.append((row_peak + jnp.log(totals))[..., 0])
    return (jnp.concatenate(outputs, axis=0), jnp.stack(totals_list), q_rot, k_rot, values)


def attention_backward(head_grad, q_rot, k_rot, values, log_total):
    length, local_kv = q_rot.shape[:2]
    cos_table, sin_table = rotary_tables(length)
    block_rows = min(512, length)
    grad_rows = head_grad.reshape(length, local_kv, GROUP, HEAD_DIM)
    key_acc = jnp.zeros((length, local_kv, HEAD_DIM), jnp.float32)
    value_acc = jnp.zeros((length, local_kv, HEAD_DIM), jnp.float32)
    query_parts = []
    for block_number, first_row in enumerate(range(0, length, block_rows)):
        key_end = first_row + block_rows
        q_block = q_rot[first_row:key_end]
        grad_block = grad_rows[first_row:key_end]
        key_part = k_rot[:key_end]
        scores = (
            jnp.einsum("qhgd,khd->hgqk", q_block, key_part, preferred_element_type=jnp.float32)
            * 0.125
        )
        causal = (first_row + jnp.arange(block_rows, dtype=jnp.int32))[:, None] >= jnp.arange(
            key_end, dtype=jnp.int32
        )[None, :]
        scores = jnp.where(causal, scores, -jnp.inf)
        probs_full = jnp.exp(scores - log_total[block_number][..., None])
        prob_grad = jnp.einsum(
            "qhgd,khd->hgqk", grad_block, values[:key_end], preferred_element_type=jnp.float32
        )
        score_grad = probs_full * (
            prob_grad - jnp.sum(probs_full * prob_grad, axis=-1, keepdims=True)
        )
        score_low = low(score_grad)
        query_parts.append(
            jnp.einsum("hgqk,khd->qhgd", score_low, key_part, preferred_element_type=jnp.float32)
            * 0.125
        )
        key_acc = key_acc.at[:key_end].add(
            jnp.einsum("hgqk,qhgd->khd", score_low, q_block, preferred_element_type=jnp.float32)
            * 0.125
        )
        value_acc = value_acc.at[:key_end].add(
            jnp.einsum(
                "hgqk,qhgd->khd", low(probs_full), grad_block, preferred_element_type=jnp.float32
            )
        )
    query_all = jnp.concatenate(query_parts, axis=0).reshape(length, -1)
    query_grad = rotate(query_all, cos_table, -sin_table)
    key_grad = rotate(key_acc.reshape(length, -1), cos_table, -sin_table)
    return jnp.concatenate(
        [low(query_grad), low(key_grad), low(value_acc).reshape(length, -1)], axis=1
    )


def token_choice(route):
    return route[..., None] == jnp.arange(EXPERTS, dtype=jnp.int32)


def routing(route_all, first_expert, count):
    chosen = jnp.any(token_choice(route_all), axis=2)
    mine = lax.dynamic_slice_in_dim(chosen, first_expert, count, axis=2)
    rows = mine.shape[1]
    earlier = jnp.tril(jnp.ones((rows, rows), jnp.bfloat16), -1)
    place = jnp.einsum(
        "ts,bsj->bjt", earlier, mine.astype(jnp.bfloat16), preferred_element_type=jnp.float32
    ).astype(jnp.int32)
    mine = jnp.transpose(mine, (0, 2, 1))
    slots = jnp.arange(CAP, dtype=jnp.int32)
    pick = (place[:, :, None, :] == slots[None, None, :, None]) & mine[:, :, None, :]
    return chosen, pick


def choose(pick, rows):
    picked = jnp.einsum("bct,btd->bcd", low(pick), rows, preferred_element_type=jnp.float32)
    return low(picked).reshape(-1, rows.shape[-1])


def give_back(picks, slot_rows):
    total = 0.0
    for pick, rows in zip(picks, slot_rows):
        blocks, count = pick.shape[:2]
        total = total + jnp.einsum(
            "bct,bcd->btd",
            low(pick),
            rows.reshape(blocks, count, -1),
            preferred_element_type=jnp.float32,
        )
    return total.reshape(-1, total.shape[-1])


def slot_values(pick, values):
    return jnp.sum(jnp.where(pick, values[:, None, :], 0.0), axis=2).reshape(-1, 1)


def forward_layer(layer_in, route_all, weights, experts, first_expert):
    attn_scale, ffn_scale, qkv_w, out_w, router_w = weights
    gate_w, up_w, down_w = experts
    count = gate_w.shape[0]
    normed_input = low(rms_norm(layer_in, attn_scale))
    normed_all = lax.all_gather(normed_input, "seq", axis=0, tiled=True)
    qkv = low(dot(normed_all, qkv_w))
    kv_width = KV_HEADS * HEAD_DIM // lax.axis_size("seq")
    q_width = GROUP * kv_width
    mixed, log_total, q_rot, k_rot, v_heads = attention_forward(
        qkv[:, :q_width], qkv[:, q_width : q_width + kv_width], qkv[:, q_width + kv_width :]
    )
    branch = lax.psum_scatter(low(dot(mixed, out_w)), "seq", scatter_dimension=0, tiled=True)
    after_update = layer_in + branch.astype(jnp.float32)
    normed_ffn = low(rms_norm(after_update, ffn_scale))
    ffn_all = lax.all_gather(normed_ffn, TOKENS, axis=0, tiled=True)
    chosen, pick = routing(route_all, first_expert, count)
    blocks, rows = chosen.shape[:2]
    logits = dot(ffn_all, router_w).reshape(blocks, rows, EXPERTS)
    logits = jnp.where(chosen, logits, -jnp.inf)
    gates = jax.nn.softmax(logits, axis=-1)
    mine = jnp.transpose(
        lax.dynamic_slice_in_dim(gates, first_expert, count, axis=2), (0, 2, 1)
    )
    ffn_blocks = ffn_all.reshape(blocks, rows, -1)
    results = []
    saved_experts = []
    for j in range(count):
        slot_rows = choose(pick[:, j], ffn_blocks)
        slot_gates = slot_values(pick[:, j], mine[:, j])
        gate_pre = dot(slot_rows, gate_w[j])
        up_pre = dot(slot_rows, up_w[j])
        hidden = jax.nn.silu(gate_pre) * up_pre
        scaled = low(slot_gates * hidden)
        results.append(low(dot(scaled, down_w[j])))
        saved_experts.append((slot_rows, slot_gates, gate_pre, up_pre, scaled))
    moe = give_back([pick[:, j] for j in range(count)], results)
    moe = lax.psum_scatter(low(moe), TOKENS, scatter_dimension=0, tiled=True)
    layer_out = after_update + moe.astype(jnp.float32)
    own_block = lax.axis_index("dp") * lax.axis_size("seq") + lax.axis_index("seq")
    own_gates = lax.dynamic_index_in_dim(gates, own_block, 0, keepdims=False)
    saved = (
        layer_in,
        normed_all,
        q_rot,
        k_rot,
        v_heads,
        log_total,
        mixed,
        after_update,
        normed_ffn,
        own_gates,
        pick,
        saved_experts,
    )
    return (layer_out, saved)


def backward_layer(layer_grad, saved, weights, experts):
    attn_scale, ffn_scale, qkv_w, out_w, router_w = weights
    gate_w, up_w, down_w = experts
    count = gate_w.shape[0]
    (
        layer_in,
        normed_all,
        q_rot,
        k_rot,
        v_heads,
        log_total,
        mixed,
        after_update,
        normed_ffn,
        own_gates,
        pick,
        saved_experts,
    ) = saved
    blocks, _, _, rows = pick.shape
    grad_all = lax.all_gather(low(layer_grad), TOKENS, axis=0, tiled=True)
    grad_blocks = grad_all.reshape(blocks, rows, -1)
    input_rows = []
    gate_terms = []
    expert_grads = ([], [], [])
    for j in range(count):
        slot_rows, slot_gates, gate_pre, up_pre, scaled = saved_experts[j]
        slot_grads = choose(pick[:, j], grad_blocks)
        plain_grad = dot_t(slot_grads, down_w[j])
        sigmoid = jax.nn.sigmoid(gate_pre)
        activated = gate_pre * sigmoid
        gate_term = jnp.sum(plain_grad * (activated * up_pre), axis=1).reshape(blocks, 1, -1)
        gate_terms.append(jnp.sum(jnp.where(pick[:, j], gate_term.reshape(blocks, -1, 1), 0.0), 1))
        hidden_grad = slot_gates * plain_grad
        gate_low = low(hidden_grad * up_pre * sigmoid * (1.0 + gate_pre * (1.0 - sigmoid)))
        up_low = low(hidden_grad * activated)
        input_rows.append(low(dot_t(gate_low, gate_w[j]) + dot_t(up_low, up_w[j])))
        expert_grads[0].append(low(t_dot(slot_rows, gate_low)))
        expert_grads[1].append(low(t_dot(slot_rows, up_low)))
        expert_grads[2].append(low(t_dot(scaled, slot_grads)))
    expert_grads = tuple(jnp.stack(parts) for parts in expert_grads)
    normed_grad = give_back([pick[:, j] for j in range(count)], input_rows)
    normed_grad = lax.psum_scatter(low(normed_grad), TOKENS, scatter_dimension=0, tiled=True)
    gate_terms = jnp.stack(gate_terms, axis=1)
    gate_terms = lax.all_to_all(gate_terms, TOKENS, split_axis=0, concat_axis=0, tiled=True)
    split = EXPERTS // (blocks * count) if blocks * count < EXPERTS else 1
    gate_terms = gate_terms.reshape(-1, rows)
    if gate_terms.shape[0] > EXPERTS:
        gate_terms = jnp.sum(gate_terms.reshape(EXPERTS, -1, rows), axis=1)
    gate_terms = gate_terms.T
    logit_grad = low(
        own_gates * (gate_terms - jnp.sum(own_gates * gate_terms, axis=-1, keepdims=True))
    )
    router_grad = t_dot(normed_ffn, logit_grad)
    normed_grad = normed_grad.astype(jnp.float32) + dot_t(logit_grad, router_w)
    after_part, ffn_gain_grad = jax.vjp(rms_norm, after_update, ffn_scale)[1](normed_grad)
    after_grad = after_part + layer_grad
    branch_all = lax.all_gather(low(after_grad), "seq", axis=0, tiled=True)
    out_grad = t_dot(mixed, branch_all)
    head_grad = low(dot_t(branch_all, out_w))
    qkv_grad = attention_backward(head_grad, q_rot, k_rot, v_heads, log_total)
    qkv_weight_grad = t_dot(normed_all, qkv_grad)
    normed_attn = low(dot_t(qkv_grad, qkv_w))
    normed_attn = lax.psum_scatter(normed_attn, "seq", scatter_dimension=0, tiled=True)
    input_part, attn_gain_grad = jax.vjp(rms_norm, layer_in, attn_scale)[1](
        normed_attn.astype(jnp.float32)
    )
    small_grads = jnp.concatenate(
        [router_grad, attn_gain_grad[:, None], ffn_gain_grad[:, None]], axis=1
    )
    return (input_part + after_grad, qkv_weight_grad, out_grad, small_grads, expert_grads)


def body(
    hidden_in,
    out_grad,
    attn_gain,
    ffn_gain,
    query_matrix,
    key_matrix,
    value_matrix,
    output_matrix,
    router_matrix,
    w_gate,
    w_up,
    w_down,
    routes,
):
    section = lax.axis_index("section")
    dp, seq = lax.axis_size("dp"), lax.axis_size("seq")
    seq_index = lax.axis_index("seq")
    first = section == 0
    slice_len = hidden_in.shape[2]
    width = hidden_in.shape[3]
    depth = query_matrix.shape[1]

    def by_layer(own, other):
        return [jnp.where(first, own, other), jnp.where(first, other, own)]

    layer_in = lax.dynamic_index_in_dim(hidden_in, section, 0, keepdims=False)[0]
    top_grad = lax.dynamic_index_in_dim(out_grad, section, 0, keepdims=False)[0]
    own_routes = lax.dynamic_index_in_dim(routes[0], section, 0, keepdims=False)[0]
    other_routes = lax.dynamic_index_in_dim(routes[0], 1 - section, 0, keepdims=False)[0]
    layer_routes = jnp.stack(by_layer(own_routes, swap(other_routes)))
    routes_all = lax.all_gather(layer_routes, TOKENS, axis=0, tiled=False)

    small = jnp.concatenate([router_matrix[0], attn_gain[0][:, None], ffn_gain[0][:, None]], axis=1)
    small = lax.all_gather(small, ("section", "dp", "seq"), axis=0, tiled=True)
    small = small.reshape(2, width, -1)
    by_group = jnp.concatenate(
        [
            matrix[0].reshape(depth, seq, -1)
            for matrix in (query_matrix, key_matrix, value_matrix)
        ],
        axis=2,
    )
    qkv_layers = []
    for part in by_layer(by_group, swap(by_group)):
        part = lax.all_to_all(part, "seq", split_axis=1, concat_axis=0, tiled=True)
        part = part.reshape(seq * depth, -1)
        qkv_layers.append(lax.all_gather(part, "dp", axis=0, tiled=True))
    devices = [(d, s) for d in range(dp) for s in range(seq)]
    to_group = []
    for flat in range(dp * seq):
        to_group.append((flat, (flat % dp) * seq + flat // dp))
    from_group = [(target, source) for source, target in to_group]
    grouped_out = lax.ppermute(output_matrix[0], TOKENS, to_group)
    out_layers = []
    for part in by_layer(grouped_out, swap(grouped_out)):
        out_layers.append(lax.all_gather(part, "dp", axis=0, tiled=True))

    local = w_gate.shape[1]
    hidden_units = w_gate.shape[3]
    if local >= seq:
        count, units = local // seq, hidden_units
        start, unit_start = seq_index * count, 0
    else:
        count, units = 1, hidden_units * local // seq
        start, unit_start = seq_index * local // seq, (seq_index % (seq // local)) * units
    first_expert = lax.axis_index("dp") * local + start
    own_experts = (
        lax.dynamic_slice(w_gate[0], (start, 0, unit_start), (count, width, units)),
        lax.dynamic_slice(w_up[0], (start, 0, unit_start), (count, width, units)),
        lax.dynamic_slice(w_down[0], (start, unit_start, 0), (count, units, width)),
    )
    expert_layers = list(zip(*[by_layer(own, swap(own)) for own in own_experts]))
    weights = []
    for number in range(2):
        weights.append(
            (
                small[number, :, EXPERTS].astype(jnp.float32),
                small[number, :, EXPERTS + 1].astype(jnp.float32),
                qkv_layers[number],
                out_layers[number],
                small[number, :, :EXPERTS],
            )
        )

    state = layer_in.astype(jnp.float32)
    layer_states = []
    saved_layers = []
    for number in range(2):
        state, saved = forward_layer(
            state, routes_all[:, number], weights[number], expert_layers[number], first_expert
        )
        layer_states.append(state)
        saved_layers.append(saved)
    grad = top_grad.astype(jnp.float32)
    layer_grads = [None, None]
    weight_grads = [None, None]
    for number in (1, 0):
        grad, *weight_grads[number] = backward_layer(
            grad, saved_layers[number], weights[number], expert_layers[number]
        )
        layer_grads[number] = grad

    def to_section(pieces):
        received = [pass_to(pieces[number], number) for number in range(2)]
        own = jnp.where(first, pieces[0], pieces[1])
        other = jnp.where(first, received[0], received[1])
        return jnp.stack(by_layer(own, other))[None, :, None]

    def summed(pieces):
        received = [pass_to(pieces[number], number) for number in range(2)]
        own = jnp.where(first, pieces[0], pieces[1]).astype(jnp.float32)
        return own + jnp.where(first, received[0], received[1]).astype(jnp.float32)

    def scatter_rows(part):
        part = lax.psum_scatter(low(part), "dp", scatter_dimension=0, tiled=True)
        return part

    qkv_parts = []
    out_parts = []
    small_parts = []
    for number in range(2):
        qkv_part, out_part, small_part, _ = weight_grads[number]
        qkv_part = scatter_rows(qkv_part).reshape(seq, depth, -1)
        qkv_part = lax.all_to_all(qkv_part, "seq", split_axis=0, concat_axis=0, tiled=True)
        qkv_parts.append(qkv_part)
        out_parts.append(lax.ppermute(scatter_rows(out_part), TOKENS, from_group))
        small_parts.append(
            lax.psum_scatter(small_part, TOKENS, scatter_dimension=0, tiled=True)
        )
    qkv_sum = summed(qkv_parts)
    out_sum = summed(out_parts)
    small_sum = summed(small_parts)
    kv_width = KV_HEADS * HEAD_DIM // seq
    q_width = GROUP * kv_width

    def columns(begin, end):
        return jnp.transpose(qkv_sum[:, :, begin:end], (1, 0, 2)).reshape(depth, -1)[None]

    expert_sums = []
    for kind in range(3):
        pieces = []
        for number in range(2):
            piece = weight_grads[number][3][kind]
            if local >= seq:
                piece = lax.all_to_all(piece, "seq", split_axis=1, concat_axis=0, tiled=True)
            else:
                share = seq // local
                if kind < 2:
                    piece = piece.reshape(seq, width // seq, units)
                    piece = lax.all_to_all(piece, "seq", split_axis=0, concat_axis=0, tiled=True)
                    piece = piece.reshape(local, share, width // seq, units)
                    piece = jnp.transpose(piece, (0, 2, 1, 3)).reshape(local, width // seq, -1)
                else:
                    rows = hidden_units // seq
                    piece = piece.reshape(-1, rows, width)
                    piece = whole_rows(piece, seq_index, share, seq)
            pieces.append(piece)
        expert_sums.append(summed(pieces)[None])
    return (
        to_section(layer_states),
        to_section(layer_grads),
        small_sum[:, EXPERTS][None],
        small_sum[:, EXPERTS + 1][None],
        columns(0, q_width),
        columns(q_width, q_width + kv_width),
        columns(q_width + kv_width, q_width + 2 * kv_width),
        out_sum[None],
        small_sum[:, :EXPERTS][None],
        *expert_sums,
    )


def whole_rows(piece, seq_index, share, seq):
    parts = piece.shape[0]
    spread = jnp.zeros((seq,) + piece.shape[1:], piece.dtype)
    spread = lax.dynamic_update_slice_in_dim(
        spread, piece, (seq_index % share) * parts, axis=0
    )
    spread = lax.all_to_all(spread, "seq", split_axis=0, concat_axis=0, tiled=True)
    spread = spread.reshape((-1, share) + piece.shape[1:])
    return jnp.sum(spread.astype(jnp.float32), axis=1).astype(piece.dtype)


def solution(mesh):
    return jax.shard_map(
        body,
        mesh=mesh,
        in_specs=(
            P(None, "dp", "seq", None),
            P(None, "dp", "seq", None),
            P("section", ("dp", "seq")),
            P("section", ("dp", "seq")),
            P("section", ("dp", "seq"), None),
            P("section", ("dp", "seq"), None),
            P("section", ("dp", "seq"), None),
            P("section", ("dp", "seq"), None),
            P("section", ("dp", "seq"), None),
            P("section", "dp", None, None),
            P("section", "dp", None, None),
            P("section", "dp", None, None),
            P("section", None, "dp", "seq", None),
        ),
        out_specs=(
            P("section", None, "dp", "seq", None),
            P("section", None, "dp", "seq", None),
            P("section", ("dp", "seq")),
            P("section", ("dp", "seq")),
            P("section", ("dp", "seq"), None),
            P("section", ("dp", "seq"), None),
            P("section", ("dp", "seq"), None),
            P("section", ("dp", "seq"), None),
            P("section", ("dp", "seq"), None),
            P("section", "dp", "seq", None),
            P("section", "dp", "seq", None),
            P("section", "dp", "seq", None),
        ),
        check_vma=False,
    )
```

time: 5020 us -> 2410 us (0.48)
  waiting for transfers between devices: 2940 us -> 1450 us
  local copies, waits for them, and re-layouts: 719 us -> 155 us
  other arithmetic: 400 us -> 137 us
  blocking collectives: 207 us -> 85.5 us
  starting transfers between devices: 231 us -> 116 us
    all_to_all x39 -> x9, waiting for transfers between devices: 1910 us -> 69.4 us  [the longest x6 58.7 us: body(): lax.all_to_all(piece, 'seq', split_axis=1, concat_axis=0, tiled=True)]
    all_gather x4 -> x12, waiting for transfers between devices: 82.1 us -> 419 us  [the longest x2 198 us: backward_layer(): grad_all = lax.all_gather(low(layer_grad), TOKENS, axis=0, tiled=True)]
    cond x70 -> x0, local copies, waits for them, and re-layouts: 184 us -> none  [the longest x7 131 us: backward_layer(): lax.cond(active, expert_backward, expert_rest, slot_rows, grad_rows, save...]
    all_to_all x39 -> x9, starting transfers between devices: 215 us -> 41.3 us  [the longest x6 27.9 us: body(): lax.all_to_all(piece, 'seq', split_axis=1, concat_axis=0, tiled=True)]
    gather x17 -> x0, local copies, waits for them, and re-layouts: 157 us -> none  [the longest x3 53 us: backward_layer(): returned.reshape(EXPERTS * CAP, width)[slots].reshape(-1, TOP_K, width)]
    all_gather x1 -> x2, blocking collectives: 183 us -> 54 us  [the longest x1 35.5 us: body(): small = lax.all_gather(small, ('section', 'dp', 'seq'), axis=0, tiled=True)]
    convert_element_type x35 -> x16, other arithmetic: 141 us -> 44.8 us  [the longest x15 44.1 us: low(): return v.astype(jnp.bfloat16)]
    another operation x35 -> x18, other arithmetic: 99.2 us -> 9.66 us  [the longest x2 4.62 us: to_section(): return jnp.stack(by_layer(own, other))[None, :, None]]
  transfers between devices with their start and end apart: 57 -> 60, of which waited for: 46 -> 38; matrix products, arithmetic and copies ran while one was open for 14% -> 16% of each run, Pallas kernels for 0% -> 0%
where the time goes in v1:
time: 2410 us; the launch traced here: 2400 us
  waiting for transfers between devices  1450 us (60%)
  matrix products  433 us (18%)
  local copies, waits for them, and re-layouts  155 us (6%)
  other arithmetic  137 us (6%)
  starting transfers between devices  116 us (5%)
  blocking collectives  85.5 us (4%)
    reduce_scatter x2, waiting for transfers between devices, forward_layer(): moe = lax.psum_scatter(low(moe), TOKENS, scatter_dimension=0, tiled=True)  258 us
    reduce_scatter x2, waiting for transfers between devices, backward_layer(): lax.psum_scatter(low(normed_grad), TOKENS, scatter_dimension=0, tiled=True)  246 us
    all_gather x2, waiting for transfers between devices, backward_layer(): grad_all = lax.all_gather(low(layer_grad), TOKENS, axis=0, tiled=True)  198 us
    ppermute x6, waiting for transfers between devices, swap(): return lax.ppermute(block, 'section', [(0, 1), (1, 0)])  177 us
    ppermute x16, waiting for transfers between devices, pass_to(): return lax.ppermute(block, 'section', [(1 - section, section)])  151 us
    dot_general x8, matrix products, give_back(): jnp.einsum('bct,bcd->btd', low(pick), rows.reshape(blocks, count, -1), pr...  104 us
    all_gather x2, waiting for transfers between devices, forward_layer(): ffn_all = lax.all_gather(normed_ffn, TOKENS, axis=0, tiled=True)  88 us
    dot_general x18, matrix products, dot_t(): lax.dot_general(a, b, (((1,), (1,)), ((), ())), preferred_element_type=jn...  82.7 us
  transfers between devices with their start and end apart: 60, of which 38 were waited for; matrix products, arithmetic and copies ran while one was open for 16% of the time, Pallas kernels for 0%

profile of v1, /device:TPU:16, one launch (start us, length us, event | category | flops | bytes accessed | tf_op | source)
XLA Modules:
  0.0 2398.8 jit_solution(6084828209198556780)
XLA Ops:
  36.1 35.5 %all-gather.2 = bf16[32,96,34]{1,2,0:T(8,128)(2,1)S(1)} all-gather(bf16[1,96,34]{1,2,0:T(8,128)(2,1)S(1)} %maximum_bitcast_fusion.2), channel_id=1, replica_groups=mesh['section'=2,'dp'=4,'seq'=4] {'section','dp','seq'}, dimensions={0}, use_global_device_ids=true | all-gather | bytes 215424 | tf_op jit(solution)/shard_map/all_gather | solution.py:369
  147.8 38.0 %reduce-scatter.19.cloned.1.call-done = bf16[256,1536]{1,0:T(8,128)(2,1)} async-done(((bf16[1024,1536]{1,0:T(8,128)(2,1)}), bf16[256,1536]{1,0:T(8,128)(2,1)}) %reduce-scatter.19.cloned.1.call-update) | async-done | bytes 786448 | tf_op jit(solution)/shard_map/reduce_scatter | solution.py:217
  206.2 58.8 %collective-permute-done.3 = s32[256,8]{0,1:T(8,128)S(1)} collective-permute-done((s32[256,8]{0,1:T(8,128)S(1)}, s32[256,8]{0,1:T(8,128)S(1)}, u32[]{:S(2)}, u32[]{:S(2)}) %collective-permute-start.3) | collective-permute-done | bytes 8224 | tf_op jit(solution)/shard_map/ppermute | solution.py:37
  265.0 18.5 all-gather
  293.5 38.9 %collective-permute-done.5 = bf16[2,1536,512]{2,1,0:T(8,128)(2,1)} collective-permute-done((bf16[2,1536,512]{2,1,0:T(8,128)(2,1)}, bf16[2,1536,512]{2,1,0:T(8,128)(2,1)}, u32[]{:S(2)}, u32[]{:S(2)}) %collective-permute-start.5) | collective-permute-done | bytes 3145760 | tf_op jit(solution)/shard_map/ppermute | solution.py:37
  338.4 60.3 %collective-permute-done.4 = bf16[2,1536,512]{2,1,0:T(8,128)(2,1)} collective-permute-done((bf16[2,1536,512]{2,1,0:T(8,128)(2,1)}, bf16[2,1536,512]{2,1,0:T(8,128)(2,1)}, u32[]{:S(2)}, u32[]{:S(2)}) %collective-permute-start.4) | collective-permute-done | bytes 3145760 | tf_op jit(solution)/shard_map/ppermute | solution.py:37
  461.7 15.5 add_convert_fusion.3
  490.0 121.3 %reduce-scatter.21.cloned.1.call-done = bf16[256,1536]{1,0:T(8,128)(2,1)} async-done(((bf16[4096,1536]{1,0:T(8,128)(2,1)}), bf16[256,1536]{1,0:T(8,128)(2,1)}) %reduce-scatter.21.cloned.1.call-update) | async-done | bytes 786448 | tf_op jit(solution)/shard_map/reduce_scatter | solution.py:242
  616.0 39.4 %all-gather.26.cloned.1.call-done = bf16[1536,640]{1,0:T(8,128)(2,1)} async-done(((bf16[384,640]{1,0:T(8,128)(2,1)}), bf16[1536,640]{1,0:T(8,128)(2,1)}) %all-gather.26.cloned.1.call-update) | async-done | bytes 1966096 | tf_op jit(solution)/shard_map/all_gather | solution.py:382
  655.4 30.8 %all-gather.24.cloned.1.call-done = bf16[1024,1536]{1,0:T(8,128)(2,1)} async-done(((bf16[256,1536]{1,0:T(8,128)(2,1)}), bf16[1024,1536]{1,0:T(8,128)(2,1)}) %all-gather.24.cloned.1.call-update) | async-done | bytes 3145744 | tf_op jit(solution)/shard_map/all_gather | solution.py:210
  724.6 35.7 %reduce-scatter.23.cloned.1.call-done = bf16[256,1536]{1,0:T(8,128)(2,1)} async-done(((bf16[1024,1536]{1,0:T(8,128)(2,1)}), bf16[256,1536]{1,0:T(8,128)(2,1)}) %reduce-scatter.23.cloned.1.call-update) | async-done | bytes 786448 | tf_op jit(solution)/shard_map/reduce_scatter | solution.py:217
  764.1 98.4 %all-gather.38.cloned.1.call-done = bf16[1,1,4096,1536]{3,2,1,0:T(8,128)(2,1)} async-done(((bf16[1,1,256,1536]{3,2,1,0:T(8,128)(2,1)}), bf16[1,1,4096,1536]{3,2,1,0:T(8,128)(2,1)}) %all-gather.38.cloned.1.call-update) | async-done | bytes 12582928 | tf_op jit(solution)/shard_map/all_gather | solution.py:282
  875.6 88.0 %all-gather.30.cloned.1.call-done = bf16[4096,1536]{1,0:T(8,128)(2,1)} async-done(((bf16[256,1536]{1,0:T(8,128)(2,1)}), bf16[4096,1536]{1,0:T(8,128)(2,1)}) %all-gather.30.cloned.1.call-update) | async-done | bytes 12582928 | tf_op jit(solution)/shard_map/all_gather | solution.py:220
  1056.7 15.6 add_convert_fusion.1
  1082.9 122.6 %reduce-scatter.27.cloned.1.call-done = bf16[256,1536]{1,0:T(8,128)(2,1)} async-done(((bf16[4096,1536]{1,0:T(8,128)(2,1)}), bf16[256,1536]{1,0:T(8,128)(2,1)}) %reduce-scatter.27.cloned.1.call-update) | async-done | bytes 786448 | tf_op jit(solution)/shard_map/reduce_scatter | solution.py:304
  1211.0 28.5 %all-gather.32.cloned.1.call-done = bf16[1024,1536]{1,0:T(8,128)(2,1)} async-done(((bf16[256,1536]{1,0:T(8,128)(2,1)}), bf16[1024,1536]{1,0:T(8,128)(2,1)}) %all-gather.32.cloned.1.call-update) | async-done | bytes 3145744 | tf_op jit(solution)/shard_map/all_gather | solution.py:319
  1309.0 15.6 add_convert_fusion.2
  1328.0 136.7 %reduce-scatter.25.cloned.1.call-done = bf16[256,1536]{1,0:T(8,128)(2,1)} async-done(((bf16[4096,1536]{1,0:T(8,128)(2,1)}), bf16[256,1536]{1,0:T(8,128)(2,1)}) %reduce-scatter.25.cloned.1.call-update) | async-done | bytes 786448 | tf_op jit(solution)/shard_map/reduce_scatter | solution.py:242
  1469.9 100.0 %all-gather.34.cloned.1.call-done = bf16[4096,1536]{1,0:T(8,128)(2,1)} async-done(((bf16[256,1536]{1,0:T(8,128)(2,1)}), bf16[4096,1536]{1,0:T(8,128)(2,1)}) %all-gather.34.cloned.1.call-update) | async-done | bytes 12582928 | tf_op jit(solution)/shard_map/all_gather | solution.py:282
  1618.3 15.5 add_convert_fusion
  1643.9 123.0 %reduce-scatter.31.cloned.1.call-done = bf16[256,1536]{1,0:T(8,128)(2,1)} async-done(((bf16[4096,1536]{1,0:T(8,128)(2,1)}), bf16[256,1536]{1,0:T(8,128)(2,1)}) %reduce-scatter.31.cloned.1.call-update) | async-done | bytes 786448 | tf_op jit(solution)/shard_map/reduce_scatter | solution.py:304
  1801.9 14.5 copy.198
  1832.3 14.7 copy.194
  1893.0 22.2 all-to-all-done.7
  1936.0 20.8 all-to-all-done.9
  2018.5 14.5 copy.192
  2120.3 31.8 %collective-permute-done.23 = bf16[8,128,1536]{2,1,0:T(8,128)(2,1)} collective-permute-done((bf16[8,128,1536]{2,1,0:T(8,128)(2,1)}, bf16[8,128,1536]{2,1,0:T(8,128)(2,1)}, u32[]{:S(2)}, u32[]{:S(2)}) %collective-permute-start.23) | collective-permute-done | bytes 3145760 | tf_op jit(solution)/shard_map/ppermute | solution.py:41
  2162.5 19.0 collective-permute-done.22
  2186.7 32.8 %collective-permute-done.21 = bf16[8,384,512]{2,1,0:T(8,128)(2,1)} collective-permute-done((bf16[8,384,512]{2,1,0:T(8,128)(2,1)}, bf16[8,384,512]{2,1,0:T(8,128)(2,1)}, u32[]{:S(2)}, u32[]{:S(2)}) %collective-permute-start.21) | collective-permute-done | bytes 3145760 | tf_op jit(solution)/shard_map/ppermute | solution.py:41
  2232.0 16.9 collective-permute-done.20
  2254.5 32.0 %collective-permute-done.19 = bf16[8,384,512]{2,1,0:T(8,128)(2,1)} collective-permute-done((bf16[8,384,512]{2,1,0:T(8,128)(2,1)}, bf16[8,384,512]{2,1,0:T(8,128)(2,1)}, u32[]{:S(2)}, u32[]{:S(2)}) %collective-permute-start.19) | collective-permute-done | bytes 3145760 | tf_op jit(solution)/shard_map/ppermute | solution.py:41
  2329.4 48.8 %reduce-scatter.43.cloned.1.call-done = f32[96,34]{1,0:T(8,128)} async-done(((f32[1536,34]{1,0:T(8,128)}), f32[96,34]{1,0:T(8,128)}) %reduce-scatter.43.cloned.1.call-update) | async-done | bytes 13072
  (880 shorter events, 876.1 us)
Async XLA Ops:
  147.8 256.9 %all-gather.22.cloned.1.call-start = ((), (), s32[]{:S(2)}) async-start(), calls=%async_computation.30 | async-start | bytes 13369344 | tf_op jit(solution)/shard_map/all_gather | solution.py:220
  189.8 421.6 %reduce-scatter.21.cloned.1.call-start = ((), (), s32[]{:S(2)}) async-start(), calls=%async_computation.31 | async-start | bytes 13369344 | tf_op jit(solution)/shard_map/reduce_scatter | solution.py:242
  199.5 133.0 %collective-permute-start.5 = (bf16[2,1536,512]{2,1,0:T(8,128)(2,1)}, bf16[2,1536,512]{2,1,0:T(8,128)(2,1)}, u32[]{:S(2)}, u32[]{:S(2)}) collective-permute-start(bf16[2,1536,512]{2,1,0:T(8,128)(2,1)} %dynamic-slice_bitcast_fusion.1), channel_id=1, source_target_pairs={{0,16},{16,0},{1,17},{17,1},{2,18},{18,2},{3,19},{19,3},{4,20},{20... | collective-permute-start | bytes 9437192 | tf_op jit(solution)/shard_map/ppermute | solution.py:37
  204.7 194.1 %collective-permute-start.4 = (bf16[2,1536,512]{2,1,0:T(8,128)(2,1)}, bf16[2,1536,512]{2,1,0:T(8,128)(2,1)}, u32[]{:S(2)}, u32[]{:S(2)}) collective-permute-start(bf16[2,1536,512]{2,1,0:T(8,128)(2,1)} %dynamic-slice_bitcast_fusion.2), channel_id=1, source_target_pairs={{0,16},{16,0},{1,17},{17,1},{2,18},{18,2},{3,19},{19,3},{4,20},{20... | collective-permute-start | bytes 9437192 | tf_op jit(solution)/shard_map/ppermute | solution.py:37
  477.2 178.2 %all-gather.26.cloned.1.call-start = ((), (), s32[]{:S(2)}) async-start(), calls=%async_computation.33 | async-start | bytes 2457600 | tf_op jit(solution)/shard_map/all_gather | solution.py:382
  489.9 196.2 %all-gather.24.cloned.1.call-start = ((), (), s32[]{:S(2)}) async-start(), calls=%async_computation.32 | async-start | bytes 3932160 | tf_op jit(solution)/shard_map/all_gather | solution.py:210
  614.8 102.6 %all-gather.28.cloned.1.call-start = ((), (), s32[]{:S(2)}) async-start(), calls=%async_computation.34 | async-start | bytes 1474560 | tf_op jit(solution)/shard_map/all_gather | solution.py:391
  615.5 144.8 %reduce-scatter.23.cloned.1.call-start = ((), (), s32[]{:S(2)}) async-start(), calls=%async_computation.35 | async-start | bytes 3932160 | tf_op jit(solution)/shard_map/reduce_scatter | solution.py:217
  722.2 140.3 %all-gather.38.cloned.1.call-start = ((), (), s32[]{:S(2)}) async-start(), calls=%async_computation.49 | async-start | bytes 13369344 | tf_op jit(solution)/shard_map/all_gather | solution.py:282
  724.6 239.0 %all-gather.30.cloned.1.call-start = ((), (), s32[]{:S(2)}) async-start(), calls=%async_computation.36 | async-start | bytes 13369344 | tf_op jit(solution)/shard_map/all_gather | solution.py:220
  763.0 442.5 %reduce-scatter.27.cloned.1.call-start = ((), (), s32[]{:S(2)}) async-start(), calls=%async_computation.38 | async-start | bytes 13369344 | tf_op jit(solution)/shard_map/reduce_scatter | solution.py:304
  1077.8 161.7 %all-gather.32.cloned.1.call-start = ((), (), s32[]{:S(2)}) async-start(), calls=%async_computation.39 | async-start | bytes 3932160 | tf_op jit(solution)/shard_map/all_gather | solution.py:319
  1210.9 115.5 %reduce-scatter.29.cloned.1.call-start = ((), (), s32[]{:S(2)}) async-start(), calls=%async_computation.40 | async-start | bytes 3932160 | tf_op jit(solution)/shard_map/reduce_scatter | solution.py:325
  1288.3 176.5 %reduce-scatter.25.cloned.1.call-start = ((), (), s32[]{:S(2)}) async-start(), calls=%async_computation.37 | async-start | bytes 13369344 | tf_op jit(solution)/shard_map/reduce_scatter | solution.py:242
  1324.7 245.2 %all-gather.34.cloned.1.call-start = ((), (), s32[]{:S(2)}) async-start(), calls=%async_computation.41 | async-start | bytes 13369344 | tf_op jit(solution)/shard_map/all_gather | solution.py:282
  1469.8 297.0 %reduce-scatter.31.cloned.1.call-start = ((), (), s32[]{:S(2)}) async-start(), calls=%async_computation.42 | async-start | bytes 13369344 | tf_op jit(solution)/shard_map/reduce_scatter | solution.py:304
  1633.8 224.4 %all-gather.36.cloned.1.call-start = ((), (), s32[]{:S(2)}) async-start(), calls=%async_computation.43 | async-start | bytes 3932160 | tf_op jit(solution)/shard_map/all_gather | solution.py:319
  1771.8 314.3 %reduce-scatter.41.cloned.1.call-start = ((), (), s32[]{:S(2)}) async-start(), calls=%async_computation.48 | async-start | bytes 1474560 | tf_op jit(solution)/shard_map/reduce_scatter | solution.py:450
  1794.2 300.4 %reduce-scatter.45.cloned.1.call-start = ((), (), s32[]{:S(2)}) async-start(), calls=%async_computation.51 | async-start | bytes 835584
  1818.8 277.2 %reduce-scatter.37.cloned.1.call-start = ((), (), s32[]{:S(2)}) async-start(), calls=%async_computation.46 | async-start | bytes 2457600 | tf_op jit(solution)/shard_map/reduce_scatter | solution.py:450
  1824.8 394.8 %reduce-scatter.39.cloned.1.call-start = ((), (), s32[]{:S(2)}) async-start(), calls=%async_computation.47 | async-start | bytes 1474560 | tf_op jit(solution)/shard_map/reduce_scatter | solution.py:450
  1960.5 337.6 %reduce-scatter.35.cloned.1.call-start = ((), (), s32[]{:S(2)}) async-start(), calls=%async_computation.45 | async-start | bytes 2457600 | tf_op jit(solution)/shard_map/reduce_scatter | solution.py:450
  2045.5 266.8 %reduce-scatter.33.cloned.1.call-start = ((), (), s32[]{:S(2)}) async-start(), calls=%async_computation.44 | async-start | bytes 3932160 | tf_op jit(solution)/shard_map/reduce_scatter | solution.py:325
  2056.7 95.5 %collective-permute-start.23 = (bf16[8,128,1536]{2,1,0:T(8,128)(2,1)}, bf16[8,128,1536]{2,1,0:T(8,128)(2,1)}, u32[]{:S(2)}, u32[]{:S(2)}) collective-permute-start(bf16[8,128,1536]{2,1,0:T(8,128)(2,1)} %bitcast.220), channel_id=1, source_target_pairs={{16,0},{17,1},{18,2},{19,3},{20,4},{21,5},{22,6},{23,7},{24,8},{25... | collective-permute-start | bytes 9437192 | tf_op jit(solution)/shard_map/ppermute | solution.py:41
  2070.6 110.9 %collective-permute-start.22 = (bf16[8,384,512]{2,1,0:T(8,128)(2,1)}, bf16[8,384,512]{2,1,0:T(8,128)(2,1)}, u32[]{:S(2)}, u32[]{:S(2)}) collective-permute-start(bf16[8,384,512]{2,1,0:T(8,128)(2,1)} %bitcast.214), channel_id=1, source_target_pairs={{0,16},{1,17},{2,18},{3,19},{4,20},{5,21},{6,22},{7,23},{8,24},{9,... | collective-permute-start | bytes 9437192 | tf_op jit(solution)/shard_map/ppermute | solution.py:41
  2084.8 134.8 %collective-permute-start.21 = (bf16[8,384,512]{2,1,0:T(8,128)(2,1)}, bf16[8,384,512]{2,1,0:T(8,128)(2,1)}, u32[]{:S(2)}, u32[]{:S(2)}) collective-permute-start(bf16[8,384,512]{2,1,0:T(8,128)(2,1)} %bitcast.209), channel_id=1, source_target_pairs={{16,0},{17,1},{18,2},{19,3},{20,4},{21,5},{22,6},{23,7},{24,8},{25... | collective-permute-start | bytes 9437192 | tf_op jit(solution)/shard_map/ppermute | solution.py:41
  2104.6 144.3 %collective-permute-start.20 = (bf16[8,384,512]{2,1,0:T(8,128)(2,1)}, bf16[8,384,512]{2,1,0:T(8,128)(2,1)}, u32[]{:S(2)}, u32[]{:S(2)}) collective-permute-start(bf16[8,384,512]{2,1,0:T(8,128)(2,1)} %bitcast.203), channel_id=1, source_target_pairs={{0,16},{1,17},{2,18},{3,19},{4,20},{5,21},{6,22},{7,23},{8,24},{9,... | collective-permute-start | bytes 9437192 | tf_op jit(solution)/shard_map/ppermute | solution.py:41
  2114.0 172.4 %collective-permute-start.19 = (bf16[8,384,512]{2,1,0:T(8,128)(2,1)}, bf16[8,384,512]{2,1,0:T(8,128)(2,1)}, u32[]{:S(2)}, u32[]{:S(2)}) collective-permute-start(bf16[8,384,512]{2,1,0:T(8,128)(2,1)} %bitcast.198), channel_id=1, source_target_pairs={{16,0},{17,1},{18,2},{19,3},{20,4},{21,5},{22,6},{23,7},{24,8},{25... | collective-permute-start | bytes 9437192 | tf_op jit(solution)/shard_map/ppermute | solution.py:41
  2152.2 150.2 %collective-permute-start.18 = (bf16[96,1536]{1,0:T(8,128)(2,1)}, bf16[96,1536]{1,0:T(8,128)(2,1)}, u32[]{:S(2)}, u32[]{:S(2)}) collective-permute-start(bf16[96,1536]{1,0:T(8,128)(2,1)} %copy-done.133), channel_id=1, source_target_pairs={{0,16},{1,17},{2,18},{3,19},{4,20},{5,21},{6,22},{7,23},{8,24},{9,... | collective-permute-start | bytes 884744 | tf_op jit(solution)/shard_map/ppermute | solution.py:41
  2181.5 138.0 %collective-permute-start.14 = (bf16[4,96,640]{2,1,0:T(8,128)(2,1)}, bf16[4,96,640]{2,1,0:T(8,128)(2,1)}, u32[]{:S(2)}, u32[]{:S(2)}) collective-permute-start(bf16[4,96,640]{2,1,0:T(8,128)(2,1)} %all-to-all-done.5), channel_id=1, source_target_pairs={{0,16},{1,17},{2,18},{3,19},{4,20},{5,21},{6,22},{7,23},{8,24},{9,... | collective-permute-start | bytes 1474568 | tf_op jit(solution)/shard_map/ppermute | solution.py:41
  2248.9 138.5 %collective-permute-start.10 = (f32[256,1536]{1,0:T(8,128)S(1)}, f32[256,1536]{1,0:T(8,128)}, u32[]{:S(2)}, u32[]{:S(2)}) collective-permute-start(f32[256,1536]{1,0:T(8,128)S(1)} %copy-done.24), channel_id=1, source_target_pairs={{0,16},{1,17},{2,18},{3,19},{4,20},{5,21},{6,22},{7,23},{8,24},{9,... | collective-permute-start | bytes 4718600 | tf_op jit(solution)/shard_map/ppermute | solution.py:41
  2286.4 97.7 %collective-permute-start.12 = (f32[96,34]{0,1:T(8,128)}, f32[96,34]{0,1:T(8,128)}, u32[]{:S(2)}, u32[]{:S(2)}) collective-permute-start(f32[96,34]{0,1:T(8,128)} %copy.241), channel_id=1, source_target_pairs={{0,16},{1,17},{2,18},{3,19},{4,20},{5,21},{6,22},{7,23},{8,24},{9,... | collective-permute-start | bytes 39176 | tf_op jit(solution)/shard_map/ppermute | solution.py:41
  (266 other events, 6838.9 us)
Sparse Core Ops, SparseCore 0:
  36.1 43.5 all-gather.17
  81.8 28.8 all-gather.15
  112.8 30.1 all-gather.19
  147.9 37.9 reduce-scatter.18
  189.9 100.6 all-gather.21
  477.4 133.8 reduce-scatter.20
  613.0 42.3 all-gather.25
  657.6 28.5 all-gather.23
  687.8 29.5 all-gather.27
  722.3 37.9 reduce-scatter.22
  762.6 99.8 all-gather.37
  864.6 98.9 all-gather.29
  1072.5 132.9 reduce-scatter.26
  1211.0 28.5 all-gather.31
  1288.4 37.9 reduce-scatter.28
  1330.8 133.8 reduce-scatter.24
  1469.9 99.8 all-gather.33
  1634.0 132.8 reduce-scatter.30
  1771.9 30.1 all-gather.35
  1804.4 29.4 reduce-scatter.40
  1837.9 55.6 reduce-scatter.44
  1895.9 40.6 reduce-scatter.36
  1938.9 27.8 reduce-scatter.38
  1969.0 40.6 reduce-scatter.34
  2052.6 55.8 reduce-scatter.32
  2319.6 58.4 reduce-scatter.42

commit v2 on v1

--- a/solution.py
+++ b/solution.py
@@ -3,6 +3,8 @@
 import jax
 import jax.numpy as jnp
 from jax import lax
+from jax.experimental import pallas as pl
+from jax.experimental.pallas import tpu as pltpu
 from jax.sharding import PartitionSpec as P
 
 HEADS = 24
@@ -39,6 +41,176 @@
 
 def pass_to(block, section):
     return lax.ppermute(block, "section", [(1 - section, section)])
+
+
+MESH = pl.DeviceIdType.MESH
+
+def rdma(src, dst, ssem, rsem, **dev):
+    return pltpu.make_async_remote_copy(src_ref=src, dst_ref=dst, send_sem=ssem, recv_sem=rsem, device_id=dev, device_id_type=MESH)
+
+def greet(d, s, last):
+    barrier = pltpu.get_barrier_semaphore()
+    def sig(**dev):
+        pl.semaphore_signal(barrier, inc=1, device_id=dev, device_id_type=MESH)
+    sig(seq=s ^ 1)
+    sig(seq=s ^ 2)
+    @pl.when(d > 0)
+    def _(): sig(dp=d - 1)
+    @pl.when(d < last)
+    def _(): sig(dp=d + 1)
+    inner = (d > 0) & (d < last)
+    @pl.when(inner)
+    def _(): pl.semaphore_wait(barrier, 4)
+    @pl.when(jnp.logical_not(inner))
+    def _(): pl.semaphore_wait(barrier, 3)
+
+def ag_kernel(x_ref, out_ref, lsem, zs, zr, ys, yr, cs, cr):
+    d, s = lax.axis_index("dp"), lax.axis_index("seq")
+    last = 3
+    greet(d, s, last)
+    def blk(z, sq): return out_ref.at[z * 4 + sq]
+    own = pltpu.make_async_copy(x_ref, blk(d, s), lsem)
+    own.start()
+    def zc(src, z, right):
+        return rdma(src, blk(z, s), zs.at[int(right), z], zr.at[z], dp=(d + 1 if right else d - 1))
+    def yc(src, z): return rdma(src, blk(z, s), ys.at[z], yr.at[z], seq=s ^ 2)
+    def cc(src, z, y):
+        sq = s ^ 2 if y else s
+        return rdma(src, blk(z, sq), cs.at[z, y], cr.at[z, y], seq=s ^ 1)
+    def send(src, z):
+        @pl.when((z <= d) & (d < last))
+        def _(): zc(src, z, True).start()
+        @pl.when((z >= d) & (d > 0))
+        def _(): zc(src, z, False).start()
+        yc(src, z).start()
+        cc(src, z, 0).start()
+    send(x_ref, d)
+    for h in (1, 2, 3):
+        for side in (-1, 1):
+            z = d + side * h
+            @pl.when((z >= 0) & (z <= last))
+            def _():
+                rdma(blk(z, s), blk(z, s), zs.at[0, z], zr.at[z], dp=d).wait_recv()
+                send(blk(z, s), z)
+    for h in (0, 1, 2, 3):
+        for side in ((-1, 1) if h else (1,)):
+            z = d + side * h
+            @pl.when((z >= 0) & (z <= last))
+            def _():
+                yc(blk(z, s ^ 2), z).wait_recv()
+                cc(blk(z, s ^ 2), z, 1).start()
+    for z in range(4):
+        for y in range(2):
+            sq = (s ^ 1) ^ (2 * y)
+            cc(blk(z, sq), z, y).wait_recv()
+    for z in range(4):
+        @pl.when((z <= d) & (d < last))
+        def _(): zc(blk(z, s), z, True).wait_send()
+        @pl.when((z >= d) & (d > 0))
+        def _(): zc(blk(z, s), z, False).wait_send()
+        yc(blk(z, s), z).wait_send()
+        cc(blk(z, s), z, 0).wait_send()
+        cc(blk(z, s), z, 1).wait_send()
+    own.wait()
+
+def ag16(x, space=pl.ANY, cid=0):
+    D=pltpu.SemaphoreType.DMA
+    return pl.pallas_call(ag_kernel,
+        out_shape=jax.ShapeDtypeStruct((16,)+x.shape, x.dtype),
+        in_specs=[pl.BlockSpec(memory_space=pl.ANY)], out_specs=pl.BlockSpec(memory_space=space),
+        scratch_shapes=[D(()), D((2,4)), D((4,)), D((4,)), D((4,)), D((4,2)), D((4,2))],
+        compiler_params=pltpu.CompilerParams(collective_id=cid, has_side_effects=True, vmem_limit_bytes=60<<20),
+        name="ag16")(x)
+
+def add_into(dst, a, b, rows, step=16):
+    @pl.loop(0, rows // step)
+    def _(i):
+        r = pl.ds(i * step, step)
+        dst[r, :] = (a[r, :].astype(jnp.float32) + b[r, :].astype(jnp.float32)).astype(dst.dtype)
+
+def rs_kernel(p_ref, out_ref, own, cbuf, ybuf, zbuf, ls, zs, zr, ys, yr, cs, cr):
+    d, s = lax.axis_index("dp"), lax.axis_index("seq")
+    last = 3
+    greet(d, s, last)
+    rows = p_ref.shape[1]
+    def cc(z, yy):
+        return rdma(p_ref.at[z * 4 + ((s ^ 1) ^ (2 * yy))], cbuf.at[z, yy], cs.at[z, yy], cr.at[z, yy], seq=s ^ 1)
+    def lc(z, yy):
+        return pltpu.make_async_copy(p_ref.at[z * 4 + (s ^ (2 * yy))], own.at[z, yy], ls.at[z, yy])
+    def yc(z): return rdma(own.at[z, 1], ybuf.at[z], ys.at[z], yr.at[z], seq=s ^ 2)
+    def zc(z, right): return rdma(own.at[z, 0], zbuf.at[int(right), z], zs.at[z], zr.at[int(right), z], dp=(d + 1 if right else d - 1))
+    for yy in (1, 0):
+        for i in range(4):
+            z = d ^ (3 - i)
+            cc(z, yy).start()
+            lc(z, yy).start()
+    for i in range(4):
+        z = d ^ (3 - i)
+        lc(z, 1).wait()
+        cc(z, 1).wait_recv()
+        add_into(own.at[z, 1], own.at[z, 1], cbuf.at[z, 1], rows)
+        yc(z).start()
+    for i in range(4):
+        z = d ^ (3 - i)
+        lc(z, 0).wait()
+        cc(z, 0).wait_recv()
+        add_into(own.at[z, 0], own.at[z, 0], cbuf.at[z, 0], rows)
+        yc(z).wait_recv()
+        add_into(own.at[z, 0], own.at[z, 0], ybuf.at[z], rows)
+        if i < 3:
+            @pl.when(z < d)
+            def _():
+                @pl.when(d < last)
+                def _():
+                    zc(z, False).wait_recv()
+                    add_into(own.at[z, 0], own.at[z, 0], zbuf.at[0, z], rows)
+                zc(z, False).start()
+            @pl.when(z > d)
+            def _():
+                @pl.when(d > 0)
+                def _():
+                    zc(z, True).wait_recv()
+                    add_into(own.at[z, 0], own.at[z, 0], zbuf.at[1, z], rows)
+                zc(z, True).start()
+        else:
+            @pl.when(d < last)
+            def _():
+                zc(d, False).wait_recv()
+                add_into(own.at[d, 0], own.at[d, 0], zbuf.at[0, d], rows)
+            @pl.when(d > 0)
+            def _():
+                zc(d, True).wait_recv()
+                add_into(own.at[d, 0], own.at[d, 0], zbuf.at[1, d], rows)
+            out_ref[...] = own[d, 0]
+    for z in range(4):
+        cc(z, 0).wait_send(); cc(z, 1).wait_send(); yc(z).wait_send()
+        @pl.when(z < d)
+        def _(): zc(z, False).wait_send()
+        @pl.when(z > d)
+        def _(): zc(z, True).wait_send()
+
+def rs16(p, cid=1):
+    D=pltpu.SemaphoreType.DMA
+    rows, w = p.shape[1:]
+    V=lambda *sh: pltpu.VMEM(sh+(rows,w), p.dtype)
+    return pl.pallas_call(rs_kernel,
+        out_shape=jax.ShapeDtypeStruct((rows,w), p.dtype),
+        in_specs=[pl.BlockSpec(memory_space=pl.ANY)], out_specs=pl.BlockSpec(memory_space=pltpu.VMEM),
+        scratch_shapes=[V(4,2),V(4,2),V(4),V(2,4), D((4,2)), D((4,)), D((2,4)), D((4,)), D((4,)), D((4,2)), D((4,2))],
+        compiler_params=pltpu.CompilerParams(collective_id=cid, has_side_effects=True, vmem_limit_bytes=60<<20),
+        name="rs16")(p)
+
+
+def whole_tokens(block):
+    if lax.axis_size("dp") == 4 and lax.axis_size("seq") == 4:
+        return ag16(block).reshape(-1, block.shape[1])
+    return lax.all_gather(block, TOKENS, axis=0, tiled=True)
+
+
+def token_sums(partial_sums):
+    if lax.axis_size("dp") == 4 and lax.axis_size("seq") == 4:
+        return rs16(partial_sums.reshape(16, -1, partial_sums.shape[1]))
+    return lax.psum_scatter(partial_sums, TOKENS, scatter_dimension=0, tiled=True)
 
 
 def rms_norm(values, norm_gain):
@@ -217,7 +389,7 @@
     branch = lax.psum_scatter(low(dot(mixed, out_w)), "seq", scatter_dimension=0, tiled=True)
     after_update = layer_in + branch.astype(jnp.float32)
     normed_ffn = low(rms_norm(after_update, ffn_scale))
-    ffn_all = lax.all_gather(normed_ffn, TOKENS, axis=0, tiled=True)
+    ffn_all = whole_tokens(normed_ffn)
     chosen, pick = routing(route_all, first_expert, count)
     blocks, rows = chosen.shape[:2]
     logits = dot(ffn_all, router_w).reshape(blocks, rows, EXPERTS)
@@ -239,7 +411,7 @@
         results.append(low(dot(scaled, down_w[j])))
         saved_experts.append((slot_rows, slot_gates, gate_pre, up_pre, scaled))
     moe = give_back([pick[:, j] for j in range(count)], results)
-    moe = lax.psum_scatter(low(moe), TOKENS, scatter_dimension=0, tiled=True)
+    moe = token_sums(low(moe))
     layer_out = after_update + moe.astype(jnp.float32)
     own_block = lax.axis_index("dp") * lax.axis_size("seq") + lax.axis_index("seq")
     own_gates = lax.dynamic_index_in_dim(gates, own_block, 0, keepdims=False)
@@ -279,7 +451,7 @@
         saved_experts,
     ) = saved
     blocks, _, _, rows = pick.shape
-    grad_all = lax.all_gather(low(layer_grad), TOKENS, axis=0, tiled=True)
+    grad_all = whole_tokens(low(layer_grad))
     grad_blocks = grad_all.reshape(blocks, rows, -1)
     input_rows = []
     gate_terms = []
@@ -301,10 +473,9 @@
         expert_grads[2].append(low(t_dot(scaled, slot_grads)))
     expert_grads = tuple(jnp.stack(parts) for parts in expert_grads)
     normed_grad = give_back([pick[:, j] for j in range(count)], input_rows)
-    normed_grad = lax.psum_scatter(low(normed_grad), TOKENS, scatter_dimension=0, tiled=True)
+    normed_grad = token_sums(low(normed_grad))
     gate_terms = jnp.stack(gate_terms, axis=1)
     gate_terms = lax.all_to_all(gate_terms, TOKENS, split_axis=0, concat_axis=0, tiled=True)
-    split = EXPERTS // (blocks * count) if blocks * count < EXPERTS else 1
     gate_terms = gate_terms.reshape(-1, rows)
     if gate_terms.shape[0] > EXPERTS:
         gate_terms = jnp.sum(gate_terms.reshape(EXPERTS, -1, rows), axis=1)

time: 2410 us -> 2260 us (0.938)
  waiting for transfers between devices: 1450 us -> 543 us
  Pallas kernels: 0 us -> 758 us
    pallas_call x0 -> x8, Pallas kernels: none -> 758 us  [the longest x4 444 us: rs16(): pl.pallas_call(rs_kernel, out_shape=jax.ShapeDtypeStruct((rows, w), p.dty...]
    reduce_scatter x4 -> x0, waiting for transfers between devices: 504 us -> none  [the longest x2 258 us: forward_layer(): moe = lax.psum_scatter(low(moe), TOKENS, scatter_dimension=0, tiled=True)]
    all_gather x4 -> x0, waiting for transfers between devices: 286 us -> none  [the longest x2 198 us: backward_layer(): grad_all = lax.all_gather(low(layer_grad), TOKENS, axis=0, tiled=True)]
    reduce_scatter x2, waiting for transfers between devices: 73.7 us -> 0.01 us  [forward_layer(): lax.psum_scatter(low(dot(mixed, out_w)), 'seq', scatter_dimension=0, tile...]
    all_gather x2, waiting for transfers between devices: 39.4 us -> 0.04 us  [body(): qkv_layers.append(lax.all_gather(part, 'dp', axis=0, tiled=True))]
    unnamed x28 -> x20, waiting for transfers between devices: 49.8 us -> 52.2 us
  transfers between devices with their start and end apart: 60 -> 54, of which waited for: 38 -> 27; matrix products, arithmetic and copies ran while one was open for 16% -> 24% of each run, Pallas kernels for 0% -> 27%
where the time goes in v2:
time: 2260 us; the launch traced here: 2250 us
  Pallas kernels  758 us (34%)
  waiting for transfers between devices  543 us (24%)
  matrix products  435 us (19%)
  local copies, waits for them, and re-layouts  156 us (7%)
  starting transfers between devices  137 us (6%)
  other arithmetic  137 us (6%)
  blocking collectives  63.1 us (3%)
    pallas_call x4, Pallas kernels, rs16(): pl.pallas_call(rs_kernel, out_shape=jax.ShapeDtypeStruct((rows, w), p.dty...  444 us
    pallas_call x4, Pallas kernels, ag16(): pl.pallas_call(ag_kernel, out_shape=jax.ShapeDtypeStruct((16,) + x.shape,...  313 us
    ppermute x6, waiting for transfers between devices, swap(): return lax.ppermute(block, 'section', [(0, 1), (1, 0)])  166 us
    ppermute x16, waiting for transfers between devices, pass_to(): return lax.ppermute(block, 'section', [(1 - section, section)])  147 us
    dot_general x8, matrix products, give_back(): jnp.einsum('bct,bcd->btd', low(pick), rows.reshape(blocks, count, -1), pr...  104 us
    dot_general x18, matrix products, dot_t(): lax.dot_general(a, b, (((1,), (1,)), ((), ())), preferred_element_type=jn...  86.5 us
    another operation x6, local copies, waits for them, and re-layouts, backward_layer(): expert_grads = tuple((jnp.stack(parts) for parts in expert_grads))  67.7 us
    dot_general x16, matrix products, dot(): return jnp.dot(a, b, preferred_element_type=jnp.float32)  67 us
  transfers between devices with their start and end apart: 54, of which 27 were waited for; matrix products, arithmetic and copies ran while one was open for 24% of the time, Pallas kernels for 27%

profile of v2, /device:TPU:16, one launch (start us, length us, event | category | flops | bytes accessed | tf_op | source)
XLA Modules:
  0.0 2247.5 jit_solution(17926677699813376363)
XLA Ops:
  36.1 35.5 %all-gather.1 = bf16[32,96,34]{1,2,0:T(8,128)(2,1)S(1)} all-gather(bf16[1,96,34]{1,2,0:T(8,128)(2,1)S(1)} %maximum_bitcast_fusion.2), channel_id=1, replica_groups=mesh['section'=2,'dp'=4,'seq'=4] {'section','dp','seq'}, dimensions={0}, use_global_device_ids=true | all-gather | bytes 215424 | tf_op jit(solution)/shard_map/all_gather | solution.py:540
  164.3 58.6 %collective-permute-done.3 = s32[256,8]{0,1:T(8,128)S(1)} collective-permute-done((s32[256,8]{0,1:T(8,128)S(1)}, s32[256,8]{0,1:T(8,128)S(1)}, u32[]{:S(2)}, u32[]{:S(2)}) %collective-permute-start.3) | collective-permute-done | bytes 8224 | tf_op jit(solution)/shard_map/ppermute | solution.py:39
  222.9 16.0 all-gather
  261.4 29.0 %collective-permute-done.5 = bf16[2,1536,512]{2,1,0:T(8,128)(2,1)} collective-permute-done((bf16[2,1536,512]{2,1,0:T(8,128)(2,1)}, bf16[2,1536,512]{2,1,0:T(8,128)(2,1)}, u32[]{:S(2)}, u32[]{:S(2)}) %collective-permute-start.5) | collective-permute-done | bytes 3145760 | tf_op jit(solution)/shard_map/ppermute | solution.py:39
  296.4 60.3 %collective-permute-done.4 = bf16[2,1536,512]{2,1,0:T(8,128)(2,1)} collective-permute-done((bf16[2,1536,512]{2,1,0:T(8,128)(2,1)}, bf16[2,1536,512]{2,1,0:T(8,128)(2,1)}, u32[]{:S(2)}, u32[]{:S(2)}) %collective-permute-start.4) | collective-permute-done | bytes 3145760 | tf_op jit(solution)/shard_map/ppermute | solution.py:39
  366.5 74.0 %ag16.4 = bf16[16,256,1536]{2,1,0:T(8,128)(2,1)} custom-call(bf16[256,1536]{1,0:T(8,128)(2,1)} %multiply_convert_fusion.14.x_ref), custom_call_target="tpu_custom_call" | custom-call | tf_op jit(solution)/shard_map/ag16/pallas_call | solution.py:118
  497.6 15.5 add_convert_fusion.3.p_ref
  513.1 111.6 %rs16.4 = bf16[256,1536]{1,0:T(8,128)(2,1)} custom-call(bf16[16,256,1536]{2,1,0:T(8,128)(2,1)} %add_convert_fusion.3.p_ref), custom_call_target="tpu_custom_call" | custom-call | tf_op jit(solution)/shard_map/rs16/pallas_call | solution.py:196
  629.6 29.8 %all-gather.17.cloned.1.call-done = bf16[1024,1536]{1,0:T(8,128)(2,1)} async-done(((bf16[256,1536]{1,0:T(8,128)(2,1)}), bf16[1024,1536]{1,0:T(8,128)(2,1)}) %all-gather.17.cloned.1.call-update) | async-done | bytes 3145744 | tf_op jit(solution)/shard_map/all_gather | solution.py:382
  678.2 12.4 all-gather.21.cloned.1.call-done
  697.8 90.1 %ag16.6 = bf16[16,256,1536]{2,1,0:T(8,128)(2,1)} custom-call(bf16[256,1536]{1,0:T(8,128)(2,1)} %dynamic-slice_bitcast_fusion.3.x_ref), custom_call_target="tpu_custom_call" | custom-call | tf_op jit(solution)/shard_map/ag16/pallas_call | solution.py:118
  805.0 75.4 %ag16.5 = bf16[16,256,1536]{2,1,0:T(8,128)(2,1)} custom-call(bf16[256,1536]{1,0:T(8,128)(2,1)} %multiply_convert_fusion.12.x_ref), custom_call_target="tpu_custom_call" | custom-call | tf_op jit(solution)/shard_map/ag16/pallas_call | solution.py:118
  981.2 15.6 add_convert_fusion.1.p_ref
  996.7 111.5 %rs16.6 = bf16[256,1536]{1,0:T(8,128)(2,1)} custom-call(bf16[16,256,1536]{2,1,0:T(8,128)(2,1)} %add_convert_fusion.1.p_ref), custom_call_target="tpu_custom_call" | custom-call | tf_op jit(solution)/shard_map/rs16/pallas_call | solution.py:196
  1114.6 29.9 %all-gather.23.cloned.1.call-done = bf16[1024,1536]{1,0:T(8,128)(2,1)} async-done(((bf16[256,1536]{1,0:T(8,128)(2,1)}), bf16[1024,1536]{1,0:T(8,128)(2,1)}) %all-gather.23.cloned.1.call-update) | async-done | bytes 3145744 | tf_op jit(solution)/shard_map/all_gather | solution.py:490
  1213.8 15.6 add_convert_fusion.2.p_ref
  1229.4 109.8 %rs16.5 = bf16[256,1536]{1,0:T(8,128)(2,1)} custom-call(bf16[16,256,1536]{2,1,0:T(8,128)(2,1)} %add_convert_fusion.2.p_ref), custom_call_target="tpu_custom_call" | custom-call | tf_op jit(solution)/shard_map/rs16/pallas_call | solution.py:196
  1345.7 73.7 %ag16.7 = bf16[16,256,1536]{2,1,0:T(8,128)(2,1)} custom-call(bf16[256,1536]{1,0:T(8,128)(2,1)} %get-tuple-element.222.x_ref), custom_call_target="tpu_custom_call" | custom-call | tf_op jit(solution)/shard_map/ag16/pallas_call | solution.py:118
  1485.0 15.5 add_convert_fusion.p_ref
  1500.5 111.5 %rs16.7 = bf16[256,1536]{1,0:T(8,128)(2,1)} custom-call(bf16[16,256,1536]{2,1,0:T(8,128)(2,1)} %add_convert_fusion.p_ref), custom_call_target="tpu_custom_call" | custom-call | tf_op jit(solution)/shard_map/rs16/pallas_call | solution.py:196
  1648.1 14.5 copy.198
  1674.1 14.5 copy.194
  1736.8 23.8 %all-to-all-done.7 = bf16[2,1536,512]{2,0,1:T(2,128)(2,1)} async-done(((bf16[2,1536,512]{2,0,1:T(2,128)(2,1)}), bf16[2,1536,512]{2,0,1:T(2,128)(2,1)}, u32[]{:S(2)}, u32[]{:S(2)}) %all-to-all-start.7) | async-done | bytes 3145760 | tf_op jit(solution)/shard_map/all_to_all | solution.py:651
  1781.5 21.3 all-to-all-done.9
  1821.1 14.5 copy.196
  1864.2 14.5 copy.192
  1967.6 30.5 %collective-permute-done.23 = bf16[8,128,1536]{2,1,0:T(8,128)(2,1)} collective-permute-done((bf16[8,128,1536]{2,1,0:T(8,128)(2,1)}, bf16[8,128,1536]{2,1,0:T(8,128)(2,1)}, u32[]{:S(2)}, u32[]{:S(2)}) %collective-permute-start.23) | collective-permute-done | bytes 3145760 | tf_op jit(solution)/shard_map/ppermute | solution.py:43
  2008.4 18.8 collective-permute-done.22
  2032.5 33.1 %collective-permute-done.21 = bf16[8,384,512]{2,1,0:T(8,128)(2,1)} collective-permute-done((bf16[8,384,512]{2,1,0:T(8,128)(2,1)}, bf16[8,384,512]{2,1,0:T(8,128)(2,1)}, u32[]{:S(2)}, u32[]{:S(2)}) %collective-permute-start.21) | collective-permute-done | bytes 3145760 | tf_op jit(solution)/shard_map/ppermute | solution.py:43
  2080.1 14.6 collective-permute-done.20
  2100.2 32.2 %collective-permute-done.19 = bf16[8,384,512]{2,1,0:T(8,128)(2,1)} collective-permute-done((bf16[8,384,512]{2,1,0:T(8,128)(2,1)}, bf16[8,384,512]{2,1,0:T(8,128)(2,1)}, u32[]{:S(2)}, u32[]{:S(2)}) %collective-permute-start.19) | collective-permute-done | bytes 3145760 | tf_op jit(solution)/shard_map/ppermute | solution.py:43
  2175.3 51.3 %reduce-scatter.31.cloned.1.call-done = f32[96,34]{1,0:T(8,128)} async-done(((f32[1536,34]{1,0:T(8,128)}), f32[96,34]{1,0:T(8,128)}) %reduce-scatter.31.cloned.1.call-update) | async-done | bytes 13072
  (867 shorter events, 854.4 us)
Async XLA Ops:
  7.2 94.0 %all-gather.13.cloned.1.call-start = ((), (), s32[]{:S(2)}) async-start(), calls=%async_computation.23 | async-start | bytes 2457600 | tf_op jit(solution)/shard_map/all_gather | solution.py:553
  100.9 261.7 %reduce-scatter.15.cloned.1.call-start = ((), (), s32[]{:S(2)}) async-start(), calls=%async_computation.25 | async-start | bytes 3932160 | tf_op jit(solution)/shard_map/reduce_scatter | solution.py:389
  151.5 103.9 %collective-permute-start.6 = (bf16[2,512,1536]{2,1,0:T(8,128)(2,1)}, bf16[2,512,1536]{2,1,0:T(8,128)(2,1)}, u32[]{:S(2)}, u32[]{:S(2)}) collective-permute-start(bf16[2,512,1536]{2,1,0:T(8,128)(2,1)} %dynamic-slice_bitcast_fusion), channel_id=1, source_target_pairs={{0,16},{16,0},{1,17},{17,1},{2,18},{18,2},{3,19},{19,3},{4,20},{20... | collective-permute-start | bytes 9437192 | tf_op jit(solution)/shard_map/ppermute | solution.py:39
  157.4 133.1 %collective-permute-start.5 = (bf16[2,1536,512]{2,1,0:T(8,128)(2,1)}, bf16[2,1536,512]{2,1,0:T(8,128)(2,1)}, u32[]{:S(2)}, u32[]{:S(2)}) collective-permute-start(bf16[2,1536,512]{2,1,0:T(8,128)(2,1)} %dynamic-slice_bitcast_fusion.1), channel_id=1, source_target_pairs={{0,16},{16,0},{1,17},{17,1},{2,18},{18,2},{3,19},{19,3},{4,20},{20... | collective-permute-start | bytes 9437192 | tf_op jit(solution)/shard_map/ppermute | solution.py:39
  162.7 194.0 %collective-permute-start.4 = (bf16[2,1536,512]{2,1,0:T(8,128)(2,1)}, bf16[2,1536,512]{2,1,0:T(8,128)(2,1)}, u32[]{:S(2)}, u32[]{:S(2)}) collective-permute-start(bf16[2,1536,512]{2,1,0:T(8,128)(2,1)} %dynamic-slice_bitcast_fusion.2), channel_id=1, source_target_pairs={{0,16},{16,0},{1,17},{17,1},{2,18},{18,2},{3,19},{19,3},{4,20},{20... | collective-permute-start | bytes 9437192 | tf_op jit(solution)/shard_map/ppermute | solution.py:39
  246.1 383.5 %all-gather.19.cloned.1.call-start = ((), (), s32[]{:S(2)}) async-start(), calls=%async_computation.27 | async-start | bytes 2457600 | tf_op jit(solution)/shard_map/all_gather | solution.py:553
  255.4 404.0 %all-gather.17.cloned.1.call-start = ((), (), s32[]{:S(2)}) async-start(), calls=%async_computation.26 | async-start | bytes 3932160 | tf_op jit(solution)/shard_map/all_gather | solution.py:382
  629.5 172.8 %reduce-scatter.17.cloned.1.call-start = ((), (), s32[]{:S(2)}) async-start(), calls=%async_computation.29 | async-start | bytes 3932160 | tf_op jit(solution)/shard_map/reduce_scatter | solution.py:389
  936.2 172.0 %all-to-all-start.2 = ((f32[16,2,256]{2,1,0:T(2,128)}), f32[16,2,256]{2,1,0:T(2,128)S(1)}, u32[]{:S(2)}, u32[]{:S(2)}) async-start(f32[16,2,256]{2,1,0:T(2,128)} %pad_maximum_fusion.28), calls=%async_computation.4 | async-start | bytes 65536 | tf_op jit(solution)/shard_map/all_to_all | solution.py:478
  943.2 201.2 %all-gather.23.cloned.1.call-start = ((), (), s32[]{:S(2)}) async-start(), calls=%async_computation.30 | async-start | bytes 3932160 | tf_op jit(solution)/shard_map/all_gather | solution.py:490
  1114.4 224.8 %reduce-scatter.19.cloned.1.call-start = ((), (), s32[]{:S(2)}) async-start(), calls=%async_computation.31 | async-start | bytes 3932160 | tf_op jit(solution)/shard_map/reduce_scatter | solution.py:496
  1443.0 169.1 %all-to-all-start.3 = ((f32[16,2,256]{2,1,0:T(2,128)}), f32[16,2,256]{2,1,0:T(2,128)S(1)}, u32[]{:S(2)}, u32[]{:S(2)}) async-start(f32[16,2,256]{2,1,0:T(2,128)} %pad_maximum_fusion.29), calls=%async_computation.6 | async-start | bytes 65536 | tf_op jit(solution)/shard_map/all_to_all | solution.py:478
  1455.0 247.6 %all-gather.25.cloned.1.call-start = ((), (), s32[]{:S(2)}) async-start(), calls=%async_computation.32 | async-start | bytes 3932160 | tf_op jit(solution)/shard_map/all_gather | solution.py:490
  1618.0 314.2 %reduce-scatter.29.cloned.1.call-start = ((), (), s32[]{:S(2)}) async-start(), calls=%async_computation.37 | async-start | bytes 1474560 | tf_op jit(solution)/shard_map/reduce_scatter | solution.py:621
  1635.6 81.0 %all-to-all-start.11 = ((bf16[2,512,1536]{2,0,1:T(2,128)(2,1)}), bf16[2,512,1536]{2,0,1:T(2,128)(2,1)}, u32[]{:S(2)}, u32[]{:S(2)}) async-start(bf16[2,512,1536]{2,0,1:T(2,128)(2,1)} %copy.202), calls=%async_computation.19 | async-start | bytes 6291456 | tf_op jit(solution)/shard_map/all_to_all | solution.py:651
  1640.4 302.4 %reduce-scatter.25.cloned.1.call-start = ((), (), s32[]{:S(2)}) async-start(), calls=%async_computation.35 | async-start | bytes 2457600 | tf_op jit(solution)/shard_map/reduce_scatter | solution.py:621
  1666.6 295.6 %reduce-scatter.33.cloned.1.call-start = ((), (), s32[]{:S(2)}) async-start(), calls=%async_computation.39 | async-start | bytes 835584
  1702.1 363.4 %reduce-scatter.27.cloned.1.call-start = ((), (), s32[]{:S(2)}) async-start(), calls=%async_computation.36 | async-start | bytes 1474560 | tf_op jit(solution)/shard_map/reduce_scatter | solution.py:621
  1806.5 337.5 %reduce-scatter.23.cloned.1.call-start = ((), (), s32[]{:S(2)}) async-start(), calls=%async_computation.34 | async-start | bytes 2457600 | tf_op jit(solution)/shard_map/reduce_scatter | solution.py:621
  1854.0 78.1 %collective-permute-start.24 = (bf16[8,128,1536]{2,1,0:T(8,128)(2,1)}, bf16[8,128,1536]{2,1,0:T(8,128)(2,1)}, u32[]{:S(2)}, u32[]{:S(2)}) collective-permute-start(bf16[8,128,1536]{2,1,0:T(8,128)(2,1)} %bitcast.217), channel_id=1, source_target_pairs={{0,16},{1,17},{2,18},{3,19},{4,20},{5,21},{6,22},{7,23},{8,24},{9,... | collective-permute-start | bytes 9437192 | tf_op jit(solution)/shard_map/ppermute | solution.py:43
  1891.4 266.7 %reduce-scatter.21.cloned.1.call-start = ((), (), s32[]{:S(2)}) async-start(), calls=%async_computation.33 | async-start | bytes 3932160 | tf_op jit(solution)/shard_map/reduce_scatter | solution.py:496
  1903.1 95.0 %collective-permute-start.23 = (bf16[8,128,1536]{2,1,0:T(8,128)(2,1)}, bf16[8,128,1536]{2,1,0:T(8,128)(2,1)}, u32[]{:S(2)}, u32[]{:S(2)}) collective-permute-start(bf16[8,128,1536]{2,1,0:T(8,128)(2,1)} %bitcast.212), channel_id=1, source_target_pairs={{16,0},{17,1},{18,2},{19,3},{20,4},{21,5},{22,6},{23,7},{24,8},{25... | collective-permute-start | bytes 9437192 | tf_op jit(solution)/shard_map/ppermute | solution.py:43
  1916.1 111.1 %collective-permute-start.22 = (bf16[8,384,512]{2,1,0:T(8,128)(2,1)}, bf16[8,384,512]{2,1,0:T(8,128)(2,1)}, u32[]{:S(2)}, u32[]{:S(2)}) collective-permute-start(bf16[8,384,512]{2,1,0:T(8,128)(2,1)} %bitcast.206), channel_id=1, source_target_pairs={{0,16},{1,17},{2,18},{3,19},{4,20},{5,21},{6,22},{7,23},{8,24},{9,... | collective-permute-start | bytes 9437192 | tf_op jit(solution)/shard_map/ppermute | solution.py:43
  1930.6 134.9 %collective-permute-start.21 = (bf16[8,384,512]{2,1,0:T(8,128)(2,1)}, bf16[8,384,512]{2,1,0:T(8,128)(2,1)}, u32[]{:S(2)}, u32[]{:S(2)}) collective-permute-start(bf16[8,384,512]{2,1,0:T(8,128)(2,1)} %bitcast.201), channel_id=1, source_target_pairs={{16,0},{17,1},{18,2},{19,3},{20,4},{21,5},{22,6},{23,7},{24,8},{25... | collective-permute-start | bytes 9437192 | tf_op jit(solution)/shard_map/ppermute | solution.py:43
  1942.8 84.5 %all-to-all-start.5 = ((bf16[4,96,640]{2,1,0:T(8,128)(2,1)}), bf16[4,96,640]{2,1,0:T(8,128)(2,1)}, u32[]{:S(2)}, u32[]{:S(2)}) async-start(bf16[4,96,640]{2,1,0:T(8,128)(2,1)} %bitcast.768), calls=%async_computation.11 | async-start | bytes 983040 | tf_op jit(solution)/shard_map/all_to_all | solution.py:630
  1951.3 143.4 %collective-permute-start.20 = (bf16[8,384,512]{2,1,0:T(8,128)(2,1)}, bf16[8,384,512]{2,1,0:T(8,128)(2,1)}, u32[]{:S(2)}, u32[]{:S(2)}) collective-permute-start(bf16[8,384,512]{2,1,0:T(8,128)(2,1)} %bitcast.195), channel_id=1, source_target_pairs={{0,16},{1,17},{2,18},{3,19},{4,20},{5,21},{6,22},{7,23},{8,24},{9,... | collective-permute-start | bytes 9437192 | tf_op jit(solution)/shard_map/ppermute | solution.py:43
  1959.9 172.5 %collective-permute-start.19 = (bf16[8,384,512]{2,1,0:T(8,128)(2,1)}, bf16[8,384,512]{2,1,0:T(8,128)(2,1)}, u32[]{:S(2)}, u32[]{:S(2)}) collective-permute-start(bf16[8,384,512]{2,1,0:T(8,128)(2,1)} %bitcast.190), channel_id=1, source_target_pairs={{16,0},{17,1},{18,2},{19,3},{20,4},{21,5},{22,6},{23,7},{24,8},{25... | collective-permute-start | bytes 9437192 | tf_op jit(solution)/shard_map/ppermute | solution.py:43
  1998.1 150.2 %collective-permute-start.18 = (bf16[96,1536]{1,0:T(8,128)(2,1)}, bf16[96,1536]{1,0:T(8,128)(2,1)}, u32[]{:S(2)}, u32[]{:S(2)}) collective-permute-start(bf16[96,1536]{1,0:T(8,128)(2,1)} %collective-permute-done.16), channel_id=1, source_target_pairs={{0,16},{1,17},{2,18},{3,19},{4,20},{5,21},{6,22},{7,23},{8,24},{9,... | collective-permute-start | bytes 884744 | tf_op jit(solution)/shard_map/ppermute | solution.py:43
  2027.3 138.1 %collective-permute-start.14 = (bf16[4,96,640]{2,1,0:T(8,128)(2,1)}, bf16[4,96,640]{2,1,0:T(8,128)(2,1)}, u32[]{:S(2)}, u32[]{:S(2)}) collective-permute-start(bf16[4,96,640]{2,1,0:T(8,128)(2,1)} %all-to-all-done.5), channel_id=1, source_target_pairs={{0,16},{1,17},{2,18},{3,19},{4,20},{5,21},{6,22},{7,23},{8,24},{9,... | collective-permute-start | bytes 1474568 | tf_op jit(solution)/shard_map/ppermute | solution.py:43
  2094.7 141.2 %collective-permute-start.10 = (f32[256,1536]{1,0:T(8,128)S(1)}, f32[256,1536]{1,0:T(8,128)}, u32[]{:S(2)}, u32[]{:S(2)}) collective-permute-start(f32[256,1536]{1,0:T(8,128)S(1)} %copy-done.23), channel_id=1, source_target_pairs={{0,16},{1,17},{2,18},{3,19},{4,20},{5,21},{6,22},{7,23},{8,24},{9,... | collective-permute-start | bytes 4718600 | tf_op jit(solution)/shard_map/ppermute | solution.py:43
  2132.4 100.2 %collective-permute-start.12 = (f32[96,34]{0,1:T(8,128)}, f32[96,34]{0,1:T(8,128)}, u32[]{:S(2)}, u32[]{:S(2)}) collective-permute-start(f32[96,34]{0,1:T(8,128)} %copy.241), channel_id=1, source_target_pairs={{0,16},{1,17},{2,18},{3,19},{4,20},{5,21},{6,22},{7,23},{8,24},{9,... | collective-permute-start | bytes 39176 | tf_op jit(solution)/shard_map/ppermute | solution.py:43
  2148.3 78.2 %reduce-scatter.31.cloned.1.call-start = ((), (), s32[]{:S(2)}) async-start(), calls=%async_computation.38 | async-start | bytes 835584
  (260 other events, 5850.5 us)
Sparse Core Ops, SparseCore 0:
  36.1 43.5 all-gather.12
  81.8 28.8 all-gather.10
  112.8 30.1 all-gather.14
  147.9 37.9 reduce-scatter.14
  255.5 44.6 all-gather.18
  628.9 30.4 all-gather.16
  661.0 29.5 all-gather.20
  695.6 54.5 reduce-scatter.16
  1114.5 29.8 all-gather.22
  1193.2 37.9 reduce-scatter.18
  1618.1 32.3 all-gather.24
  1652.8 27.4 reduce-scatter.28
  1682.7 40.6 reduce-scatter.24
  1727.3 57.6 reduce-scatter.32
  1787.1 27.8 reduce-scatter.26
  1817.2 40.6 reduce-scatter.22
  1899.1 54.6 reduce-scatter.20
  2165.5 60.9 reduce-scatter.30

commit v3 on v1

v3 whole, which is shorter than its diff:
```python
import jax
import jax.numpy as jnp
from jax import lax
from jax.experimental import pallas as pl
from jax.experimental.pallas import tpu as pltpu
from jax.sharding import PartitionSpec as P

HEADS = 24
KV_HEADS = 8
HEAD_DIM = 64
TOP_K = 8
EXPERTS = 32
CAP = 80
GROUP = HEADS // KV_HEADS
TOKENS = ("dp", "seq")
MESH = pl.DeviceIdType.MESH
DMA = pltpu.SemaphoreType.DMA

epsilon = 1e-06


def dot(a, b):
    return jnp.dot(a, b, preferred_element_type=jnp.float32)


def dot_t(a, b):
    return lax.dot_general(a, b, (((1,), (1,)), ((), ())), preferred_element_type=jnp.float32)


def t_dot(a, b):
    return lax.dot_general(a, b, (((0,), (0,)), ((), ())), preferred_element_type=jnp.float32)


def low(v):
    return v.astype(jnp.bfloat16)


def swap(block):
    return lax.ppermute(block, "section", [(0, 1), (1, 0)])


def pass_to(block, section):
    return lax.ppermute(block, "section", [(1 - section, section)])


def rms_norm(values, norm_gain):
    return (
        values * lax.rsqrt(jnp.mean(values * values, axis=-1, keepdims=True) + epsilon) * norm_gain
    )


def rotary_tables(length):
    half_dim = HEAD_DIM // 2
    frequency = 10000.0 ** (-jnp.arange(half_dim, dtype=jnp.float32) * 2.0 / HEAD_DIM)
    angles = jnp.arange(length, dtype=jnp.float32)[:, None] * frequency[None, :]
    return (jnp.cos(angles)[:, None, :], jnp.sin(angles)[:, None, :])


def rotate(values, cos_table, sin_table):
    length = values.shape[0]
    split_heads = values.reshape(length, -1, HEAD_DIM)
    first_half = split_heads[..., : HEAD_DIM // 2]
    second_half = split_heads[..., HEAD_DIM // 2 :]
    turned = jnp.concatenate(
        [
            first_half * cos_table - second_half * sin_table,
            second_half * cos_table + first_half * sin_table,
        ],
        axis=-1,
    )
    return turned.reshape(length, -1)


def attention_forward(q_heads, k_heads, v_heads):
    length = q_heads.shape[0]
    local_kv = k_heads.shape[1] // HEAD_DIM
    cos_table, sin_table = rotary_tables(length)
    q_rot = low(rotate(q_heads.astype(jnp.float32), cos_table, sin_table)).reshape(
        length, local_kv, GROUP, HEAD_DIM
    )
    k_rot = low(rotate(k_heads.astype(jnp.float32), cos_table, sin_table)).reshape(
        length, local_kv, HEAD_DIM
    )
    values = v_heads.reshape(length, local_kv, HEAD_DIM)
    block_rows = min(512, length)
    outputs = []
    totals_list = []
    for first_row in range(0, length, block_rows):
        key_end = first_row + block_rows
        scores = (
            jnp.einsum(
                "qhgd,khd->hgqk",
                q_rot[first_row:key_end],
                k_rot[:key_end],
                preferred_element_type=jnp.float32,
            )
            * 0.125
        )
        causal = (first_row + jnp.arange(block_rows, dtype=jnp.int32))[:, None] >= jnp.arange(
            key_end, dtype=jnp.int32
        )[None, :]
        scores = jnp.where(causal, scores, -jnp.inf)
        row_peak = jnp.max(scores, axis=-1, keepdims=True)
        exponents = jnp.exp(scores - row_peak)
        totals = jnp.sum(exponents, axis=-1, keepdims=True)
        attended = jnp.einsum(
            "hgqk,khd->qhgd",
            low(exponents / totals),
            values[:key_end],
            preferred_element_type=jnp.float32,
        )
        outputs.append(low(attended).reshape(block_rows, -1))
        totals_list.append((row_peak + jnp.log(totals))[..., 0])
    return (jnp.concatenate(outputs, axis=0), jnp.stack(totals_list), q_rot, k_rot, values)


def attention_backward(head_grad, q_rot, k_rot, values, log_total):
    length, local_kv = q_rot.shape[:2]
    cos_table, sin_table = rotary_tables(length)
    block_rows = min(512, length)
    grad_rows = head_grad.reshape(length, local_kv, GROUP, HEAD_DIM)
    key_acc = jnp.zeros((length, local_kv, HEAD_DIM), jnp.float32)
    value_acc = jnp.zeros((length, local_kv, HEAD_DIM), jnp.float32)
    query_parts = []
    for block_number, first_row in enumerate(range(0, length, block_rows)):
        key_end = first_row + block_rows
        q_block = q_rot[first_row:key_end]
        grad_block = grad_rows[first_row:key_end]
        key_part = k_rot[:key_end]
        scores = (
            jnp.einsum("qhgd,khd->hgqk", q_block, key_part, preferred_element_type=jnp.float32)
            * 0.125
        )
        causal = (first_row + jnp.arange(block_rows, dtype=jnp.int32))[:, None] >= jnp.arange(
            key_end, dtype=jnp.int32
        )[None, :]
        scores = jnp.where(causal, scores, -jnp.inf)
        probs_full = jnp.exp(scores - log_total[block_number][..., None])
        prob_grad = jnp.einsum(
            "qhgd,khd->hgqk", grad_block, values[:key_end], preferred_element_type=jnp.float32
        )
        score_grad = probs_full * (
            prob_grad - jnp.sum(probs_full * prob_grad, axis=-1, keepdims=True)
        )
        score_low = low(score_grad)
        query_parts.append(
            jnp.einsum("hgqk,khd->qhgd", score_low, key_part, preferred_element_type=jnp.float32)
            * 0.125
        )
        key_acc = key_acc.at[:key_end].add(
            jnp.einsum("hgqk,qhgd->khd", score_low, q_block, preferred_element_type=jnp.float32)
            * 0.125
        )
        value_acc = value_acc.at[:key_end].add(
            jnp.einsum(
                "hgqk,qhgd->khd", low(probs_full), grad_block, preferred_element_type=jnp.float32
            )
        )
    query_all = jnp.concatenate(query_parts, axis=0).reshape(length, -1)
    query_grad = rotate(query_all, cos_table, -sin_table)
    key_grad = rotate(key_acc.reshape(length, -1), cos_table, -sin_table)
    return jnp.concatenate(
        [low(query_grad), low(key_grad), low(value_acc).reshape(length, -1)], axis=1
    )


def remote(src, dst, send_sem, recv_sem, **device):
    return pltpu.make_async_remote_copy(
        src_ref=src,
        dst_ref=dst,
        send_sem=send_sem,
        recv_sem=recv_sem,
        device_id=device,
        device_id_type=MESH,
    )


def greet(d, s):
    barrier = pltpu.get_barrier_semaphore()

    def signal(**device):
        pl.semaphore_signal(barrier, inc=1, device_id=device, device_id_type=MESH)

    signal(seq=s ^ 1)
    signal(seq=s ^ 2)

    @pl.when(d > 0)
    def _():
        signal(dp=d - 1)

    @pl.when(d < 3)
    def _():
        signal(dp=d + 1)

    inner = (d > 0) & (d < 3)

    @pl.when(inner)
    def _():
        pl.semaphore_wait(barrier, 4)

    @pl.when(jnp.logical_not(inner))
    def _():
        pl.semaphore_wait(barrier, 3)


def gather_scratch(rows, width):
    return [
        pltpu.VMEM((16, rows, width), jnp.bfloat16),
        DMA(()),
        DMA((2, 4)),
        DMA((4,)),
        DMA((4,)),
        DMA((4,)),
        DMA((4, 2)),
        DMA((4, 2)),
    ]


def gather_blocks(x_ref, scratch, compute):
    land, lsem, zs, zr, ys, yr, cs, cr = scratch
    d, s = lax.axis_index("dp"), lax.axis_index("seq")

    def place(z, column):
        return land.at[z * 4 + column]

    def z_copy(src, z, right):
        target = d + 1 if right else d - 1
        return remote(src, place(z, s), zs.at[int(right), z], zr.at[z], dp=target)

    def y_copy(src, z):
        return remote(src, place(z, s), ys.at[z], yr.at[z], seq=s ^ 2)

    def core_copy(src, z, across):
        column = s ^ 2 if across else s
        return remote(src, place(z, column), cs.at[z, across], cr.at[z, across], seq=s ^ 1)

    greet(d, s)
    own = pltpu.make_async_copy(x_ref, place(d, s), lsem)
    own.start()

    @pl.when(d < 3)
    def _():
        z_copy(x_ref, d, True).start()

    @pl.when(d > 0)
    def _():
        z_copy(x_ref, d, False).start()

    y_copy(x_ref, d).start()
    core_copy(x_ref, d, 0).start()
    own.wait()

    @pl.loop(0, 4)
    def _(i):
        @pl.when(i < 3)
        def _():
            left, right = d - (i + 1), d + (i + 1)

            @pl.when(left >= 0)
            def _():
                z_copy(place(left, s), left, True).wait_recv()

                @pl.when(d < 3)
                def _():
                    z_copy(place(left, s), left, True).start()

            @pl.when(right <= 3)
            def _():
                z_copy(place(right, s), right, False).wait_recv()

                @pl.when(d > 0)
                def _():
                    z_copy(place(right, s), right, False).start()

            following = d ^ (i + 1)
            y_copy(place(following, s), following).start()
            core_copy(place(following, s), following, 0).start()

        z = d ^ i
        y_copy(place(z, s ^ 2), z).wait_recv()
        core_copy(place(z, s ^ 2), z, 1).start()
        core_copy(place(z, s ^ 1), z, 0).wait_recv()
        core_copy(place(z, s ^ 3), z, 1).wait_recv()
        compute(z)

    for z in range(4):

        @pl.when((z <= d) & (d < 3))
        def _():
            z_copy(place(z, s), z, True).wait_send()

        @pl.when((z >= d) & (d > 0))
        def _():
            z_copy(place(z, s), z, False).wait_send()

        y_copy(place(z, s), z).wait_send()
        core_copy(place(z, s), z, 0).wait_send()
        core_copy(place(z, s), z, 1).wait_send()
    return land


def pick_weights(own_refs, other_refs, held, sems, own_layer):
    mine = lax.axis_index("section") == own_layer

    @pl.when(mine)
    def _():
        for k, ref in enumerate(own_refs):
            pltpu.make_async_copy(ref, held[k], sems.at[k]).start()

    @pl.when(jnp.logical_not(mine))
    def _():
        for k, ref in enumerate(other_refs):
            pltpu.make_async_copy(ref, held[k], sems.at[k]).start()

    def ready(k):
        pltpu.make_async_copy(own_refs[k], held[k], sems.at[k]).wait()

    return ready


def expert_forward_kernel(
    layer, x_ref, pick_ref, chosen_ref, router_ref, mine_ref,
    wg_own, wu_own, wd_own, wg_other, wu_other, wd_other,
    rows_out, gate_out, up_out, hidden_out, slot_gate_out, y_out,
    wg, wu, wd, rows, gate, up, hidden, slot_gate, y, wsem, osem, *gather
):
    count = wg.shape[0]
    ready = pick_weights(
        (wg_own, wu_own, wd_own), (wg_other, wu_other, wd_other), (wg, wu, wd), wsem, layer
    )
    land = gather[0]
    d = lax.axis_index("dp")

    def outs(z):
        part = pl.ds(z * 4 * CAP, 4 * CAP)
        return [
            pltpu.make_async_copy(held.at[:, part], out.at[:, part], osem.at[k, z])
            for k, (held, out) in enumerate(
                ((rows, rows_out), (gate, gate_out), (up, up_out), (hidden, hidden_out), (slot_gate, slot_gate_out))
            )
        ] + [pltpu.make_async_copy(y.at[pl.ds(z * 4, 4)], y_out.at[pl.ds(z * 4, 4)], osem.at[5, z])]

    def compute(z):
        @pl.when(z == d)
        def _():
            for k in range(3):
                ready(k)

        for q in range(4):
            b = z * 4 + q
            picked = low(dot(pick_ref[b], land[b]))
            for j in range(count):
                rows[j, pl.ds(b * CAP, CAP), :] = picked[j * CAP : (j + 1) * CAP]
        part = pl.ds(z * 4 * CAP, 4 * CAP)

        @pl.loop(0, count)
        def _(j):
            x = rows[j, part, :]
            g = dot(x, wg[j])
            u = dot(x, wu[j])
            logits = dot(x, router_ref[...])
            for q in range(4):
                b = z * 4 + q
                slots = slice(q * CAP, (q + 1) * CAP)
                seen = dot(pick_ref[b, pl.ds(j * CAP, CAP), :], chosen_ref[b])
                masked = jnp.where(seen > 0.5, logits[slots], -1e30)
                power = jnp.exp(masked - jnp.max(masked, axis=1, keepdims=True))
                own = jnp.sum(power * mine_ref[j], axis=1, keepdims=True)
                value = own / jnp.sum(power, axis=1, keepdims=True)
                slot_gate[j, pl.ds(b * CAP, CAP), :] = jnp.broadcast_to(value, (CAP, 128))
            gate[j, part, :] = low(g)
            up[j, part, :] = low(u)
            h = low(g * jax.nn.sigmoid(g) * u * slot_gate[j, part, :][:, :1])
            hidden[j, part, :] = h
            result = low(dot(h, wd[j]))
            for q in range(4):
                y[z * 4 + q, pl.ds(j * CAP, CAP), :] = result[q * CAP : (q + 1) * CAP]

        for copy in outs(z):
            copy.start()

    gather_blocks(x_ref, gather, compute)
    for z in range(4):
        for copy in outs(z):
            copy.wait()


def expert_forward(layer, x, pick, chosen, router, mine, own, other, collective_id):
    count, width, units = own[0].shape
    rows = x.shape[0]
    slots = 16 * CAP
    bf = jnp.bfloat16
    anywhere = pl.BlockSpec(memory_space=pl.ANY)
    near = pl.BlockSpec(memory_space=pltpu.VMEM)
    results = [
        ((count, slots, width), bf),
        ((count, slots, units), bf),
        ((count, slots, units), bf),
        ((count, slots, units), bf),
        ((count, slots, 128), jnp.float32),
        ((16, count * CAP, width), bf),
    ]
    def kernel(*refs):
        expert_forward_kernel(layer, *refs)
    return pl.pallas_call(
        kernel,
        out_shape=[jax.ShapeDtypeStruct(*result) for result in results],
        in_specs=[anywhere, near, near, near, near] + [anywhere] * 6,
        out_specs=[anywhere] * 6,
        scratch_shapes=[pltpu.VMEM(weight.shape, bf) for weight in own]
        + [pltpu.VMEM(*result) for result in results]
        + [DMA((3,)), DMA((6, 4))]
        + gather_scratch(rows, width),
        compiler_params=pltpu.CompilerParams(
            collective_id=collective_id, has_side_effects=True, vmem_limit_bytes=60 << 20
        ),
        name="expert_forward",
    )(x, pick, chosen, router, mine, *own, *other)


def combine_kernel(pick_ref, y_ref, out_ref, y, sent, own, core_in, y_in, z_in, lsem, zs, zr, ys, yr, cs, cr):
    d, s = lax.axis_index("dp"), lax.axis_index("seq")
    half = out_ref.shape[0] // 2

    def loaded(b):
        return pltpu.make_async_copy(y_ref.at[b], y.at[b], lsem.at[b])

    def column(across, other_core):
        return s ^ (2 * across) ^ other_core

    for i in range(4):
        z = d ^ (3 - i)
        for across in (1, 0):
            for other_core in (1, 0):
                loaded(z * 4 + column(across, other_core)).start()
    greet(d, s)

    def rows(k):
        return pl.ds(pl.multiple_of(k * half, half), half)

    def partial_sum(z, k, across, other_core):
        b = z * 4 + column(across, other_core)

        @pl.when(k == 0)
        def _():
            loaded(b).wait()

        return dot(pick_ref[b, rows(k), :], y[b])

    def core_copy(z, k, across):
        return remote(
            sent.at[z, across, rows(k)],
            core_in.at[z, across, rows(k)],
            cs.at[z, k, across],
            cr.at[z, k, across],
            seq=s ^ 1,
        )

    def y_copy(z, k):
        return remote(own.at[z, 1, rows(k)], y_in.at[z, rows(k)], ys.at[z, k], yr.at[z, k], seq=s ^ 2)

    def z_copy(z, k, right):
        target = d + 1 if right else d - 1
        return remote(
            own.at[z, 0, rows(k)],
            z_in.at[int(right), z, rows(k)],
            zs.at[z, k],
            zr.at[int(right), z, k],
            dp=target,
        )

    def start(i):
        z, k = d ^ (3 - i // 2), i % 2
        sent[z, 1, rows(k), :] = low(partial_sum(z, k, 1, 1))
        core_copy(z, k, 1).start()
        total = partial_sum(z, k, 1, 0)
        core_copy(z, k, 1).wait_recv()
        own[z, 1, rows(k), :] = low(total + core_in[z, 1, rows(k), :].astype(jnp.float32))
        y_copy(z, k).start()
        sent[z, 0, rows(k), :] = low(partial_sum(z, k, 0, 1))
        core_copy(z, k, 0).start()

    start(0)

    @pl.loop(0, 8)
    def _(i):
        @pl.when(i < 7)
        def _():
            start(i + 1)

        z, k = d ^ (3 - i // 2), i % 2
        total = partial_sum(z, k, 0, 0)
        core_copy(z, k, 0).wait_recv()
        total = total + core_in[z, 0, rows(k), :].astype(jnp.float32)
        y_copy(z, k).wait_recv()
        total = total + y_in[z, rows(k), :].astype(jnp.float32)

        @pl.when(z < d)
        def _():
            @pl.when(d < 3)
            def _():
                z_copy(z, k, False).wait_recv()
                own[z, 0, rows(k), :] = low(total + z_in[0, z, rows(k), :].astype(jnp.float32))

            @pl.when(d == 3)
            def _():
                own[z, 0, rows(k), :] = low(total)

            z_copy(z, k, False).start()

        @pl.when(z > d)
        def _():
            @pl.when(d > 0)
            def _():
                z_copy(z, k, True).wait_recv()
                own[z, 0, rows(k), :] = low(total + z_in[1, z, rows(k), :].astype(jnp.float32))

            @pl.when(d == 0)
            def _():
                own[z, 0, rows(k), :] = low(total)

            z_copy(z, k, True).start()

        @pl.when(z == d)
        def _():
            out_ref[rows(k), :] = total

    for k in range(2):

        @pl.when(d < 3)
        def _():
            z_copy(d, k, False).wait_recv()
            out_ref[rows(k), :] += z_in[0, d, rows(k), :].astype(jnp.float32)

        @pl.when(d > 0)
        def _():
            z_copy(d, k, True).wait_recv()
            out_ref[rows(k), :] += z_in[1, d, rows(k), :].astype(jnp.float32)

    for z in range(4):
        for k in range(2):
            core_copy(z, k, 0).wait_send()
            core_copy(z, k, 1).wait_send()
            y_copy(z, k).wait_send()

            @pl.when(z < d)
            def _():
                z_copy(z, k, False).wait_send()

            @pl.when(z > d)
            def _():
                z_copy(z, k, True).wait_send()


def combine(pick_t, y, collective_id):
    rows, width = pick_t.shape[1], y.shape[2]

    def blocks(*lead):
        return pltpu.VMEM(lead + (rows, width), jnp.bfloat16)

    return pl.pallas_call(
        combine_kernel,
        out_shape=jax.ShapeDtypeStruct((rows, width), jnp.float32),
        in_specs=[pl.BlockSpec(memory_space=pltpu.VMEM), pl.BlockSpec(memory_space=pl.ANY)],
        out_specs=pl.BlockSpec(memory_space=pltpu.VMEM),
        scratch_shapes=[
            pltpu.VMEM(y.shape, jnp.bfloat16),
            blocks(4, 2),
            blocks(4, 2),
            blocks(4, 2),
            blocks(4),
            blocks(2, 4),
            DMA((16,)),
            DMA((4, 2)),
            DMA((2, 4, 2)),
            DMA((4, 2)),
            DMA((4, 2)),
            DMA((4, 2, 2)),
            DMA((4, 2, 2)),
        ],
        compiler_params=pltpu.CompilerParams(
            collective_id=collective_id, has_side_effects=True, vmem_limit_bytes=60 << 20
        ),
        name="combine",
    )(pick_t, y)


def expert_backward_kernel(
    layer, x_ref, pick_ref, gate_in, up_in, slot_gate_in,
    wg_own, wu_own, wd_own, wg_other, wu_other, wd_other,
    rows_out, gate_out, up_out, term_out, y_out,
    wg, wu, wd, rows, gate, up, slot_gate, y, wsem, isem, osem, *gather
):
    count = wg.shape[0]
    ready = pick_weights(
        (wg_own, wu_own, wd_own), (wg_other, wu_other, wd_other), (wg, wu, wd), wsem, layer
    )
    land = gather[0]
    d = lax.axis_index("dp")
    ins = [
        pltpu.make_async_copy(src, held, isem.at[k])
        for k, (src, held) in enumerate(((gate_in, gate), (up_in, up), (slot_gate_in, slot_gate)))
    ]
    for copy in ins:
        copy.start()

    def outs(z):
        part = pl.ds(z * 4 * CAP, 4 * CAP)
        return [
            pltpu.make_async_copy(held.at[:, part], out.at[:, part], osem.at[k, z])
            for k, (held, out) in enumerate(
                ((rows, rows_out), (gate, gate_out), (up, up_out), (slot_gate, term_out))
            )
        ] + [pltpu.make_async_copy(y.at[pl.ds(z * 4, 4)], y_out.at[pl.ds(z * 4, 4)], osem.at[4, z])]

    def compute(z):
        @pl.when(z == d)
        def _():
            for k in range(3):
                ready(k)
            for copy in ins:
                copy.wait()

        for q in range(4):
            b = z * 4 + q
            picked = low(dot(pick_ref[b], land[b]))
            for j in range(count):
                rows[j, pl.ds(b * CAP, CAP), :] = picked[j * CAP : (j + 1) * CAP]
        part = pl.ds(z * 4 * CAP, 4 * CAP)

        @pl.loop(0, count)
        def _(j):
            plain = dot_t(rows[j, part, :], wd[j])
            g = gate[j, part, :].astype(jnp.float32)
            u = up[j, part, :].astype(jnp.float32)
            sigmoid = jax.nn.sigmoid(g)
            active = g * sigmoid
            term = jnp.sum(plain * (active * u), axis=1, keepdims=True)
            grad = plain * slot_gate[j, part, :][:, :1]
            dg = low(grad * u * sigmoid * (1.0 + g * (1.0 - sigmoid)))
            du = low(grad * active)
            slot_gate[j, part, :] = jnp.broadcast_to(term, (4 * CAP, 128))
            gate[j, part, :] = dg
            up[j, part, :] = du
            result = low(dot_t(dg, wg[j]) + dot_t(du, wu[j]))
            for q in range(4):
                y[z * 4 + q, pl.ds(j * CAP, CAP), :] = result[q * CAP : (q + 1) * CAP]

        for copy in outs(z):
            copy.start()

    gather_blocks(x_ref, gather, compute)
    for z in range(4):
        for copy in outs(z):
            copy.wait()


def expert_backward(layer, x, pick, gate, up, slot_gate, own, other, collective_id):
    count, width, units = own[0].shape
    rows = x.shape[0]
    slots = 16 * CAP
    bf = jnp.bfloat16
    anywhere = pl.BlockSpec(memory_space=pl.ANY)
    near = pl.BlockSpec(memory_space=pltpu.VMEM)
    results = [
        ((count, slots, width), bf),
        ((count, slots, units), bf),
        ((count, slots, units), bf),
        ((count, slots, 128), jnp.float32),
        ((16, count * CAP, width), bf),
    ]
    def kernel(*refs):
        expert_backward_kernel(layer, *refs)
    return pl.pallas_call(
        kernel,
        out_shape=[jax.ShapeDtypeStruct(*result) for result in results],
        in_specs=[anywhere, near] + [anywhere] * 9,
        out_specs=[anywhere] * 5,
        scratch_shapes=[pltpu.VMEM(weight.shape, bf) for weight in own]
        + [pltpu.VMEM(*result) for result in results]
        + [DMA((3,)), DMA((3,)), DMA((5, 4))]
        + gather_scratch(rows, width),
        compiler_params=pltpu.CompilerParams(
            collective_id=collective_id, has_side_effects=True, vmem_limit_bytes=60 << 20
        ),
        name="expert_backward",
    )(x, pick, gate, up, slot_gate, *own, *other)


def token_choice(route):
    return route[..., None] == jnp.arange(EXPERTS, dtype=jnp.int32)


def routing(route_all, first_expert, count):
    chosen = jnp.any(token_choice(route_all), axis=2)
    blocks, rows = chosen.shape[:2]
    mine = lax.dynamic_slice_in_dim(chosen, first_expert, count, axis=2)
    earlier = jnp.tril(jnp.ones((rows, rows), jnp.bfloat16), -1)
    place = jnp.einsum(
        "ts,bsj->bjt", earlier, mine.astype(jnp.bfloat16), preferred_element_type=jnp.float32
    ).astype(jnp.int32)
    mine = jnp.transpose(mine, (0, 2, 1))
    place = jnp.where(mine, place, -1)
    slots = jnp.arange(CAP, dtype=jnp.int32)
    pick = low(place[:, :, None, :] == slots[None, None, :, None]).reshape(blocks, -1, rows)
    return chosen, pick, jnp.transpose(pick, (0, 2, 1))


def choose(pick, rows, count):
    picked = jnp.einsum("bct,btd->bcd", pick, rows, preferred_element_type=jnp.float32)
    blocks = pick.shape[0]
    picked = low(picked).reshape(blocks, count, CAP, -1)
    return jnp.transpose(picked, (1, 0, 2, 3)).reshape(count, blocks * CAP, -1)


def give_back(pick_t, slot_rows):
    blocks, rows = pick_t.shape[:2]
    count, _, width = slot_rows.shape
    slot_rows = jnp.transpose(slot_rows.reshape(count, blocks, CAP, width), (1, 0, 2, 3))
    slot_rows = slot_rows.reshape(blocks, count * CAP, width)
    total = jnp.einsum("btc,bcd->btd", pick_t, slot_rows, preferred_element_type=jnp.float32)
    return low(total).reshape(-1, width)


def each_dot(form, a, b):
    return jnp.einsum(form, a, b, preferred_element_type=jnp.float32)


def after(value, *others):
    return lax.optimization_barrier((value, *others))[0]


def has_kernels():
    return lax.axis_size("dp") == 4 and lax.axis_size("seq") == 4


def forward_layer(number, layer_in, picking, weights, experts):
    attn_scale, ffn_scale, qkv_w, out_w, router_w = weights
    chosen, pick, pick_t, first_expert = picking
    own, other = experts
    count = own[0].shape[0]
    blocks, rows = chosen.shape[:2]
    normed_input = low(rms_norm(layer_in, attn_scale))
    normed_all = lax.all_gather(normed_input, "seq", axis=0, tiled=True)
    qkv = low(dot(normed_all, qkv_w))
    kv_width = KV_HEADS * HEAD_DIM // lax.axis_size("seq")
    q_width = GROUP * kv_width
    mixed, log_total, q_rot, k_rot, v_heads = attention_forward(
        qkv[:, :q_width], qkv[:, q_width : q_width + kv_width], qkv[:, q_width + kv_width :]
    )
    branch = lax.psum_scatter(low(dot(mixed, out_w)), "seq", scatter_dimension=0, tiled=True)
    after_update = layer_in + branch.astype(jnp.float32)
    normed_ffn = low(rms_norm(after_update, ffn_scale))
    own_block = lax.axis_index("dp") * lax.axis_size("seq") + lax.axis_index("seq")
    own_chosen = lax.dynamic_index_in_dim(chosen, own_block, 0, keepdims=False)
    own_logits = jnp.where(own_chosen, dot(normed_ffn, router_w), -jnp.inf)
    own_gates = jax.nn.softmax(own_logits, axis=-1)
    mine = (
        jnp.arange(EXPERTS)[None, None, :] == first_expert + jnp.arange(count)[:, None, None]
    ).astype(jnp.float32)
    if has_kernels():
        *expert_state, slot_out = expert_forward(
            number, normed_ffn, pick, low(chosen), router_w, mine, own, other, 1 + number
        )
        moe = combine(pick_t, slot_out, 3)
    else:
        gate_w, up_w, down_w = by_layer(number, own, other)
        ffn_all = lax.all_gather(normed_ffn, TOKENS, axis=0, tiled=True)
        logits = dot(ffn_all, router_w).reshape(blocks, rows, EXPERTS)
        gates = jax.nn.softmax(jnp.where(chosen, logits, -jnp.inf), axis=-1)
        slot_rows = choose(pick, ffn_all.reshape(blocks, rows, -1), count)
        mine_gates = jnp.einsum("bte,jxe->bjt", gates, mine, precision=lax.Precision.HIGHEST)
        slot_gates = jnp.sum(
            pick.reshape(blocks, count, CAP, rows).astype(jnp.float32) * mine_gates[:, :, None, :],
            axis=3,
        )
        slot_gates = jnp.transpose(slot_gates, (1, 0, 2)).reshape(count, -1, 1)
        gate_pre = each_dot("ecd,edf->ecf", slot_rows, gate_w)
        up_pre = each_dot("ecd,edf->ecf", slot_rows, up_w)
        scaled = low(slot_gates * jax.nn.silu(gate_pre) * up_pre)
        slot_out = low(each_dot("ecf,efd->ecd", scaled, down_w))
        moe = lax.psum_scatter(
            give_back(pick_t, slot_out), TOKENS, scatter_dimension=0, tiled=True
        ).astype(jnp.float32)
        expert_state = (slot_rows, gate_pre, up_pre, scaled, slot_gates)
    layer_out = after_update + moe
    saved = (
        layer_in,
        normed_all,
        q_rot,
        k_rot,
        v_heads,
        log_total,
        mixed,
        after_update,
        normed_ffn,
        own_gates,
        expert_state,
    )
    return (layer_out, saved)


def backward_layer(number, layer_grad, saved, picking, weights, experts):
    attn_scale, ffn_scale, qkv_w, out_w, router_w = weights
    chosen, pick, pick_t, first_expert = picking
    own, other = experts
    count = own[0].shape[0]
    blocks, rows = chosen.shape[:2]
    (
        layer_in,
        normed_all,
        q_rot,
        k_rot,
        v_heads,
        log_total,
        mixed,
        after_update,
        normed_ffn,
        own_gates,
        (slot_rows, gate_pre, up_pre, scaled, slot_gates),
    ) = saved
    if has_kernels():
        slot_grads, gate_low, up_low, gate_term, slot_out = expert_backward(
            number, low(layer_grad), pick, gate_pre, up_pre, slot_gates, own, other, 4 + number
        )
        gate_term = gate_term[:, :, :1]
    else:
        gate_w, up_w, down_w = by_layer(number, own, other)
        grad_all = lax.all_gather(low(layer_grad), TOKENS, axis=0, tiled=True)
        slot_grads = choose(pick, grad_all.reshape(blocks, rows, -1), count)
        plain_grad = each_dot("ecd,efd->ecf", slot_grads, down_w)
        sigmoid = jax.nn.sigmoid(gate_pre)
        activated = gate_pre * sigmoid
        gate_term = jnp.sum(plain_grad * (activated * up_pre), axis=2, keepdims=True)
        hidden_grad = slot_gates * plain_grad
        gate_low = low(hidden_grad * up_pre * sigmoid * (1.0 + gate_pre * (1.0 - sigmoid)))
        up_low = low(hidden_grad * activated)
        slot_out = low(
            each_dot("ecf,edf->ecd", gate_low, gate_w) + each_dot("ecf,edf->ecd", up_low, up_w)
        )
    expert_grads = (
        low(each_dot("ecd,ecf->edf", slot_rows, gate_low)),
        low(each_dot("ecd,ecf->edf", slot_rows, up_low)),
        low(each_dot("ecf,ecd->efd", scaled, slot_grads)),
    )
    slot_out, *expert_grads = lax.optimization_barrier((slot_out, *expert_grads))
    if has_kernels():
        normed_grad = combine(pick_t, slot_out, 3)
    else:
        normed_grad = lax.psum_scatter(
            give_back(pick_t, slot_out), TOKENS, scatter_dimension=0, tiled=True
        ).astype(jnp.float32)
    by_slot = jnp.transpose(gate_term.reshape(count, blocks, CAP), (1, 0, 2))
    gate_terms = jnp.sum(
        pick.reshape(blocks, count, CAP, rows).astype(jnp.float32) * by_slot[..., None], axis=2
    )
    gate_terms = lax.all_to_all(gate_terms, TOKENS, split_axis=0, concat_axis=0, tiled=True)
    gate_terms = jnp.sum(gate_terms.reshape(EXPERTS, -1, rows), axis=1).T
    logit_grad = low(
        own_gates * (gate_terms - jnp.sum(own_gates * gate_terms, axis=-1, keepdims=True))
    )
    router_grad = t_dot(normed_ffn, logit_grad)
    normed_grad = normed_grad + dot_t(logit_grad, router_w)
    after_part, ffn_gain_grad = jax.vjp(rms_norm, after_update, ffn_scale)[1](normed_grad)
    after_grad = after_part + layer_grad
    branch_all = lax.all_gather(low(after_grad), "seq", axis=0, tiled=True)
    out_grad = t_dot(mixed, branch_all)
    head_grad = low(dot_t(branch_all, out_w))
    qkv_grad = attention_backward(head_grad, q_rot, k_rot, v_heads, log_total)
    qkv_weight_grad = t_dot(normed_all, qkv_grad)
    normed_attn = low(dot_t(qkv_grad, qkv_w))
    normed_attn = lax.psum_scatter(normed_attn, "seq", scatter_dimension=0, tiled=True)
    input_part, attn_gain_grad = jax.vjp(rms_norm, layer_in, attn_scale)[1](
        normed_attn.astype(jnp.float32)
    )
    gain_grads = jnp.stack([attn_gain_grad, ffn_gain_grad])
    return (
        input_part + after_grad,
        (low(qkv_weight_grad), low(out_grad), low(router_grad), gain_grads),
        expert_grads,
    )


def by_layer(number, own, other):
    is_own = lax.axis_index("section") == number
    return jax.tree.map(lambda mine, received: jnp.where(is_own, mine, received), own, other)


def body(
    hidden_in,
    out_grad,
    attn_gain,
    ffn_gain,
    query_matrix,
    key_matrix,
    value_matrix,
    output_matrix,
    router_matrix,
    w_gate,
    w_up,
    w_down,
    routes,
):
    section = lax.axis_index("section")
    dp, seq = lax.axis_size("dp"), lax.axis_size("seq")
    seq_index = lax.axis_index("seq")
    first = section == 0
    width = hidden_in.shape[3]
    depth = query_matrix.shape[1]

    layer_in = lax.dynamic_index_in_dim(hidden_in, section, 0, keepdims=False)[0]
    top_grad = lax.dynamic_index_in_dim(out_grad, section, 0, keepdims=False)[0]
    own_routes = lax.dynamic_index_in_dim(routes[0], section, 0, keepdims=False)[0]
    other_routes = lax.dynamic_index_in_dim(routes[0], 1 - section, 0, keepdims=False)[0]

    own_group = jnp.concatenate(
        [
            matrix[0].reshape(depth, seq, -1)
            for matrix in (query_matrix, key_matrix, value_matrix)
        ],
        axis=2,
    )
    to_group = []
    for flat in range(dp * seq):
        to_group.append((flat, (flat % dp) * seq + flat // dp))
    from_group = [(target, source) for source, target in to_group]
    other_group = swap(own_group)
    own_out = lax.ppermute(output_matrix[0], TOKENS, to_group)
    other_out = swap(own_out)
    other_routes = swap(other_routes)
    small = jnp.concatenate([router_matrix[0], attn_gain[0][:, None], ffn_gain[0][:, None]], axis=1)
    small = lax.all_gather(small, ("section", "dp", "seq"), axis=0, tiled=True)
    small = small.reshape(2, width, -1)

    local = w_gate.shape[1]
    hidden_units = w_gate.shape[3]
    if local >= seq:
        count, units = local // seq, hidden_units
        start, unit_start = seq_index * count, 0
    else:
        count, units = 1, hidden_units * local // seq
        start, unit_start = seq_index * local // seq, (seq_index % (seq // local)) * units
    first_expert = lax.axis_index("dp") * local + start
    own_experts = (
        lax.dynamic_slice(w_gate[0], (start, 0, unit_start), (count, width, units)),
        lax.dynamic_slice(w_up[0], (start, 0, unit_start), (count, width, units)),
        lax.dynamic_slice(w_down[0], (start, unit_start, 0), (count, units, width)),
    )
    other_gate = swap(after(own_experts[0], other_group, other_out))
    other_up = swap(after(own_experts[1], other_gate))
    other_down = swap(after(own_experts[2], other_up))
    experts = (own_experts, (other_gate, other_up, other_down))

    weights = []
    pickings = []
    for number in range(2):
        part = by_layer(number, own_group, other_group)
        part = lax.all_to_all(part, "seq", split_axis=1, concat_axis=0, tiled=True)
        qkv_w = lax.all_gather(part.reshape(seq * depth, -1), "dp", axis=0, tiled=True)
        out_w = lax.all_gather(
            by_layer(number, own_out, other_out), "dp", axis=0, tiled=True
        )
        weights.append(
            (
                small[number, :, EXPERTS].astype(jnp.float32),
                small[number, :, EXPERTS + 1].astype(jnp.float32),
                qkv_w,
                out_w,
                small[number, :, :EXPERTS],
            )
        )
        route = by_layer(number, own_routes, other_routes)
        route_all = lax.all_gather(route, TOKENS, axis=0, tiled=False)
        pickings.append(routing(route_all, first_expert, count) + (first_expert,))

    state = layer_in.astype(jnp.float32)
    layer_states = []
    saved_layers = []
    for number in range(2):
        state, saved = forward_layer(number, state, pickings[number], weights[number], experts)
        layer_states.append(state)
        saved_layers.append(saved)
    grad = top_grad.astype(jnp.float32)
    layer_grads = [None, None]
    dense_grads = [None, None]
    expert_grads = [None, None]
    received = [[None] * 3, [None] * 3]
    for number in (1, 0):
        grad, dense_grads[number], expert_grads[number] = backward_layer(
            number, grad, saved_layers[number], pickings[number], weights[number], experts
        )
        layer_grads[number] = grad
        last = None
        for kind in range(3):
            piece = expert_grads[number][kind]
            piece = piece if last is None else after(piece, last)
            last = received[number][kind] = pass_to(piece, number)

    def own_layer(pieces):
        return jnp.where(first, pieces[0], pieces[1])

    def to_section(pieces):
        other = own_layer([pass_to(pieces[number], number) for number in range(2)])
        own = own_layer(pieces)
        return jnp.stack([jnp.where(first, own, other), jnp.where(first, other, own)])[
            None, :, None
        ]

    def summed(pieces):
        other = own_layer([pass_to(pieces[number], number) for number in range(2)])
        return own_layer(pieces).astype(jnp.float32) + other.astype(jnp.float32)

    kv_width = KV_HEADS * HEAD_DIM // seq
    q_width = GROUP * kv_width
    qkv_width = q_width + 2 * kv_width
    qkv_parts = []
    out_parts = []
    gain_parts = []
    for number in range(2):
        qkv_part, out_part, router_part, gain_part = dense_grads[number]
        qkv_part = jnp.concatenate([qkv_part, router_part], axis=1)
        qkv_part = lax.psum_scatter(qkv_part, "dp", scatter_dimension=0, tiled=True)
        qkv_part = qkv_part.reshape(seq, depth, -1)
        qkv_parts.append(
            lax.all_to_all(qkv_part, "seq", split_axis=0, concat_axis=0, tiled=True)
        )
        out_part = lax.psum_scatter(out_part, "dp", scatter_dimension=0, tiled=True)
        out_parts.append(lax.ppermute(out_part, TOKENS, from_group))
        gain_part = gain_part.reshape(2, dp * seq, depth)
        gain_part = lax.all_to_all(gain_part, TOKENS, split_axis=1, concat_axis=1, tiled=True)
        gain_parts.append(jnp.sum(gain_part, axis=1))
    qkv_sum = summed(qkv_parts)
    out_sum = summed(out_parts)
    gain_sum = summed(gain_parts)

    def columns(begin, end):
        return jnp.transpose(qkv_sum[:, :, begin:end], (1, 0, 2)).reshape(depth, -1)[None]

    expert_sums = []
    for kind in range(3):
        own = own_layer([expert_grads[number][kind] for number in range(2)])
        other = own_layer([received[number][kind] for number in range(2)])
        piece = low(own.astype(jnp.float32) + other.astype(jnp.float32))
        rows = piece.shape[1] // seq
        if local >= seq:
            piece = piece.reshape(count, seq, rows, -1)
            piece = jnp.transpose(piece, (1, 0, 2, 3))
            piece = lax.all_to_all(piece, "seq", split_axis=0, concat_axis=0, tiled=True)
            piece = piece.reshape(local, rows, -1)
        elif kind < 2:
            share = seq // local
            piece = piece.reshape(seq, rows, units)
            piece = lax.all_to_all(piece, "seq", split_axis=0, concat_axis=0, tiled=True)
            piece = piece.reshape(local, share, rows, units)
            piece = jnp.transpose(piece, (0, 2, 1, 3)).reshape(local, rows, -1)
        else:
            rows = hidden_units // seq
            piece = whole_rows(piece.reshape(-1, rows, width), seq_index, seq // local, seq)
        expert_sums.append(piece.astype(jnp.float32)[None])
    return (
        to_section(layer_states),
        to_section(layer_grads),
        gain_sum[0][None],
        gain_sum[1][None],
        columns(0, q_width),
        columns(q_width, q_width + kv_width),
        columns(q_width + kv_width, qkv_width),
        out_sum[None],
        jnp.sum(qkv_sum[:, :, qkv_width:], axis=0)[None],
        *expert_sums,
    )


def whole_rows(piece, seq_index, share, seq):
    parts = piece.shape[0]
    spread = jnp.zeros((seq,) + piece.shape[1:], piece.dtype)
    spread = lax.dynamic_update_slice_in_dim(
        spread, piece, (seq_index % share) * parts, axis=0
    )
    spread = lax.all_to_all(spread, "seq", split_axis=0, concat_axis=0, tiled=True)
    spread = spread.reshape((-1, share) + piece.shape[1:])
    return jnp.sum(spread.astype(jnp.float32), axis=1).astype(piece.dtype)


def solution(mesh):
    return jax.shard_map(
        body,
        mesh=mesh,
        in_specs=(
            P(None, "dp", "seq", None),
            P(None, "dp", "seq", None),
            P("section", ("dp", "seq")),
            P("section", ("dp", "seq")),
            P("section", ("dp", "seq"), None),
            P("section", ("dp", "seq"), None),
            P("section", ("dp", "seq"), None),
            P("section", ("dp", "seq"), None),
            P("section", ("dp", "seq"), None),
            P("section", "dp", None, None),
            P("section", "dp", None, None),
            P("section", "dp", None, None),
            P("section", None, "dp", "seq", None),
        ),
        out_specs=(
            P("section", None, "dp", "seq", None),
            P("section", None, "dp", "seq", None),
            P("section", ("dp", "seq")),
            P("section", ("dp", "seq")),
            P("section", ("dp", "seq"), None),
            P("section", ("dp", "seq"), None),
            P("section", ("dp", "seq"), None),
            P("section", ("dp", "seq"), None),
            P("section", ("dp", "seq"), None),
            P("section", "dp", "seq", None),
            P("section", "dp", "seq", None),
            P("section", "dp", "seq", None),
        ),
        check_vma=False,
    )
```

time: 2410 us -> 1830 us (0.76)
  waiting for transfers between devices: 1450 us -> 447 us
  Pallas kernels: 0 us -> 749 us
  matrix products: 433 us -> 184 us
  local copies, waits for them, and re-layouts: 155 us -> 93.9 us
    pallas_call x0 -> x8, Pallas kernels: none -> 749 us  [the longest x4 414 us: combine(): pl.pallas_call(combine_kernel, out_shape=jax.ShapeDtypeStruct((rows, widt...]
    reduce_scatter x8 -> x4, waiting for transfers between devices: 504 us -> 0.06 us  [the longest x2 0.04 us: body(): out_part = lax.psum_scatter(out_part, 'dp', scatter_dimension=0, tiled=True)]
    all_gather x8 -> x4, waiting for transfers between devices: 351 us -> 22.2 us  [the longest x2 22.2 us: body(): lax.all_gather(by_layer(number, own_out, other_out), 'dp', axis=0, tiled=...]
    dot_general x16 -> x6, matrix products: 145 us -> 55.6 us  [each_dot(): return jnp.einsum(form, a, b, preferred_element_type=jnp.float32)]
    ppermute x6, waiting for transfers between devices: 177 us -> 99.6 us  [swap(): return lax.ppermute(block, 'section', [(0, 1), (1, 0)])]
    another operation x11 -> x4, local copies, waits for them, and re-layouts: 68.5 us -> 0.33 us  [backward_layer(): gain_grads = jnp.stack([attn_gain_grad, ffn_gain_grad])]
    dot_general x18 -> x6, matrix products: 82.7 us -> 23.8 us  [dot_t(): lax.dot_general(a, b, (((1,), (1,)), ((), ())), preferred_element_type=jn...]
    unnamed x28 -> x16, waiting for transfers between devices: 49.8 us -> 0.94 us
  transfers between devices with their start and end apart: 60 -> 51, of which waited for: 38 -> 21; matrix products, arithmetic and copies ran while one was open for 16% -> 17% of each run, Pallas kernels for 0% -> 27%
where the time goes in v3:
time: 1830 us; the launch traced here: 1820 us
  Pallas kernels  749 us (41%)
  waiting for transfers between devices  447 us (24%)
  matrix products  184 us (10%)
  other arithmetic  129 us (7%)
  starting transfers between devices  121 us (7%)
  local copies, waits for them, and re-layouts  93.9 us (5%)
  blocking collectives  82.1 us (4%)
    pallas_call x4, Pallas kernels, combine(): pl.pallas_call(combine_kernel, out_shape=jax.ShapeDtypeStruct((rows, widt...  414 us
    pallas_call x2, Pallas kernels, expert_forward(): pl.pallas_call(kernel, out_shape=[jax.ShapeDtypeStruct(*result) for resul...  168 us
    pallas_call x2, Pallas kernels, expert_backward(): pl.pallas_call(kernel, out_shape=[jax.ShapeDtypeStruct(*result) for resul...  167 us
    ppermute x16, waiting for transfers between devices, pass_to(): return lax.ppermute(block, 'section', [(1 - section, section)])  162 us
    ppermute x6, waiting for transfers between devices, swap(): return lax.ppermute(block, 'section', [(0, 1), (1, 0)])  99.6 us
    convert_element_type x20, other arithmetic, low(): return v.astype(jnp.bfloat16)  59.8 us
    dot_general x6, matrix products, each_dot(): return jnp.einsum(form, a, b, preferred_element_type=jnp.float32)  55.6 us
    ppermute x16, starting transfers between devices, pass_to(): return lax.ppermute(block, 'section', [(1 - section, section)])  42.5 us
  transfers between devices with their start and end apart: 51, of which 21 were waited for; matrix products, arithmetic and copies ran while one was open for 17% of the time, Pallas kernels for 27%

profile of v3, /device:TPU:16, one launch (start us, length us, event | category | flops | bytes accessed | tf_op | source)
XLA Modules:
  0.0 1821.6 jit_solution(16297936934571149954)
XLA Ops:
  12.0 11.5 collective-permute-done
  24.4 11.6 all_to_all.75
  36.1 35.5 %all-gather.2 = bf16[32,96,34]{1,2,0:T(8,128)(2,1)S(1)} all-gather(bf16[1,96,34]{1,2,0:T(8,128)(2,1)S(1)} %maximum_bitcast_fusion.2), channel_id=1, replica_groups=mesh['section'=2,'dp'=4,'seq'=4] {'section','dp','seq'}, dimensions={0}, use_global_device_ids=true | all-gather | bytes 215424 | tf_op jit(solution)/shard_map/all_gather | solution.py:932
  134.3 9.3 all-gather.16.cloned.1.call-done
  152.4 18.6 %collective-permute-done.4.refs_8_ = bf16[2,1536,512]{2,1,0:T(8,128)(2,1)} collective-permute-done((bf16[2,1536,512]{2,1,0:T(8,128)(2,1)S(1)}, bf16[2,1536,512]{2,1,0:T(8,128)(2,1)}, u32[]{:S(2)}, u32[]{:S(2)}) %collective-permute-start.4) | collective-permute-done | bytes 3145760 | tf_op jit(solution)/shard_map/ppermute | solution.py:39
  177.5 62.9 %collective-permute-done.5.refs_9_ = bf16[2,1536,512]{2,1,0:T(8,128)(2,1)} collective-permute-done((bf16[2,1536,512]{2,1,0:T(8,128)(2,1)}, bf16[2,1536,512]{2,1,0:T(8,128)(2,1)}, u32[]{:S(2)}, u32[]{:S(2)}) %collective-permute-start.5) | collective-permute-done | bytes 3145760 | tf_op jit(solution)/shard_map/ppermute | solution.py:39
  246.3 14.1 all-gather.1
  270.6 21.0 %all-gather = s32[4096,8]{0,1:T(8,128)} all-gather(s32[256,8]{0,1:T(8,128)} %get-tuple-element.346), channel_id=2, replica_groups=mesh['section'=2,'dp'=4,'seq'=4] {'dp','seq'}, dimensions={0}, use_global_device_ids=true | all-gather | bytes 139264 | tf_op jit(solution)/shard_map/all_gather | solution.py:973
  327.8 86.2 %expert_forward.2 = (bf16[2,1280,1536]{2,1,0:T(8,128)(2,1)}, bf16[2,1280,512]{2,1,0:T(8,128)(2,1)}, bf16[2,1280,512]{2,1,0:T(8,128)(2,1)}, bf16[2,1280,512]{2,1,...) custom-call(bf16[256,1536]{1,0:T(8,128)(2,1)} %multiply_convert_fusion.2.refs_0_, ...), custom_call_target="tpu_custom_call" | custom-call | tf_op jit(solution)/shard_map/expert_forward/pallas_call | solution.py:405
  414.0 98.1 %combine.4 = f32[256,1536]{1,0:T(8,128)} custom-call(bf16[16,256,160]{2,1,0:T(8,128)(2,1)} %bitcast.450, bf16[16,160,1536]{2,1,0:T(8,128)(2,1)} %get-tuple-element.180.y_ref), custom_call_target="tpu_custom_call" | custom-call | tf_op jit(solution)/shard_map/combine/pallas_call | solution.py:561
  516.9 27.3 %all-gather.18.cloned.1.call-done = bf16[1024,1536]{1,0:T(8,128)(2,1)} async-done(((bf16[256,1536]{1,0:T(8,128)(2,1)}), bf16[1024,1536]{1,0:T(8,128)(2,1)}) %all-gather.18.cloned.1.call-update) | async-done | bytes 3145744 | tf_op jit(solution)/shard_map/all_gather | solution.py:744
  562.6 12.9 all-gather.22.cloned.1.call-done
  587.9 30.5 %reduce-scatter.15.cloned.1.call-done = bf16[256,1536]{1,0:T(8,128)(2,1)} async-done(((bf16[1024,1536]{1,0:T(8,128)(2,1)}), bf16[256,1536]{1,0:T(8,128)(2,1)}) %reduce-scatter.15.cloned.1.call-update) | async-done | bytes 786448 | tf_op jit(solution)/shard_map/reduce_scatter | solution.py:751
  621.4 81.9 %expert_forward.3 = (bf16[2,1280,1536]{2,1,0:T(8,128)(2,1)}, bf16[2,1280,512]{2,1,0:T(8,128)(2,1)}, bf16[2,1280,512]{2,1,0:T(8,128)(2,1)}, bf16[2,1280,512]{2,1,...) custom-call(bf16[256,1536]{1,0:T(8,128)(2,1)} %copy-done.24, ...), custom_call_target="tpu_custom_call" | custom-call | tf_op jit(solution)/shard_map/expert_forward/pallas_call | solution.py:405
  703.4 85.6 %expert_backward.2 = (bf16[2,1280,1536]{2,1,0:T(8,128)(2,1)}, bf16[2,1280,512]{2,1,0:T(8,128)(2,1)}, bf16[2,1280,512]{2,1,0:T(8,128)(2,1)}, f32[2,1280,128]{2,1,0:T(8,128)}, bf16[16,160,1536]{2,1,0:T(8,128)(2,1)}) custom-call(bf16[256,1536]{1,0:T(8,128)(2,1)} %dynamic-slice_bitcast_fusion.3.refs_0_, bf16[16,160,256]{2,1,0:T(8,128)(2,1)} %copy.288.refs_1_, ...), custom_call_target="tpu_custom_call" | custom-call | tf_op jit(solution)/shard_map/expert_backward/pallas_call | solution.py:674
  799.6 10.1 convolution_convert_fusion.5
  809.7 10.1 convolution_convert_fusion.4
  827.4 100.1 %combine.6 = f32[256,1536]{1,0:T(8,128)} custom-call(bf16[16,256,160]{2,1,0:T(8,128)(2,1)} %bitcast.452, bf16[16,160,1536]{2,1,0:T(8,128)(2,1)} %get-tuple-element.191.y_ref), custom_call_target="tpu_custom_call" | custom-call | tf_op jit(solution)/shard_map/combine/pallas_call | solution.py:561
  933.9 27.0 %all-gather.24.cloned.1.call-done = bf16[1024,1536]{1,0:T(8,128)(2,1)} async-done(((bf16[256,1536]{1,0:T(8,128)(2,1)}), bf16[1024,1536]{1,0:T(8,128)(2,1)}) %all-gather.24.cloned.1.call-update) | async-done | bytes 3145744 | tf_op jit(solution)/shard_map/all_gather | solution.py:866
  1012.2 115.6 %combine.5 = f32[256,1536]{1,0:T(8,128)} custom-call(bf16[16,256,160]{2,1,0:T(8,128)(2,1)} %bitcast.453, bf16[16,160,1536]{2,1,0:T(8,128)(2,1)} %get-tuple-element.181.y_ref), custom_call_target="tpu_custom_call" | custom-call | tf_op jit(solution)/shard_map/combine/pallas_call | solution.py:561
  1135.1 81.2 %expert_backward.3 = (bf16[2,1280,1536]{2,1,0:T(8,128)(2,1)}, bf16[2,1280,512]{2,1,0:T(8,128)(2,1)}, bf16[2,1280,512]{2,1,0:T(8,128)(2,1)}, f32[2,1280,128]{2,1,0:T(8,128)}, bf16[16,160,1536]{2,1,0:T(8,128)(2,1)}) custom-call(bf16[256,1536]{1,0:T(8,128)(2,1)} %get-tuple-element.300.refs_0_, bf16[16,160,256]{2,1,0:T(8,128)(2,1)} %copy.279.refs_1_, ...), custom_call_target="tpu_custom_call" | custom-call | tf_op jit(solution)/shard_map/expert_backward/pallas_call | solution.py:674
  1227.6 10.1 convolution_convert_fusion.2
  1237.7 10.1 convolution_convert_fusion.1
  1255.4 100.5 %combine.7 = f32[256,1536]{1,0:T(8,128)} custom-call(bf16[16,256,160]{2,1,0:T(8,128)(2,1)} %bitcast.451, bf16[16,160,1536]{2,1,0:T(8,128)(2,1)} %get-tuple-element.202.y_ref), custom_call_target="tpu_custom_call" | custom-call | tf_op jit(solution)/shard_map/combine/pallas_call | solution.py:561
  1375.7 13.4 all-gather.26.cloned.1.call-done
  1451.2 60.5 %collective-permute-done.20 = bf16[2,1536,512]{2,1,0:T(8,128)(2,1)} collective-permute-done((bf16[2,1536,512]{2,1,0:T(8,128)(2,1)}, bf16[2,1536,512]{2,1,0:T(8,128)(2,1)}, u32[]{:S(2)}, u32[]{:S(2)}) %collective-permute-start.20) | collective-permute-done | bytes 3145760 | tf_op jit(solution)/shard_map/ppermute | solution.py:43
  1542.7 40.8 %collective-permute-done.22 = bf16[2,1536,512]{2,1,0:T(8,128)(2,1)} collective-permute-done((bf16[2,1536,512]{2,1,0:T(8,128)(2,1)}, bf16[2,1536,512]{2,1,0:T(8,128)(2,1)}, u32[]{:S(2)}, u32[]{:S(2)}) %collective-permute-start.22) | collective-permute-done | bytes 3145760 | tf_op jit(solution)/shard_map/ppermute | solution.py:43
  1616.0 24.5 %all-to-all-done.9 = bf16[4,2,384,512]{3,2,1,0:T(8,128)(2,1)} async-done(((bf16[4,2,384,512]{3,2,1,0:T(8,128)(2,1)}), bf16[4,2,384,512]{3,2,1,0:T(8,128)(2,1)}, u32[]{:S(2)}, u32[]{:S(2)}) %all-to-all-start.9) | async-done | bytes 3145760 | tf_op jit(solution)/shard_map/all_to_all | solution.py:1048
  1648.4 13.5 collective-permute-done.16
  1682.9 9.9 collective-permute-done.15
  1695.9 23.3 %collective-permute-done.18 = bf16[96,1536]{1,0:T(8,128)(2,1)} collective-permute-done((bf16[96,1536]{1,0:T(8,128)(2,1)S(1)}, bf16[96,1536]{1,0:T(8,128)(2,1)}, u32[]{:S(2)}, u32[]{:S(2)}) %collective-permute-start.18) | collective-permute-done | bytes 294944 | tf_op jit(solution)/shard_map/ppermute | solution.py:43
  1772.8 31.5 %collective-permute-done.11 = f32[2,96]{1,0:T(2,128)S(1)} collective-permute-done((f32[2,96]{1,0:T(2,128)S(1)}, f32[2,96]{1,0:T(2,128)S(1)}, u32[]{:S(2)}, u32[]{:S(2)}) %collective-permute-start.11) | collective-permute-done | bytes 800 | tf_op jit(solution)/shard_map/ppermute | solution.py:43
  (601 shorter events, 515.9 us)
Async XLA Ops:
  7.2 96.9 %all-gather.14.cloned.1.call-start = ((), (), s32[]{:S(2)}) async-start(), calls=%async_computation.20 | async-start | bytes 2457600 | tf_op jit(solution)/shard_map/all_gather | solution.py:959
  36.0 74.7 %all-gather.12.cloned.1.call-start = ((), (), s32[]{:S(2)}) async-start(), calls=%async_computation.19 | async-start | bytes 3932160 | tf_op jit(solution)/shard_map/all_gather | solution.py:744
  74.7 68.9 %all-gather.16.cloned.1.call-start = ((), (), s32[]{:S(2)}) async-start(), calls=%async_computation.21 | async-start | bytes 1474560 | tf_op jit(solution)/shard_map/all_gather | solution.py:960
  101.0 70.0 %collective-permute-start.4 = (bf16[2,1536,512]{2,1,0:T(8,128)(2,1)S(1)}, bf16[2,1536,512]{2,1,0:T(8,128)(2,1)}, u32[]{:S(2)}, u32[]{:S(2)}) collective-permute-start(bf16[2,1536,512]{2,1,0:T(8,128)(2,1)S(1)} %dynamic-slice_bitcast_fusion.2.refs_5_), channel_id=1, source_target_pairs={{0,16},{16,0},{1,17},{17,1},{2,18},{18,2},{3,19},{19,3},{4,20},{20... | collective-permute-start | bytes 9437192 | tf_op jit(solution)/shard_map/ppermute | solution.py:39
  104.0 218.8 %reduce-scatter.13.cloned.1.call-start = ((), (), s32[]{:S(2)}) async-start(), calls=%async_computation.22 | async-start | bytes 3932160 | tf_op jit(solution)/shard_map/reduce_scatter | solution.py:751
  171.0 69.4 %collective-permute-start.5 = (bf16[2,1536,512]{2,1,0:T(8,128)(2,1)}, bf16[2,1536,512]{2,1,0:T(8,128)(2,1)}, u32[]{:S(2)}, u32[]{:S(2)}) collective-permute-start(bf16[2,1536,512]{2,1,0:T(8,128)(2,1)} %dynamic-slice_bitcast_fusion.1.refs_6_), channel_id=1, source_target_pairs={{0,16},{16,0},{1,17},{17,1},{2,18},{18,2},{3,19},{19,3},{4,20},{20... | collective-permute-start | bytes 9437192 | tf_op jit(solution)/shard_map/ppermute | solution.py:39
  173.6 71.4 %collective-permute-start.3 = (s32[256,8]{0,1:T(8,128)}, s32[256,8]{0,1:T(8,128)}, u32[]{:S(2)}, u32[]{:S(2)}) collective-permute-start(s32[256,8]{0,1:T(8,128)} %dynamic-slice_bitcast_fusion.4), channel_id=1, source_target_pairs={{0,16},{16,0},{1,17},{17,1},{2,18},{18,2},{3,19},{19,3},{4,20},{20... | collective-permute-start | bytes 24584 | tf_op jit(solution)/shard_map/ppermute | solution.py:39
  240.4 87.4 %collective-permute-start.6 = (bf16[2,512,1536]{2,1,0:T(8,128)(2,1)S(1)}, bf16[2,512,1536]{2,1,0:T(8,128)(2,1)}, u32[]{:S(2)}, u32[]{:S(2)}) collective-permute-start(bf16[2,512,1536]{2,1,0:T(8,128)(2,1)S(1)} %dynamic-slice_bitcast_fusion.refs_7_), channel_id=1, source_target_pairs={{0,16},{16,0},{1,17},{17,1},{2,18},{18,2},{3,19},{19,3},{4,20},{20... | collective-permute-start | bytes 9437192 | tf_op jit(solution)/shard_map/ppermute | solution.py:39
  268.2 248.7 %all-gather.20.cloned.1.call-start = ((), (), s32[]{:S(2)}) async-start(), calls=%async_computation.24 | async-start | bytes 2457600 | tf_op jit(solution)/shard_map/all_gather | solution.py:959
  291.6 252.6 %all-gather.18.cloned.1.call-start = ((), (), s32[]{:S(2)}) async-start(), calls=%async_computation.23 | async-start | bytes 3932160 | tf_op jit(solution)/shard_map/all_gather | solution.py:744
  516.7 101.7 %reduce-scatter.15.cloned.1.call-start = ((), (), s32[]{:S(2)}) async-start(), calls=%async_computation.26 | async-start | bytes 3932160 | tf_op jit(solution)/shard_map/reduce_scatter | solution.py:751
  792.6 134.9 %all-to-all-start.2 = ((f32[16,2,256]{2,1,0:T(2,128)}), f32[16,2,256]{2,1,0:T(2,128)S(1)}, u32[]{:S(2)}, u32[]{:S(2)}) async-start(f32[16,2,256]{2,1,0:T(2,128)} %multiply_reduce_fusion.1), calls=%async_computation.4 | async-start | bytes 65536 | tf_op jit(solution)/shard_map/all_to_all | solution.py:857
  799.2 161.7 %all-gather.24.cloned.1.call-start = ((), (), s32[]{:S(2)}) async-start(), calls=%async_computation.27 | async-start | bytes 3932160 | tf_op jit(solution)/shard_map/all_gather | solution.py:866
  933.2 194.6 %reduce-scatter.17.cloned.1.call-start = ((), (), s32[]{:S(2)}) async-start(), calls=%async_computation.28 | async-start | bytes 3932160 | tf_op jit(solution)/shard_map/reduce_scatter | solution.py:872
  1219.9 135.9 %all-to-all-start.3 = ((f32[16,2,256]{2,1,0:T(2,128)}), f32[16,2,256]{2,1,0:T(2,128)S(1)}, u32[]{:S(2)}, u32[]{:S(2)}) async-start(f32[16,2,256]{2,1,0:T(2,128)} %multiply_reduce_fusion), calls=%async_computation.6 | async-start | bytes 65536 | tf_op jit(solution)/shard_map/all_to_all | solution.py:857
  1227.5 161.7 %all-gather.26.cloned.1.call-start = ((), (), s32[]{:S(2)}) async-start(), calls=%async_computation.29 | async-start | bytes 3932160 | tf_op jit(solution)/shard_map/all_gather | solution.py:866
  1361.4 162.4 %reduce-scatter.27.cloned.1.call-start = ((), (), s32[]{:S(2)}) async-start(), calls=%async_computation.34 | async-start | bytes 2949120 | tf_op jit(solution)/shard_map/reduce_scatter | solution.py:1022
  1373.7 266.9 %reduce-scatter.25.cloned.1.call-start = ((), (), s32[]{:S(2)}) async-start(), calls=%async_computation.33 | async-start | bytes 2949120 | tf_op jit(solution)/shard_map/reduce_scatter | solution.py:1022
  1440.1 204.6 %reduce-scatter.23.cloned.1.call-start = ((), (), s32[]{:S(2)}) async-start(), calls=%async_computation.32 | async-start | bytes 1474560 | tf_op jit(solution)/shard_map/reduce_scatter | solution.py:1027
  1440.1 71.6 %collective-permute-start.20 = (bf16[2,1536,512]{2,1,0:T(8,128)(2,1)}, bf16[2,1536,512]{2,1,0:T(8,128)(2,1)}, u32[]{:S(2)}, u32[]{:S(2)}) collective-permute-start(bf16[2,1536,512]{2,1,0:T(8,128)(2,1)} %convolution_convert_fusion.5), channel_id=1, source_target_pairs={{0,16},{1,17},{2,18},{3,19},{4,20},{5,21},{6,22},{7,23},{8,24},{9,... | collective-permute-start | bytes 9437192 | tf_op jit(solution)/shard_map/ppermute | solution.py:43
  1445.2 72.6 %collective-permute-start.19 = (bf16[2,1536,512]{2,1,0:T(8,128)(2,1)}, bf16[2,1536,512]{2,1,0:T(8,128)(2,1)}, u32[]{:S(2)}, u32[]{:S(2)}) collective-permute-start(bf16[2,1536,512]{2,1,0:T(8,128)(2,1)} %convolution_convert_fusion.2), channel_id=1, source_target_pairs={{16,0},{17,1},{18,2},{19,3},{20,4},{21,5},{22,6},{23,7},{24,8},{25... | collective-permute-start | bytes 9437192 | tf_op jit(solution)/shard_map/ppermute | solution.py:43
  1451.1 223.6 %reduce-scatter.21.cloned.1.call-start = ((), (), s32[]{:S(2)}) async-start(), calls=%async_computation.31 | async-start | bytes 1474560 | tf_op jit(solution)/shard_map/reduce_scatter | solution.py:1027
  1511.7 71.7 %collective-permute-start.22 = (bf16[2,1536,512]{2,1,0:T(8,128)(2,1)}, bf16[2,1536,512]{2,1,0:T(8,128)(2,1)}, u32[]{:S(2)}, u32[]{:S(2)}) collective-permute-start(bf16[2,1536,512]{2,1,0:T(8,128)(2,1)} %convolution_convert_fusion.4), channel_id=1, source_target_pairs={{0,16},{1,17},{2,18},{3,19},{4,20},{5,21},{6,22},{7,23},{8,24},{9,... | collective-permute-start | bytes 9437192 | tf_op jit(solution)/shard_map/ppermute | solution.py:43
  1517.8 71.5 %collective-permute-start.21 = (bf16[2,1536,512]{2,1,0:T(8,128)(2,1)}, bf16[2,1536,512]{2,1,0:T(8,128)(2,1)}, u32[]{:S(2)}, u32[]{:S(2)}) collective-permute-start(bf16[2,1536,512]{2,1,0:T(8,128)(2,1)} %convolution_convert_fusion.1), channel_id=1, source_target_pairs={{16,0},{17,1},{18,2},{19,3},{20,4},{21,5},{22,6},{23,7},{24,8},{25... | collective-permute-start | bytes 9437192 | tf_op jit(solution)/shard_map/ppermute | solution.py:43
  1528.0 204.6 %reduce-scatter.19.cloned.1.call-start = ((), (), s32[]{:S(2)}) async-start(), calls=%async_computation.30 | async-start | bytes 3932160 | tf_op jit(solution)/shard_map/reduce_scatter | solution.py:872
  1603.6 64.3 %collective-permute-start.7 = (f32[256,1536]{1,0:T(8,128)S(1)}, f32[256,1536]{1,0:T(8,128)}, u32[]{:S(2)}, u32[]{:S(2)}) collective-permute-start(f32[256,1536]{1,0:T(8,128)S(1)} %copy-done.5), channel_id=1, source_target_pairs={{16,0},{17,1},{18,2},{19,3},{20,4},{21,5},{22,6},{23,7},{24,8},{25... | collective-permute-start | bytes 4718600 | tf_op jit(solution)/shard_map/ppermute | solution.py:43
  1604.9 69.8 %collective-permute-start.8 = (f32[256,1536]{1,0:T(8,128)}, f32[256,1536]{1,0:T(8,128)}, u32[]{:S(2)}, u32[]{:S(2)}) collective-permute-start(f32[256,1536]{1,0:T(8,128)} %get-tuple-element.308), channel_id=1, source_target_pairs={{0,16},{1,17},{2,18},{3,19},{4,20},{5,21},{6,22},{7,23},{8,24},{9,... | collective-permute-start | bytes 4718600 | tf_op jit(solution)/shard_map/ppermute | solution.py:43
  1611.8 123.4 %collective-permute-start.24 = (bf16[2,512,1536]{2,1,0:T(8,128)(2,1)}, bf16[2,512,1536]{2,1,0:T(8,128)(2,1)}, u32[]{:S(2)}, u32[]{:S(2)}) collective-permute-start(bf16[2,512,1536]{2,1,0:T(8,128)(2,1)} %convolution_convert_fusion.3), channel_id=1, source_target_pairs={{0,16},{1,17},{2,18},{3,19},{4,20},{5,21},{6,22},{7,23},{8,24},{9,... | collective-permute-start | bytes 9437192 | tf_op jit(solution)/shard_map/ppermute | solution.py:43
  1614.7 128.2 %collective-permute-start.23 = (bf16[2,512,1536]{2,1,0:T(8,128)(2,1)}, bf16[2,512,1536]{2,1,0:T(8,128)(2,1)}, u32[]{:S(2)}, u32[]{:S(2)}) collective-permute-start(bf16[2,512,1536]{2,1,0:T(8,128)(2,1)} %convolution_convert_fusion), channel_id=1, source_target_pairs={{16,0},{17,1},{18,2},{19,3},{20,4},{21,5},{22,6},{23,7},{24,8},{25... | collective-permute-start | bytes 9437192 | tf_op jit(solution)/shard_map/ppermute | solution.py:43
  1667.9 92.0 %collective-permute-start.14 = (bf16[4,96,672]{2,1,0:T(8,128)(2,1)}, bf16[4,96,672]{2,1,0:T(8,128)(2,1)}, u32[]{:S(2)}, u32[]{:S(2)}) collective-permute-start(bf16[4,96,672]{2,1,0:T(8,128)(2,1)} %all-to-all-done.7), channel_id=1, source_target_pairs={{0,16},{1,17},{2,18},{3,19},{4,20},{5,21},{6,22},{7,23},{8,24},{9,... | collective-permute-start | bytes 1548296 | tf_op jit(solution)/shard_map/ppermute | solution.py:43
  1670.0 66.5 %all-to-all-start.8 = ((bf16[4,2,384,512]{3,2,1,0:T(8,128)(2,1)}), bf16[4,2,384,512]{3,2,1,0:T(8,128)(2,1)}, u32[]{:S(2)}, u32[]{:S(2)}) async-start(bf16[4,2,384,512]{3,2,1,0:T(8,128)(2,1)} %bitcast.462), calls=%async_computation.14 | async-start | bytes 6291456 | tf_op jit(solution)/shard_map/all_to_all | solution.py:1048
  1719.3 91.0 %collective-permute-start.10 = (f32[256,1536]{1,0:T(8,128)S(1)}, f32[256,1536]{1,0:T(8,128)}, u32[]{:S(2)}, u32[]{:S(2)}) collective-permute-start(f32[256,1536]{1,0:T(8,128)S(1)} %copy-done.20), channel_id=1, source_target_pairs={{0,16},{1,17},{2,18},{3,19},{4,20},{5,21},{6,22},{7,23},{8,24},{9,... | collective-permute-start | bytes 4718600 | tf_op jit(solution)/shard_map/ppermute | solution.py:43
  (160 other events, 4938.7 us)
Sparse Core Ops, SparseCore 0:
  36.1 43.5 all-gather.13
  81.8 28.8 all-gather.11
  112.8 30.7 all-gather.15
  148.7 37.9 reduce-scatter.12
  291.7 44.6 all-gather.19
  516.0 28.1 all-gather.17
  545.9 29.5 all-gather.21
  580.4 37.9 reduce-scatter.14
  933.3 27.5 all-gather.23
  1009.8 44.2 reduce-scatter.16
  1361.5 27.5 all-gather.25
  1392.0 47.5 reduce-scatter.26
  1442.6 47.5 reduce-scatter.24
  1492.4 27.8 reduce-scatter.22
  1523.8 30.8 reduce-scatter.20
  1557.9 37.9 reduce-scatter.18

commit v4 on v3

--- a/solution.py
+++ b/solution.py
@@ -175,7 +175,7 @@
     )
 
 
-def greet(d, s):
+def greet(d, s, section=None):
     barrier = pltpu.get_barrier_semaphore()
 
     def signal(**device):
@@ -192,15 +192,56 @@
     def _():
         signal(dp=d + 1)
 
+    known = 3
+    if section is not None:
+        signal(section=1 - section)
+        known = 4
     inner = (d > 0) & (d < 3)
 
     @pl.when(inner)
     def _():
-        pl.semaphore_wait(barrier, 4)
+        pl.semaphore_wait(barrier, known + 1)
 
     @pl.when(jnp.logical_not(inner))
     def _():
-        pl.semaphore_wait(barrier, 3)
+        pl.semaphore_wait(barrier, known)
+
+
+class Carried:
+    def __init__(self, sections, sources, targets, sems):
+        self.section = lax.axis_index("section")
+        self.copies = []
+        for k, (to, source, target) in enumerate(zip(sections, sources, targets)):
+            copy = remote(source, target, sems.at[k, 0], sems.at[k, 1], section=1 - self.section)
+            self.copies.append((to, copy))
+
+    def start(self):
+        for to, copy in self.copies:
+            if to is None:
+                copy.start()
+            else:
+
+                @pl.when(self.section != to)
+                def _():
+                    copy.start()
+
+    def finish(self):
+        for to, copy in self.copies:
+            if to is None:
+                copy.wait()
+            else:
+
+                @pl.when(self.section != to)
+                def _():
+                    copy.wait_send()
+
+                @pl.when(self.section == to)
+                def _():
+                    copy.wait_recv()
+
+
+def cost():
+    return pl.CostEstimate(flops=80_000_000_000, bytes_accessed=100_000_000, transcendentals=0)
 
 
 def gather_scratch(rows, width):
@@ -216,7 +257,7 @@
     ]
 
 
-def gather_blocks(x_ref, scratch, compute):
+def gather_blocks(x_ref, scratch, compute, carried=None):
     land, lsem, zs, zr, ys, yr, cs, cr = scratch
     d, s = lax.axis_index("dp"), lax.axis_index("seq")
 
@@ -234,9 +275,11 @@
         column = s ^ 2 if across else s
         return remote(src, place(z, column), cs.at[z, across], cr.at[z, across], seq=s ^ 1)
 
-    greet(d, s)
+    greet(d, s, None if carried is None else carried.section)
     own = pltpu.make_async_copy(x_ref, place(d, s), lsem)
     own.start()
+    if carried is not None:
+        carried.start()
 
     @pl.when(d < 3)
     def _():
@@ -322,12 +365,17 @@
     layer, x_ref, pick_ref, chosen_ref, router_ref, mine_ref,
     wg_own, wu_own, wd_own, wg_other, wu_other, wd_other,
     rows_out, gate_out, up_out, hidden_out, slot_gate_out, y_out,
-    wg, wu, wd, rows, gate, up, hidden, slot_gate, y, wsem, osem, *gather
+    wg, wu, wd, rows, gate, up, hidden, slot_gate, y, wsem, osem, carry_sem, *gather
 ):
     count = wg.shape[0]
-    ready = pick_weights(
-        (wg_own, wu_own, wd_own), (wg_other, wu_other, wd_other), (wg, wu, wd), wsem, layer
-    )
+    carried = None
+    if layer == 0:
+        carried = Carried((None,), (wd_own,), (wd_other,), carry_sem)
+        ready = pick_weights((wg_own, wu_own), (wg_other, wu_other), (wg, wu), wsem, layer)
+    else:
+        ready = pick_weights(
+            (wg_own, wu_own, wd_own), (wg_other, wu_other, wd_other), (wg, wu, wd), wsem, layer
+        )
     land = gather[0]
     d = lax.axis_index("dp")
 
@@ -340,10 +388,19 @@
             )
         ] + [pltpu.make_async_copy(y.at[pl.ds(z * 4, 4)], y_out.at[pl.ds(z * 4, 4)], osem.at[5, z])]
 
+    def down(z):
+        part = pl.ds(z * 4 * CAP, 4 * CAP)
+
+        @pl.loop(0, count)
+        def _(j):
+            result = low(dot(hidden[j, part, :], wd[j]))
+            for q in range(4):
+                y[z * 4 + q, pl.ds(j * CAP, CAP), :] = result[q * CAP : (q + 1) * CAP]
+
     def compute(z):
         @pl.when(z == d)
         def _():
-            for k in range(3):
+            for k in range(2 if layer == 0 else 3):
                 ready(k)
 
         for q in range(4):
@@ -372,14 +429,20 @@
             up[j, part, :] = low(u)
             h = low(g * jax.nn.sigmoid(g) * u * slot_gate[j, part, :][:, :1])
             hidden[j, part, :] = h
-            result = low(dot(h, wd[j]))
-            for q in range(4):
-                y[z * 4 + q, pl.ds(j * CAP, CAP), :] = result[q * CAP : (q + 1) * CAP]
-
-        for copy in outs(z):
+
+        if layer != 0:
+            down(z)
+        for copy in outs(z)[: 5 if layer == 0 else 6]:
             copy.start()
 
-    gather_blocks(x_ref, gather, compute)
+    gather_blocks(x_ref, gather, compute, carried)
+    if layer == 0:
+        carried.finish()
+        ready = pick_weights((wd_own,), (wd_other,), (wd,), wsem, layer)
+        ready(0)
+        for z in range(4):
+            down(z)
+            outs(z)[5].start()
     for z in range(4):
         for copy in outs(z):
             copy.wait()
@@ -400,25 +463,39 @@
         ((count, slots, 128), jnp.float32),
         ((16, count * CAP, width), bf),
     ]
+
     def kernel(*refs):
+        if layer == 0:
+            refs = refs[:10] + refs[16:17] + refs[10:16] + refs[17:]
         expert_forward_kernel(layer, *refs)
+
+    shapes = [jax.ShapeDtypeStruct(*result) for result in results]
+    if layer == 0:
+        shapes.append(jax.ShapeDtypeStruct(own[2].shape, bf))
+        other = other[:2]
+    operands = (x, pick, chosen, router, mine, *own, *other)
     return pl.pallas_call(
         kernel,
-        out_shape=[jax.ShapeDtypeStruct(*result) for result in results],
-        in_specs=[anywhere, near, near, near, near] + [anywhere] * 6,
-        out_specs=[anywhere] * 6,
+        out_shape=shapes,
+        in_specs=[anywhere, near, near, near, near] + [anywhere] * (len(operands) - 5),
+        out_specs=[anywhere] * len(shapes),
         scratch_shapes=[pltpu.VMEM(weight.shape, bf) for weight in own]
         + [pltpu.VMEM(*result) for result in results]
-        + [DMA((3,)), DMA((6, 4))]
+        + [DMA((3,)), DMA((6, 4)), DMA((1, 2))]
         + gather_scratch(rows, width),
         compiler_params=pltpu.CompilerParams(
             collective_id=collective_id, has_side_effects=True, vmem_limit_bytes=60 << 20
         ),
+        cost_estimate=cost(),
         name="expert_forward",
-    )(x, pick, chosen, router, mine, *own, *other)
-
-
-def combine_kernel(pick_ref, y_ref, out_ref, y, sent, own, core_in, y_in, z_in, lsem, zs, zr, ys, yr, cs, cr):
+    )(*operands)
+
+
+def combine_kernel(sections, pick_ref, y_ref, *refs):
+    kept = len(sections)
+    sources, out_ref, targets = refs[:kept], refs[kept], refs[kept + 1 : 2 * kept + 1]
+    y, sent, own, core_in, y_in, z_in, lsem, zs, zr, ys, yr, cs, cr, carry_sem = refs[2 * kept + 1 :]
+    carried = Carried(sections, sources, targets, carry_sem)
     d, s = lax.axis_index("dp"), lax.axis_index("seq")
     half = out_ref.shape[0] // 2
 
@@ -433,7 +510,8 @@
         for across in (1, 0):
             for other_core in (1, 0):
                 loaded(z * 4 + column(across, other_core)).start()
-    greet(d, s)
+    greet(d, s, carried.section)
+    carried.start()
 
     def rows(k):
         return pl.ds(pl.multiple_of(k * half, half), half)
@@ -551,18 +629,28 @@
             def _():
                 z_copy(z, k, True).wait_send()
 
-
-def combine(pick_t, y, collective_id):
+    carried.finish()
+
+
+def combine(pick_t, y, collective_id, carry):
     rows, width = pick_t.shape[1], y.shape[2]
+    anywhere = pl.BlockSpec(memory_space=pl.ANY)
+    near = pl.BlockSpec(memory_space=pltpu.VMEM)
+    sections = tuple(to for to, _ in carry)
+    arrays = [array for _, array in carry]
+
+    def kernel(*refs):
+        combine_kernel(sections, *refs)
 
     def blocks(*lead):
         return pltpu.VMEM(lead + (rows, width), jnp.bfloat16)
 
     return pl.pallas_call(
-        combine_kernel,
-        out_shape=jax.ShapeDtypeStruct((rows, width), jnp.float32),
-        in_specs=[pl.BlockSpec(memory_space=pltpu.VMEM), pl.BlockSpec(memory_space=pl.ANY)],
-        out_specs=pl.BlockSpec(memory_space=pltpu.VMEM),
+        kernel,
+        out_shape=[jax.ShapeDtypeStruct((rows, width), jnp.float32)]
+        + [jax.ShapeDtypeStruct(array.shape, array.dtype) for array in arrays],
+        in_specs=[near, anywhere] + [anywhere] * len(arrays),
+        out_specs=[near] + [anywhere] * len(arrays),
         scratch_shapes=[
             pltpu.VMEM(y.shape, jnp.bfloat16),
             blocks(4, 2),
@@ -577,20 +665,26 @@
             DMA((4, 2)),
             DMA((4, 2, 2)),
             DMA((4, 2, 2)),
+            DMA((max(1, len(arrays)), 2)),
         ],
         compiler_params=pltpu.CompilerParams(
             collective_id=collective_id, has_side_effects=True, vmem_limit_bytes=60 << 20
         ),
+        cost_estimate=cost(),
         name="combine",
-    )(pick_t, y)
+    )(pick_t, y, *arrays)
 
 
 def expert_backward_kernel(
-    layer, x_ref, pick_ref, gate_in, up_in, slot_gate_in,
-    wg_own, wu_own, wd_own, wg_other, wu_other, wd_other,
-    rows_out, gate_out, up_out, term_out, y_out,
-    wg, wu, wd, rows, gate, up, slot_gate, y, wsem, isem, osem, *gather
+    layer, sections, x_ref, pick_ref, gate_in, up_in, slot_gate_in,
+    wg_own, wu_own, wd_own, wg_other, wu_other, wd_other, *refs
 ):
+    kept = len(sections)
+    sources, refs = refs[:kept], refs[kept:]
+    rows_out, gate_out, up_out, term_out, y_out, *refs = refs
+    targets, refs = refs[:kept], refs[kept:]
+    wg, wu, wd, rows, gate, up, slot_gate, y, wsem, isem, osem, carry_sem, *gather = refs
+    carried = Carried(sections, sources, targets, carry_sem)
     count = wg.shape[0]
     ready = pick_weights(
         (wg_own, wu_own, wd_own), (wg_other, wu_other, wd_other), (wg, wu, wd), wsem, layer
@@ -649,13 +743,14 @@
         for copy in outs(z):
             copy.start()
 
-    gather_blocks(x_ref, gather, compute)
+    gather_blocks(x_ref, gather, compute, carried)
+    carried.finish()
     for z in range(4):
         for copy in outs(z):
             copy.wait()
 
 
-def expert_backward(layer, x, pick, gate, up, slot_gate, own, other, collective_id):
+def expert_backward(layer, x, pick, gate, up, slot_gate, own, other, collective_id, carry):
     count, width, units = own[0].shape
     rows = x.shape[0]
     slots = 16 * CAP
@@ -669,22 +764,28 @@
         ((count, slots, 128), jnp.float32),
         ((16, count * CAP, width), bf),
     ]
+    sections = tuple(to for to, _ in carry)
+    arrays = [array for _, array in carry]
+
     def kernel(*refs):
-        expert_backward_kernel(layer, *refs)
+        expert_backward_kernel(layer, sections, *refs)
+
     return pl.pallas_call(
         kernel,
-        out_shape=[jax.ShapeDtypeStruct(*result) for result in results],
-        in_specs=[anywhere, near] + [anywhere] * 9,
-        out_specs=[anywhere] * 5,
+        out_shape=[jax.ShapeDtypeStruct(*result) for result in results]
+        + [jax.ShapeDtypeStruct(array.shape, array.dtype) for array in arrays],
+        in_specs=[anywhere, near] + [anywhere] * (9 + len(arrays)),
+        out_specs=[anywhere] * (5 + len(arrays)),
         scratch_shapes=[pltpu.VMEM(weight.shape, bf) for weight in own]
         + [pltpu.VMEM(*result) for result in results]
-        + [DMA((3,)), DMA((3,)), DMA((5, 4))]
+        + [DMA((3,)), DMA((3,)), DMA((5, 4)), DMA((max(1, len(arrays)), 2))]
         + gather_scratch(rows, width),
         compiler_params=pltpu.CompilerParams(
             collective_id=collective_id, has_side_effects=True, vmem_limit_bytes=60 << 20
         ),
+        cost_estimate=cost(),
         name="expert_backward",
-    )(x, pick, gate, up, slot_gate, *own, *other)
+    )(x, pick, gate, up, slot_gate, *own, *other, *arrays)
 
 
 def token_choice(route):
@@ -762,8 +863,12 @@
         *expert_state, slot_out = expert_forward(
             number, normed_ffn, pick, low(chosen), router_w, mine, own, other, 1 + number
         )
-        moe = combine(pick_t, slot_out, 3)
+        if number == 0:
+            *expert_state, slot_out, other_down = (*expert_state, slot_out)
+            other = other[:2] + (other_down,)
     else:
+        if number == 0:
+            other = other[:2] + (swap(own[2]),)
         gate_w, up_w, down_w = by_layer(number, own, other)
         ffn_all = lax.all_gather(normed_ffn, TOKENS, axis=0, tiled=True)
         logits = dot(ffn_all, router_w).reshape(blocks, rows, EXPERTS)
@@ -779,11 +884,7 @@
         up_pre = each_dot("ecd,edf->ecf", slot_rows, up_w)
         scaled = low(slot_gates * jax.nn.silu(gate_pre) * up_pre)
         slot_out = low(each_dot("ecf,efd->ecd", scaled, down_w))
-        moe = lax.psum_scatter(
-            give_back(pick_t, slot_out), TOKENS, scatter_dimension=0, tiled=True
-        ).astype(jnp.float32)
         expert_state = (slot_rows, gate_pre, up_pre, scaled, slot_gates)
-    layer_out = after_update + moe
     saved = (
         layer_in,
         normed_all,
@@ -797,31 +898,26 @@
         own_gates,
         expert_state,
     )
-    return (layer_out, saved)
-
-
-def backward_layer(number, layer_grad, saved, picking, weights, experts):
-    attn_scale, ffn_scale, qkv_w, out_w, router_w = weights
+    return (after_update, slot_out, saved, (own, other))
+
+
+def token_sums(pick_t, slot_out, collective_id, *carry):
+    if has_kernels():
+        sums, *received = combine(pick_t, slot_out, collective_id, carry)
+        return sums, received
+    sums = lax.psum_scatter(give_back(pick_t, slot_out), TOKENS, scatter_dimension=0, tiled=True)
+    return sums.astype(jnp.float32), [pass_to(array, to) for to, array in carry]
+
+
+def expert_gradients(number, layer_grad, saved, picking, experts, *carry):
     chosen, pick, pick_t, first_expert = picking
     own, other = experts
     count = own[0].shape[0]
     blocks, rows = chosen.shape[:2]
-    (
-        layer_in,
-        normed_all,
-        q_rot,
-        k_rot,
-        v_heads,
-        log_total,
-        mixed,
-        after_update,
-        normed_ffn,
-        own_gates,
-        (slot_rows, gate_pre, up_pre, scaled, slot_gates),
-    ) = saved
+    slot_rows, gate_pre, up_pre, scaled, slot_gates = saved[-1]
     if has_kernels():
-        slot_grads, gate_low, up_low, gate_term, slot_out = expert_backward(
-            number, low(layer_grad), pick, gate_pre, up_pre, slot_gates, own, other, 4 + number
+        slot_grads, gate_low, up_low, gate_term, slot_out, *received = expert_backward(
+            number, low(layer_grad), pick, gate_pre, up_pre, slot_gates, own, other, 4 + number, carry
         )
         gate_term = gate_term[:, :, :1]
     else:
@@ -838,18 +934,34 @@
         slot_out = low(
             each_dot("ecf,edf->ecd", gate_low, gate_w) + each_dot("ecf,edf->ecd", up_low, up_w)
         )
+        received = [pass_to(array, to) for to, array in carry]
     expert_grads = (
         low(each_dot("ecd,ecf->edf", slot_rows, gate_low)),
         low(each_dot("ecd,ecf->edf", slot_rows, up_low)),
         low(each_dot("ecf,ecd->efd", scaled, slot_grads)),
     )
     slot_out, *expert_grads = lax.optimization_barrier((slot_out, *expert_grads))
-    if has_kernels():
-        normed_grad = combine(pick_t, slot_out, 3)
-    else:
-        normed_grad = lax.psum_scatter(
-            give_back(pick_t, slot_out), TOKENS, scatter_dimension=0, tiled=True
-        ).astype(jnp.float32)
+    return slot_out, gate_term, expert_grads, received
+
+
+def backward_layer(layer_grad, normed_grad, gate_term, saved, picking, weights):
+    attn_scale, ffn_scale, qkv_w, out_w, router_w = weights
+    chosen, pick, _, _ = picking
+    (
+        layer_in,
+        normed_all,
+        q_rot,
+        k_rot,
+        v_heads,
+        log_total,
+        mixed,
+        after_update,
+        normed_ffn,
+        own_gates,
+        _,
+    ) = saved
+    blocks, rows = chosen.shape[:2]
+    count = gate_term.shape[0]
     by_slot = jnp.transpose(gate_term.reshape(count, blocks, CAP), (1, 0, 2))
     gate_terms = jnp.sum(
         pick.reshape(blocks, count, CAP, rows).astype(jnp.float32) * by_slot[..., None], axis=2
@@ -877,7 +989,6 @@
     return (
         input_part + after_grad,
         (low(qkv_weight_grad), low(out_grad), low(router_grad), gain_grads),
-        expert_grads,
     )
 
 
@@ -910,9 +1021,6 @@
 
     layer_in = lax.dynamic_index_in_dim(hidden_in, section, 0, keepdims=False)[0]
     top_grad = lax.dynamic_index_in_dim(out_grad, section, 0, keepdims=False)[0]
-    own_routes = lax.dynamic_index_in_dim(routes[0], section, 0, keepdims=False)[0]
-    other_routes = lax.dynamic_index_in_dim(routes[0], 1 - section, 0, keepdims=False)[0]
-
     own_group = jnp.concatenate(
         [
             matrix[0].reshape(depth, seq, -1)
@@ -927,10 +1035,18 @@
     other_group = swap(own_group)
     own_out = lax.ppermute(output_matrix[0], TOKENS, to_group)
     other_out = swap(own_out)
-    other_routes = swap(other_routes)
-    small = jnp.concatenate([router_matrix[0], attn_gain[0][:, None], ffn_gain[0][:, None]], axis=1)
-    small = lax.all_gather(small, ("section", "dp", "seq"), axis=0, tiled=True)
-    small = small.reshape(2, width, -1)
+    small = jnp.concatenate([router_matrix[0].T, attn_gain, ffn_gain], axis=0).reshape(-1)
+    known = small.shape[0]
+    wide = jnp.concatenate(
+        [low(routes[0, :, 0].reshape(-1)), small, jnp.zeros((-known % 4096,), jnp.bfloat16)]
+    )
+    wide = lax.all_gather(wide.reshape(-1, 256), ("section", "dp", "seq"), axis=0, tiled=True)
+    wide = wide.reshape(2, dp * seq, -1)
+    paths = wide[:, :, : routes[0].size].reshape(2, dp * seq, 2, -1, TOP_K)
+    paths = lax.dynamic_index_in_dim(paths, section, 2, keepdims=False).astype(jnp.int32)
+    small = wide[:, :, routes[0].size : routes[0].size + known]
+    small = jnp.transpose(small.reshape(2, dp * seq, EXPERTS + 2, depth), (0, 2, 1, 3))
+    small = small.reshape(2, EXPERTS + 2, width)
 
     local = w_gate.shape[1]
     hidden_units = w_gate.shape[3]
@@ -946,10 +1062,9 @@
         lax.dynamic_slice(w_up[0], (start, 0, unit_start), (count, width, units)),
         lax.dynamic_slice(w_down[0], (start, unit_start, 0), (count, units, width)),
     )
-    other_gate = swap(after(own_experts[0], other_group, other_out))
+    other_gate = swap(after(own_experts[0], other_group))
     other_up = swap(after(own_experts[1], other_gate))
-    other_down = swap(after(own_experts[2], other_up))
-    experts = (own_experts, (other_gate, other_up, other_down))
+    experts = (own_experts, (other_gate, other_up))
 
     weights = []
     pickings = []
@@ -962,39 +1077,51 @@
         )
         weights.append(
             (
-                small[number, :, EXPERTS].astype(jnp.float32),
-                small[number, :, EXPERTS + 1].astype(jnp.float32),
+                small[number, EXPERTS].astype(jnp.float32),
+                small[number, EXPERTS + 1].astype(jnp.float32),
                 qkv_w,
                 out_w,
-                small[number, :, :EXPERTS],
+                small[number, :EXPERTS].T,
             )
         )
-        route = by_layer(number, own_routes, other_routes)
-        route_all = lax.all_gather(route, TOKENS, axis=0, tiled=False)
-        pickings.append(routing(route_all, first_expert, count) + (first_expert,))
-
-    state = layer_in.astype(jnp.float32)
-    layer_states = []
-    saved_layers = []
-    for number in range(2):
-        state, saved = forward_layer(number, state, pickings[number], weights[number], experts)
-        layer_states.append(state)
-        saved_layers.append(saved)
-    grad = top_grad.astype(jnp.float32)
-    layer_grads = [None, None]
-    dense_grads = [None, None]
-    expert_grads = [None, None]
+        pickings.append(routing(paths[number], first_expert, count) + (first_expert,))
+
+    first_in = layer_in.astype(jnp.float32)
+    updated, slot_out, first_saved, experts = forward_layer(
+        0, first_in, pickings[0], weights[0], experts
+    )
+    sums, _ = token_sums(pickings[0][2], slot_out, 3)
+    first_out = updated + sums
+    second_updated, second_slots, second_saved, experts = forward_layer(
+        1, first_out, pickings[1], weights[1], experts
+    )
     received = [[None] * 3, [None] * 3]
-    for number in (1, 0):
-        grad, dense_grads[number], expert_grads[number] = backward_layer(
-            number, grad, saved_layers[number], pickings[number], weights[number], experts
-        )
-        layer_grads[number] = grad
-        last = None
-        for kind in range(3):
-            piece = expert_grads[number][kind]
-            piece = piece if last is None else after(piece, last)
-            last = received[number][kind] = pass_to(piece, number)
+    top_grad = top_grad.astype(jnp.float32)
+    slot_out, gate_term, second_experts, _ = expert_gradients(
+        1, top_grad, second_saved, pickings[1], experts
+    )
+    sums, (received[1][0],) = token_sums(pickings[1][2], slot_out, 6, (1, second_experts[0]))
+    middle_grad, second_dense = backward_layer(
+        top_grad, sums, gate_term, second_saved, pickings[1], weights[1]
+    )
+    slot_out, gate_term, first_experts, (received[1][1],) = expert_gradients(
+        0, middle_grad, first_saved, pickings[0], experts, (1, second_experts[1])
+    )
+    sums, (received[0][0], received[1][2]) = token_sums(
+        pickings[0][2], slot_out, 7, (0, first_experts[0]), (1, second_experts[2])
+    )
+    received[0][1] = pass_to(after(first_experts[1], received[0][0]), 0)
+    bottom_grad, first_dense = backward_layer(
+        middle_grad, sums, gate_term, first_saved, pickings[0], weights[0]
+    )
+    second_slots = after(second_slots, received[0][1], bottom_grad)
+    sums, (received[0][2],) = token_sums(
+        pickings[1][2], second_slots, 8, (0, first_experts[2])
+    )
+    layer_states = [first_out, second_updated + sums]
+    layer_grads = [bottom_grad, middle_grad]
+    dense_grads = [first_dense, second_dense]
+    expert_grads = [first_experts, second_experts]
 
     def own_layer(pieces):
         return jnp.where(first, pieces[0], pieces[1])

time: 1830 us -> 1700 us (0.929)
  waiting for transfers between devices: 447 us -> 380 us
  blocking collectives: 82.1 us -> 48 us
  starting transfers between devices: 121 us -> 99 us
    ppermute x16 -> x11, waiting for transfers between devices: 162 us -> 26.3 us  [pass_to(): return lax.ppermute(block, 'section', [(1 - section, section)])]
    reduce_scatter x2, waiting for transfers between devices: 0.02 us -> 35.4 us  [backward_layer(): lax.psum_scatter(normed_attn, 'seq', scatter_dimension=0, tiled=True)]
    all_gather x3 -> x1, blocking collectives: 70.5 us -> 36.3 us  [body(): lax.all_gather(wide.reshape(-1, 256), ('section', 'dp', 'seq'), axis=0, t...]
    ppermute x16 -> x11, starting transfers between devices: 42.5 us -> 25.3 us  [pass_to(): return lax.ppermute(block, 'section', [(1 - section, section)])]
    convert_element_type x20 -> x22, other arithmetic: 59.8 us -> 60.4 us  [low(): return v.astype(jnp.bfloat16)]
    ppermute x6 -> x4, waiting for transfers between devices: 99.6 us -> 99.8 us  [swap(): return lax.ppermute(block, 'section', [(0, 1), (1, 0)])]
  transfers between devices with their start and end apart: 51 -> 44, of which waited for: 21 -> 21; matrix products, arithmetic and copies ran while one was open for 17% -> 17% of each run, Pallas kernels for 27% -> 29%
where the time goes in v4:
time: 1700 us; the launch traced here: 1690 us
  Pallas kernels  746 us (44%)
  waiting for transfers between devices  380 us (22%)
  matrix products  174 us (10%)
  other arithmetic  133 us (8%)
  starting transfers between devices  99 us (6%)
  local copies, waits for them, and re-layouts  92.7 us (5%)
  blocking collectives  48 us (3%)
  between operations  17.2 us (1%)
    pallas_call x4, Pallas kernels, combine(): pl.pallas_call(kernel, out_shape=[jax.ShapeDtypeStruct((rows, width), jnp...  402 us
    pallas_call x2, Pallas kernels, expert_forward(): pl.pallas_call(kernel, out_shape=shapes, in_specs=[anywhere, near, near,...  178 us
    pallas_call x2, Pallas kernels, expert_backward(): pl.pallas_call(kernel, out_shape=[jax.ShapeDtypeStruct(*result) for resul...  166 us
    ppermute x4, waiting for transfers between devices, swap(): return lax.ppermute(block, 'section', [(0, 1), (1, 0)])  99.8 us
    convert_element_type x22, other arithmetic, low(): return v.astype(jnp.bfloat16)  60.4 us
    dot_general x6, matrix products, each_dot(): return jnp.einsum(form, a, b, preferred_element_type=jnp.float32)  52.2 us
    all_gather x2, waiting for transfers between devices, backward_layer(): branch_all = lax.all_gather(low(after_grad), 'seq', axis=0, tiled=True)  44.3 us
    all_to_all x3, waiting for transfers between devices, body(): lax.all_to_all(piece, 'seq', split_axis=0, concat_axis=0, tiled=True)  42.7 us
  transfers between devices with their start and end apart: 44, of which 21 were waited for; matrix products, arithmetic and copies ran while one was open for 17% of the time, Pallas kernels for 29%

profile of v4, /device:TPU:16, one launch (start us, length us, event | category | flops | bytes accessed | tf_op | source)
XLA Modules:
  0.0 1690.0 jit_solution(12927053615171158997)
XLA Ops:
  12.0 11.5 collective-permute-done
  24.4 11.7 all_to_all.75
  36.8 36.3 %all_gather.27 = bf16[1024,256]{1,0:T(8,128)(2,1)S(1)} all-gather(bf16[32,256]{1,0:T(8,128)(2,1)S(1)} %reshape.746), channel_id=1, replica_groups=mesh['section'=2,'dp'=4,'seq'=4] {'section','dp','seq'}, dimensions={0}, use_global_device_ids=true | all-gather | bytes 540672 | tf_op jit(solution)/shard_map/all_gather | solution.py:1043
  77.0 7.8 collective-permute-start.1
  86.2 8.0 collective-permute-done.1
  104.7 7.8 all-gather.9.cloned.1.call-done
  134.0 11.9 all-gather.13.cloned.1.call-done
  170.2 54.5 %collective-permute-done.3.refs_8_ = bf16[2,1536,512]{2,1,0:T(8,128)(2,1)} collective-permute-done((bf16[2,1536,512]{2,1,0:T(8,128)(2,1)}, bf16[2,1536,512]{2,1,0:T(8,128)(2,1)}, u32[]{:S(2)}, u32[]{:S(2)}) %collective-permute-start.3) | collective-permute-done | bytes 3145760 | tf_op jit(solution)/shard_map/ppermute | solution.py:39
  267.1 26.9 %collective-permute-done.4.refs_9_ = bf16[2,1536,512]{2,1,0:T(8,128)(2,1)} collective-permute-done((bf16[2,1536,512]{2,1,0:T(8,128)(2,1)}, bf16[2,1536,512]{2,1,0:T(8,128)(2,1)}, u32[]{:S(2)}, u32[]{:S(2)}) %collective-permute-start.4) | collective-permute-done | bytes 3145760 | tf_op jit(solution)/shard_map/ppermute | solution.py:39
  294.0 95.8 %expert_forward.2 = (bf16[2,1280,1536]{2,1,0:T(8,128)(2,1)}, bf16[2,1280,512]{2,1,0:T(8,128)(2,1)}, bf16[2,1280,512]{2,1,0:T(8,128)(2,1)}, bf16[2,1280,512]{2,1,...) custom-call(bf16[256,1536]{1,0:T(8,128)(2,1)} %multiply_convert_fusion.2.ref, ...), custom_call_target="tpu_custom_call" | custom-call | flops 80000000000 | bytes 100000000 | tf_op jit(solution)/shard_map/expert_forward/pallas_call | solution.py:477
  389.8 96.9 %combine.4 = f32[256,1536]{1,0:T(8,128)} custom-call(bf16[16,256,160]{2,1,0:T(8,128)(2,1)} %bitcast.475, bf16[16,160,1536]{2,1,0:T(8,128)(2,1)} %get-tuple-element.185.refs_1_), custom_call_target="tpu_custom_call" | custom-call | flops 80000000000 | bytes 100000000 | tf_op jit(solution)/shard_map/combine/pallas_call | solution.py:648
  492.2 28.7 %all-gather.15.cloned.1.call-done = bf16[1024,1536]{1,0:T(8,128)(2,1)} async-done(((bf16[256,1536]{1,0:T(8,128)(2,1)}), bf16[1024,1536]{1,0:T(8,128)(2,1)}) %all-gather.15.cloned.1.call-update) | async-done | bytes 3145744 | tf_op jit(solution)/shard_map/all_gather | solution.py:845
  539.5 12.7 all-gather.19.cloned.1.call-done
  564.1 31.0 %reduce-scatter.15.cloned.1.call-done = bf16[256,1536]{1,0:T(8,128)(2,1)} async-done(((bf16[1024,1536]{1,0:T(8,128)(2,1)}), bf16[256,1536]{1,0:T(8,128)(2,1)}) %reduce-scatter.15.cloned.1.call-update) | async-done | bytes 786448 | tf_op jit(solution)/shard_map/reduce_scatter | solution.py:852
  598.5 81.9 %expert_forward.3 = (bf16[2,1280,1536]{2,1,0:T(8,128)(2,1)}, bf16[2,1280,512]{2,1,0:T(8,128)(2,1)}, bf16[2,1280,512]{2,1,0:T(8,128)(2,1)}, bf16[2,1280,512]{2,1,...) custom-call(bf16[256,1536]{1,0:T(8,128)(2,1)} %copy-done.26, ...), custom_call_target="tpu_custom_call" | custom-call | flops 80000000000 | bytes 100000000 | tf_op jit(solution)/shard_map/expert_forward/pallas_call | solution.py:477
  680.4 85.7 %expert_backward.2 = (bf16[2,1280,1536]{2,1,0:T(8,128)(2,1)}, bf16[2,1280,512]{2,1,0:T(8,128)(2,1)}, bf16[2,1280,512]{2,1,0:T(8,128)(2,1)}, f32[2,1280,128]{2,1,0:T(8,128)}, bf16[16,160,1536]{2,1,0:T(8,128)(2,1)}) custom-call(bf16[256,1536]{1,0:T(8,128)(2,1)} %dynamic-slice_bitcast_fusion.3.refs_0_, bf16[16,160,256]{2,1,0:T(8,128)(2,1)} %copy.301.refs_1_, ...), custom_call_target="tpu_custom_call" | custom-call | flops 80000000000 | bytes 100000000 | tf_op jit(solution)/shard_map/expert_backward/pallas_call | solution.py:773
  776.4 10.1 convolution_convert_fusion.4.refs_11_
  786.5 7.6 convolution_convert_fusion.5.refs_2_
  794.0 8.9 convolution_convert_fusion.3.refs_3_
  803.0 100.5 %combine.5 = (f32[256,1536]{1,0:T(8,128)}, bf16[2,1536,512]{2,1,0:T(8,128)(2,1)}) custom-call(bf16[16,256,160]{2,1,0:T(8,128)(2,1)} %bitcast.473, bf16[16,160,1536]{2,1,0:T(8,128)(2,1)} %get-tuple-element.197.refs_1_, bf16[2,1536,512]{2,1,0:T(8,128)(2,1)} %convolution_convert_fusion.5.refs_2_), custom_call_target="tpu_custom_call" | custom-call | flops 80000000000 | bytes 100000000 | tf_op jit(solution)/shard_map/combine/pallas_call | solution.py:648
  909.4 28.1 %all-gather.21.cloned.1.call-done = bf16[1024,1536]{1,0:T(8,128)(2,1)} async-done(((bf16[256,1536]{1,0:T(8,128)(2,1)}), bf16[1024,1536]{1,0:T(8,128)(2,1)}) %all-gather.21.cloned.1.call-update) | async-done | bytes 3145744 | tf_op jit(solution)/shard_map/all_gather | solution.py:978
  987.3 35.4 %reduce-scatter.17.cloned.1.call-done = bf16[256,1536]{1,0:T(8,128)(2,1)} async-done(((bf16[1024,1536]{1,0:T(8,128)(2,1)}), bf16[256,1536]{1,0:T(8,128)(2,1)}) %reduce-scatter.17.cloned.1.call-update) | async-done | bytes 786448 | tf_op jit(solution)/shard_map/reduce_scatter | solution.py:984
  1028.6 80.6 %expert_backward.3 = (bf16[2,1280,1536]{2,1,0:T(8,128)(2,1)}, bf16[2,1280,512]{2,1,0:T(8,128)(2,1)}, bf16[2,1280,512]{2,1,0:T(8,128)(2,1)}, f32[2,1280,128]{2,1,...) custom-call(bf16[256,1536]{1,0:T(8,128)(2,1)} %get-tuple-element.312.refs_0_, ...), custom_call_target="tpu_custom_call" | custom-call | flops 80000000000 | bytes 100000000 | tf_op jit(solution)/shard_map/expert_backward/pallas_call | solution.py:773
  1119.3 10.0 convolution_convert_fusion.1
  1129.4 10.1 convolution_convert_fusion.2.refs_2_
  1145.1 101.5 %combine.6 = (f32[256,1536]{1,0:T(8,128)}, bf16[2,1536,512]{2,1,0:T(8,128)(2,1)}, bf16[2,512,1536]{2,1,0:T(8,128)(2,1)}) custom-call(bf16[16,256,160]{2,1,0:T(8,128)(2,1)} %bitcast.476, bf16[16,160,1536]{2,1,0:T(8,128)(2,1)} %get-tuple-element.212.refs_1_, bf16[2,1536,512]{2,1,0:T(8,128)(2,1)} %convolution_convert_fusion.2.refs_2_, ...), custom_call_target="tpu_custom_call" | custom-call | flops 80000000000 | bytes 100000000 | tf_op jit(solution)/shard_map/combine/pallas_call | solution.py:648
  1264.8 16.1 all-gather.23.cloned.1.call-done
  1368.9 31.3 %all-to-all-done.8 = bf16[4,2,384,512]{3,2,1,0:T(8,128)(2,1)} async-done(((bf16[4,2,384,512]{3,2,1,0:T(8,128)(2,1)}), bf16[4,2,384,512]{3,2,1,0:T(8,128)(2,1)}, u32[]{:S(2)}, u32[]{:S(2)}) %all-to-all-start.8) | async-done | bytes 3145760 | tf_op jit(solution)/shard_map/all_to_all | solution.py:1175
  1426.3 25.4 %collective-permute-done.15 = bf16[96,1536]{1,0:T(8,128)(2,1)S(1)} collective-permute-done((bf16[96,1536]{1,0:T(8,128)(2,1)}, bf16[96,1536]{1,0:T(8,128)(2,1)S(1)}, u32[]{:S(2)}, u32[]{:S(2)}) %collective-permute-start.15) | collective-permute-done | bytes 294944 | tf_op jit(solution)/shard_map/ppermute | solution.py:1155
  1519.0 103.2 %combine.7 = (f32[256,1536]{1,0:T(8,128)}, bf16[2,512,1536]{2,1,0:T(8,128)(2,1)}) custom-call(bf16[16,256,160]{2,1,0:T(8,128)(2,1)} %bitcast.474, bf16[16,160,1536]{2,1,0:T(8,128)(2,1)} %get-tuple-element.219.refs_1_, bf16[2,512,1536]{2,1,0:T(8,128)(2,1)} %convolution_convert_fusion.refs_2_), custom_call_target="tpu_custom_call" | custom-call | flops 80000000000 | bytes 100000000 | tf_op jit(solution)/shard_map/combine/pallas_call | solution.py:648
  1645.5 16.7 collective-permute-done.7
  1666.1 11.4 all-to-all-done.10
  (655 shorter events, 466.9 us)
Async XLA Ops:
  7.2 97.5 %all-gather.11.cloned.1.call-start = ((), (), s32[]{:S(2)}) async-start(), calls=%async_computation.20 | async-start | bytes 2457600 | tf_op jit(solution)/shard_map/all_gather | solution.py:1074
  36.1 76.4 %all-gather.9.cloned.1.call-start = ((), (), s32[]{:S(2)}) async-start(), calls=%async_computation.19 | async-start | bytes 3932160 | tf_op jit(solution)/shard_map/all_gather | solution.py:845
  77.0 68.9 %all-gather.13.cloned.1.call-start = ((), (), s32[]{:S(2)}) async-start(), calls=%async_computation.21 | async-start | bytes 1474560 | tf_op jit(solution)/shard_map/all_gather | solution.py:1075
  104.1 159.1 %reduce-scatter.13.cloned.1.call-start = ((), (), s32[]{:S(2)}) async-start(), calls=%async_computation.22 | async-start | bytes 3932160 | tf_op jit(solution)/shard_map/reduce_scatter | solution.py:852
  154.6 70.2 %collective-permute-start.3 = (bf16[2,1536,512]{2,1,0:T(8,128)(2,1)}, bf16[2,1536,512]{2,1,0:T(8,128)(2,1)}, u32[]{:S(2)}, u32[]{:S(2)}) collective-permute-start(bf16[2,1536,512]{2,1,0:T(8,128)(2,1)} %dynamic-slice_bitcast_fusion.2.refs_5_), channel_id=1, source_target_pairs={{0,16},{16,0},{1,17},{17,1},{2,18},{18,2},{3,19},{19,3},{4,20},{20... | collective-permute-start | bytes 9437192 | tf_op jit(solution)/shard_map/ppermute | solution.py:39
  224.7 69.3 %collective-permute-start.4 = (bf16[2,1536,512]{2,1,0:T(8,128)(2,1)}, bf16[2,1536,512]{2,1,0:T(8,128)(2,1)}, u32[]{:S(2)}, u32[]{:S(2)}) collective-permute-start(bf16[2,1536,512]{2,1,0:T(8,128)(2,1)} %dynamic-slice_bitcast_fusion.1.refs_6_), channel_id=1, source_target_pairs={{0,16},{16,0},{1,17},{17,1},{2,18},{18,2},{3,19},{19,3},{4,20},{20... | collective-permute-start | bytes 9437192 | tf_op jit(solution)/shard_map/ppermute | solution.py:39
  252.8 239.4 %all-gather.17.cloned.1.call-start = ((), (), s32[]{:S(2)}) async-start(), calls=%async_computation.24 | async-start | bytes 2457600 | tf_op jit(solution)/shard_map/all_gather | solution.py:1074
  263.1 257.8 %all-gather.15.cloned.1.call-start = ((), (), s32[]{:S(2)}) async-start(), calls=%async_computation.23 | async-start | bytes 3932160 | tf_op jit(solution)/shard_map/all_gather | solution.py:845
  491.0 61.2 %all-gather.19.cloned.1.call-start = ((), (), s32[]{:S(2)}) async-start(), calls=%async_computation.25 | async-start | bytes 1474560 | tf_op jit(solution)/shard_map/all_gather | solution.py:1075
  491.8 103.3 %reduce-scatter.15.cloned.1.call-start = ((), (), s32[]{:S(2)}) async-start(), calls=%async_computation.26 | async-start | bytes 3932160 | tf_op jit(solution)/shard_map/reduce_scatter | solution.py:852
  769.7 133.9 %all-to-all-start.2 = ((f32[16,2,256]{2,1,0:T(2,128)}), f32[16,2,256]{2,1,0:T(2,128)S(1)}, u32[]{:S(2)}, u32[]{:S(2)}) async-start(f32[16,2,256]{2,1,0:T(2,128)} %multiply_reduce_fusion.1), calls=%async_computation.4 | async-start | bytes 65536 | tf_op jit(solution)/shard_map/all_to_all | solution.py:969
  776.1 161.4 %all-gather.21.cloned.1.call-start = ((), (), s32[]{:S(2)}) async-start(), calls=%async_computation.27 | async-start | bytes 3932160 | tf_op jit(solution)/shard_map/all_gather | solution.py:978
  909.3 113.5 %reduce-scatter.17.cloned.1.call-start = ((), (), s32[]{:S(2)}) async-start(), calls=%async_computation.28 | async-start | bytes 3932160 | tf_op jit(solution)/shard_map/reduce_scatter | solution.py:984
  1112.8 133.9 %all-to-all-start.3 = ((f32[16,2,256]{2,1,0:T(2,128)}), f32[16,2,256]{2,1,0:T(2,128)S(1)}, u32[]{:S(2)}, u32[]{:S(2)}) async-start(f32[16,2,256]{2,1,0:T(2,128)} %multiply_reduce_fusion), calls=%async_computation.6 | async-start | bytes 65536 | tf_op jit(solution)/shard_map/all_to_all | solution.py:969
  1119.1 161.9 %all-gather.23.cloned.1.call-start = ((), (), s32[]{:S(2)}) async-start(), calls=%async_computation.29 | async-start | bytes 3932160 | tf_op jit(solution)/shard_map/all_gather | solution.py:978
  1253.2 80.3 %reduce-scatter.27.cloned.1.call-start = ((), (), s32[]{:S(2)}) async-start(), calls=%async_computation.34 | async-start | bytes 2949120 | tf_op jit(solution)/shard_map/reduce_scatter | solution.py:1149
  1263.9 136.3 %reduce-scatter.25.cloned.1.call-start = ((), (), s32[]{:S(2)}) async-start(), calls=%async_computation.33 | async-start | bytes 2949120 | tf_op jit(solution)/shard_map/reduce_scatter | solution.py:1149
  1328.8 92.3 %reduce-scatter.23.cloned.1.call-start = ((), (), s32[]{:S(2)}) async-start(), calls=%async_computation.32 | async-start | bytes 1474560 | tf_op jit(solution)/shard_map/reduce_scatter | solution.py:1154
  1337.1 121.0 %reduce-scatter.21.cloned.1.call-start = ((), (), s32[]{:S(2)}) async-start(), calls=%async_computation.31 | async-start | bytes 1474560 | tf_op jit(solution)/shard_map/reduce_scatter | solution.py:1154
  1337.1 72.6 %collective-permute-start.5 = (bf16[2,1536,512]{2,1,0:T(8,128)(2,1)}, bf16[2,1536,512]{2,1,0:T(8,128)(2,1)}, u32[]{:S(2)}, u32[]{:S(2)}) collective-permute-start(bf16[2,1536,512]{2,1,0:T(8,128)(2,1)} %convolution_convert_fusion.1), channel_id=1, source_target_pairs={{16,0},{17,1},{18,2},{19,3},{20,4},{21,5},{22,6},{23,7},{24,8},{25... | collective-permute-start | bytes 9437192 | tf_op jit(solution)/shard_map/ppermute | solution.py:43
  1358.4 41.8 %all-to-all-start.8 = ((bf16[4,2,384,512]{3,2,1,0:T(8,128)(2,1)}), bf16[4,2,384,512]{3,2,1,0:T(8,128)(2,1)}, u32[]{:S(2)}, u32[]{:S(2)}) async-start(bf16[4,2,384,512]{3,2,1,0:T(8,128)(2,1)} %bitcast.467), calls=%async_computation.14 | async-start | bytes 6291456 | tf_op jit(solution)/shard_map/all_to_all | solution.py:1175
  1363.2 143.1 %reduce-scatter.19.cloned.1.call-start = ((), (), s32[]{:S(2)}) async-start(), calls=%async_computation.30 | async-start | bytes 3932160 | tf_op jit(solution)/shard_map/reduce_scatter | solution.py:984
  1416.4 58.6 %all-to-all-start.9 = ((bf16[4,2,384,512]{3,2,1,0:T(8,128)(2,1)}), bf16[4,2,384,512]{3,2,1,0:T(8,128)(2,1)}, u32[]{:S(2)}, u32[]{:S(2)}) async-start(bf16[4,2,384,512]{3,2,1,0:T(8,128)(2,1)} %bitcast.465), calls=%async_computation.15 | async-start | bytes 6291456 | tf_op jit(solution)/shard_map/all_to_all | solution.py:1175
  1421.2 30.6 %collective-permute-start.15 = (bf16[96,1536]{1,0:T(8,128)(2,1)}, bf16[96,1536]{1,0:T(8,128)(2,1)S(1)}, u32[]{:S(2)}, u32[]{:S(2)}) collective-permute-start(bf16[96,1536]{1,0:T(8,128)(2,1)} %reduce-scatter.23.cloned.1.call-done), channel_id=1, source_target_pairs={{0,0},{4,1},{8,2},{12,3},{1,4},{5,5},{9,6},{13,7},{2,8},{6,9},{10,... | collective-permute-start | bytes 884744 | tf_op jit(solution)/shard_map/ppermute | solution.py:1155
  1425.0 220.5 %collective-permute-start.6 = (f32[256,1536]{1,0:T(8,128)S(1)}, f32[256,1536]{1,0:T(8,128)}, u32[]{:S(2)}, u32[]{:S(2)}) collective-permute-start(f32[256,1536]{1,0:T(8,128)S(1)} %copy-done.4), channel_id=1, source_target_pairs={{16,0},{17,1},{18,2},{19,3},{20,4},{21,5},{22,6},{23,7},{24,8},{25... | collective-permute-start | bytes 4718600 | tf_op jit(solution)/shard_map/ppermute | solution.py:43
  1455.2 36.4 %collective-permute-start.13 = (bf16[4,96,672]{2,1,0:T(8,128)(2,1)}, bf16[4,96,672]{2,1,0:T(8,128)(2,1)}, u32[]{:S(2)}, u32[]{:S(2)}) collective-permute-start(bf16[4,96,672]{2,1,0:T(8,128)(2,1)} %copy-done.45), channel_id=1, source_target_pairs={{0,16},{1,17},{2,18},{3,19},{4,20},{5,21},{6,22},{7,23},{8,24},{9,... | collective-permute-start | bytes 1548296 | tf_op jit(solution)/shard_map/ppermute | solution.py:43
  1480.6 160.5 %collective-permute-start.9 = (f32[256,1536]{1,0:T(8,128)}, f32[256,1536]{1,0:T(8,128)}, u32[]{:S(2)}, u32[]{:S(2)}) collective-permute-start(f32[256,1536]{1,0:T(8,128)} %get-tuple-element.313), channel_id=1, source_target_pairs={{0,16},{1,17},{2,18},{3,19},{4,20},{5,21},{6,22},{7,23},{8,24},{9,... | collective-permute-start | bytes 4718600 | tf_op jit(solution)/shard_map/ppermute | solution.py:43
  1487.8 140.2 %collective-permute-start.11 = (f32[2,96]{1,0:T(2,128)}, f32[2,96]{1,0:T(2,128)}, u32[]{:S(2)}, u32[]{:S(2)}) collective-permute-start(f32[2,96]{1,0:T(2,128)} %reduce_sum.350), channel_id=1, source_target_pairs={{0,16},{1,17},{2,18},{3,19},{4,20},{5,21},{6,22},{7,23},{8,24},{9,... | collective-permute-start | bytes 2312 | tf_op jit(solution)/shard_map/ppermute | solution.py:43
  1511.6 129.5 %collective-permute-start.8 = (f32[256,1536]{1,0:T(8,128)}, f32[256,1536]{1,0:T(8,128)}, u32[]{:S(2)}, u32[]{:S(2)}) collective-permute-start(f32[256,1536]{1,0:T(8,128)} %fusion.51), channel_id=1, source_target_pairs={{16,0},{17,1},{18,2},{19,3},{20,4},{21,5},{22,6},{23,7},{24,8},{25... | collective-permute-start | bytes 4718600 | tf_op jit(solution)/shard_map/ppermute | solution.py:43
  1513.6 114.4 %all-to-all-start.4 = ((f32[2,16,96]{2,0,1:T(2,128)}), f32[2,16,96]{2,0,1:T(2,128)S(1)}, u32[]{:S(2)}, u32[]{:S(2)}) async-start(f32[2,16,96]{2,0,1:T(2,128)} %pad_maximum_fusion.22), calls=%async_computation.8 | async-start | bytes 32768 | tf_op jit(solution)/shard_map/all_to_all | solution.py:1157
  1625.1 37.1 %collective-permute-start.7 = (f32[256,1536]{1,0:T(8,128)}, f32[256,1536]{1,0:T(8,128)S(1)}, u32[]{:S(2)}, u32[]{:S(2)}) collective-permute-start(f32[256,1536]{1,0:T(8,128)} %fusion.155), channel_id=1, source_target_pairs={{0,16},{1,17},{2,18},{3,19},{4,20},{5,21},{6,22},{7,23},{8,24},{9,... | collective-permute-start | bytes 4718600 | tf_op jit(solution)/shard_map/ppermute | solution.py:43
  1635.9 41.7 %all-to-all-start.10 = ((bf16[4,2,128,1536]{3,2,1,0:T(8,128)(2,1)}), bf16[4,2,128,1536]{3,2,1,0:T(8,128)(2,1)}, u32[]{:S(2)}, u32[]{:S(2)}) async-start(bf16[4,2,128,1536]{3,2,1,0:T(8,128)(2,1)} %bitcast.466), calls=%async_computation.16 | async-start | bytes 6291456 | tf_op jit(solution)/shard_map/all_to_all | solution.py:1175
  (181 other events, 4291.5 us)
Sparse Core Ops, SparseCore 0:
  36.3 44.3 all-gather.10
  82.8 29.6 all-gather.8
  114.7 31.1 all-gather.12
  150.9 37.8 reduce-scatter.12
  263.3 48.8 all-gather.16
  491.1 29.7 all-gather.14
  522.6 29.5 all-gather.18
  557.1 37.9 reduce-scatter.14
  909.4 28.1 all-gather.20
  984.8 37.9 reduce-scatter.16
  1253.3 27.5 all-gather.22
  1283.2 47.5 reduce-scatter.26
  1333.8 47.7 reduce-scatter.24
  1383.9 27.9 reduce-scatter.22
  1414.1 38.7 reduce-scatter.20
  1456.0 38.8 reduce-scatter.18

commit v5 on v4

--- a/solution.py
+++ b/solution.py
@@ -340,6 +340,24 @@
         core_copy(place(z, s), z, 0).wait_send()
         core_copy(place(z, s), z, 1).wait_send()
     return land
+
+
+def gather_small(x, collective_id):
+    rows, width = x.shape
+
+    def kernel(x_ref, out_ref, *scratch):
+        gather_blocks(x_ref, scratch, lambda z: None)
+        out_ref[...] = scratch[0][...]
+
+    return pl.pallas_call(
+        kernel,
+        out_shape=jax.ShapeDtypeStruct((16, rows, width), x.dtype),
+        in_specs=[pl.BlockSpec(memory_space=pl.ANY)],
+        out_specs=pl.BlockSpec(memory_space=pltpu.VMEM),
+        scratch_shapes=gather_scratch(rows, width),
+        compiler_params=pltpu.CompilerParams(collective_id=collective_id, has_side_effects=True),
+        name="gather_small",
+    )(x)
 
 
 def pick_weights(own_refs, other_refs, held, sems, own_layer):
@@ -788,6 +806,358 @@
     )(x, pick, gate, up, slot_gate, *own, *other, *arrays)
 
 
+def rope(x, cos_table, sin_table):
+    lane = lax.broadcasted_iota(jnp.int32, x.shape, 1)
+    turned = jnp.where(lane % HEAD_DIM < HEAD_DIM // 2, pltpu.roll(x, 128 - HEAD_DIM // 2, 1), pltpu.roll(x, HEAD_DIM // 2, 1))
+    return x * cos_table + turned * sin_table
+
+
+def seq_greet(s, section):
+    barrier = pltpu.get_barrier_semaphore()
+    for device in (dict(seq=s ^ 1), dict(seq=s ^ 2), dict(section=1 - section)):
+        pl.semaphore_signal(barrier, inc=1, device_id=device, device_id_type=MESH)
+    pl.semaphore_wait(barrier, 3)
+
+
+def seq_scratch(rows, width):
+    return [
+        pltpu.VMEM((4, rows, width), jnp.bfloat16),
+        pltpu.VMEM((2, rows, width), jnp.bfloat16),
+        pltpu.VMEM((2, rows, width), jnp.bfloat16),
+        pltpu.VMEM((rows, width), jnp.bfloat16),
+        pltpu.VMEM((rows, width), jnp.bfloat16),
+        DMA(()),
+        DMA((4, 2)),
+        DMA((3, 2)),
+    ]
+
+
+class Line:
+    def __init__(self, scratch):
+        self.land, self.sent, self.core_in, self.y_sent, self.y_in, self.lsem, self.ag, self.rs = scratch
+        self.s = lax.axis_index("seq")
+
+    def hop(self, src, dst, sems, k, flip):
+        return remote(src, dst, sems.at[k, 0], sems.at[k, 1], seq=self.s ^ flip)
+
+    def gather(self, x_ref, use):
+        s, land = self.s, self.land
+        own = pltpu.make_async_copy(x_ref, land.at[s], self.lsem)
+        own.start()
+        over = self.hop(x_ref, land.at[s], self.ag, 0, 2)
+        beside = self.hop(x_ref, land.at[s], self.ag, 1, 1)
+        over.start()
+        beside.start()
+        own.wait()
+        use(s)
+        beside.wait_recv()
+        use(s ^ 1)
+        over.wait_recv()
+        further = self.hop(land.at[s ^ 2], land.at[s ^ 2], self.ag, 2, 1)
+        further.start()
+        use(s ^ 2)
+        further.wait_recv()
+        use(s ^ 3)
+        over.wait_send()
+        beside.wait_send()
+        further.wait_send()
+
+    def hand_over(self, t, partial, out_ref):
+        relation = t ^ self.s
+
+        @pl.when(relation == 3)
+        def _():
+            self.sent[0] = low(partial[...])
+            self.hop(self.sent.at[0], self.core_in.at[0], self.rs, 0, 1).start()
+
+        @pl.when(relation == 2)
+        def _():
+            self.hop(self.sent.at[0], self.core_in.at[0], self.rs, 0, 1).wait_recv()
+            self.y_sent[...] = low(partial[...] + self.core_in[0].astype(jnp.float32))
+            self.hop(self.y_sent, self.y_in, self.rs, 1, 2).start()
+
+        @pl.when(relation == 1)
+        def _():
+            self.sent[1] = low(partial[...])
+            self.hop(self.sent.at[1], self.core_in.at[1], self.rs, 2, 1).start()
+
+        @pl.when(relation == 0)
+        def _():
+            out_ref[...] = partial[...]
+
+    def finish(self, out_ref):
+        self.hop(self.sent.at[1], self.core_in.at[1], self.rs, 2, 1).wait()
+        out_ref[...] += self.core_in[1].astype(jnp.float32)
+        self.hop(self.y_sent, self.y_in, self.rs, 1, 2).wait()
+        out_ref[...] += self.y_in[...].astype(jnp.float32)
+        self.hop(self.sent.at[0], self.core_in.at[0], self.rs, 0, 1).wait_send()
+
+
+def attention_forward_kernel(sections, x_ref, qkv_ref, wo_ref, cos_ref, sin_ref, *refs):
+    kept = len(sections)
+    sources, refs = refs[:kept], refs[kept:]
+    out_ref, all_out, heads_out, lse_out, ot_out, *refs = refs
+    targets, refs = refs[:kept], refs[kept:]
+    wqkv, wo, heads, lse, ot, partial, wsem, osem, carry_sem, *line = refs
+    line = Line(line)
+    carried = Carried(sections, sources, targets, carry_sem)
+    s = line.s
+    rows = out_ref.shape[0]
+    kv = heads.shape[0] // (GROUP + 2)
+    queries = GROUP * kv
+    loads = [pltpu.make_async_copy(qkv_ref, wqkv, wsem.at[0]), pltpu.make_async_copy(wo_ref, wo, wsem.at[1])]
+    for load in loads:
+        load.start()
+    seq_greet(s, carried.section)
+    carried.start()
+    lse[...] = jnp.zeros_like(lse)
+
+    def project(t):
+        part = pl.ds(pl.multiple_of(t * rows, rows), rows)
+
+        @pl.when(t == s)
+        def _():
+            loads[0].wait()
+
+        qkv = low(dot(line.land[t], wqkv[...]))
+        for chunk in range((queries + kv) // 2):
+            x = qkv[:, chunk * 128 : (chunk + 1) * 128].astype(jnp.float32)
+            x = low(rope(x, cos_ref[part, :], sin_ref[part, :]))
+            heads[2 * chunk, part, :] = x[:, :HEAD_DIM]
+            heads[2 * chunk + 1, part, :] = x[:, HEAD_DIM:]
+        for j in range(kv):
+            begin = (queries + kv + j) * HEAD_DIM
+            heads[queries + kv + j, part, :] = qkv[:, begin : begin + HEAD_DIM]
+
+    line.gather(x_ref, project)
+    saves = [pltpu.make_async_copy(line.land, all_out, osem.at[0]), pltpu.make_async_copy(heads, heads_out, osem.at[1])]
+    for save in saves:
+        save.start()
+    loads[1].wait()
+
+    def attend(block):
+        keys = (block + 1) * rows
+        columns = slice(block * rows, (block + 1) * rows)
+
+        @pl.loop(0, queries)
+        def _(h):
+            j = h // GROUP
+            scores = dot_t(heads[queries + j, :keys, :], heads[h, columns, :]) * 0.125
+            key_at = lax.broadcasted_iota(jnp.int32, scores.shape, 0)
+            query_at = lax.broadcasted_iota(jnp.int32, scores.shape, 1) + block * rows
+            scores = jnp.where(key_at <= query_at, scores, -jnp.inf)
+            peak = jnp.max(scores, axis=0, keepdims=True)
+            power = jnp.exp(scores - peak)
+            total = jnp.sum(power, axis=0, keepdims=True)
+            attended = t_dot(heads[queries + kv + j, :keys, :], low(power / total))
+            ot[pl.ds(pl.multiple_of(h * HEAD_DIM, HEAD_DIM), HEAD_DIM), columns] = low(attended)
+            lse[pl.ds(h, 1), columns] = peak + jnp.log(total)
+
+        partial[...] = t_dot(ot[:, columns], wo[...])
+
+    @pl.loop(0, 4)
+    def _(i):
+        t = s ^ (3 - i)
+        for block in range(4):
+
+            @pl.when(t == block)
+            def _():
+                attend(block)
+
+        line.hand_over(t, partial, out_ref)
+
+    saves += [pltpu.make_async_copy(lse, lse_out, osem.at[2]), pltpu.make_async_copy(ot, ot_out, osem.at[3])]
+    for save in saves[2:]:
+        save.start()
+    line.finish(out_ref)
+    carried.finish()
+    for save in saves:
+        save.wait()
+
+
+def attention_forward_call(x, qkv_w, out_w, tables, collective_id, carry):
+    rows, width = x.shape
+    local_heads = qkv_w.shape[1] // HEAD_DIM
+    bf, f32 = jnp.bfloat16, jnp.float32
+    anywhere = pl.BlockSpec(memory_space=pl.ANY)
+    near = pl.BlockSpec(memory_space=pltpu.VMEM)
+    sections = tuple(to for to, _ in carry)
+    arrays = [array for _, array in carry]
+    results = [
+        ((rows, width), f32),
+        ((4, rows, width), bf),
+        ((local_heads, 4 * rows, HEAD_DIM), bf),
+        ((8, 4 * rows), f32),
+        ((out_w.shape[0], 4 * rows), bf),
+    ]
+
+    def kernel(*refs):
+        attention_forward_kernel(sections, *refs)
+
+    return pl.pallas_call(
+        kernel,
+        out_shape=[jax.ShapeDtypeStruct(*result) for result in results]
+        + [jax.ShapeDtypeStruct(array.shape, array.dtype) for array in arrays],
+        in_specs=[anywhere] * 3 + [near] * 2 + [anywhere] * len(arrays),
+        out_specs=[near] + [anywhere] * (4 + len(arrays)),
+        scratch_shapes=[
+            pltpu.VMEM(qkv_w.shape, bf),
+            pltpu.VMEM(out_w.shape, bf),
+            pltpu.VMEM(*results[2]),
+            pltpu.VMEM(*results[3]),
+            pltpu.VMEM(*results[4]),
+            pltpu.VMEM((rows, width), f32),
+            DMA((2,)),
+            DMA((4,)),
+            DMA((max(1, len(arrays)), 2)),
+        ]
+        + seq_scratch(rows, width),
+        compiler_params=pltpu.CompilerParams(
+            collective_id=collective_id, has_side_effects=True, vmem_limit_bytes=60 << 20
+        ),
+        cost_estimate=cost(),
+        name="attention_forward",
+    )(x, qkv_w, out_w, *tables, *arrays)
+
+
+def attention_backward_kernel(sections, x_ref, qkv_ref, wo_ref, cos_ref, sin_ref, heads_in, lse_ref, *refs):
+    kept = len(sections)
+    sources, refs = refs[:kept], refs[kept:]
+    out_ref, all_out, grads_out, *refs = refs
+    targets, refs = refs[:kept], refs[kept:]
+    wqkv, wo, heads, douts, dk, dv, dqt, grads, partial, wsem, osem, carry_sem, *line = refs
+    line = Line(line)
+    carried = Carried(sections, sources, targets, carry_sem)
+    s = line.s
+    rows = out_ref.shape[0]
+    kv = heads.shape[0] // (GROUP + 2)
+    queries = GROUP * kv
+    loads = [
+        pltpu.make_async_copy(wo_ref, wo, wsem.at[0]),
+        pltpu.make_async_copy(qkv_ref, wqkv, wsem.at[1]),
+        pltpu.make_async_copy(heads_in, heads, wsem.at[2]),
+    ]
+    for load in loads:
+        load.start()
+    seq_greet(s, carried.section)
+    carried.start()
+    dk[...] = jnp.zeros_like(dk)
+    dv[...] = jnp.zeros_like(dv)
+
+    def project(t):
+        part = pl.ds(pl.multiple_of(t * rows, rows), rows)
+
+        @pl.when(t == s)
+        def _():
+            loads[0].wait()
+
+        grad = low(dot_t(line.land[t], wo[...]))
+        for h in range(queries):
+            douts[h, part, :] = grad[:, h * HEAD_DIM : (h + 1) * HEAD_DIM]
+
+    line.gather(x_ref, project)
+    saves = [pltpu.make_async_copy(line.land, all_out, osem.at[0])]
+    saves[0].start()
+    loads[1].wait()
+    loads[2].wait()
+
+    for block in (3, 2, 1, 0):
+        keys = (block + 1) * rows
+        part = slice(block * rows, (block + 1) * rows)
+
+        @pl.loop(0, queries)
+        def _(h):
+            j = h // GROUP
+            key = heads[queries + j, :keys, :]
+            query = heads[h, part, :]
+            grad = douts[h, part, :]
+            scores = dot_t(key, query) * 0.125
+            key_at = lax.broadcasted_iota(jnp.int32, scores.shape, 0)
+            query_at = lax.broadcasted_iota(jnp.int32, scores.shape, 1) + block * rows
+            scores = jnp.where(key_at <= query_at, scores, -jnp.inf)
+            probs = jnp.exp(scores - lse_ref[pl.ds(h, 1), part])
+            dprobs = dot_t(heads[queries + kv + j, :keys, :], grad)
+            mean = jnp.sum(probs * dprobs, axis=0, keepdims=True)
+            dscores = low(probs * (dprobs - mean))
+            dk[j, :keys, :] += dot(dscores, query) * 0.125
+            dv[j, :keys, :] += dot(low(probs), grad)
+            dqt[pl.ds(pl.multiple_of(h * HEAD_DIM, HEAD_DIM), HEAD_DIM), :] = t_dot(key, dscores) * 0.125
+
+        cos_part, sin_part = cos_ref[part, :], -sin_ref[part, :]
+        dq = dqt[...].T
+        for chunk in range(queries // 2):
+            lanes = slice(chunk * 128, (chunk + 1) * 128)
+            grads[part, lanes] = low(rope(dq[:, lanes], cos_part, sin_part))
+        for pair in range(kv // 2):
+            both = jnp.concatenate([dk[2 * pair, part, :], dk[2 * pair + 1, part, :]], axis=1)
+            begin = queries * HEAD_DIM + pair * 128
+            grads[part, begin : begin + 128] = low(rope(both, cos_part, sin_part))
+            both = jnp.concatenate([dv[2 * pair, part, :], dv[2 * pair + 1, part, :]], axis=1)
+            begin = (queries + kv) * HEAD_DIM + pair * 128
+            grads[part, begin : begin + 128] = low(both)
+        partial[...] = dot_t(grads[part, :], wqkv[...])
+        line.hand_over(block, partial, out_ref)
+
+    saves.append(pltpu.make_async_copy(grads, grads_out, osem.at[1]))
+    saves[1].start()
+    line.finish(out_ref)
+    carried.finish()
+    for save in saves:
+        save.wait()
+
+
+def attention_backward_call(x, qkv_w, out_w, tables, heads, lse, collective_id, carry):
+    rows, width = x.shape
+    bf, f32 = jnp.bfloat16, jnp.float32
+    anywhere = pl.BlockSpec(memory_space=pl.ANY)
+    near = pl.BlockSpec(memory_space=pltpu.VMEM)
+    sections = tuple(to for to, _ in carry)
+    arrays = [array for _, array in carry]
+    results = [((rows, width), f32), ((4, rows, width), bf), ((4 * rows, qkv_w.shape[1]), bf)]
+    kv = heads.shape[0] // (GROUP + 2)
+    queries = GROUP * kv
+
+    def kernel(*refs):
+        attention_backward_kernel(sections, *refs)
+
+    return pl.pallas_call(
+        kernel,
+        out_shape=[jax.ShapeDtypeStruct(*result) for result in results]
+        + [jax.ShapeDtypeStruct(array.shape, array.dtype) for array in arrays],
+        in_specs=[anywhere] * 3 + [near] * 2 + [anywhere, near] + [anywhere] * len(arrays),
+        out_specs=[near] + [anywhere] * (2 + len(arrays)),
+        scratch_shapes=[
+            pltpu.VMEM(qkv_w.shape, bf),
+            pltpu.VMEM(out_w.shape, bf),
+            pltpu.VMEM(heads.shape, bf),
+            pltpu.VMEM((queries, 4 * rows, HEAD_DIM), bf),
+            pltpu.VMEM((kv, 4 * rows, HEAD_DIM), f32),
+            pltpu.VMEM((kv, 4 * rows, HEAD_DIM), f32),
+            pltpu.VMEM((queries * HEAD_DIM, rows), f32),
+            pltpu.VMEM(*results[2]),
+            pltpu.VMEM((rows, width), f32),
+            DMA((3,)),
+            DMA((2,)),
+            DMA((max(1, len(arrays)), 2)),
+        ]
+        + seq_scratch(rows, width),
+        compiler_params=pltpu.CompilerParams(
+            collective_id=collective_id, has_side_effects=True, vmem_limit_bytes=60 << 20
+        ),
+        cost_estimate=cost(),
+        name="attention_backward",
+    )(x, qkv_w, out_w, *tables, heads, lse, *arrays)
+
+
+def wide_tables(length):
+    cos_table, sin_table = rotary_tables(length)
+    cos_table, sin_table = cos_table[:, 0], sin_table[:, 0]
+    return (
+        jnp.concatenate([cos_table] * 4, axis=1),
+        jnp.concatenate([-sin_table, sin_table] * 2, axis=1),
+    )
+
+
 def token_choice(route):
     return route[..., None] == jnp.arange(EXPERTS, dtype=jnp.int32)
 
@@ -835,27 +1205,37 @@
     return lax.axis_size("dp") == 4 and lax.axis_size("seq") == 4
 
 
-def forward_layer(number, layer_in, picking, weights, experts):
+def forward_layer(number, layer_in, picking, weights, experts, *carry):
     attn_scale, ffn_scale, qkv_w, out_w, router_w = weights
     chosen, pick, pick_t, first_expert = picking
     own, other = experts
     count = own[0].shape[0]
     blocks, rows = chosen.shape[:2]
+    received = []
     normed_input = low(rms_norm(layer_in, attn_scale))
-    normed_all = lax.all_gather(normed_input, "seq", axis=0, tiled=True)
-    qkv = low(dot(normed_all, qkv_w))
-    kv_width = KV_HEADS * HEAD_DIM // lax.axis_size("seq")
-    q_width = GROUP * kv_width
-    mixed, log_total, q_rot, k_rot, v_heads = attention_forward(
-        qkv[:, :q_width], qkv[:, q_width : q_width + kv_width], qkv[:, q_width + kv_width :]
-    )
-    branch = lax.psum_scatter(low(dot(mixed, out_w)), "seq", scatter_dimension=0, tiled=True)
+    if has_kernels():
+        branch, normed_all, heads, log_total, mixed_t, *received = attention_forward_call(
+            normed_input, qkv_w, out_w, wide_tables(4 * layer_in.shape[0]), 9 + number, carry
+        )
+        attention_state = (normed_all.reshape(-1, layer_in.shape[1]), mixed_t, heads, log_total)
+    else:
+        received = [swap(array) for _, array in carry]
+        normed_all = lax.all_gather(normed_input, "seq", axis=0, tiled=True)
+        qkv = low(dot(normed_all, qkv_w))
+        kv_width = KV_HEADS * HEAD_DIM // lax.axis_size("seq")
+        q_width = GROUP * kv_width
+        mixed, log_total, q_rot, k_rot, v_heads = attention_forward(
+            qkv[:, :q_width], qkv[:, q_width : q_width + kv_width], qkv[:, q_width + kv_width :]
+        )
+        branch = lax.psum_scatter(low(dot(mixed, out_w)), "seq", scatter_dimension=0, tiled=True)
+        attention_state = (normed_all, mixed.T, (q_rot, k_rot, v_heads), log_total)
     after_update = layer_in + branch.astype(jnp.float32)
     normed_ffn = low(rms_norm(after_update, ffn_scale))
     own_block = lax.axis_index("dp") * lax.axis_size("seq") + lax.axis_index("seq")
     own_chosen = lax.dynamic_index_in_dim(chosen, own_block, 0, keepdims=False)
     own_logits = jnp.where(own_chosen, dot(normed_ffn, router_w), -jnp.inf)
     own_gates = jax.nn.softmax(own_logits, axis=-1)
+    other = tuple(other) + tuple(received)
     mine = (
         jnp.arange(EXPERTS)[None, None, :] == first_expert + jnp.arange(count)[:, None, None]
     ).astype(jnp.float32)
@@ -887,12 +1267,7 @@
         expert_state = (slot_rows, gate_pre, up_pre, scaled, slot_gates)
     saved = (
         layer_in,
-        normed_all,
-        q_rot,
-        k_rot,
-        v_heads,
-        log_total,
-        mixed,
+        attention_state,
         after_update,
         normed_ffn,
         own_gates,
@@ -905,8 +1280,9 @@
     if has_kernels():
         sums, *received = combine(pick_t, slot_out, collective_id, carry)
         return sums, received
-    sums = lax.psum_scatter(give_back(pick_t, slot_out), TOKENS, scatter_dimension=0, tiled=True)
-    return sums.astype(jnp.float32), [pass_to(array, to) for to, array in carry]
+    sums = give_back(pick_t, slot_out).astype(jnp.float32)
+    sums = lax.psum_scatter(sums, TOKENS, scatter_dimension=0, tiled=True)
+    return sums, [pass_to(array, to) for to, array in carry]
 
 
 def expert_gradients(number, layer_grad, saved, picking, experts, *carry):
@@ -944,17 +1320,12 @@
     return slot_out, gate_term, expert_grads, received
 
 
-def backward_layer(layer_grad, normed_grad, gate_term, saved, picking, weights):
+def backward_layer(number, layer_grad, normed_grad, gate_term, saved, picking, weights, *carry):
     attn_scale, ffn_scale, qkv_w, out_w, router_w = weights
     chosen, pick, _, _ = picking
     (
         layer_in,
-        normed_all,
-        q_rot,
-        k_rot,
-        v_heads,
-        log_total,
-        mixed,
+        (normed_all, mixed_t, heads, log_total),
         after_update,
         normed_ffn,
         own_gates,
@@ -975,13 +1346,27 @@
     normed_grad = normed_grad + dot_t(logit_grad, router_w)
     after_part, ffn_gain_grad = jax.vjp(rms_norm, after_update, ffn_scale)[1](normed_grad)
     after_grad = after_part + layer_grad
-    branch_all = lax.all_gather(low(after_grad), "seq", axis=0, tiled=True)
-    out_grad = t_dot(mixed, branch_all)
-    head_grad = low(dot_t(branch_all, out_w))
-    qkv_grad = attention_backward(head_grad, q_rot, k_rot, v_heads, log_total)
+    if has_kernels():
+        normed_attn, branch_all, qkv_grad, *received = attention_backward_call(
+            low(after_grad),
+            qkv_w,
+            out_w,
+            wide_tables(4 * layer_in.shape[0]),
+            heads,
+            log_total,
+            11 + number,
+            carry,
+        )
+        branch_all = branch_all.reshape(-1, layer_in.shape[1])
+    else:
+        branch_all = lax.all_gather(low(after_grad), "seq", axis=0, tiled=True)
+        head_grad = low(dot_t(branch_all, out_w))
+        qkv_grad = attention_backward(head_grad, *heads, log_total)
+        normed_attn = low(dot_t(qkv_grad, qkv_w))
+        normed_attn = lax.psum_scatter(normed_attn, "seq", scatter_dimension=0, tiled=True)
+        received = [pass_to(array, to) for to, array in carry]
+    out_grad = dot(mixed_t, branch_all)
     qkv_weight_grad = t_dot(normed_all, qkv_grad)
-    normed_attn = low(dot_t(qkv_grad, qkv_w))
-    normed_attn = lax.psum_scatter(normed_attn, "seq", scatter_dimension=0, tiled=True)
     input_part, attn_gain_grad = jax.vjp(rms_norm, layer_in, attn_scale)[1](
         normed_attn.astype(jnp.float32)
     )
@@ -989,6 +1374,7 @@
     return (
         input_part + after_grad,
         (low(qkv_weight_grad), low(out_grad), low(router_grad), gain_grads),
+        received,
     )
 
 
@@ -1040,8 +1426,15 @@
     wide = jnp.concatenate(
         [low(routes[0, :, 0].reshape(-1)), small, jnp.zeros((-known % 4096,), jnp.bfloat16)]
     )
-    wide = lax.all_gather(wide.reshape(-1, 256), ("section", "dp", "seq"), axis=0, tiled=True)
-    wide = wide.reshape(2, dp * seq, -1)
+    wide = wide.reshape(-1, 256)
+    if has_kernels():
+        other_wide = swap(wide)
+        wide = jnp.stack(by_layer(0, [wide, other_wide], [other_wide, wide]))
+        wide = gather_small(wide.reshape(-1, 256), 13).reshape(dp * seq, 2, -1)
+        wide = jnp.transpose(wide, (1, 0, 2))
+    else:
+        wide = lax.all_gather(wide, ("section", "dp", "seq"), axis=0, tiled=True)
+        wide = wide.reshape(2, dp * seq, -1)
     paths = wide[:, :, : routes[0].size].reshape(2, dp * seq, 2, -1, TOP_K)
     paths = lax.dynamic_index_in_dim(paths, section, 2, keepdims=False).astype(jnp.int32)
     small = wide[:, :, routes[0].size : routes[0].size + known]
@@ -1063,8 +1456,7 @@
         lax.dynamic_slice(w_down[0], (start, unit_start, 0), (count, units, width)),
     )
     other_gate = swap(after(own_experts[0], other_group))
-    other_up = swap(after(own_experts[1], other_gate))
-    experts = (own_experts, (other_gate, other_up))
+    experts = (own_experts, (other_gate,))
 
     weights = []
     pickings = []
@@ -1086,9 +1478,9 @@
         )
         pickings.append(routing(paths[number], first_expert, count) + (first_expert,))
 
-    first_in = layer_in.astype(jnp.float32)
+    first_in = after(layer_in, other_gate).astype(jnp.float32)
     updated, slot_out, first_saved, experts = forward_layer(
-        0, first_in, pickings[0], weights[0], experts
+        0, first_in, pickings[0], weights[0], experts, (None, own_experts[1])
     )
     sums, _ = token_sums(pickings[0][2], slot_out, 3)
     first_out = updated + sums
@@ -1101,20 +1493,17 @@
         1, top_grad, second_saved, pickings[1], experts
     )
     sums, (received[1][0],) = token_sums(pickings[1][2], slot_out, 6, (1, second_experts[0]))
-    middle_grad, second_dense = backward_layer(
-        top_grad, sums, gate_term, second_saved, pickings[1], weights[1]
-    )
-    slot_out, gate_term, first_experts, (received[1][1],) = expert_gradients(
-        0, middle_grad, first_saved, pickings[0], experts, (1, second_experts[1])
-    )
-    sums, (received[0][0], received[1][2]) = token_sums(
-        pickings[0][2], slot_out, 7, (0, first_experts[0]), (1, second_experts[2])
-    )
-    received[0][1] = pass_to(after(first_experts[1], received[0][0]), 0)
-    bottom_grad, first_dense = backward_layer(
-        middle_grad, sums, gate_term, first_saved, pickings[0], weights[0]
-    )
-    second_slots = after(second_slots, received[0][1], bottom_grad)
+    middle_grad, second_dense, (received[1][1],) = backward_layer(
+        1, top_grad, sums, gate_term, second_saved, pickings[1], weights[1], (1, second_experts[1])
+    )
+    slot_out, gate_term, first_experts, (received[1][2],) = expert_gradients(
+        0, middle_grad, first_saved, pickings[0], experts, (1, second_experts[2])
+    )
+    sums, (received[0][0],) = token_sums(pickings[0][2], slot_out, 7, (0, first_experts[0]))
+    bottom_grad, first_dense, (received[0][1],) = backward_layer(
+        0, middle_grad, sums, gate_term, first_saved, pickings[0], weights[0], (0, first_experts[1])
+    )
+    second_slots = after(second_slots, received[0][1])
     sums, (received[0][2],) = token_sums(
         pickings[1][2], second_slots, 8, (0, first_experts[2])
     )

time: 1700 us -> 1550 us (0.912)
  Pallas kernels: 746 us -> 1090 us
  waiting for transfers between devices: 380 us -> 81.7 us
  matrix products: 174 us -> 83.7 us
  blocking collectives: 48 us -> 0 us
  other arithmetic: 133 us -> 95.5 us
    pallas_call x0 -> x5, Pallas kernels: none -> 289 us  [the longest x2 146 us: attention_backward_call(): pl.pallas_call(kernel, out_shape=[jax.ShapeDtypeStruct(*result) for resul...]
    ppermute x4, waiting for transfers between devices: 99.8 us -> 16 us  [swap(): return lax.ppermute(block, 'section', [(0, 1), (1, 0)])]
    all_gather x4 -> x0, waiting for transfers between devices: 80.8 us -> none  [the longest x2 44.3 us: backward_layer(): branch_all = lax.all_gather(low(after_grad), 'seq', axis=0, tiled=True)]
    reduce_scatter x4 -> x0, waiting for transfers between devices: 66.4 us -> none  [the longest x2 35.4 us: backward_layer(): lax.psum_scatter(normed_attn, 'seq', scatter_dimension=0, tiled=True)]
    dot_general x24 -> x0, matrix products: 59.5 us -> none  [the longest x4 25.8 us: attention_backward(): jnp.einsum('qhgd,khd->hgqk', grad_block, values[:key_end], preferred_elem...]
    pallas_call x4, Pallas kernels: 402 us -> 457 us  [combine(): pl.pallas_call(kernel, out_shape=[jax.ShapeDtypeStruct((rows, width), jnp...]
    all_gather x1 -> x0, blocking collectives: 36.3 us -> none  [body(): lax.all_gather(wide.reshape(-1, 256), ('section', 'dp', 'seq'), axis=0, t...]
    all_to_all x3, waiting for transfers between devices: 42.7 us -> 9.48 us  [body(): lax.all_to_all(piece, 'seq', split_axis=0, concat_axis=0, tiled=True)]
  transfers between devices with their start and end apart: 44 -> 36, of which waited for: 21 -> 10; matrix products, arithmetic and copies ran while one was open for 17% -> 11% of each run, Pallas kernels for 29% -> 46%
where the time goes in v5:
time: 1550 us; the launch traced here: 1540 us
  Pallas kernels  1090 us (70%)
  starting transfers between devices  98.3 us (6%)
  other arithmetic  95.5 us (6%)
  matrix products  83.7 us (5%)
  local copies, waits for them, and re-layouts  82.1 us (5%)
  waiting for transfers between devices  81.7 us (5%)
  between operations  16 us (1%)
    pallas_call x4, Pallas kernels, combine(): pl.pallas_call(kernel, out_shape=[jax.ShapeDtypeStruct((rows, width), jnp...  457 us
    pallas_call x2, Pallas kernels, expert_forward(): pl.pallas_call(kernel, out_shape=shapes, in_specs=[anywhere, near, near,...  175 us
    pallas_call x2, Pallas kernels, expert_backward(): pl.pallas_call(kernel, out_shape=[jax.ShapeDtypeStruct(*result) for resul...  166 us
    pallas_call x2, Pallas kernels, attention_backward_call(): pl.pallas_call(kernel, out_shape=[jax.ShapeDtypeStruct(*result) for resul...  146 us
    pallas_call x2, Pallas kernels, attention_forward_call(): pl.pallas_call(kernel, out_shape=[jax.ShapeDtypeStruct(*result) for resul...  129 us
    dot_general x6, matrix products, each_dot(): return jnp.einsum(form, a, b, preferred_element_type=jnp.float32)  53.6 us
    convert_element_type x16, other arithmetic, low(): return v.astype(jnp.bfloat16)  32.2 us
  transfers between devices with their start and end apart: 36, of which 10 were waited for; matrix products, arithmetic and copies ran while one was open for 11% of the time, Pallas kernels for 46%

profile of v5, /device:TPU:16, one launch (start us, length us, event | category | flops | bytes accessed | tf_op | source)
XLA Modules:
  0.0 1544.7 jit_solution(8396091771383538410)
XLA Ops:
  10.6 13.6 collective-permute-done.3
  37.5 10.7 collective-permute-done
  55.5 6.5 all-to-all-done
  81.4 14.9 gather_small.1
  125.8 6.6 compare_convert_fusion
  148.6 7.2 all-to-all-done.1
  158.1 72.7 %attention_forward.2 = (f32[256,1536]{1,0:T(8,128)}, bf16[4,256,1536]{2,1,0:T(8,128)(2,1)}, bf16[10,1024,64]{2,1,0:T(8,128)(2,1)}, f32[8,1024]{1,0:T(8,128)}, bf...) custom-call(bf16[256,1536]{1,0:T(8,128)(2,1)} %fusion.6.refs_0_, ...), custom_call_target="tpu_custom_call" | custom-call | flops 80000000000 | bytes 100000000 | tf_op jit(solution)/shard_map/attention_forward/pallas_call | solution.py:997
  234.8 92.3 %expert_forward.2 = (bf16[2,1280,1536]{2,1,0:T(8,128)(2,1)}, bf16[2,1280,512]{2,1,0:T(8,128)(2,1)}, bf16[2,1280,512]{2,1,0:T(8,128)(2,1)}, bf16[2,1280,512]{2,1,...) custom-call(bf16[256,1536]{1,0:T(8,128)(2,1)} %multiply_convert_fusion.2.ref, ...), custom_call_target="tpu_custom_call" | custom-call | flops 80000000000 | bytes 100000000 | tf_op jit(solution)/shard_map/expert_forward/pallas_call | solution.py:495
  327.1 97.6 %combine.4 = f32[256,1536]{1,0:T(8,128)} custom-call(bf16[16,256,160]{2,1,0:T(8,128)(2,1)} %bitcast.213, bf16[16,160,1536]{2,1,0:T(8,128)(2,1)} %get-tuple-element.76.refs_1_), custom_call_target="tpu_custom_call" | custom-call | flops 80000000000 | bytes 100000000 | tf_op jit(solution)/shard_map/combine/pallas_call | solution.py:666
  428.6 55.8 %attention_forward.3 = (f32[256,1536]{1,0:T(8,128)}, bf16[4,256,1536]{2,1,0:T(8,128)(2,1)}, bf16[10,1024,64]{2,1,0:T(8,128)(2,1)}, f32[8,1024]{1,0:T(8,128)}, bf16[384,1024]{1,0:T(8,128)(2,1)}) custom-call(bf16[256,1536]{1,0:T(8,128)(2,1)} %multiply_convert_fusion.1.refs_0_, bf16[1536,640]{1,0:T(8,128)(2,1)} %all-gather.9.cloned.1.call-done.refs_1_, ...), custom_call_target="tpu_custom_call" | custom-call | flops 80000000000 | bytes 100000000 | tf_op jit(solution)/shard_map/attention_forward/pallas_call | solution.py:997
  491.1 83.1 %expert_forward.3 = (bf16[2,1280,1536]{2,1,0:T(8,128)(2,1)}, bf16[2,1280,512]{2,1,0:T(8,128)(2,1)}, bf16[2,1280,512]{2,1,0:T(8,128)(2,1)}, bf16[2,1280,512]{2,1,...) custom-call(bf16[256,1536]{1,0:T(8,128)(2,1)} %copy-done.23, ...), custom_call_target="tpu_custom_call" | custom-call | flops 80000000000 | bytes 100000000 | tf_op jit(solution)/shard_map/expert_forward/pallas_call | solution.py:495
  574.2 85.2 %expert_backward.2 = (bf16[2,1280,1536]{2,1,0:T(8,128)(2,1)}, bf16[2,1280,512]{2,1,0:T(8,128)(2,1)}, bf16[2,1280,512]{2,1,0:T(8,128)(2,1)}, f32[2,1280,128]{2,1,0:T(8,128)}, bf16[16,160,1536]{2,1,0:T(8,128)(2,1)}) custom-call(bf16[256,1536]{1,0:T(8,128)(2,1)} %dynamic-slice_bitcast_fusion.3.refs_0_, bf16[16,160,256]{2,1,0:T(8,128)(2,1)} %copy.232.refs_1_, ...), custom_call_target="tpu_custom_call" | custom-call | flops 80000000000 | bytes 100000000 | tf_op jit(solution)/shard_map/expert_backward/pallas_call | solution.py:791
  659.4 10.1 convolution_convert_fusion.5.refs_2_
  669.4 7.6 convolution_convert_fusion.4.refs_7_
  677.0 9.2 convolution_convert_fusion.3.refs_11_
  688.5 8.3 all-to-all-start.2
  696.9 100.1 %combine.5 = (f32[256,1536]{1,0:T(8,128)}, bf16[2,1536,512]{2,1,0:T(8,128)(2,1)}) custom-call(bf16[16,256,160]{2,1,0:T(8,128)(2,1)} %bitcast.211, bf16[16,160,1536]{2,1,0:T(8,128)(2,1)} %get-tuple-element.89.refs_1_, bf16[2,1536,512]{2,1,0:T(8,128)(2,1)} %convolution_convert_fusion.5.refs_2_), custom_call_target="tpu_custom_call" | custom-call | flops 80000000000 | bytes 100000000 | tf_op jit(solution)/shard_map/combine/pallas_call | solution.py:666
  802.9 71.8 %attention_backward.2 = (f32[256,1536]{1,0:T(8,128)}, bf16[4,256,1536]{2,1,0:T(8,128)(2,1)}, bf16[1024,640]{1,0:T(8,128)(2,1)}, bf16[2,1536,512]{2,1,0:T(8,128)(2,1)}) custom-call(bf16[256,1536]{1,0:T(8,128)(2,1)} %fusion.57.refs_0_, bf16[1536,640]{1,0:T(8,128)(2,1)} %all-gather.9.cloned.1.call-done.refs_1_, ...), custom_call_target="tpu_custom_call" | custom-call | flops 80000000000 | bytes 100000000 | tf_op jit(solution)/shard_map/attention_backward/pallas_call | solution.py:1123
  880.5 80.5 %expert_backward.3 = (bf16[2,1280,1536]{2,1,0:T(8,128)(2,1)}, bf16[2,1280,512]{2,1,0:T(8,128)(2,1)}, bf16[2,1280,512]{2,1,0:T(8,128)(2,1)}, f32[2,1280,128]{2,1,...) custom-call(bf16[256,1536]{1,0:T(8,128)(2,1)} %get-tuple-element.218.refs_0_, ...), custom_call_target="tpu_custom_call" | custom-call | flops 80000000000 | bytes 100000000 | tf_op jit(solution)/shard_map/expert_backward/pallas_call | solution.py:791
  961.1 10.1 convolution_convert_fusion.2.refs_2_
  971.1 7.6 convolution_convert_fusion.1.refs_7_
  978.7 9.1 convolution_convert_fusion.refs_2_
  990.2 6.5 all-to-all-start.3
  1007.2 130.7 %combine.6 = (f32[256,1536]{1,0:T(8,128)}, bf16[2,1536,512]{2,1,0:T(8,128)(2,1)}) custom-call(bf16[16,256,160]{2,1,0:T(8,128)(2,1)} %bitcast.214, bf16[16,160,1536]{2,1,0:T(8,128)(2,1)} %get-tuple-element.107.refs_1_, bf16[2,1536,512]{2,1,0:T(8,128)(2,1)} %convolution_convert_fusion.2.refs_2_), custom_call_target="tpu_custom_call" | custom-call | flops 80000000000 | bytes 100000000 | tf_op jit(solution)/shard_map/combine/pallas_call | solution.py:666
  1154.0 74.1 %attention_backward.3 = (f32[256,1536]{1,0:T(8,128)}, bf16[4,256,1536]{2,1,0:T(8,128)(2,1)}, bf16[1024,640]{1,0:T(8,128)(2,1)}, bf16[2,1536,512]{2,1,0:T(8,128)(2,1)}) custom-call(bf16[256,1536]{1,0:T(8,128)(2,1)} %get-tuple-element.216.refs_0_, bf16[1536,640]{1,0:T(8,128)(2,1)} %all-gather.5.cloned.1.call-done.refs_1_, ...), custom_call_target="tpu_custom_call" | custom-call | flops 80000000000 | bytes 100000000 | tf_op jit(solution)/shard_map/attention_backward/pallas_call | solution.py:1123
  1253.1 128.7 %combine.7 = (f32[256,1536]{1,0:T(8,128)}, bf16[2,512,1536]{2,1,0:T(8,128)(2,1)}) custom-call(bf16[16,256,160]{2,1,0:T(8,128)(2,1)} %bitcast.212, bf16[16,160,1536]{2,1,0:T(8,128)(2,1)} %get-tuple-element.115.refs_1_, bf16[2,512,1536]{2,1,0:T(8,128)(2,1)} %convolution_convert_fusion.refs_2_), custom_call_target="tpu_custom_call" | custom-call | flops 80000000000 | bytes 100000000 | tf_op jit(solution)/shard_map/combine/pallas_call | solution.py:666
  1399.0 6.9 collective-permute-start.8
  1415.9 7.0 collective-permute-start.6
  1422.9 6.3 add_convert_fusion.1
  1429.2 10.6 collective-permute-done.10
  1457.6 12.6 collective-permute-done.9
  1516.5 9.5 all-to-all-done.9
  (389 shorter events, 275.3 us)
Async XLA Ops:
  7.2 150.8 %all-gather.7.cloned.1.call-start = ((), (), s32[]{:S(2)}) async-start(), calls=%async_computation.16 | async-start | bytes 1474560 | tf_op jit(solution)/shard_map/all_gather | solution.py:1467
  7.3 16.9 %collective-permute-start.3 = (bf16[96,1536]{1,0:T(8,128)(2,1)}, bf16[96,1536]{1,0:T(8,128)(2,1)S(1)}, u32[]{:S(2)}, u32[]{:S(2)}) collective-permute-start(bf16[96,1536]{1,0:T(8,128)(2,1)} %bitcast.225), channel_id=1, source_target_pairs={{0,0},{1,4},{2,8},{3,12},{4,1},{5,5},{6,9},{7,13},{8,2},{9,6},{10,... | collective-permute-start | bytes 884744 | tf_op jit(solution)/shard_map/ppermute | solution.py:1422
  34.8 13.5 collective-permute-start
  36.9 43.8 %collective-permute-start.2 = (bf16[32,256]{1,0:T(8,128)(2,1)S(1)}, bf16[32,256]{1,0:T(8,128)(2,1)S(1)}, u32[]{:S(2)}, u32[]{:S(2)}) collective-permute-start(bf16[32,256]{1,0:T(8,128)(2,1)S(1)} %reshape.322), channel_id=1, source_target_pairs={{0,16},{16,0},{1,17},{17,1},{2,18},{18,2},{3,19},{19,3},{4,20},{20... | collective-permute-start | bytes 49160 | tf_op jit(solution)/shard_map/ppermute | solution.py:39
  53.4 104.6 %all-gather.5.cloned.1.call-start = ((), (), s32[]{:S(2)}) async-start(), calls=%async_computation.15 | async-start | bytes 2457600 | tf_op jit(solution)/shard_map/all_gather | solution.py:1466
  62.0 366.6 %all-gather.11.cloned.1.call-start = ((), (), s32[]{:S(2)}) async-start(), calls=%async_computation.18 | async-start | bytes 1474560 | tf_op jit(solution)/shard_map/all_gather | solution.py:1467
  77.9 78.7 %collective-permute-start.1 = (bf16[2,1536,512]{2,1,0:T(8,128)(2,1)}, bf16[2,1536,512]{2,1,0:T(8,128)(2,1)}, u32[]{:S(2)}, u32[]{:S(2)}) collective-permute-start(bf16[2,1536,512]{2,1,0:T(8,128)(2,1)} %dynamic-slice_bitcast_fusion.2.refs_5_), channel_id=1, source_target_pairs={{0,16},{16,0},{1,17},{17,1},{2,18},{18,2},{3,19},{19,3},{4,20},{20... | collective-permute-start | bytes 9437192 | tf_op jit(solution)/shard_map/ppermute | solution.py:39
  147.4 281.2 %all-gather.9.cloned.1.call-start = ((), (), s32[]{:S(2)}) async-start(), calls=%async_computation.17 | async-start | bytes 2457600 | tf_op jit(solution)/shard_map/all_gather | solution.py:1466
  688.5 109.1 %all-to-all-start.2 = ((f32[16,2,256]{2,1,0:T(2,128)}), f32[16,2,256]{2,1,0:T(2,128)S(1)}, u32[]{:S(2)}, u32[]{:S(2)}) async-start(f32[16,2,256]{2,1,0:T(2,128)} %multiply_reduce_fusion.1), calls=%async_computation.2 | async-start | bytes 65536 | tf_op jit(solution)/shard_map/all_to_all | solution.py:1340
  990.2 155.0 %all-to-all-start.3 = ((f32[16,2,256]{2,1,0:T(2,128)}), f32[16,2,256]{2,1,0:T(2,128)S(1)}, u32[]{:S(2)}, u32[]{:S(2)}) async-start(f32[16,2,256]{2,1,0:T(2,128)} %multiply_reduce_fusion), calls=%async_computation.3 | async-start | bytes 65536 | tf_op jit(solution)/shard_map/all_to_all | solution.py:1340
  996.7 444.4 %reduce-scatter.15.cloned.1.call-start = ((), (), s32[]{:S(2)}) async-start(), calls=%async_computation.22 | async-start | bytes 2949120 | tf_op jit(solution)/shard_map/reduce_scatter | solution.py:1538
  1145.2 92.3 %all-to-all-start.5 = ((f32[2,16,96]{2,0,1:T(2,128)}), f32[2,16,96]{2,0,1:T(2,128)}, u32[]{:S(2)}, u32[]{:S(2)}) async-start(f32[2,16,96]{2,0,1:T(2,128)} %pad_maximum_fusion.6), calls=%async_computation.5 | async-start | bytes 32768 | tf_op jit(solution)/shard_map/all_to_all | solution.py:1546
  1242.7 210.3 %reduce-scatter.13.cloned.1.call-start = ((), (), s32[]{:S(2)}) async-start(), calls=%async_computation.21 | async-start | bytes 2949120 | tf_op jit(solution)/shard_map/reduce_scatter | solution.py:1538
  1248.4 139.9 %all-to-all-start.8 = ((bf16[4,2,384,512]{3,2,1,0:T(8,128)(2,1)}), bf16[4,2,384,512]{3,2,1,0:T(8,128)(2,1)}, u32[]{:S(2)}, u32[]{:S(2)}) async-start(bf16[4,2,384,512]{3,2,1,0:T(8,128)(2,1)} %bitcast.203), calls=%async_computation.10 | async-start | bytes 6291456 | tf_op jit(solution)/shard_map/all_to_all | solution.py:1564
  1388.3 52.8 %all-to-all-start.10 = ((bf16[4,2,128,1536]{3,2,1,0:T(8,128)(2,1)}), bf16[4,2,128,1536]{3,2,1,0:T(8,128)(2,1)}, u32[]{:S(2)}, u32[]{:S(2)}) async-start(bf16[4,2,128,1536]{3,2,1,0:T(8,128)(2,1)} %bitcast.205), calls=%async_computation.12 | async-start | bytes 6291456 | tf_op jit(solution)/shard_map/all_to_all | solution.py:1564
  1392.9 91.0 %reduce-scatter.11.cloned.1.call-start = ((), (), s32[]{:S(2)}) async-start(), calls=%async_computation.20 | async-start | bytes 1474560 | tf_op jit(solution)/shard_map/reduce_scatter | solution.py:1543
  1397.7 78.6 %collective-permute-start.5 = (f32[256,1536]{1,0:T(8,128)S(1)}, f32[256,1536]{1,0:T(8,128)}, u32[]{:S(2)}, u32[]{:S(2)}) collective-permute-start(f32[256,1536]{1,0:T(8,128)S(1)} %copy-done.7), channel_id=1, source_target_pairs={{16,0},{17,1},{18,2},{19,3},{20,4},{21,5},{22,6},{23,7},{24,8},{25... | collective-permute-start | bytes 4718600 | tf_op jit(solution)/shard_map/ppermute | solution.py:43
  1399.0 77.4 %collective-permute-start.8 = (f32[256,1536]{1,0:T(8,128)}, f32[256,1536]{1,0:T(8,128)}, u32[]{:S(2)}, u32[]{:S(2)}) collective-permute-start(f32[256,1536]{1,0:T(8,128)} %get-tuple-element.219), channel_id=1, source_target_pairs={{0,16},{1,17},{2,18},{3,19},{4,20},{5,21},{6,22},{7,23},{8,24},{9,... | collective-permute-start | bytes 4718600 | tf_op jit(solution)/shard_map/ppermute | solution.py:43
  1406.7 33.1 %collective-permute-start.10 = (f32[2,96]{1,0:T(2,128)S(1)}, f32[2,96]{1,0:T(2,128)S(1)}, u32[]{:S(2)}, u32[]{:S(2)}) collective-permute-start(f32[2,96]{1,0:T(2,128)S(1)} %reduce_sum.226), channel_id=1, source_target_pairs={{0,16},{1,17},{2,18},{3,19},{4,20},{5,21},{6,22},{7,23},{8,24},{9,... | collective-permute-start | bytes 2312 | tf_op jit(solution)/shard_map/ppermute | solution.py:43
  1411.6 64.7 %collective-permute-start.7 = (f32[256,1536]{1,0:T(8,128)}, f32[256,1536]{1,0:T(8,128)}, u32[]{:S(2)}, u32[]{:S(2)}) collective-permute-start(f32[256,1536]{1,0:T(8,128)} %fusion.11), channel_id=1, source_target_pairs={{16,0},{17,1},{18,2},{19,3},{20,4},{21,5},{22,6},{23,7},{24,8},{25... | collective-permute-start | bytes 4718600 | tf_op jit(solution)/shard_map/ppermute | solution.py:43
  1415.9 60.5 %collective-permute-start.6 = (f32[256,1536]{1,0:T(8,128)}, f32[256,1536]{1,0:T(8,128)}, u32[]{:S(2)}, u32[]{:S(2)}) collective-permute-start(f32[256,1536]{1,0:T(8,128)} %add.176), channel_id=1, source_target_pairs={{0,16},{1,17},{2,18},{3,19},{4,20},{5,21},{6,22},{7,23},{8,24},{9,... | collective-permute-start | bytes 4718600 | tf_op jit(solution)/shard_map/ppermute | solution.py:43
  1439.8 30.4 %collective-permute-start.9 = (f32[2,96]{1,0:T(2,128)S(1)}, f32[2,96]{1,0:T(2,128)S(1)}, u32[]{:S(2)}, u32[]{:S(2)}) collective-permute-start(f32[2,96]{1,0:T(2,128)S(1)} %reduce_sum.223), channel_id=1, source_target_pairs={{16,0},{17,1},{18,2},{19,3},{20,4},{21,5},{22,6},{23,7},{24,8},{25... | collective-permute-start | bytes 2312 | tf_op jit(solution)/shard_map/ppermute | solution.py:43
  1441.1 13.0 all-to-all-start.7
  1444.6 46.8 %reduce-scatter.9.cloned.1.call-start = ((), (), s32[]{:S(2)}) async-start(), calls=%async_computation.19 | async-start | bytes 1474560 | tf_op jit(solution)/shard_map/reduce_scatter | solution.py:1543
  1454.1 16.6 %all-to-all-start.6 = ((bf16[4,96,672]{2,1,0:T(8,128)(2,1)}), bf16[4,96,672]{2,1,0:T(8,128)(2,1)S(1)}, u32[]{:S(2)}, u32[]{:S(2)}) async-start(bf16[4,96,672]{2,1,0:T(8,128)(2,1)} %bitcast.219), calls=%async_computation.6 | async-start | bytes 1179648 | tf_op jit(solution)/shard_map/all_to_all | solution.py:1541
  1471.5 54.5 %all-to-all-start.9 = ((bf16[4,2,384,512]{3,2,1,0:T(8,128)(2,1)}), bf16[4,2,384,512]{3,2,1,0:T(8,128)(2,1)}, u32[]{:S(2)}, u32[]{:S(2)}) async-start(bf16[4,2,384,512]{3,2,1,0:T(8,128)(2,1)} %bitcast.204), calls=%async_computation.11 | async-start | bytes 6291456 | tf_op jit(solution)/shard_map/all_to_all | solution.py:1564
  1484.0 18.7 %collective-permute-start.14 = (bf16[96,1536]{1,0:T(8,128)(2,1)}, bf16[96,1536]{1,0:T(8,128)(2,1)S(1)}, u32[]{:S(2)}, u32[]{:S(2)}) collective-permute-start(bf16[96,1536]{1,0:T(8,128)(2,1)} %reduce-scatter.11.cloned.1.call-done), channel_id=1, source_target_pairs={{0,0},{4,1},{8,2},{12,3},{1,4},{5,5},{9,6},{13,7},{2,8},{6,9},{10,... | collective-permute-start | bytes 884744 | tf_op jit(solution)/shard_map/ppermute | solution.py:1544
  1491.3 17.3 %collective-permute-start.13 = (bf16[96,1536]{1,0:T(8,128)(2,1)}, bf16[96,1536]{1,0:T(8,128)(2,1)S(1)}, u32[]{:S(2)}, u32[]{:S(2)}) collective-permute-start(bf16[96,1536]{1,0:T(8,128)(2,1)} %reduce-scatter.9.cloned.1.call-done), channel_id=1, source_target_pairs={{0,0},{4,1},{8,2},{12,3},{1,4},{5,5},{9,6},{13,7},{2,8},{6,9},{10,... | collective-permute-start | bytes 884744 | tf_op jit(solution)/shard_map/ppermute | solution.py:1544
  1502.6 28.8 %collective-permute-start.16 = (bf16[96,1536]{1,0:T(8,128)(2,1)S(1)}, bf16[96,1536]{1,0:T(8,128)(2,1)S(1)}, u32[]{:S(2)}, u32[]{:S(2)}) collective-permute-start(bf16[96,1536]{1,0:T(8,128)(2,1)S(1)} %collective-permute-done.14), channel_id=1, source_target_pairs={{0,16},{1,17},{2,18},{3,19},{4,20},{5,21},{6,22},{7,23},{8,24},{9,... | collective-permute-start | bytes 884744 | tf_op jit(solution)/shard_map/ppermute | solution.py:43
  1508.6 22.8 %collective-permute-start.15 = (bf16[96,1536]{1,0:T(8,128)(2,1)S(1)}, bf16[96,1536]{1,0:T(8,128)(2,1)}, u32[]{:S(2)}, u32[]{:S(2)}) collective-permute-start(bf16[96,1536]{1,0:T(8,128)(2,1)S(1)} %collective-permute-done.13), channel_id=1, source_target_pairs={{16,0},{17,1},{18,2},{19,3},{20,4},{21,5},{22,6},{23,7},{24,8},{25... | collective-permute-start | bytes 884744 | tf_op jit(solution)/shard_map/ppermute | solution.py:43
  1509.9 23.5 %collective-permute-start.12 = (bf16[4,96,672]{2,1,0:T(8,128)(2,1)S(1)}, bf16[4,96,672]{2,1,0:T(8,128)(2,1)S(1)}, u32[]{:S(2)}, u32[]{:S(2)}) collective-permute-start(bf16[4,96,672]{2,1,0:T(8,128)(2,1)S(1)} %copy-done.30), channel_id=1, source_target_pairs={{0,16},{1,17},{2,18},{3,19},{4,20},{5,21},{6,22},{7,23},{8,24},{9,... | collective-permute-start | bytes 1548296 | tf_op jit(solution)/shard_map/ppermute | solution.py:43
  1515.2 18.2 %collective-permute-start.11 = (bf16[4,96,672]{2,1,0:T(8,128)(2,1)S(1)}, bf16[4,96,672]{2,1,0:T(8,128)(2,1)S(1)}, u32[]{:S(2)}, u32[]{:S(2)}) collective-permute-start(bf16[4,96,672]{2,1,0:T(8,128)(2,1)S(1)} %copy-done.32), channel_id=1, source_target_pairs={{16,0},{17,1},{18,2},{19,3},{20,4},{21,5},{22,6},{23,7},{24,8},{25... | collective-permute-start | bytes 1548296 | tf_op jit(solution)/shard_map/ppermute | solution.py:43
  (91 other events, 2393.2 us)
Sparse Core Ops, SparseCore 0:
  34.8 30.7 all-gather.6
  67.2 43.0 all-gather.4
  111.9 30.9 all-gather.10
  156.8 45.3 all-gather.8
  1007.3 77.0 reduce-scatter.14
  1248.5 47.5 reduce-scatter.12
  1397.8 27.4 reduce-scatter.10
  1453.1 29.5 reduce-scatter.8

commit v6 on v5

--- a/solution.py
+++ b/solution.py
@@ -257,7 +257,7 @@
     ]
 
 
-def gather_blocks(x_ref, scratch, compute, carried=None):
+def gather_blocks(x_ref, scratch, compute, carried=None, first=None):
     land, lsem, zs, zr, ys, yr, cs, cr = scratch
     d, s = lax.axis_index("dp"), lax.axis_index("seq")
 
@@ -276,9 +276,11 @@
         return remote(src, place(z, column), cs.at[z, across], cr.at[z, across], seq=s ^ 1)
 
     greet(d, s, None if carried is None else carried.section)
+    if first is not None:
+        first()
     own = pltpu.make_async_copy(x_ref, place(d, s), lsem)
     own.start()
-    if carried is not None:
+    if carried is not None and first is None:
         carried.start()
 
     @pl.when(d < 3)
@@ -342,21 +344,89 @@
     return land
 
 
-def gather_small(x, collective_id):
-    rows, width = x.shape
-
-    def kernel(x_ref, out_ref, *scratch):
-        gather_blocks(x_ref, scratch, lambda z: None)
-        out_ref[...] = scratch[0][...]
-
+def prepare_kernel(x_ref, pick_out, pick_t_out, chosen_out, small_out, both, places, lsem, carry_sem, *gather):
+    d, s, section = lax.axis_index("dp"), lax.axis_index("seq"), lax.axis_index("section")
+    known = x_ref.shape[0]
+    count = pick_out.shape[2] // CAP
+    rows = pick_out.shape[3]
+    land = gather[0]
+    part = both.at[pl.ds(pl.multiple_of(section * known, known), known)]
+    carried = Carried((None,), (x_ref,), (part,), carry_sem)
+
+    def swap_first():
+        carried.start()
+        own = pltpu.make_async_copy(x_ref, part, lsem)
+        own.start()
+        own.wait()
+        carried.finish()
+
+    gather_blocks(both, gather, lambda z: None, carried, swap_first)
+    first_expert = (d * 4 + s) * count
+    before = lax.broadcasted_iota(jnp.int32, (rows, rows), 0)
+    before = low(before < lax.broadcasted_iota(jnp.int32, (rows, rows), 1))
+    slot = lax.broadcasted_iota(jnp.int32, (CAP, rows), 0)
+    expert = lax.broadcasted_iota(jnp.int32, (EXPERTS, rows), 0)
+    lane = lax.broadcasted_iota(jnp.int32, (rows, count * CAP), 1)
+
+    @pl.loop(0, 2)
+    def _(layer):
+        @pl.loop(0, 16)
+        def _(b):
+            paths = land[b, pl.ds(pl.multiple_of(layer * known, 16), 16), :].astype(jnp.float32)
+            paths = jnp.where(section == 0, paths[:TOP_K], paths[TOP_K:]).astype(jnp.int32)
+            chosen = expert == paths[0:1]
+            for k in range(1, TOP_K):
+                chosen = chosen | (expert == paths[k : k + 1])
+            chosen_out[layer, b] = low(chosen)
+            mine = [
+                jnp.max((paths == first_expert + j).astype(jnp.float32), axis=0, keepdims=True)
+                for j in range(count)
+            ]
+            mine = jnp.concatenate(mine + [jnp.zeros((8 - count, rows), jnp.float32)], axis=0)
+            place = jnp.where(mine > 0.5, dot(low(mine), before), -10000.0)
+            places[...] = place
+            for j in range(count):
+                pick_out[layer, b, j * CAP : (j + 1) * CAP, :] = low(
+                    slot == place[j : j + 1].astype(jnp.int32)
+                )
+            turned = places[...].T.astype(jnp.int32)
+            pick_t = turned[:, 0:1] == lane
+            for j in range(1, count):
+                pick_t = pick_t & (lane < j * CAP) | (turned[:, j : j + 1] == lane - j * CAP)
+            pick_t_out[layer, b] = low(pick_t)
+
+        depth = small_out.shape[2] // 16
+        for b in range(16):
+            small = land[b, pl.ds(pl.multiple_of(layer * known + 16, 16), known - 16), :]
+            small_out[layer, :, b * depth : (b + 1) * depth] = small[:, :depth]
+
+
+def prepare(x, count, rows, depth, collective_id):
+    known, width = x.shape
+    bf = jnp.bfloat16
+    near = pl.BlockSpec(memory_space=pltpu.VMEM)
     return pl.pallas_call(
-        kernel,
-        out_shape=jax.ShapeDtypeStruct((16, rows, width), x.dtype),
+        prepare_kernel,
+        out_shape=[
+            jax.ShapeDtypeStruct((2, 16, count * CAP, rows), bf),
+            jax.ShapeDtypeStruct((2, 16, rows, count * CAP), bf),
+            jax.ShapeDtypeStruct((2, 16, EXPERTS, rows), bf),
+            jax.ShapeDtypeStruct((2, known - 16, 16 * depth), bf),
+        ],
         in_specs=[pl.BlockSpec(memory_space=pl.ANY)],
-        out_specs=pl.BlockSpec(memory_space=pltpu.VMEM),
-        scratch_shapes=gather_scratch(rows, width),
-        compiler_params=pltpu.CompilerParams(collective_id=collective_id, has_side_effects=True),
-        name="gather_small",
+        out_specs=[near] * 4,
+        scratch_shapes=[
+            pltpu.VMEM((2 * known, width), bf),
+            pltpu.VMEM((8, rows), jnp.float32),
+            DMA(()),
+            DMA((1, 2)),
+        ]
+        + gather_scratch(2 * known, width),
+        compiler_params=pltpu.CompilerParams(
+            collective_id=collective_id, has_side_effects=True, vmem_limit_bytes=60 << 20
+        ),
+        cost_estimate=pl.CostEstimate(flops=20_000_000_000, bytes_accessed=10_000_000, transcendentals=0),
+        name="prepare",
     )(x)
 
 
@@ -433,11 +503,11 @@
             x = rows[j, part, :]
             g = dot(x, wg[j])
             u = dot(x, wu[j])
-            logits = dot(x, router_ref[...])
+            logits = dot_t(x, router_ref[...])
             for q in range(4):
                 b = z * 4 + q
                 slots = slice(q * CAP, (q + 1) * CAP)
-                seen = dot(pick_ref[b, pl.ds(j * CAP, CAP), :], chosen_ref[b])
+                seen = dot_t(pick_ref[b, pl.ds(j * CAP, CAP), :], chosen_ref[b])
                 masked = jnp.where(seen > 0.5, logits[slots], -1e30)
                 power = jnp.exp(masked - jnp.max(masked, axis=1, keepdims=True))
                 own = jnp.sum(power * mine_ref[j], axis=1, keepdims=True)
@@ -1166,6 +1236,7 @@
     chosen = jnp.any(token_choice(route_all), axis=2)
     blocks, rows = chosen.shape[:2]
     mine = lax.dynamic_slice_in_dim(chosen, first_expert, count, axis=2)
+    chosen = low(jnp.transpose(chosen, (0, 2, 1)))
     earlier = jnp.tril(jnp.ones((rows, rows), jnp.bfloat16), -1)
     place = jnp.einsum(
         "ts,bsj->bjt", earlier, mine.astype(jnp.bfloat16), preferred_element_type=jnp.float32
@@ -1210,7 +1281,7 @@
     chosen, pick, pick_t, first_expert = picking
     own, other = experts
     count = own[0].shape[0]
-    blocks, rows = chosen.shape[:2]
+    blocks, _, rows = chosen.shape
     received = []
     normed_input = low(rms_norm(layer_in, attn_scale))
     if has_kernels():
@@ -1219,7 +1290,7 @@
         )
         attention_state = (normed_all.reshape(-1, layer_in.shape[1]), mixed_t, heads, log_total)
     else:
-        received = [swap(array) for _, array in carry]
+        received = [swap(array) if to is None else pass_to(array, to) for to, array in carry]
         normed_all = lax.all_gather(normed_input, "seq", axis=0, tiled=True)
         qkv = low(dot(normed_all, qkv_w))
         kv_width = KV_HEADS * HEAD_DIM // lax.axis_size("seq")
@@ -1233,15 +1304,16 @@
     normed_ffn = low(rms_norm(after_update, ffn_scale))
     own_block = lax.axis_index("dp") * lax.axis_size("seq") + lax.axis_index("seq")
     own_chosen = lax.dynamic_index_in_dim(chosen, own_block, 0, keepdims=False)
-    own_logits = jnp.where(own_chosen, dot(normed_ffn, router_w), -jnp.inf)
-    own_gates = jax.nn.softmax(own_logits, axis=-1)
-    other = tuple(other) + tuple(received)
+    own_logits = jnp.where(own_chosen > 0, dot_t(router_w, normed_ffn), -jnp.inf)
+    own_gates = jax.nn.softmax(own_logits, axis=0)
+    if number == 0:
+        other = other + (received[0],)
     mine = (
         jnp.arange(EXPERTS)[None, None, :] == first_expert + jnp.arange(count)[:, None, None]
     ).astype(jnp.float32)
     if has_kernels():
         *expert_state, slot_out = expert_forward(
-            number, normed_ffn, pick, low(chosen), router_w, mine, own, other, 1 + number
+            number, normed_ffn, pick, chosen, router_w, mine, own, other, 1 + number
         )
         if number == 0:
             *expert_state, slot_out, other_down = (*expert_state, slot_out)
@@ -1251,8 +1323,9 @@
             other = other[:2] + (swap(own[2]),)
         gate_w, up_w, down_w = by_layer(number, own, other)
         ffn_all = lax.all_gather(normed_ffn, TOKENS, axis=0, tiled=True)
-        logits = dot(ffn_all, router_w).reshape(blocks, rows, EXPERTS)
-        gates = jax.nn.softmax(jnp.where(chosen, logits, -jnp.inf), axis=-1)
+        logits = dot_t(ffn_all, router_w).reshape(blocks, rows, EXPERTS)
+        used = jnp.transpose(chosen, (0, 2, 1)) > 0
+        gates = jax.nn.softmax(jnp.where(used, logits, -jnp.inf), axis=-1)
         slot_rows = choose(pick, ffn_all.reshape(blocks, rows, -1), count)
         mine_gates = jnp.einsum("bte,jxe->bjt", gates, mine, precision=lax.Precision.HIGHEST)
         slot_gates = jnp.sum(
@@ -1273,7 +1346,7 @@
         own_gates,
         expert_state,
     )
-    return (after_update, slot_out, saved, (own, other))
+    return (after_update, slot_out, saved, (own, other), received)
 
 
 def token_sums(pick_t, slot_out, collective_id, *carry):
@@ -1289,7 +1362,7 @@
     chosen, pick, pick_t, first_expert = picking
     own, other = experts
     count = own[0].shape[0]
-    blocks, rows = chosen.shape[:2]
+    blocks, _, rows = chosen.shape
     slot_rows, gate_pre, up_pre, scaled, slot_gates = saved[-1]
     if has_kernels():
         slot_grads, gate_low, up_low, gate_term, slot_out, *received = expert_backward(
@@ -1331,19 +1404,19 @@
         own_gates,
         _,
     ) = saved
-    blocks, rows = chosen.shape[:2]
+    blocks, _, rows = chosen.shape
     count = gate_term.shape[0]
     by_slot = jnp.transpose(gate_term.reshape(count, blocks, CAP), (1, 0, 2))
     gate_terms = jnp.sum(
         pick.reshape(blocks, count, CAP, rows).astype(jnp.float32) * by_slot[..., None], axis=2
     )
     gate_terms = lax.all_to_all(gate_terms, TOKENS, split_axis=0, concat_axis=0, tiled=True)
-    gate_terms = jnp.sum(gate_terms.reshape(EXPERTS, -1, rows), axis=1).T
+    gate_terms = jnp.sum(gate_terms.reshape(EXPERTS, -1, rows), axis=1)
     logit_grad = low(
-        own_gates * (gate_terms - jnp.sum(own_gates * gate_terms, axis=-1, keepdims=True))
-    )
-    router_grad = t_dot(normed_ffn, logit_grad)
-    normed_grad = normed_grad + dot_t(logit_grad, router_w)
+        own_gates * (gate_terms - jnp.sum(own_gates * gate_terms, axis=0, keepdims=True))
+    )
+    router_grad = dot(logit_grad, normed_ffn)
+    normed_grad = normed_grad + t_dot(logit_grad, router_w)
     after_part, ffn_gain_grad = jax.vjp(rms_norm, after_update, ffn_scale)[1](normed_grad)
     after_grad = after_part + layer_grad
     if has_kernels():
@@ -1370,12 +1443,10 @@
     input_part, attn_gain_grad = jax.vjp(rms_norm, layer_in, attn_scale)[1](
         normed_attn.astype(jnp.float32)
     )
-    gain_grads = jnp.stack([attn_gain_grad, ffn_gain_grad])
-    return (
-        input_part + after_grad,
-        (low(qkv_weight_grad), low(out_grad), low(router_grad), gain_grads),
-        received,
-    )
+    small = [router_grad, attn_gain_grad[None], ffn_gain_grad[None]]
+    small = jnp.concatenate(small + [jnp.zeros((128 - EXPERTS - 2, small[0].shape[1]))], axis=0)
+    qkv_weight_grad = jnp.concatenate([low(qkv_weight_grad), low(small).T], axis=1)
+    return (input_part + after_grad, (qkv_weight_grad, low(out_grad)), received)
 
 
 def by_layer(number, own, other):
@@ -1421,26 +1492,6 @@
     other_group = swap(own_group)
     own_out = lax.ppermute(output_matrix[0], TOKENS, to_group)
     other_out = swap(own_out)
-    small = jnp.concatenate([router_matrix[0].T, attn_gain, ffn_gain], axis=0).reshape(-1)
-    known = small.shape[0]
-    wide = jnp.concatenate(
-        [low(routes[0, :, 0].reshape(-1)), small, jnp.zeros((-known % 4096,), jnp.bfloat16)]
-    )
-    wide = wide.reshape(-1, 256)
-    if has_kernels():
-        other_wide = swap(wide)
-        wide = jnp.stack(by_layer(0, [wide, other_wide], [other_wide, wide]))
-        wide = gather_small(wide.reshape(-1, 256), 13).reshape(dp * seq, 2, -1)
-        wide = jnp.transpose(wide, (1, 0, 2))
-    else:
-        wide = lax.all_gather(wide, ("section", "dp", "seq"), axis=0, tiled=True)
-        wide = wide.reshape(2, dp * seq, -1)
-    paths = wide[:, :, : routes[0].size].reshape(2, dp * seq, 2, -1, TOP_K)
-    paths = lax.dynamic_index_in_dim(paths, section, 2, keepdims=False).astype(jnp.int32)
-    small = wide[:, :, routes[0].size : routes[0].size + known]
-    small = jnp.transpose(small.reshape(2, dp * seq, EXPERTS + 2, depth), (0, 2, 1, 3))
-    small = small.reshape(2, EXPERTS + 2, width)
-
     local = w_gate.shape[1]
     hidden_units = w_gate.shape[3]
     if local >= seq:
@@ -1458,8 +1509,25 @@
     other_gate = swap(after(own_experts[0], other_group))
     experts = (own_experts, (other_gate,))
 
+    small = jnp.concatenate([router_matrix[0].T, attn_gain, ffn_gain], axis=0)
+    paths = routes[0, :, 0]
+    if has_kernels():
+        small = jnp.pad(small, ((0, -small.shape[0] % 16), (0, 256 - depth)))
+        paths = low(jnp.transpose(paths, (0, 2, 1)).reshape(2 * TOP_K, -1))
+        picks, picks_t, chosens, small = prepare(
+            jnp.concatenate([paths, small], axis=0), count, hidden_in.shape[2], depth, 13
+        )
+        pickings = [(chosens[n], picks[n], picks_t[n], first_expert) for n in range(2)]
+    else:
+        small = lax.all_gather(small, ("section", "dp", "seq"), axis=0, tiled=False)
+        small = jnp.transpose(small.reshape(2, dp * seq, -1, depth), (0, 2, 1, 3))
+        small = small.reshape(2, -1, width)
+        paths = lax.all_gather(paths, ("section", "dp", "seq"), axis=0, tiled=False)
+        paths = lax.dynamic_index_in_dim(paths, section, 1, keepdims=False)
+        paths = paths.reshape(2, dp * seq, -1, TOP_K)
+        pickings = [routing(paths[n], first_expert, count) + (first_expert,) for n in range(2)]
+
     weights = []
-    pickings = []
     for number in range(2):
         part = by_layer(number, own_group, other_group)
         part = lax.all_to_all(part, "seq", split_axis=1, concat_axis=0, tiled=True)
@@ -1473,90 +1541,30 @@
                 small[number, EXPERTS + 1].astype(jnp.float32),
                 qkv_w,
                 out_w,
-                small[number, :EXPERTS].T,
+                small[number, :EXPERTS],
             )
         )
-        pickings.append(routing(paths[number], first_expert, count) + (first_expert,))
-
-    first_in = after(layer_in, other_gate).astype(jnp.float32)
-    updated, slot_out, first_saved, experts = forward_layer(
-        0, first_in, pickings[0], weights[0], experts, (None, own_experts[1])
-    )
-    sums, _ = token_sums(pickings[0][2], slot_out, 3)
-    first_out = updated + sums
-    second_updated, second_slots, second_saved, experts = forward_layer(
-        1, first_out, pickings[1], weights[1], experts
-    )
-    received = [[None] * 3, [None] * 3]
-    top_grad = top_grad.astype(jnp.float32)
-    slot_out, gate_term, second_experts, _ = expert_gradients(
-        1, top_grad, second_saved, pickings[1], experts
-    )
-    sums, (received[1][0],) = token_sums(pickings[1][2], slot_out, 6, (1, second_experts[0]))
-    middle_grad, second_dense, (received[1][1],) = backward_layer(
-        1, top_grad, sums, gate_term, second_saved, pickings[1], weights[1], (1, second_experts[1])
-    )
-    slot_out, gate_term, first_experts, (received[1][2],) = expert_gradients(
-        0, middle_grad, first_saved, pickings[0], experts, (1, second_experts[2])
-    )
-    sums, (received[0][0],) = token_sums(pickings[0][2], slot_out, 7, (0, first_experts[0]))
-    bottom_grad, first_dense, (received[0][1],) = backward_layer(
-        0, middle_grad, sums, gate_term, first_saved, pickings[0], weights[0], (0, first_experts[1])
-    )
-    second_slots = after(second_slots, received[0][1])
-    sums, (received[0][2],) = token_sums(
-        pickings[1][2], second_slots, 8, (0, first_experts[2])
-    )
-    layer_states = [first_out, second_updated + sums]
-    layer_grads = [bottom_grad, middle_grad]
-    dense_grads = [first_dense, second_dense]
-    expert_grads = [first_experts, second_experts]
+
+    def spread(dense):
+        qkv_part, out_part = dense
+        qkv_part = lax.psum_scatter(qkv_part, "dp", scatter_dimension=0, tiled=True)
+        qkv_part = qkv_part.reshape(seq, depth, -1)
+        qkv_part = lax.all_to_all(qkv_part, "seq", split_axis=0, concat_axis=0, tiled=True)
+        out_part = lax.psum_scatter(out_part, "dp", scatter_dimension=0, tiled=True)
+        return (qkv_part, lax.ppermute(out_part, TOKENS, from_group))
 
     def own_layer(pieces):
         return jnp.where(first, pieces[0], pieces[1])
 
-    def to_section(pieces):
-        other = own_layer([pass_to(pieces[number], number) for number in range(2)])
-        own = own_layer(pieces)
+    def both_micros(own, other):
         return jnp.stack([jnp.where(first, own, other), jnp.where(first, other, own)])[
             None, :, None
         ]
 
-    def summed(pieces):
-        other = own_layer([pass_to(pieces[number], number) for number in range(2)])
-        return own_layer(pieces).astype(jnp.float32) + other.astype(jnp.float32)
-
-    kv_width = KV_HEADS * HEAD_DIM // seq
-    q_width = GROUP * kv_width
-    qkv_width = q_width + 2 * kv_width
-    qkv_parts = []
-    out_parts = []
-    gain_parts = []
-    for number in range(2):
-        qkv_part, out_part, router_part, gain_part = dense_grads[number]
-        qkv_part = jnp.concatenate([qkv_part, router_part], axis=1)
-        qkv_part = lax.psum_scatter(qkv_part, "dp", scatter_dimension=0, tiled=True)
-        qkv_part = qkv_part.reshape(seq, depth, -1)
-        qkv_parts.append(
-            lax.all_to_all(qkv_part, "seq", split_axis=0, concat_axis=0, tiled=True)
-        )
-        out_part = lax.psum_scatter(out_part, "dp", scatter_dimension=0, tiled=True)
-        out_parts.append(lax.ppermute(out_part, TOKENS, from_group))
-        gain_part = gain_part.reshape(2, dp * seq, depth)
-        gain_part = lax.all_to_all(gain_part, TOKENS, split_axis=1, concat_axis=1, tiled=True)
-        gain_parts.append(jnp.sum(gain_part, axis=1))
-    qkv_sum = summed(qkv_parts)
-    out_sum = summed(out_parts)
-    gain_sum = summed(gain_parts)
-
-    def columns(begin, end):
-        return jnp.transpose(qkv_sum[:, :, begin:end], (1, 0, 2)).reshape(depth, -1)[None]
-
-    expert_sums = []
-    for kind in range(3):
-        own = own_layer([expert_grads[number][kind] for number in range(2)])
-        other = own_layer([received[number][kind] for number in range(2)])
-        piece = low(own.astype(jnp.float32) + other.astype(jnp.float32))
+    def summed(own, other):
+        return own_layer(own).astype(jnp.float32) + own_layer(other).astype(jnp.float32)
+
+    def rows_to_owners(piece, kind):
         rows = piece.shape[1] // seq
         if local >= seq:
             piece = piece.reshape(count, seq, rows, -1)
@@ -1572,17 +1580,81 @@
         else:
             rows = hidden_units // seq
             piece = whole_rows(piece.reshape(-1, rows, width), seq_index, seq // local, seq)
-        expert_sums.append(piece.astype(jnp.float32)[None])
+        return piece
+
+    first_in = after(layer_in, other_gate).astype(jnp.float32)
+    updated, slot_out, first_saved, experts, _ = forward_layer(
+        0, first_in, pickings[0], weights[0], experts, (None, own_experts[1])
+    )
+    sums, _ = token_sums(pickings[0][2], slot_out, 3)
+    first_out = updated + sums
+    second_updated, second_slots, second_saved, experts, (other_out,) = forward_layer(
+        1, first_out, pickings[1], weights[1], experts, (0, first_out)
+    )
+    top_grad = top_grad.astype(jnp.float32)
+    slot_out, gate_term, second_experts, _ = expert_gradients(
+        1, top_grad, second_saved, pickings[1], experts
+    )
+    sums, (second_gate,) = token_sums(pickings[1][2], slot_out, 6, (1, second_experts[0]))
+    middle_grad, second_dense, (second_up,) = backward_layer(
+        1, top_grad, sums, gate_term, second_saved, pickings[1], weights[1], (1, second_experts[1])
+    )
+    second_dense = spread(second_dense)
+    slot_out, gate_term, first_experts, (second_down,) = expert_gradients(
+        0, middle_grad, first_saved, pickings[0], experts, (1, second_experts[2])
+    )
+    sums, (first_gate, other_middle, *second_dense_in) = token_sums(
+        pickings[0][2],
+        slot_out,
+        7,
+        (0, first_experts[0]),
+        (1, middle_grad),
+        (1, second_dense[0]),
+        (1, second_dense[1]),
+    )
+    gate_sum = low(summed((first_experts[0], second_experts[0]), (first_gate, second_gate)))
+    gate_rows = rows_to_owners(gate_sum, 0)
+    bottom_grad, first_dense, (first_up,) = backward_layer(
+        0, middle_grad, sums, gate_term, first_saved, pickings[0], weights[0], (0, first_experts[1])
+    )
+    up_sum = low(summed((first_experts[1], second_experts[1]), (first_up, second_up)))
+    second_slots = after(second_slots, up_sum, gate_rows, *first_dense)
+    sums, (first_down, other_bottom) = token_sums(
+        pickings[1][2], second_slots, 8, (0, first_experts[2]), (0, bottom_grad)
+    )
+    up_rows = rows_to_owners(up_sum, 1)
+    second_out = second_updated + sums
+    down_sum = low(summed((first_experts[2], second_experts[2]), (first_down, second_down)))
+    expert_sums = [gate_rows, up_rows, rows_to_owners(down_sum, 2)]
+    expert_sums = [piece.astype(jnp.float32)[None] for piece in expert_sums]
+    own_out = own_layer((first_out, second_out))
+    layer_outs = both_micros(own_out, own_layer((other_out, pass_to(second_out, 1))))
+    own_grad = own_layer((bottom_grad, middle_grad))
+    section_grads = both_micros(own_grad, own_layer((other_bottom, other_middle)))
+    first_dense = spread(first_dense)
+    first_dense_in = [pass_to(piece, 0) for piece in first_dense]
+    qkv_sum, out_sum = [
+        summed((first_dense[k], second_dense[k]), (first_dense_in[k], second_dense_in[k]))
+        for k in range(2)
+    ]
+    kv_width = KV_HEADS * HEAD_DIM // seq
+    q_width = GROUP * kv_width
+    qkv_width = q_width + 2 * kv_width
+    small_sum = jnp.sum(qkv_sum[:, :, qkv_width:], axis=0)
+
+    def columns(begin, end):
+        return jnp.transpose(qkv_sum[:, :, begin:end], (1, 0, 2)).reshape(depth, -1)[None]
+
     return (
-        to_section(layer_states),
-        to_section(layer_grads),
-        gain_sum[0][None],
-        gain_sum[1][None],
+        layer_outs,
+        section_grads,
+        small_sum[:, EXPERTS][None],
+        small_sum[:, EXPERTS + 1][None],
         columns(0, q_width),
         columns(q_width, q_width + kv_width),
         columns(q_width + kv_width, qkv_width),
         out_sum[None],
-        jnp.sum(qkv_sum[:, :, qkv_width:], axis=0)[None],
+        small_sum[:, :EXPERTS][None],
         *expert_sums,
     )
 

time: 1550 us -> 1580 us (1.019)
  waiting for transfers between devices: 81.7 us -> 175 us
  starting transfers between devices: 98.3 us -> 65.5 us
  local copies, waits for them, and re-layouts: 82.1 us -> 58 us
    all_to_all x7 -> x5, waiting for transfers between devices: 10.6 us -> 87.8 us  [the longest x3 81.1 us: rows_to_owners(): lax.all_to_all(piece, 'seq', split_axis=0, concat_axis=0, tiled=True)]
    pallas_call x4, Pallas kernels: 457 us -> 408 us  [combine(): pl.pallas_call(kernel, out_shape=[jax.ShapeDtypeStruct((rows, width), jnp...]
    pallas_call x2, Pallas kernels: 166 us -> 208 us  [expert_backward(): pl.pallas_call(kernel, out_shape=[jax.ShapeDtypeStruct(*result) for resul...]
    ppermute x4 -> x3, waiting for transfers between devices: 16 us -> 54.9 us  [swap(): return lax.ppermute(block, 'section', [(0, 1), (1, 0)])]
    ppermute x10 -> x3, starting transfers between devices: 28.4 us -> 5.19 us  [pass_to(): return lax.ppermute(block, 'section', [(1 - section, section)])]
    ppermute x10 -> x3, waiting for transfers between devices: 23.1 us -> 0.01 us  [pass_to(): return lax.ppermute(block, 'section', [(1 - section, section)])]
    pallas_call x1, Pallas kernels: 14.9 us -> 35 us  [prepare(): pl.pallas_call(prepare_kernel, out_shape=[jax.ShapeDtypeStruct((2, 16, co...]
    convert_element_type x16 -> x13, other arithmetic: 32.2 us -> 26.7 us  [low(): return v.astype(jnp.bfloat16)]
  transfers between devices with their start and end apart: 36 -> 26, of which waited for: 10 -> 13; matrix products, arithmetic and copies ran while one was open for 11% -> 10% of each run, Pallas kernels for 46% -> 33%
where the time goes in v6:
time: 1580 us; the launch traced here: 1570 us
  Pallas kernels  1090 us (69%)
  waiting for transfers between devices  175 us (11%)
  other arithmetic  80.8 us (5%)
  matrix products  78.2 us (5%)
  starting transfers between devices  65.5 us (4%)
  local copies, waits for them, and re-layouts  58 us (4%)
    pallas_call x4, Pallas kernels, combine(): pl.pallas_call(kernel, out_shape=[jax.ShapeDtypeStruct((rows, width), jnp...  408 us
    pallas_call x2, Pallas kernels, expert_backward(): pl.pallas_call(kernel, out_shape=[jax.ShapeDtypeStruct(*result) for resul...  208 us
    pallas_call x2, Pallas kernels, expert_forward(): pl.pallas_call(kernel, out_shape=shapes, in_specs=[anywhere, near, near,...  172 us
    pallas_call x2, Pallas kernels, attention_backward_call(): pl.pallas_call(kernel, out_shape=[jax.ShapeDtypeStruct(*result) for resul...  145 us
    pallas_call x2, Pallas kernels, attention_forward_call(): pl.pallas_call(kernel, out_shape=[jax.ShapeDtypeStruct(*result) for resul...  127 us
    all_to_all x3, waiting for transfers between devices, rows_to_owners(): lax.all_to_all(piece, 'seq', split_axis=0, concat_axis=0, tiled=True)  81.1 us
    ppermute x3, waiting for transfers between devices, swap(): return lax.ppermute(block, 'section', [(0, 1), (1, 0)])  54.9 us
    dot_general x6, matrix products, each_dot(): return jnp.einsum(form, a, b, preferred_element_type=jnp.float32)  53.2 us
  transfers between devices with their start and end apart: 26, of which 13 were waited for; matrix products, arithmetic and copies ran while one was open for 10% of the time, Pallas kernels for 33%

profile of v6, /device:TPU:16, one launch (start us, length us, event | category | flops | bytes accessed | tf_op | source)
XLA Modules:
  0.0 1568.1 jit_solution(17759201034183316262)
XLA Ops:
  11.6 12.5 collective-permute-done.2
  27.6 6.1 collective-permute-done.3
  39.5 8.4 collective-permute-done
  61.8 35.0 %prepare.1 = (bf16[2,16,160,256]{3,2,1,0:T(8,128)(2,1)}, bf16[2,16,256,160]{3,2,1,0:T(8,128)(2,1)}, bf16[2,16,32,256]{3,2,1,0:T(8,128)(2,1)}, bf16[2,48,1536]{2,1,0:T(8,128)(2,1)}) custom-call(bf16[64,256]{1,0:T(8,128)(2,1)} %pad_maximum_fusion.4.x_ref), custom_call_target="tpu_custom_call" | custom-call | flops 20000000000 | bytes 10000000 | tf_op jit(solution)/shard_map/prepare/pallas_call | solution.py:408
  127.0 40.3 %collective-permute-done.1.refs_8_ = bf16[2,1536,512]{2,1,0:T(8,128)(2,1)} collective-permute-done((bf16[2,1536,512]{2,1,0:T(8,128)(2,1)}, bf16[2,1536,512]{2,1,0:T(8,128)(2,1)}, u32[]{:S(2)}, u32[]{:S(2)}) %collective-permute-start.1) | collective-permute-done | bytes 3145760 | tf_op jit(solution)/shard_map/ppermute | solution.py:39
  168.7 72.2 %attention_forward.2 = (f32[256,1536]{1,0:T(8,128)}, bf16[4,256,1536]{2,1,0:T(8,128)(2,1)}, bf16[10,1024,64]{2,1,0:T(8,128)(2,1)}, f32[8,1024]{1,0:T(8,128)}, bf...) custom-call(bf16[256,1536]{1,0:T(8,128)(2,1)} %fusion.4.refs_0_, ...), custom_call_target="tpu_custom_call" | custom-call | flops 80000000000 | bytes 100000000 | tf_op jit(solution)/shard_map/attention_forward/pallas_call | solution.py:1067
  245.1 89.7 %expert_forward.2 = (bf16[2,1280,1536]{2,1,0:T(8,128)(2,1)}, bf16[2,1280,512]{2,1,0:T(8,128)(2,1)}, bf16[2,1280,512]{2,1,0:T(8,128)(2,1)}, bf16[2,1280,512]{2,1,...) custom-call(bf16[256,1536]{1,0:T(8,128)(2,1)} %multiply_convert_fusion.2.ref, ...), custom_call_target="tpu_custom_call" | custom-call | flops 80000000000 | bytes 100000000 | tf_op jit(solution)/shard_map/expert_forward/pallas_call | solution.py:565
  334.8 98.4 %combine.4 = f32[256,1536]{1,0:T(8,128)} custom-call(bf16[16,256,160]{2,1,0:T(8,128)(2,1)} %get-tuple-element.227.refs_0_, bf16[16,160,1536]{2,1,0:T(8,128)(2,1)} %get-tuple-element.89.refs_1_), custom_call_target="tpu_custom_call" | custom-call | flops 80000000000 | bytes 100000000 | tf_op jit(solution)/shard_map/combine/pallas_call | solution.py:736
  437.2 54.7 %attention_forward.3 = (f32[256,1536]{1,0:T(8,128)}, bf16[4,256,1536]{2,1,0:T(8,128)(2,1)}, bf16[10,1024,64]{2,1,0:T(8,128)(2,1)}, f32[8,1024]{1,0:T(8,128)}, bf...) custom-call(bf16[256,1536]{1,0:T(8,128)(2,1)} %multiply_convert_fusion.1.refs_0_, ...), custom_call_target="tpu_custom_call" | custom-call | flops 80000000000 | bytes 100000000 | tf_op jit(solution)/shard_map/attention_forward/pallas_call | solution.py:1067
  499.2 82.1 %expert_forward.3 = (bf16[2,1280,1536]{2,1,0:T(8,128)(2,1)}, bf16[2,1280,512]{2,1,0:T(8,128)(2,1)}, bf16[2,1280,512]{2,1,0:T(8,128)(2,1)}, bf16[2,1280,512]{2,1,...) custom-call(bf16[256,1536]{1,0:T(8,128)(2,1)} %copy-done.18, ...), custom_call_target="tpu_custom_call" | custom-call | flops 80000000000 | bytes 100000000 | tf_op jit(solution)/shard_map/expert_forward/pallas_call | solution.py:565
  581.3 85.9 %expert_backward.2 = (bf16[2,1280,1536]{2,1,0:T(8,128)(2,1)}, bf16[2,1280,512]{2,1,0:T(8,128)(2,1)}, bf16[2,1280,512]{2,1,0:T(8,128)(2,1)}, f32[2,1280,128]{2,1,0:T(8,128)}, bf16[16,160,1536]{2,1,0:T(8,128)(2,1)}) custom-call(bf16[256,1536]{1,0:T(8,128)(2,1)} %dynamic-slice_bitcast_fusion.3.refs_0_, bf16[16,160,256]{2,1,0:T(8,128)(2,1)} %get-tuple-element.230.refs_1_, ...), custom_call_target="tpu_custom_call" | custom-call | flops 80000000000 | bytes 100000000 | tf_op jit(solution)/shard_map/expert_backward/pallas_call | solution.py:861
  670.4 7.6 all-to-all-start.2
  678.2 10.1 convolution_convert_fusion.5.refs_2_
  688.3 7.4 convolution_convert_fusion.4.refs_7_
  695.7 9.9 convolution_convert_fusion.3.refs_11_
  706.2 100.8 %combine.5 = (f32[256,1536]{1,0:T(8,128)}, bf16[2,1536,512]{2,1,0:T(8,128)(2,1)}) custom-call(bf16[16,256,160]{2,1,0:T(8,128)(2,1)} %get-tuple-element.226.refs_0_, bf16[16,160,1536]{2,1,0:T(8,128)(2,1)} %get-tuple-element.102.refs_1_, bf16[2,1536,512]{2,1,0:T(8,128)(2,1)} %convolution_convert_fusion.5.refs_2_), custom_call_target="tpu_custom_call" | custom-call | flops 80000000000 | bytes 100000000 | tf_op jit(solution)/shard_map/combine/pallas_call | solution.py:736
  810.9 72.4 %attention_backward.2 = (f32[256,1536]{1,0:T(8,128)}, bf16[4,256,1536]{2,1,0:T(8,128)(2,1)}, bf16[1024,640]{1,0:T(8,128)(2,1)}, bf16[2,1536,512]{2,1,0:T(8,128)(2,1)}) custom-call(bf16[256,1536]{1,0:T(8,128)(2,1)} %fusion.33.refs_0_, bf16[1536,640]{1,0:T(8,128)(2,1)} %all-gather.9.cloned.1.call-done.refs_1_, ...), custom_call_target="tpu_custom_call" | custom-call | flops 80000000000 | bytes 100000000 | tf_op jit(solution)/shard_map/attention_backward/pallas_call | solution.py:1193
  904.6 122.5 %expert_backward.3 = (bf16[2,1280,1536]{2,1,0:T(8,128)(2,1)}, bf16[2,1280,512]{2,1,0:T(8,128)(2,1)}, bf16[2,1280,512]{2,1,0:T(8,128)(2,1)}, f32[2,1280,128]{2,1,...) custom-call(bf16[256,1536]{1,0:T(8,128)(2,1)} %get-tuple-element.214.refs_0_, ...), custom_call_target="tpu_custom_call" | custom-call | flops 80000000000 | bytes 100000000 | tf_op jit(solution)/shard_map/expert_backward/pallas_call | solution.py:861
  1030.2 9.9 all-to-all-start.4
  1040.1 10.1 convolution_convert_fusion.2.refs_2_
  1050.2 10.1 convolution_convert_fusion.1.refs_7_
  1060.3 5.6 convolution_convert_fusion.refs_2_
  1073.9 9.0 collective-permute-done.4.refs_5_
  1087.4 101.9 %combine.6 = (f32[256,1536]{1,0:T(8,128)}, bf16[2,1536,512]{2,1,0:T(8,128)(2,1)}, f32[256,1536]{1,0:T(8,128)}, bf16[4,96,768]{2,1,0:T(8,128)(2,1)}, bf16[96,1536]{1,0:T(8,128)(2,1)}) custom-call(bf16[16,256,160]{2,1,0:T(8,128)(2,1)} %get-tuple-element.227.refs_0_, bf16[16,160,1536]{2,1,0:T(8,128)(2,1)} %get-tuple-element.121.refs_1_, ...), custom_call_target="tpu_custom_call" | custom-call | flops 80000000000 | bytes 100000000 | tf_op jit(solution)/shard_map/combine/pallas_call | solution.py:736
  1193.7 72.7 %attention_backward.3 = (f32[256,1536]{1,0:T(8,128)}, bf16[4,256,1536]{2,1,0:T(8,128)(2,1)}, bf16[1024,640]{1,0:T(8,128)(2,1)}, bf16[2,1536,512]{2,1,0:T(8,128)(2,1)}) custom-call(bf16[256,1536]{1,0:T(8,128)(2,1)} %get-tuple-element.212.refs_0_, bf16[1536,640]{1,0:T(8,128)(2,1)} %all-gather.5.cloned.1.call-done.refs_1_, ...), custom_call_target="tpu_custom_call" | custom-call | flops 80000000000 | bytes 100000000 | tf_op jit(solution)/shard_map/attention_backward/pallas_call | solution.py:1193
  1278.7 6.4 add_convert_fusion.2
  1290.4 106.5 %combine.7 = (f32[256,1536]{1,0:T(8,128)}, bf16[2,512,1536]{2,1,0:T(8,128)(2,1)}, f32[256,1536]{1,0:T(8,128)}) custom-call(bf16[16,256,160]{2,1,0:T(8,128)(2,1)} %get-tuple-element.226.refs_0_, bf16[16,160,1536]{2,1,0:T(8,128)(2,1)} %get-tuple-element.138.refs_1_, bf16[2,512,1536]{2,1,0:T(8,128)(2,1)} %convolution_convert_fusion.refs_2_, ...), custom_call_target="tpu_custom_call" | custom-call | flops 80000000000 | bytes 100000000 | tf_op jit(solution)/shard_map/combine/pallas_call | solution.py:736
  1412.6 32.5 %all-to-all-done.8 = bf16[4,2,128,1536]{3,2,1,0:T(8,128)(2,1)} async-done(((bf16[4,2,128,1536]{3,2,1,0:T(8,128)(2,1)}), bf16[4,2,128,1536]{3,2,1,0:T(8,128)(2,1)}, u32[]{:S(2)}, u32[]{:S(2)}) %all-to-all-start.8) | async-done | bytes 3145760 | tf_op jit(solution)/shard_map/all_to_all | solution.py:1572
  1454.1 32.9 %all-to-all-done.7 = bf16[4,2,384,512]{3,2,1,0:T(8,128)(2,1)} async-done(((bf16[4,2,384,512]{3,2,1,0:T(8,128)(2,1)}), bf16[4,2,384,512]{3,2,1,0:T(8,128)(2,1)}, u32[]{:S(2)}, u32[]{:S(2)}) %all-to-all-start.7) | async-done | bytes 3145760 | tf_op jit(solution)/shard_map/all_to_all | solution.py:1572
  1522.6 5.5 bitcast_convert_fusion.1
  1533.4 15.7 %all-to-all-done.6 = bf16[4,2,384,512]{3,2,1,0:T(8,128)(2,1)} async-done(((bf16[4,2,384,512]{3,2,1,0:T(8,128)(2,1)}), bf16[4,2,384,512]{3,2,1,0:T(8,128)(2,1)}, u32[]{:S(2)}, u32[]{:S(2)}) %all-to-all-start.6) | async-done | bytes 3145760 | tf_op jit(solution)/shard_map/all_to_all | solution.py:1572
  1549.1 5.5 bitcast_convert_fusion.2
  (335 shorter events, 211.9 us)
Async XLA Ops:
  7.2 161.5 %all-gather.7.cloned.1.call-start = ((), (), s32[]{:S(2)}) async-start(), calls=%async_computation.14 | async-start | bytes 1474560 | tf_op jit(solution)/shard_map/all_gather | solution.py:1535
  7.2 16.9 %collective-permute-start.2 = (bf16[96,1536]{1,0:T(8,128)(2,1)}, bf16[96,1536]{1,0:T(8,128)(2,1)S(1)}, u32[]{:S(2)}, u32[]{:S(2)}) collective-permute-start(bf16[96,1536]{1,0:T(8,128)(2,1)} %bitcast.181), channel_id=1, source_target_pairs={{0,0},{1,4},{2,8},{3,12},{4,1},{5,5},{6,9},{7,13},{8,2},{9,6},{10,... | collective-permute-start | bytes 884744 | tf_op jit(solution)/shard_map/ppermute | solution.py:1493
  24.1 9.6 collective-permute-start.3
  34.6 13.3 collective-permute-start
  49.0 11.9 all-to-all-start
  52.5 116.3 %all-gather.5.cloned.1.call-start = ((), (), s32[]{:S(2)}) async-start(), calls=%async_computation.13 | async-start | bytes 2457600 | tf_op jit(solution)/shard_map/all_gather | solution.py:1534
  61.7 375.5 %all-gather.11.cloned.1.call-start = ((), (), s32[]{:S(2)}) async-start(), calls=%async_computation.16 | async-start | bytes 1474560 | tf_op jit(solution)/shard_map/all_gather | solution.py:1535
  96.8 70.5 %collective-permute-start.1 = (bf16[2,1536,512]{2,1,0:T(8,128)(2,1)}, bf16[2,1536,512]{2,1,0:T(8,128)(2,1)}, u32[]{:S(2)}, u32[]{:S(2)}) collective-permute-start(bf16[2,1536,512]{2,1,0:T(8,128)(2,1)} %dynamic-slice_bitcast_fusion.2.refs_5_), channel_id=1, source_target_pairs={{0,16},{16,0},{1,17},{17,1},{2,18},{18,2},{3,19},{19,3},{4,20},{20... | collective-permute-start | bytes 9437192 | tf_op jit(solution)/shard_map/ppermute | solution.py:39
  100.0 141.0 %copy-start.11 = (bf16[256,1536]{1,0:T(8,128)(2,1)}, bf16[256,1536]{1,0:T(8,128)(2,1)S(1)}, u32[]{:S(2)}) copy-start(bf16[256,1536]{1,0:T(8,128)(2,1)S(1)} %dynamic-slice_bitcast_fusion.4) | copy-start | bytes 2359300
  104.5 138.2 %copy-start.49 = (f32[1536]{0:T(1024)}, f32[1536]{0:T(1024)S(1)}, u32[]{:S(2)}) copy-start(f32[1536]{0:T(1024)S(1)} %get-tuple-element.208) | copy-start | bytes 18436
  114.3 11.9 all-to-all-start.1
  117.7 319.5 %all-gather.9.cloned.1.call-start = ((), (), s32[]{:S(2)}) async-start(), calls=%async_computation.15 | async-start | bytes 2457600 | tf_op jit(solution)/shard_map/all_gather | solution.py:1534
  670.4 136.7 %all-to-all-start.2 = ((f32[16,2,256]{2,1,0:T(2,128)}), f32[16,2,256]{2,1,0:T(2,128)S(1)}, u32[]{:S(2)}, u32[]{:S(2)}) async-start(f32[16,2,256]{2,1,0:T(2,128)} %fusion.1), calls=%async_computation.2 | async-start | bytes 65536 | tf_op jit(solution)/shard_map/all_to_all | solution.py:1413
  678.0 388.1 %reduce-scatter.9.cloned.1.call-start = ((), (), s32[]{:S(2)}) async-start(), calls=%async_computation.17 | async-start | bytes 1474560 | tf_op jit(solution)/shard_map/reduce_scatter | solution.py:1553
  706.2 101.0 %copy-start.54 = (f32[256]{0:T(256)S(1)}, f32[256]{0:T(256)}, u32[]{:S(2)}) copy-start(f32[256]{0:T(256)} %copy-done.53) | copy-start | bytes 3076
  888.1 181.4 %reduce-scatter.13.cloned.1.call-start = ((), (), s32[]{:S(2)}) async-start(), calls=%async_computation.19 | async-start | bytes 2949120 | tf_op jit(solution)/shard_map/reduce_scatter | solution.py:1550
  1030.2 35.7 %all-to-all-start.4 = ((f32[16,2,256]{2,1,0:T(2,128)}), f32[16,2,256]{2,1,0:T(2,128)S(1)}, u32[]{:S(2)}, u32[]{:S(2)}) async-start(f32[16,2,256]{2,1,0:T(2,128)} %fusion), calls=%async_computation.5 | async-start | bytes 65536 | tf_op jit(solution)/shard_map/all_to_all | solution.py:1413
  1066.1 16.8 %collective-permute-start.4 = (bf16[96,1536]{1,0:T(8,128)(2,1)}, bf16[96,1536]{1,0:T(8,128)(2,1)S(1)}, u32[]{:S(2)}, u32[]{:S(2)}) collective-permute-start(bf16[96,1536]{1,0:T(8,128)(2,1)} %reduce-scatter.9.cloned.1.call-done), channel_id=1, source_target_pairs={{0,0},{4,1},{8,2},{12,3},{1,4},{5,5},{9,6},{13,7},{2,8},{6,9},{10,... | collective-permute-start | bytes 884744 | tf_op jit(solution)/shard_map/ppermute | solution.py:1554
  1069.5 17.1 %all-to-all-start.3 = ((bf16[4,96,768]{2,1,0:T(8,128)(2,1)}), bf16[4,96,768]{2,1,0:T(8,128)(2,1)S(1)}, u32[]{:S(2)}, u32[]{:S(2)}) async-start(bf16[4,96,768]{2,1,0:T(8,128)(2,1)} %bitcast.174), calls=%async_computation.3 | async-start | bytes 1179648 | tf_op jit(solution)/shard_map/all_to_all | solution.py:1552
  1087.4 101.9 %copy-start.10 = (f32[256,1536]{1,0:T(8,128)S(1)}, f32[256,1536]{1,0:T(8,128)}, u32[]{:S(2)}) copy-start(f32[256,1536]{1,0:T(8,128)} %copy-done.8) | copy-start | bytes 4718596
  1087.4 101.9 %copy-start.50 = (f32[1536]{0:T(1024)S(1)}, f32[1536]{0:T(1024)}, u32[]{:S(2)}) copy-start(f32[1536]{0:T(1024)} %copy-done.49) | copy-start | bytes 18436
  1087.4 102.0 %copy-start.56 = (f32[256]{0:T(256)S(1)}, f32[256]{0:T(256)}, u32[]{:S(2)}) copy-start(f32[256]{0:T(256)} %copy-done.55) | copy-start | bytes 3076
  1403.4 41.7 %all-to-all-start.8 = ((bf16[4,2,128,1536]{3,2,1,0:T(8,128)(2,1)}), bf16[4,2,128,1536]{3,2,1,0:T(8,128)(2,1)}, u32[]{:S(2)}, u32[]{:S(2)}) async-start(bf16[4,2,128,1536]{3,2,1,0:T(8,128)(2,1)} %bitcast.166), calls=%async_computation.10 | async-start | bytes 6291456 | tf_op jit(solution)/shard_map/all_to_all | solution.py:1572
  1408.1 78.9 %reduce-scatter.15.cloned.1.call-start = ((), (), s32[]{:S(2)}) async-start(), calls=%async_computation.20 | async-start | bytes 2949120 | tf_op jit(solution)/shard_map/reduce_scatter | solution.py:1550
  1445.1 41.9 %all-to-all-start.7 = ((bf16[4,2,384,512]{3,2,1,0:T(8,128)(2,1)}), bf16[4,2,384,512]{3,2,1,0:T(8,128)(2,1)}, u32[]{:S(2)}, u32[]{:S(2)}) async-start(bf16[4,2,384,512]{3,2,1,0:T(8,128)(2,1)} %bitcast.165), calls=%async_computation.9 | async-start | bytes 6291456 | tf_op jit(solution)/shard_map/all_to_all | solution.py:1572
  1450.0 63.4 %reduce-scatter.11.cloned.1.call-start = ((), (), s32[]{:S(2)}) async-start(), calls=%async_computation.18 | async-start | bytes 1474560 | tf_op jit(solution)/shard_map/reduce_scatter | solution.py:1553
  1451.4 54.4 %collective-permute-start.5 = (f32[256,1536]{1,0:T(8,128)}, f32[256,1536]{1,0:T(8,128)}, u32[]{:S(2)}, u32[]{:S(2)}) collective-permute-start(f32[256,1536]{1,0:T(8,128)} %add.155), channel_id=1, source_target_pairs={{0,16},{1,17},{2,18},{3,19},{4,20},{5,21},{6,22},{7,23},{8,24},{9,... | collective-permute-start | bytes 4718600 | tf_op jit(solution)/shard_map/ppermute | solution.py:43
  1487.0 13.0 all-to-all-start.5
  1500.8 48.3 %all-to-all-start.6 = ((bf16[4,2,384,512]{3,2,1,0:T(8,128)(2,1)}), bf16[4,2,384,512]{3,2,1,0:T(8,128)(2,1)}, u32[]{:S(2)}, u32[]{:S(2)}) async-start(bf16[4,2,384,512]{3,2,1,0:T(8,128)(2,1)} %bitcast.164), calls=%async_computation.8 | async-start | bytes 6291456 | tf_op jit(solution)/shard_map/all_to_all | solution.py:1572
  1513.4 17.4 %collective-permute-start.7 = (bf16[96,1536]{1,0:T(8,128)(2,1)}, bf16[96,1536]{1,0:T(8,128)(2,1)S(1)}, u32[]{:S(2)}, u32[]{:S(2)}) collective-permute-start(bf16[96,1536]{1,0:T(8,128)(2,1)} %reduce-scatter.11.cloned.1.call-done), channel_id=1, source_target_pairs={{0,0},{4,1},{8,2},{12,3},{1,4},{5,5},{9,6},{13,7},{2,8},{6,9},{10,... | collective-permute-start | bytes 884744 | tf_op jit(solution)/shard_map/ppermute | solution.py:1554
  1530.8 23.8 %collective-permute-start.8 = (bf16[96,1536]{1,0:T(8,128)(2,1)S(1)}, bf16[96,1536]{1,0:T(8,128)(2,1)S(1)}, u32[]{:S(2)}, u32[]{:S(2)}) collective-permute-start(bf16[96,1536]{1,0:T(8,128)(2,1)S(1)} %collective-permute-done.7), channel_id=1, source_target_pairs={{16,0},{17,1},{18,2},{19,3},{20,4},{21,5},{22,6},{23,7},{24,8},{25... | collective-permute-start | bytes 884744 | tf_op jit(solution)/shard_map/ppermute | solution.py:43
  1532.1 23.5 %collective-permute-start.6 = (bf16[4,96,768]{2,1,0:T(8,128)(2,1)S(1)}, bf16[4,96,768]{2,1,0:T(8,128)(2,1)S(1)}, u32[]{:S(2)}, u32[]{:S(2)}) collective-permute-start(bf16[4,96,768]{2,1,0:T(8,128)(2,1)S(1)} %copy-done.30), channel_id=1, source_target_pairs={{16,0},{17,1},{18,2},{19,3},{20,4},{21,5},{22,6},{23,7},{24,8},{25... | collective-permute-start | bytes 1769480 | tf_op jit(solution)/shard_map/ppermute | solution.py:43
  (81 other events, 1416.0 us)
Sparse Core Ops, SparseCore 0:
  34.7 30.7 all-gather.6
  67.1 42.3 all-gather.4
  111.1 29.5 all-gather.10
  142.7 42.3 all-gather.8
  888.2 34.6 reduce-scatter.8
  925.0 63.6 reduce-scatter.12
  1411.2 47.2 reduce-scatter.14
  1460.8 27.8 reduce-scatter.10

commit v7 on v6

--- a/solution.py
+++ b/solution.py
@@ -175,7 +175,7 @@
     )
 
 
-def greet(d, s, section=None):
+def greet(d, s, section=None, spread=False):
     barrier = pltpu.get_barrier_semaphore()
 
     def signal(**device):
@@ -196,6 +196,9 @@
     if section is not None:
         signal(section=1 - section)
         known = 4
+    if spread:
+        signal(seq=s ^ 3)
+        known = known + 1
     inner = (d > 0) & (d < 3)
 
     @pl.when(inner)
@@ -238,6 +241,26 @@
                 @pl.when(self.section == to)
                 def _():
                     copy.wait_recv()
+
+
+class Spread:
+    def __init__(self, source, target, sems):
+        s = lax.axis_index("seq")
+        self.local = pltpu.make_async_copy(source.at[s], target.at[s], sems.at[0, 0])
+        self.copies = [
+            remote(source.at[s ^ flip], target.at[s], sems.at[flip, 0], sems.at[flip, 1], seq=s ^ flip)
+            for flip in (3, 2, 1)
+        ]
+
+    def start(self):
+        for copy in self.copies:
+            copy.start()
+        self.local.start()
+
+    def finish(self):
+        self.local.wait()
+        for copy in self.copies:
+            copy.wait()
 
 
 def cost():
@@ -425,7 +448,6 @@
         compiler_params=pltpu.CompilerParams(
             collective_id=collective_id, has_side_effects=True, vmem_limit_bytes=60 << 20
         ),
-        cost_estimate=pl.CostEstimate(flops=20_000_000_000, bytes_accessed=10_000_000, transcendentals=0),
         name="prepare",
     )(x)
 
@@ -579,11 +601,16 @@
     )(*operands)
 
 
-def combine_kernel(sections, pick_ref, y_ref, *refs):
+def combine_kernel(sections, spreads, pick_ref, y_ref, *refs):
     kept = len(sections)
-    sources, out_ref, targets = refs[:kept], refs[kept], refs[kept + 1 : 2 * kept + 1]
-    y, sent, own, core_in, y_in, z_in, lsem, zs, zr, ys, yr, cs, cr, carry_sem = refs[2 * kept + 1 :]
+    sources, refs = refs[:kept], refs[kept:]
+    spread_sources, refs = refs[:spreads], refs[spreads:]
+    out_ref, *refs = refs
+    targets, refs = refs[:kept], refs[kept:]
+    spread_targets, refs = refs[:spreads], refs[spreads:]
+    y, sent, own, core_in, y_in, z_in, lsem, zs, zr, ys, yr, cs, cr, carry_sem, spread_sem = refs
     carried = Carried(sections, sources, targets, carry_sem)
+    spread = [Spread(a, b, spread_sem) for a, b in zip(spread_sources, spread_targets)]
     d, s = lax.axis_index("dp"), lax.axis_index("seq")
     half = out_ref.shape[0] // 2
 
@@ -598,7 +625,7 @@
         for across in (1, 0):
             for other_core in (1, 0):
                 loaded(z * 4 + column(across, other_core)).start()
-    greet(d, s, carried.section)
+    greet(d, s, carried.section, spreads > 0)
     carried.start()
 
     def rows(k):
@@ -647,6 +674,8 @@
         core_copy(z, k, 0).start()
 
     start(0)
+    for side in spread:
+        side.start()
 
     @pl.loop(0, 8)
     def _(i):
@@ -718,17 +747,21 @@
                 z_copy(z, k, True).wait_send()
 
     carried.finish()
-
-
-def combine(pick_t, y, collective_id, carry):
+    for side in spread:
+        side.finish()
+
+
+def combine(pick_t, y, collective_id, carry, spread=()):
     rows, width = pick_t.shape[1], y.shape[2]
     anywhere = pl.BlockSpec(memory_space=pl.ANY)
     near = pl.BlockSpec(memory_space=pltpu.VMEM)
     sections = tuple(to for to, _ in carry)
     arrays = [array for _, array in carry]
 
+    arrays = arrays + list(spread)
+
     def kernel(*refs):
-        combine_kernel(sections, *refs)
+        combine_kernel(sections, len(spread), *refs)
 
     def blocks(*lead):
         return pltpu.VMEM(lead + (rows, width), jnp.bfloat16)
@@ -754,6 +787,7 @@
             DMA((4, 2, 2)),
             DMA((4, 2, 2)),
             DMA((max(1, len(arrays)), 2)),
+            DMA((4, 2)),
         ],
         compiler_params=pltpu.CompilerParams(
             collective_id=collective_id, has_side_effects=True, vmem_limit_bytes=60 << 20
@@ -882,11 +916,14 @@
     return x * cos_table + turned * sin_table
 
 
-def seq_greet(s, section):
+def seq_greet(s, section, spread=False):
     barrier = pltpu.get_barrier_semaphore()
-    for device in (dict(seq=s ^ 1), dict(seq=s ^ 2), dict(section=1 - section)):
+    devices = [dict(seq=s ^ 1), dict(seq=s ^ 2), dict(section=1 - section)]
+    if spread:
+        devices.append(dict(seq=s ^ 3))
+    for device in devices:
         pl.semaphore_signal(barrier, inc=1, device_id=device, device_id_type=MESH)
-    pl.semaphore_wait(barrier, 3)
+    pl.semaphore_wait(barrier, len(devices))
 
 
 def seq_scratch(rows, width):
@@ -1090,12 +1127,17 @@
     )(x, qkv_w, out_w, *tables, *arrays)
 
 
-def attention_backward_kernel(sections, x_ref, qkv_ref, wo_ref, cos_ref, sin_ref, heads_in, lse_ref, *refs):
+def attention_backward_kernel(
+    sections, spreads, x_ref, qkv_ref, wo_ref, cos_ref, sin_ref, heads_in, lse_ref, *refs
+):
     kept = len(sections)
     sources, refs = refs[:kept], refs[kept:]
+    spread_sources, refs = refs[:spreads], refs[spreads:]
     out_ref, all_out, grads_out, *refs = refs
     targets, refs = refs[:kept], refs[kept:]
-    wqkv, wo, heads, douts, dk, dv, dqt, grads, partial, wsem, osem, carry_sem, *line = refs
+    spread_targets, refs = refs[:spreads], refs[spreads:]
+    wqkv, wo, heads, douts, dk, dv, dqt, grads, partial, wsem, osem, carry_sem, spread_sem, *line = refs
+    spread = [Spread(a, b, spread_sem) for a, b in zip(spread_sources, spread_targets)]
     line = Line(line)
     carried = Carried(sections, sources, targets, carry_sem)
     s = line.s
@@ -1109,7 +1151,7 @@
     ]
     for load in loads:
         load.start()
-    seq_greet(s, carried.section)
+    seq_greet(s, carried.section, spreads > 0)
     carried.start()
     dk[...] = jnp.zeros_like(dk)
     dv[...] = jnp.zeros_like(dv)
@@ -1128,6 +1170,8 @@
     line.gather(x_ref, project)
     saves = [pltpu.make_async_copy(line.land, all_out, osem.at[0])]
     saves[0].start()
+    for side in spread:
+        side.start()
     loads[1].wait()
     loads[2].wait()
 
@@ -1172,11 +1216,13 @@
     saves[1].start()
     line.finish(out_ref)
     carried.finish()
+    for side in spread:
+        side.finish()
     for save in saves:
         save.wait()
 
 
-def attention_backward_call(x, qkv_w, out_w, tables, heads, lse, collective_id, carry):
+def attention_backward_call(x, qkv_w, out_w, tables, heads, lse, collective_id, carry, spread=()):
     rows, width = x.shape
     bf, f32 = jnp.bfloat16, jnp.float32
     anywhere = pl.BlockSpec(memory_space=pl.ANY)
@@ -1187,8 +1233,10 @@
     kv = heads.shape[0] // (GROUP + 2)
     queries = GROUP * kv
 
+    arrays = arrays + list(spread)
+
     def kernel(*refs):
-        attention_backward_kernel(sections, *refs)
+        attention_backward_kernel(sections, len(spread), *refs)
 
     return pl.pallas_call(
         kernel,
@@ -1209,6 +1257,7 @@
             DMA((3,)),
             DMA((2,)),
             DMA((max(1, len(arrays)), 2)),
+            DMA((4, 2)),
         ]
         + seq_scratch(rows, width),
         compiler_params=pltpu.CompilerParams(
@@ -1217,6 +1266,93 @@
         cost_estimate=cost(),
         name="attention_backward",
     )(x, qkv_w, out_w, *tables, heads, lse, *arrays)
+
+
+def last_kernel(sections, down_ref, cols_ref, cols_other, out_ref, out_other, *refs):
+    kept = len(sections)
+    sources, refs = refs[:kept], refs[kept:]
+    down_out, cols_out, rows_out, *refs = refs
+    targets, refs = refs[:kept], refs[kept:]
+    cols_in, cols, out_in, out_sum, down_sem, cols_sem, row_sem, swap_sem, carry_sem = refs
+    d, s, section = lax.axis_index("dp"), lax.axis_index("seq"), lax.axis_index("section")
+    barrier = pltpu.get_barrier_semaphore()
+
+    def signal(**device):
+        pl.semaphore_signal(barrier, inc=1, device_id=device, device_id_type=MESH)
+
+    for flip in (1, 2, 3):
+        signal(seq=s ^ flip)
+    signal(section=1 - section)
+
+    @pl.when(d != s)
+    def _():
+        signal(dp=s, seq=d)
+        pl.semaphore_wait(barrier, 5)
+
+    @pl.when(d == s)
+    def _():
+        pl.semaphore_wait(barrier, 4)
+
+    swaps = Carried((None, None), (cols_other, out_other), (cols_in, out_in), swap_sem)
+    carried = Carried(sections, sources, targets, carry_sem)
+    down = Spread(down_ref, down_out, down_sem)
+    swaps.start()
+    down.start()
+    swaps.finish()
+    carried.start()
+    cols[...] = low(cols_ref[...].astype(jnp.float32) + cols_in[...].astype(jnp.float32))
+    out_sum[...] = low(out_ref[...].astype(jnp.float32) + out_in[...].astype(jnp.float32))
+    spread = Spread(cols, cols_out, cols_sem)
+    spread.start()
+    rows = remote(out_sum, rows_out, row_sem.at[0], row_sem.at[1], dp=s, seq=d)
+
+    @pl.when(d != s)
+    def _():
+        rows.start()
+        rows.wait()
+
+    @pl.when(d == s)
+    def _():
+        rows_out[...] = out_sum[...]
+
+    spread.finish()
+    down.finish()
+    carried.finish()
+
+
+def last_exchange(down, cols, cols_other, out, out_other, collective_id, carry):
+    bf = jnp.bfloat16
+    anywhere = pl.BlockSpec(memory_space=pl.ANY)
+    near = pl.BlockSpec(memory_space=pltpu.VMEM)
+    sections = tuple(to for to, _ in carry)
+    arrays = [array for _, array in carry]
+
+    def kernel(*refs):
+        last_kernel(sections, *refs)
+
+    return pl.pallas_call(
+        kernel,
+        out_shape=[
+            jax.ShapeDtypeStruct(array.shape, array.dtype) for array in (down, cols, out, *arrays)
+        ],
+        in_specs=[anywhere, near, anywhere, near, anywhere] + [anywhere] * len(arrays),
+        out_specs=[anywhere, near, near] + [anywhere] * len(arrays),
+        scratch_shapes=[
+            pltpu.VMEM(cols.shape, bf),
+            pltpu.VMEM(cols.shape, bf),
+            pltpu.VMEM(out.shape, bf),
+            pltpu.VMEM(out.shape, bf),
+            DMA((4, 2)),
+            DMA((4, 2)),
+            DMA((2,)),
+            DMA((2, 2)),
+            DMA((max(1, len(arrays)), 2)),
+        ],
+        compiler_params=pltpu.CompilerParams(
+            collective_id=collective_id, has_side_effects=True, vmem_limit_bytes=60 << 20
+        ),
+        name="last_exchange",
+    )(down, cols, cols_other, out, out_other, *arrays)
 
 
 def wide_tables(length):
@@ -1349,13 +1485,18 @@
     return (after_update, slot_out, saved, (own, other), received)
 
 
-def token_sums(pick_t, slot_out, collective_id, *carry):
+def token_sums(pick_t, slot_out, collective_id, *carry, spread=()):
     if has_kernels():
-        sums, *received = combine(pick_t, slot_out, collective_id, carry)
+        sums, *received = combine(pick_t, slot_out, collective_id, carry, spread)
         return sums, received
     sums = give_back(pick_t, slot_out).astype(jnp.float32)
     sums = lax.psum_scatter(sums, TOKENS, scatter_dimension=0, tiled=True)
-    return sums, [pass_to(array, to) for to, array in carry]
+    received = [pass_to(array, to) for to, array in carry]
+    return sums, received + [spread_rows(array) for array in spread]
+
+
+def spread_rows(parts):
+    return lax.all_to_all(parts, "seq", split_axis=0, concat_axis=0, tiled=True)
 
 
 def expert_gradients(number, layer_grad, saved, picking, experts, *carry):
@@ -1393,7 +1534,9 @@
     return slot_out, gate_term, expert_grads, received
 
 
-def backward_layer(number, layer_grad, normed_grad, gate_term, saved, picking, weights, *carry):
+def backward_layer(
+    number, layer_grad, normed_grad, gate_term, saved, picking, weights, *carry, spread=()
+):
     attn_scale, ffn_scale, qkv_w, out_w, router_w = weights
     chosen, pick, _, _ = picking
     (
@@ -1429,6 +1572,7 @@
             log_total,
             11 + number,
             carry,
+            spread,
         )
         branch_all = branch_all.reshape(-1, layer_in.shape[1])
     else:
@@ -1438,6 +1582,7 @@
         normed_attn = low(dot_t(qkv_grad, qkv_w))
         normed_attn = lax.psum_scatter(normed_attn, "seq", scatter_dimension=0, tiled=True)
         received = [pass_to(array, to) for to, array in carry]
+        received = received + [spread_rows(array) for array in spread]
     out_grad = dot(mixed_t, branch_all)
     qkv_weight_grad = t_dot(normed_all, qkv_grad)
     input_part, attn_gain_grad = jax.vjp(rms_norm, layer_in, attn_scale)[1](
@@ -1506,7 +1651,8 @@
         lax.dynamic_slice(w_up[0], (start, 0, unit_start), (count, width, units)),
         lax.dynamic_slice(w_down[0], (start, unit_start, 0), (count, units, width)),
     )
-    other_gate = swap(after(own_experts[0], other_group))
+    gate_slice, other_group = lax.optimization_barrier((own_experts[0], other_group))
+    other_gate = swap(gate_slice)
     experts = (own_experts, (other_gate,))
 
     small = jnp.concatenate([router_matrix[0].T, attn_gain, ffn_gain], axis=0)
@@ -1545,14 +1691,6 @@
             )
         )
 
-    def spread(dense):
-        qkv_part, out_part = dense
-        qkv_part = lax.psum_scatter(qkv_part, "dp", scatter_dimension=0, tiled=True)
-        qkv_part = qkv_part.reshape(seq, depth, -1)
-        qkv_part = lax.all_to_all(qkv_part, "seq", split_axis=0, concat_axis=0, tiled=True)
-        out_part = lax.psum_scatter(out_part, "dp", scatter_dimension=0, tiled=True)
-        return (qkv_part, lax.ppermute(out_part, TOKENS, from_group))
-
     def own_layer(pieces):
         return jnp.where(first, pieces[0], pieces[1])
 
@@ -1564,25 +1702,36 @@
     def summed(own, other):
         return own_layer(own).astype(jnp.float32) + own_layer(other).astype(jnp.float32)
 
-    def rows_to_owners(piece, kind):
-        rows = piece.shape[1] // seq
+    def dp_sums(dense):
+        return [lax.psum_scatter(part, "dp", scatter_dimension=0, tiled=True) for part in dense]
+
+    def row_parts(piece, kind):
         if local >= seq:
-            piece = piece.reshape(count, seq, rows, -1)
-            piece = jnp.transpose(piece, (1, 0, 2, 3))
-            piece = lax.all_to_all(piece, "seq", split_axis=0, concat_axis=0, tiled=True)
-            piece = piece.reshape(local, rows, -1)
-        elif kind < 2:
-            share = seq // local
-            piece = piece.reshape(seq, rows, units)
-            piece = lax.all_to_all(piece, "seq", split_axis=0, concat_axis=0, tiled=True)
-            piece = piece.reshape(local, share, rows, units)
-            piece = jnp.transpose(piece, (0, 2, 1, 3)).reshape(local, rows, -1)
-        else:
-            rows = hidden_units // seq
-            piece = whole_rows(piece.reshape(-1, rows, width), seq_index, seq // local, seq)
-        return piece
-
-    first_in = after(layer_in, other_gate).astype(jnp.float32)
+            piece = piece.reshape(count, seq, piece.shape[1] // seq, -1)
+            return jnp.transpose(piece, (1, 0, 2, 3))
+        if kind < 2:
+            return piece.reshape(seq, -1, units)
+        piece = piece.reshape(-1, hidden_units // seq, width)
+        share = seq // local
+        parts = jnp.zeros((seq,) + piece.shape[1:], piece.dtype)
+        return lax.dynamic_update_slice_in_dim(
+            parts, piece, (seq_index % share) * piece.shape[0], axis=0
+        )
+
+    def whole_rows(parts, kind):
+        parts = parts.astype(jnp.float32)
+        if local < seq:
+            parts = parts.reshape((local, seq // local) + parts.shape[1:])
+            if kind < 2:
+                parts = jnp.transpose(parts, (0, 2, 1, 3))
+            else:
+                parts = jnp.sum(parts, axis=1)
+            return parts.reshape((local,) + parts.shape[1 : 2] + (-1,))[None]
+        return parts.reshape((local,) + parts.shape[2:])[None]
+
+    layer_in, other_gate = lax.optimization_barrier((layer_in, other_gate))
+    experts = (own_experts, (other_gate,))
+    first_in = layer_in.astype(jnp.float32)
     updated, slot_out, first_saved, experts, _ = forward_layer(
         0, first_in, pickings[0], weights[0], experts, (None, own_experts[1])
     )
@@ -1599,44 +1748,68 @@
     middle_grad, second_dense, (second_up,) = backward_layer(
         1, top_grad, sums, gate_term, second_saved, pickings[1], weights[1], (1, second_experts[1])
     )
-    second_dense = spread(second_dense)
     slot_out, gate_term, first_experts, (second_down,) = expert_gradients(
         0, middle_grad, first_saved, pickings[0], experts, (1, second_experts[2])
     )
-    sums, (first_gate, other_middle, *second_dense_in) = token_sums(
-        pickings[0][2],
-        slot_out,
-        7,
-        (0, first_experts[0]),
-        (1, middle_grad),
-        (1, second_dense[0]),
-        (1, second_dense[1]),
-    )
+    sums, (first_gate, other_middle) = token_sums(
+        pickings[0][2], slot_out, 7, (0, first_experts[0]), (1, middle_grad)
+    )
+    sums, *second_dense = lax.optimization_barrier((sums, *second_dense))
+    second_dense = dp_sums(second_dense)
     gate_sum = low(summed((first_experts[0], second_experts[0]), (first_gate, second_gate)))
-    gate_rows = rows_to_owners(gate_sum, 0)
-    bottom_grad, first_dense, (first_up,) = backward_layer(
-        0, middle_grad, sums, gate_term, first_saved, pickings[0], weights[0], (0, first_experts[1])
+    bottom_grad, first_dense, (first_up, gate_rows) = backward_layer(
+        0,
+        middle_grad,
+        sums,
+        gate_term,
+        first_saved,
+        pickings[0],
+        weights[0],
+        (0, first_experts[1]),
+        spread=(row_parts(gate_sum, 0),),
     )
     up_sum = low(summed((first_experts[1], second_experts[1]), (first_up, second_up)))
-    second_slots = after(second_slots, up_sum, gate_rows, *first_dense)
-    sums, (first_down, other_bottom) = token_sums(
-        pickings[1][2], second_slots, 8, (0, first_experts[2]), (0, bottom_grad)
-    )
-    up_rows = rows_to_owners(up_sum, 1)
+    second_slots, *first_dense, second_dense[0], second_dense[1] = lax.optimization_barrier(
+        (second_slots, *first_dense, *second_dense)
+    )
+    first_dense = dp_sums(first_dense)
+    sums, (first_down, up_rows) = token_sums(
+        pickings[1][2],
+        second_slots,
+        8,
+        (0, first_experts[2]),
+        spread=(row_parts(up_sum, 1),),
+    )
+    sums, *first_dense = lax.optimization_barrier((sums, *first_dense))
     second_out = second_updated + sums
     down_sum = low(summed((first_experts[2], second_experts[2]), (first_down, second_down)))
-    expert_sums = [gate_rows, up_rows, rows_to_owners(down_sum, 2)]
-    expert_sums = [piece.astype(jnp.float32)[None] for piece in expert_sums]
-    own_out = own_layer((first_out, second_out))
-    layer_outs = both_micros(own_out, own_layer((other_out, pass_to(second_out, 1))))
-    own_grad = own_layer((bottom_grad, middle_grad))
-    section_grads = both_micros(own_grad, own_layer((other_bottom, other_middle)))
-    first_dense = spread(first_dense)
-    first_dense_in = [pass_to(piece, 0) for piece in first_dense]
-    qkv_sum, out_sum = [
-        summed((first_dense[k], second_dense[k]), (first_dense_in[k], second_dense_in[k]))
-        for k in range(2)
-    ]
+    own_cols, own_rows = [own_layer((first_dense[k], second_dense[k])) for k in range(2)]
+    other_cols, other_rows = [own_layer((second_dense[k], first_dense[k])) for k in range(2)]
+    if has_kernels():
+        down_rows, cols_sum, out_sum, other_second, other_bottom = last_exchange(
+            row_parts(down_sum, 2),
+            own_cols.reshape(seq, depth, -1),
+            other_cols.reshape(seq, depth, -1),
+            own_rows,
+            other_rows,
+            14,
+            ((1, second_out), (0, bottom_grad)),
+        )
+    else:
+        down_rows = spread_rows(row_parts(down_sum, 2))
+        cols_sum = low(own_cols.astype(jnp.float32) + swap(other_cols).astype(jnp.float32))
+        cols_sum = spread_rows(cols_sum.reshape(seq, depth, -1))
+        out_sum = low(own_rows.astype(jnp.float32) + swap(other_rows).astype(jnp.float32))
+        out_sum = lax.ppermute(out_sum, TOKENS, from_group)
+        other_second, other_bottom = pass_to(second_out, 1), pass_to(bottom_grad, 0)
+    expert_sums = [whole_rows(rows, k) for k, rows in enumerate((gate_rows, up_rows, down_rows))]
+    layer_outs = both_micros(
+        own_layer((first_out, second_out)), own_layer((other_out, other_second))
+    )
+    section_grads = both_micros(
+        own_layer((bottom_grad, middle_grad)), own_layer((other_bottom, other_middle))
+    )
+    qkv_sum, out_sum = cols_sum.astype(jnp.float32), out_sum.astype(jnp.float32)
     kv_width = KV_HEADS * HEAD_DIM // seq
     q_width = GROUP * kv_width
     qkv_width = q_width + 2 * kv_width
@@ -1657,17 +1830,6 @@
         small_sum[:, :EXPERTS][None],
         *expert_sums,
     )
-
-
-def whole_rows(piece, seq_index, share, seq):
-    parts = piece.shape[0]
-    spread = jnp.zeros((seq,) + piece.shape[1:], piece.dtype)
-    spread = lax.dynamic_update_slice_in_dim(
-        spread, piece, (seq_index % share) * parts, axis=0
-    )
-    spread = lax.all_to_all(spread, "seq", split_axis=0, concat_axis=0, tiled=True)
-    spread = spread.reshape((-1, share) + piece.shape[1:])
-    return jnp.sum(spread.astype(jnp.float32), axis=1).astype(piece.dtype)
 
 
 def solution(mesh):

time: 1580 us -> 1510 us (0.956)
  waiting for transfers between devices: 175 us -> 70.5 us
  Pallas kernels: 1090 us -> 1160 us
  starting transfers between devices: 65.5 us -> 24.6 us
    all_to_all x5 -> x0, waiting for transfers between devices: 87.8 us -> none  [the longest x3 81.1 us: rows_to_owners(): lax.all_to_all(piece, 'seq', split_axis=0, concat_axis=0, tiled=True)]
    pallas_call x0 -> x1, Pallas kernels: none -> 59.7 us  [last_exchange(): pl.pallas_call(kernel, out_shape=[jax.ShapeDtypeStruct(array.shape, array...]
    pallas_call x2, Pallas kernels: 208 us -> 166 us  [expert_backward(): pl.pallas_call(kernel, out_shape=[jax.ShapeDtypeStruct(*result) for resul...]
    pallas_call x4, Pallas kernels: 408 us -> 449 us  [combine(): pl.pallas_call(kernel, out_shape=[jax.ShapeDtypeStruct((rows, width), jnp...]
    all_to_all x5 -> x0, starting transfers between devices: 21.5 us -> none  [the longest x3 14.5 us: rows_to_owners(): lax.all_to_all(piece, 'seq', split_axis=0, concat_axis=0, tiled=True)]
  transfers between devices with their start and end apart: 26 -> 15, of which waited for: 13 -> 5; matrix products, arithmetic and copies ran while one was open for 10% -> 8% of each run, Pallas kernels for 33% -> 42%
where the time goes in v7:
time: 1510 us; the launch traced here: 1500 us
  Pallas kernels  1160 us (77%)
  matrix products  73 us (5%)
  other arithmetic  72.4 us (5%)
  waiting for transfers between devices  70.5 us (5%)
  local copies, waits for them, and re-layouts  69 us (5%)
  starting transfers between devices  24.6 us (2%)
  between operations  15.5 us (1%)
    pallas_call x4, Pallas kernels, combine(): pl.pallas_call(kernel, out_shape=[jax.ShapeDtypeStruct((rows, width), jnp...  449 us
    pallas_call x2, Pallas kernels, expert_forward(): pl.pallas_call(kernel, out_shape=shapes, in_specs=[anywhere, near, near,...  172 us
    pallas_call x2, Pallas kernels, expert_backward(): pl.pallas_call(kernel, out_shape=[jax.ShapeDtypeStruct(*result) for resul...  166 us
    pallas_call x2, Pallas kernels, attention_backward_call(): pl.pallas_call(kernel, out_shape=[jax.ShapeDtypeStruct(*result) for resul...  152 us
    pallas_call x2, Pallas kernels, attention_forward_call(): pl.pallas_call(kernel, out_shape=[jax.ShapeDtypeStruct(*result) for resul...  127 us
    pallas_call x1, Pallas kernels, last_exchange(): pl.pallas_call(kernel, out_shape=[jax.ShapeDtypeStruct(array.shape, array...  59.7 us
    dot_general x6, matrix products, each_dot(): return jnp.einsum(form, a, b, preferred_element_type=jnp.float32)  53.4 us
    ppermute x3, waiting for transfers between devices, swap(): return lax.ppermute(block, 'section', [(0, 1), (1, 0)])  53.2 us
  transfers between devices with their start and end apart: 15, of which 5 were waited for; matrix products, arithmetic and copies ran while one was open for 8% of the time, Pallas kernels for 42%

profile of v7, /device:TPU:16, one launch (start us, length us, event | category | flops | bytes accessed | tf_op | source)
XLA Modules:
  0.0 1496.6 jit_solution(2791082136352741884)
XLA Ops:
  10.6 13.6 collective-permute-done.2
  28.5 5.2 collective-permute-done.3
  40.1 8.0 collective-permute-done
  49.0 11.6 all_to_all.40
  61.3 34.5 %prepare.1 = (bf16[2,16,160,256]{3,2,1,0:T(8,128)(2,1)}, bf16[2,16,256,160]{3,2,1,0:T(8,128)(2,1)}, bf16[2,16,32,256]{3,2,1,0:T(8,128)(2,1)}, bf16[2,48,1536]{2,1,0:T(8,128)(2,1)}) custom-call(bf16[64,256]{1,0:T(8,128)(2,1)} %pad_maximum_fusion.4.x_ref), custom_call_target="tpu_custom_call" | custom-call | tf_op jit(solution)/shard_map/prepare/pallas_call | solution.py:431
  120.5 4.7 slice_bitcast_fusion
  129.6 40.0 %collective-permute-done.1.refs_8_ = bf16[2,1536,512]{2,1,0:T(8,128)(2,1)} collective-permute-done((bf16[2,1536,512]{2,1,0:T(8,128)(2,1)}, bf16[2,1536,512]{2,1,0:T(8,128)(2,1)}, u32[]{:S(2)}, u32[]{:S(2)}) %collective-permute-start.1) | collective-permute-done | bytes 3145760 | tf_op jit(solution)/shard_map/ppermute | solution.py:39
  171.0 72.3 %attention_forward.2 = (f32[256,1536]{1,0:T(8,128)}, bf16[4,256,1536]{2,1,0:T(8,128)(2,1)}, bf16[10,1024,64]{2,1,0:T(8,128)(2,1)}, f32[8,1024]{1,0:T(8,128)}, bf...) custom-call(bf16[256,1536]{1,0:T(8,128)(2,1)} %fusion.4.refs_0_, ...), custom_call_target="tpu_custom_call" | custom-call | flops 80000000000 | bytes 100000000 | tf_op jit(solution)/shard_map/attention_forward/pallas_call | solution.py:1104
  247.4 90.0 %expert_forward.2 = (bf16[2,1280,1536]{2,1,0:T(8,128)(2,1)}, bf16[2,1280,512]{2,1,0:T(8,128)(2,1)}, bf16[2,1280,512]{2,1,0:T(8,128)(2,1)}, bf16[2,1280,512]{2,1,...) custom-call(bf16[256,1536]{1,0:T(8,128)(2,1)} %multiply_convert_fusion.2.ref, ...), custom_call_target="tpu_custom_call" | custom-call | flops 80000000000 | bytes 100000000 | tf_op jit(solution)/shard_map/expert_forward/pallas_call | solution.py:587
  337.4 98.4 %combine.4 = f32[256,1536]{1,0:T(8,128)} custom-call(bf16[16,256,160]{2,1,0:T(8,128)(2,1)} %get-tuple-element.259.refs_0_, bf16[16,160,1536]{2,1,0:T(8,128)(2,1)} %get-tuple-element.107.refs_1_), custom_call_target="tpu_custom_call" | custom-call | flops 80000000000 | bytes 100000000 | tf_op jit(solution)/shard_map/combine/pallas_call | solution.py:769
  439.7 54.8 %attention_forward.3 = (f32[256,1536]{1,0:T(8,128)}, bf16[4,256,1536]{2,1,0:T(8,128)(2,1)}, bf16[10,1024,64]{2,1,0:T(8,128)(2,1)}, f32[8,1024]{1,0:T(8,128)}, bf...) custom-call(bf16[256,1536]{1,0:T(8,128)(2,1)} %multiply_convert_fusion.1.refs_0_, ...), custom_call_target="tpu_custom_call" | custom-call | flops 80000000000 | bytes 100000000 | tf_op jit(solution)/shard_map/attention_forward/pallas_call | solution.py:1104
  499.0 82.1 %expert_forward.3 = (bf16[2,1280,1536]{2,1,0:T(8,128)(2,1)}, bf16[2,1280,512]{2,1,0:T(8,128)(2,1)}, bf16[2,1280,512]{2,1,0:T(8,128)(2,1)}, bf16[2,1280,512]{2,1,...) custom-call(bf16[256,1536]{1,0:T(8,128)(2,1)} %multiply_convert_fusion.refs_0_, ...), custom_call_target="tpu_custom_call" | custom-call | flops 80000000000 | bytes 100000000 | tf_op jit(solution)/shard_map/expert_forward/pallas_call | solution.py:587
  581.0 86.2 %expert_backward.2 = (bf16[2,1280,1536]{2,1,0:T(8,128)(2,1)}, bf16[2,1280,512]{2,1,0:T(8,128)(2,1)}, bf16[2,1280,512]{2,1,0:T(8,128)(2,1)}, f32[2,1280,128]{2,1,0:T(8,128)}, bf16[16,160,1536]{2,1,0:T(8,128)(2,1)}) custom-call(bf16[256,1536]{1,0:T(8,128)(2,1)} %dynamic-slice_bitcast_fusion.3.refs_0_, bf16[16,160,256]{2,1,0:T(8,128)(2,1)} %get-tuple-element.262.refs_1_, ...), custom_call_target="tpu_custom_call" | custom-call | flops 80000000000 | bytes 100000000 | tf_op jit(solution)/shard_map/expert_backward/pallas_call | solution.py:895
  670.4 7.0 all-to-all-start.2
  677.7 10.1 convolution_convert_fusion.5.refs_2_
  687.7 7.6 convolution_convert_fusion.4.refs_7_
  695.3 9.0 convolution_convert_fusion.3.refs_11_
  705.4 100.9 %combine.5 = (f32[256,1536]{1,0:T(8,128)}, bf16[2,1536,512]{2,1,0:T(8,128)(2,1)}) custom-call(bf16[16,256,160]{2,1,0:T(8,128)(2,1)} %get-tuple-element.258.refs_0_, bf16[16,160,1536]{2,1,0:T(8,128)(2,1)} %get-tuple-element.121.refs_1_, bf16[2,1536,512]{2,1,0:T(8,128)(2,1)} %convolution_convert_fusion.5.refs_2_), custom_call_target="tpu_custom_call" | custom-call | flops 80000000000 | bytes 100000000 | tf_op jit(solution)/shard_map/combine/pallas_call | solution.py:769
  811.6 72.7 %attention_backward.2 = (f32[256,1536]{1,0:T(8,128)}, bf16[4,256,1536]{2,1,0:T(8,128)(2,1)}, bf16[1024,640]{1,0:T(8,128)(2,1)}, bf16[2,1536,512]{2,1,0:T(8,128)(2,1)}) custom-call(bf16[256,1536]{1,0:T(8,128)(2,1)} %fusion.32.refs_0_, bf16[1536,640]{1,0:T(8,128)(2,1)} %all-gather.9.cloned.1.call-done.refs_1_, ...), custom_call_target="tpu_custom_call" | custom-call | flops 80000000000 | bytes 100000000 | tf_op jit(solution)/shard_map/attention_backward/pallas_call | solution.py:1241
  890.1 79.4 %expert_backward.3 = (bf16[2,1280,1536]{2,1,0:T(8,128)(2,1)}, bf16[2,1280,512]{2,1,0:T(8,128)(2,1)}, bf16[2,1280,512]{2,1,0:T(8,128)(2,1)}, f32[2,1280,128]{2,1,...) custom-call(bf16[256,1536]{1,0:T(8,128)(2,1)} %get-tuple-element.246.refs_0_, ...), custom_call_target="tpu_custom_call" | custom-call | flops 80000000000 | bytes 100000000 | tf_op jit(solution)/shard_map/expert_backward/pallas_call | solution.py:895
  969.5 10.1 convolution_convert_fusion.2.refs_2_
  979.6 7.6 convolution_convert_fusion.1.refs_7_
  987.1 9.2 convolution_convert_fusion.refs_2_
  1004.1 98.5 %combine.6 = (f32[256,1536]{1,0:T(8,128)}, bf16[2,1536,512]{2,1,0:T(8,128)(2,1)}, f32[256,1536]{1,0:T(8,128)}) custom-call(bf16[16,256,160]{2,1,0:T(8,128)(2,1)} %get-tuple-element.259.refs_0_, bf16[16,160,1536]{2,1,0:T(8,128)(2,1)} %get-tuple-element.139.refs_1_, bf16[2,1536,512]{2,1,0:T(8,128)(2,1)} %convolution_convert_fusion.2.refs_2_, ...), custom_call_target="tpu_custom_call" | custom-call | flops 80000000000 | bytes 100000000 | tf_op jit(solution)/shard_map/combine/pallas_call | solution.py:769
  1110.4 6.3 all-to-all-start.3
  1116.7 4.6 add_convert_fusion.2
  1127.8 79.1 %attention_backward.3 = (f32[256,1536]{1,0:T(8,128)}, bf16[4,256,1536]{2,1,0:T(8,128)(2,1)}, bf16[1024,640]{1,0:T(8,128)(2,1)}, bf16[2,1536,512]{2,1,0:T(8,128)(2,1)}, bf16[4,2,384,512]{3,2,1,0:T(8,128)(2,1)}) custom-call(bf16[256,1536]{1,0:T(8,128)(2,1)} %get-tuple-element.244.refs_0_, bf16[1536,640]{1,0:T(8,128)(2,1)} %all-gather.5.cloned.1.call-done.refs_1_, ...), custom_call_target="tpu_custom_call" | custom-call | flops 80000000000 | bytes 100000000 | tf_op jit(solution)/shard_map/attention_backward/pallas_call | solution.py:1241
  1222.2 4.6 add_convert_fusion.1
  1231.5 151.5 %combine.7 = (f32[256,1536]{1,0:T(8,128)}, bf16[2,512,1536]{2,1,0:T(8,128)(2,1)}, bf16[4,2,384,512]{3,2,1,0:T(8,128)(2,1)}) custom-call(bf16[16,256,160]{2,1,0:T(8,128)(2,1)} %get-tuple-element.258.refs_0_, bf16[16,160,1536]{2,1,0:T(8,128)(2,1)} %get-tuple-element.159.refs_1_, bf16[2,512,1536]{2,1,0:T(8,128)(2,1)} %convolution_convert_fusion.refs_2_, ...), custom_call_target="tpu_custom_call" | custom-call | flops 80000000000 | bytes 100000000 | tf_op jit(solution)/shard_map/combine/pallas_call | solution.py:769
  1383.0 4.5 add_convert_fusion
  1391.5 6.5 bitcast_convert_fusion.1
  1405.4 59.7 %last_exchange.1 = (bf16[4,2,128,1536]{3,2,1,0:T(8,128)(2,1)}, bf16[4,96,768]{2,1,0:T(8,128)(2,1)}, bf16[96,1536]{1,0:T(8,128)(2,1)}, f32[256,1536]{1,0:T(8,128)}, f32[256,1536]{1,0:T(8,128)}) custom-call(bf16[4,2,128,1536]{3,2,1,0:T(8,128)(2,1)} %bitcast.164, bf16[4,96,768]{2,1,0:T(8,128)(2,1)} %bitcast.176, bf16[4,96,768]{2,1,0:T(8,128)(2,1)} %bitcast.175, ...), custom_call_target="tpu_custom_call" | custom-call | tf_op jit(solution)/shard_map/last_exchange/pallas_call | solution.py:1333
  (319 shorter events, 151.2 us)
Async XLA Ops:
  7.2 95.5 %copy-start = (bf16[2,1,256,1536]{3,2,1,0:T(8,128)(2,1)S(1)}, bf16[2,1,256,1536]{3,2,1,0:T(8,128)(2,1)}, u32[]{:S(2)}) copy-start(bf16[2,1,256,1536]{3,2,1,0:T(8,128)(2,1)} %param.13) | copy-start | bytes 4718596
  7.2 163.8 %all-gather.7.cloned.1.call-start = ((), (), s32[]{:S(2)}) async-start(), calls=%async_computation.9 | async-start | bytes 1474560 | tf_op jit(solution)/shard_map/all_gather | solution.py:1681
  7.2 16.9 %collective-permute-start.2 = (bf16[96,1536]{1,0:T(8,128)(2,1)}, bf16[96,1536]{1,0:T(8,128)(2,1)S(1)}, u32[]{:S(2)}, u32[]{:S(2)}) collective-permute-start(bf16[96,1536]{1,0:T(8,128)(2,1)} %bitcast.184), channel_id=1, source_target_pairs={{0,0},{1,4},{2,8},{3,12},{4,1},{5,5},{6,9},{7,13},{8,2},{9,6},{10,... | collective-permute-start | bytes 884744 | tf_op jit(solution)/shard_map/ppermute | solution.py:1638
  24.1 9.6 collective-permute-start.3
  34.6 136.4 %all-gather.5.cloned.1.call-start = ((), (), s32[]{:S(2)}) async-start(), calls=%async_computation.8 | async-start | bytes 2457600 | tf_op jit(solution)/shard_map/all_gather | solution.py:1680
  34.8 13.3 collective-permute-start
  60.6 379.1 %all-gather.11.cloned.1.call-start = ((), (), s32[]{:S(2)}) async-start(), calls=%async_computation.11 | async-start | bytes 1474560 | tf_op jit(solution)/shard_map/all_gather | solution.py:1681
  99.1 70.5 %collective-permute-start.1 = (bf16[2,1536,512]{2,1,0:T(8,128)(2,1)}, bf16[2,1536,512]{2,1,0:T(8,128)(2,1)}, u32[]{:S(2)}, u32[]{:S(2)}) collective-permute-start(bf16[2,1536,512]{2,1,0:T(8,128)(2,1)} %dynamic-slice_bitcast_fusion.2.refs_5_), channel_id=1, source_target_pairs={{0,16},{16,0},{1,17},{17,1},{2,18},{18,2},{3,19},{19,3},{4,20},{20... | collective-permute-start | bytes 9437192 | tf_op jit(solution)/shard_map/ppermute | solution.py:39
  102.7 140.7 %copy-start.11 = (bf16[256,1536]{1,0:T(8,128)(2,1)}, bf16[256,1536]{1,0:T(8,128)(2,1)S(1)}, u32[]{:S(2)}) copy-start(bf16[256,1536]{1,0:T(8,128)(2,1)S(1)} %dynamic-slice_bitcast_fusion.4) | copy-start | bytes 2359300
  107.1 138.0 %copy-start.49 = (f32[1536]{0:T(1024)}, f32[1536]{0:T(1024)S(1)}, u32[]{:S(2)}) copy-start(f32[1536]{0:T(1024)S(1)} %get-tuple-element.240) | copy-start | bytes 18436
  116.8 11.9 all-to-all-start.1
  120.3 319.4 %all-gather.9.cloned.1.call-start = ((), (), s32[]{:S(2)}) async-start(), calls=%async_computation.10 | async-start | bytes 2457600 | tf_op jit(solution)/shard_map/all_gather | solution.py:1680
  169.9 73.5 %copy-start.63 = (f32[256]{0:T(256)}, f32[256]{0:T(256)S(1)}, u32[]{:S(2)}) copy-start(f32[256]{0:T(256)S(1)} %fusion.10) | copy-start | bytes 3076
  169.9 73.5 %copy-start.61 = (f32[256]{0:T(256)}, f32[256]{0:T(256)S(1)}, u32[]{:S(2)}) copy-start(f32[256]{0:T(256)S(1)} %fusion.28) | copy-start | bytes 3076
  245.1 92.3 %copy-start.65 = (f32[256]{0:T(256)}, f32[256]{0:T(256)S(1)}, u32[]{:S(2)}) copy-start(f32[256]{0:T(256)S(1)} %get-tuple-element.252) | copy-start | bytes 3076
  337.4 98.4 %copy-start.9 = (f32[256,1536]{1,0:T(8,128)S(1)}, f32[256,1536]{1,0:T(8,128)}, u32[]{:S(2)}) copy-start(f32[256,1536]{1,0:T(8,128)} %copy-done.8) | copy-start | bytes 4718596
  670.4 136.0 %all-to-all-start.2 = ((f32[16,2,256]{2,1,0:T(2,128)}), f32[16,2,256]{2,1,0:T(2,128)S(1)}, u32[]{:S(2)}, u32[]{:S(2)}) async-start(f32[16,2,256]{2,1,0:T(2,128)} %fusion.1), calls=%async_computation.2 | async-start | bytes 65536 | tf_op jit(solution)/shard_map/all_to_all | solution.py:1556
  677.4 540.1 %reduce-scatter.13.cloned.1.call-start = ((), (), s32[]{:S(2)}) async-start(), calls=%async_computation.14 | async-start | bytes 2949120
  705.4 102.0 %copy-start.3 = (f32[256,1536]{1,0:T(8,128)S(1)}, f32[256,1536]{1,0:T(8,128)}, u32[]{:S(2)}) copy-start(f32[256,1536]{1,0:T(8,128)} %copy-done.2) | copy-start | bytes 4718596
  705.4 102.0 %copy-start.46 = (f32[1536]{0:T(1024)S(1)}, f32[1536]{0:T(1024)}, u32[]{:S(2)}) copy-start(f32[1536]{0:T(1024)} %get-tuple-element.238) | copy-start | bytes 18436
  705.4 102.0 %copy-start.54 = (f32[256]{0:T(256)S(1)}, f32[256]{0:T(256)}, u32[]{:S(2)}) copy-start(f32[256]{0:T(256)} %copy-done.53) | copy-start | bytes 3076
  811.6 72.8 %copy-start.6 = (f32[256,1536]{1,0:T(8,128)S(1)}, f32[256,1536]{1,0:T(8,128)}, u32[]{:S(2)}) copy-start(f32[256,1536]{1,0:T(8,128)} %copy-done.5) | copy-start | bytes 4718596
  811.6 72.8 %copy-start.52 = (f32[1536]{0:T(1024)S(1)}, f32[1536]{0:T(1024)}, u32[]{:S(2)}) copy-start(f32[1536]{0:T(1024)} %get-tuple-element.239) | copy-start | bytes 18436
  811.6 72.8 %copy-start.59 = (f32[256]{0:T(256)S(1)}, f32[256]{0:T(256)}, u32[]{:S(2)}) copy-start(f32[256]{0:T(256)} %copy-done.58) | copy-start | bytes 3076
  1110.4 13.2 all-to-all-start.3
  1116.7 103.0 %reduce-scatter.9.cloned.1.call-start = ((), (), s32[]{:S(2)}) async-start(), calls=%async_computation.12 | async-start | bytes 1474560 | tf_op jit(solution)/shard_map/reduce_scatter | solution.py:1706
  1123.3 274.7 %reduce-scatter.15.cloned.1.call-start = ((), (), s32[]{:S(2)}) async-start(), calls=%async_computation.15 | async-start | bytes 2949120
  1127.8 79.1 %copy-start.12 = (bf16[256,1536]{1,0:T(8,128)(2,1)S(1)}, bf16[256,1536]{1,0:T(8,128)(2,1)}, u32[]{:S(2)}) copy-start(bf16[256,1536]{1,0:T(8,128)(2,1)} %copy-done.11) | copy-start | bytes 2359300
  1127.8 79.1 %copy-start.48 = (f32[1536]{0:T(1024)S(1)}, f32[1536]{0:T(1024)}, u32[]{:S(2)}) copy-start(f32[1536]{0:T(1024)} %copy-done.47) | copy-start | bytes 18436
  1127.8 79.1 %copy-start.62 = (f32[256]{0:T(256)S(1)}, f32[256]{0:T(256)}, u32[]{:S(2)}) copy-start(f32[256]{0:T(256)} %copy-done.61) | copy-start | bytes 3076
  1222.1 177.3 %reduce-scatter.11.cloned.1.call-start = ((), (), s32[]{:S(2)}) async-start(), calls=%async_computation.13 | async-start | bytes 1474560 | tf_op jit(solution)/shard_map/reduce_scatter | solution.py:1706
  1231.5 151.5 %copy-start.30 = (bf16[2,512,1536]{2,1,0:T(8,128)(2,1)S(1)}, bf16[2,512,1536]{2,1,0:T(8,128)(2,1)}, u32[]{:S(2)}) copy-start(bf16[2,512,1536]{2,1,0:T(8,128)(2,1)} %convolution_convert_fusion.3.refs_11_) | copy-start | bytes 9437188
  (70 other events, 375.4 us)
Sparse Core Ops, SparseCore 0:
  34.7 30.7 all-gather.6
  67.1 42.5 all-gather.4
  111.3 29.5 all-gather.10
  142.3 42.3 all-gather.8
  1105.2 50.0 reduce-scatter.12
  1157.5 27.8 reduce-scatter.8
  1222.3 56.4 reduce-scatter.14
  1281.1 43.6 reduce-scatter.10

commit v8 on v7

--- a/solution.py
+++ b/solution.py
@@ -280,7 +280,7 @@
     ]
 
 
-def gather_blocks(x_ref, scratch, compute, carried=None, first=None):
+def gather_blocks(x_ref, scratch, compute, carried=None, first=None, spread=False):
     land, lsem, zs, zr, ys, yr, cs, cr = scratch
     d, s = lax.axis_index("dp"), lax.axis_index("seq")
 
@@ -298,7 +298,7 @@
         column = s ^ 2 if across else s
         return remote(src, place(z, column), cs.at[z, across], cr.at[z, across], seq=s ^ 1)
 
-    greet(d, s, None if carried is None else carried.section)
+    greet(d, s, None if carried is None else carried.section, spread)
     if first is not None:
         first()
     own = pltpu.make_async_copy(x_ref, place(d, s), lsem)
@@ -367,23 +367,70 @@
     return land
 
 
-def prepare_kernel(x_ref, pick_out, pick_t_out, chosen_out, small_out, both, places, lsem, carry_sem, *gather):
+def prepare_kernel(
+    x_ref, group_ref, gate_ref,
+    pick_out, pick_t_out, chosen_out, small_out, qkv_out, parts_out, gate_out,
+    both, places, groups, parts, lsem, carry_sem, spread_sem, qs, qr, *gather
+):
     d, s, section = lax.axis_index("dp"), lax.axis_index("seq"), lax.axis_index("section")
     known = x_ref.shape[0]
     count = pick_out.shape[2] // CAP
     rows = pick_out.shape[3]
     land = gather[0]
     part = both.at[pl.ds(pl.multiple_of(section * known, known), known)]
-    carried = Carried((None,), (x_ref,), (part,), carry_sem)
-
-    def swap_first():
-        carried.start()
-        own = pltpu.make_async_copy(x_ref, part, lsem)
-        own.start()
-        own.wait()
-        carried.finish()
-
-    gather_blocks(both, gather, lambda z: None, carried, swap_first)
+    swaps = Carried((None, None), (x_ref, group_ref), (part, groups.at[section]), carry_sem)
+    gates = Carried((None,), (gate_ref,), (gate_out,), carry_sem.at[pl.ds(2, 1)])
+    spreads = [Spread(groups.at[n], parts.at[n], spread_sem.at[n]) for n in range(2)]
+    own_columns = pltpu.make_async_copy(parts.at[0], qkv_out.at[d], lsem.at[2])
+
+    def along(src, z, right):
+        target = d + 1 if right else d - 1
+        return remote(src, qkv_out.at[z], qs.at[int(right), z], qr.at[z], dp=target)
+
+    def first():
+        swaps.start()
+        own = [
+            pltpu.make_async_copy(x_ref, part, lsem.at[0]),
+            pltpu.make_async_copy(group_ref, groups.at[section], lsem.at[1]),
+        ]
+        for copy in own:
+            copy.start()
+        for copy in own:
+            copy.wait()
+        swaps.finish()
+        gates.start()
+        for side in spreads:
+            side.start()
+        spreads[0].finish()
+        own_columns.start()
+
+        @pl.when(d < 3)
+        def _():
+            along(parts.at[0], d, True).start()
+
+        @pl.when(d > 0)
+        def _():
+            along(parts.at[0], d, False).start()
+
+    def hop(h):
+        @pl.when(d - h >= 0)
+        def _():
+            along(qkv_out.at[d - h], d - h, True).wait_recv()
+
+            @pl.when(d < 3)
+            def _():
+                along(qkv_out.at[d - h], d - h, True).start()
+
+        @pl.when(d + h <= 3)
+        def _():
+            along(qkv_out.at[d + h], d + h, False).wait_recv()
+
+            @pl.when(d > 0)
+            def _():
+                along(qkv_out.at[d + h], d + h, False).start()
+
+    gather_blocks(both, gather, lambda z: None, gates, first, True)
+    hop(1)
     first_expert = (d * 4 + s) * count
     before = lax.broadcasted_iota(jnp.int32, (rows, rows), 0)
     before = low(before < lax.broadcasted_iota(jnp.int32, (rows, rows), 1))
@@ -423,10 +470,33 @@
             small = land[b, pl.ds(pl.multiple_of(layer * known + 16, 16), known - 16), :]
             small_out[layer, :, b * depth : (b + 1) * depth] = small[:, :depth]
 
-
-def prepare(x, count, rows, depth, collective_id):
+        @pl.when(layer == 0)
+        def _():
+            hop(2)
+
+    hop(3)
+    spreads[1].finish()
+    layer_1 = pltpu.make_async_copy(parts.at[1], parts_out, lsem.at[0])
+    layer_1.start()
+    for z in range(4):
+
+        @pl.when((z <= d) & (d < 3))
+        def _():
+            along(parts.at[0], z, True).wait_send()
+
+        @pl.when((z >= d) & (d > 0))
+        def _():
+            along(parts.at[0], z, False).wait_send()
+
+    own_columns.wait()
+    layer_1.wait()
+    gates.finish()
+
+
+def prepare(x, group, gate, count, rows, depth, collective_id):
     known, width = x.shape
     bf = jnp.bfloat16
+    anywhere = pl.BlockSpec(memory_space=pl.ANY)
     near = pl.BlockSpec(memory_space=pltpu.VMEM)
     return pl.pallas_call(
         prepare_kernel,
@@ -435,21 +505,30 @@
             jax.ShapeDtypeStruct((2, 16, rows, count * CAP), bf),
             jax.ShapeDtypeStruct((2, 16, EXPERTS, rows), bf),
             jax.ShapeDtypeStruct((2, known - 16, 16 * depth), bf),
+            jax.ShapeDtypeStruct((4,) + group.shape, bf),
+            jax.ShapeDtypeStruct(group.shape, bf),
+            jax.ShapeDtypeStruct(gate.shape, bf),
         ],
-        in_specs=[pl.BlockSpec(memory_space=pl.ANY)],
-        out_specs=[near] * 4,
+        in_specs=[anywhere] * 3,
+        out_specs=[near] * 4 + [anywhere] * 3,
         scratch_shapes=[
             pltpu.VMEM((2 * known, width), bf),
             pltpu.VMEM((8, rows), jnp.float32),
-            DMA(()),
-            DMA((1, 2)),
+            pltpu.VMEM((2,) + group.shape, bf),
+            pltpu.VMEM((2,) + group.shape, bf),
+            DMA((3,)),
+            DMA((3, 2)),
+            DMA((2, 4, 2)),
+            DMA((2, 4)),
+            DMA((4,)),
         ]
         + gather_scratch(2 * known, width),
         compiler_params=pltpu.CompilerParams(
             collective_id=collective_id, has_side_effects=True, vmem_limit_bytes=60 << 20
         ),
+        cost_estimate=cost(),
         name="prepare",
-    )(x)
+    )(x, group, gate)
 
 
 def pick_weights(own_refs, other_refs, held, sems, own_layer):
@@ -1630,11 +1709,11 @@
         ],
         axis=2,
     )
+    own_group = jnp.transpose(own_group, (1, 0, 2))
     to_group = []
     for flat in range(dp * seq):
         to_group.append((flat, (flat % dp) * seq + flat // dp))
     from_group = [(target, source) for source, target in to_group]
-    other_group = swap(own_group)
     own_out = lax.ppermute(output_matrix[0], TOKENS, to_group)
     other_out = swap(own_out)
     local = w_gate.shape[1]
@@ -1651,19 +1730,25 @@
         lax.dynamic_slice(w_up[0], (start, 0, unit_start), (count, width, units)),
         lax.dynamic_slice(w_down[0], (start, unit_start, 0), (count, units, width)),
     )
-    gate_slice, other_group = lax.optimization_barrier((own_experts[0], other_group))
-    other_gate = swap(gate_slice)
-    experts = (own_experts, (other_gate,))
-
     small = jnp.concatenate([router_matrix[0].T, attn_gain, ffn_gain], axis=0)
     paths = routes[0, :, 0]
     if has_kernels():
         small = jnp.pad(small, ((0, -small.shape[0] % 16), (0, 256 - depth)))
         paths = low(jnp.transpose(paths, (0, 2, 1)).reshape(2 * TOP_K, -1))
-        picks, picks_t, chosens, small = prepare(
-            jnp.concatenate([paths, small], axis=0), count, hidden_in.shape[2], depth, 13
+        picks, picks_t, chosens, small, qkv_first, qkv_second, other_gate = prepare(
+            jnp.concatenate([paths, small], axis=0),
+            own_group,
+            own_experts[0],
+            count,
+            hidden_in.shape[2],
+            depth,
+            13,
         )
         pickings = [(chosens[n], picks[n], picks_t[n], first_expert) for n in range(2)]
+        qkv_second = lax.all_gather(
+            qkv_second.reshape(seq * depth, -1), "dp", axis=0, tiled=True
+        )
+        qkv_layers = [qkv_first.reshape(width, -1), qkv_second]
     else:
         small = lax.all_gather(small, ("section", "dp", "seq"), axis=0, tiled=False)
         small = jnp.transpose(small.reshape(2, dp * seq, -1, depth), (0, 2, 1, 3))
@@ -1672,12 +1757,16 @@
         paths = lax.dynamic_index_in_dim(paths, section, 1, keepdims=False)
         paths = paths.reshape(2, dp * seq, -1, TOP_K)
         pickings = [routing(paths[n], first_expert, count) + (first_expert,) for n in range(2)]
+        other_gate = swap(own_experts[0])
+        other_group = swap(own_group)
+        qkv_layers = []
+        for number in range(2):
+            part = spread_rows(by_layer(number, own_group, other_group))
+            part = part.reshape(seq * depth, -1)
+            qkv_layers.append(lax.all_gather(part, "dp", axis=0, tiled=True))
 
     weights = []
     for number in range(2):
-        part = by_layer(number, own_group, other_group)
-        part = lax.all_to_all(part, "seq", split_axis=1, concat_axis=0, tiled=True)
-        qkv_w = lax.all_gather(part.reshape(seq * depth, -1), "dp", axis=0, tiled=True)
         out_w = lax.all_gather(
             by_layer(number, own_out, other_out), "dp", axis=0, tiled=True
         )
@@ -1685,7 +1774,7 @@
             (
                 small[number, EXPERTS].astype(jnp.float32),
                 small[number, EXPERTS + 1].astype(jnp.float32),
-                qkv_w,
+                qkv_layers[number],
                 out_w,
                 small[number, :EXPERTS],
             )
@@ -1729,7 +1818,6 @@
             return parts.reshape((local,) + parts.shape[1 : 2] + (-1,))[None]
         return parts.reshape((local,) + parts.shape[2:])[None]
 
-    layer_in, other_gate = lax.optimization_barrier((layer_in, other_gate))
     experts = (own_experts, (other_gate,))
     first_in = layer_in.astype(jnp.float32)
     updated, slot_out, first_saved, experts, _ = forward_layer(

time: 1510 us -> 1480 us (0.980)
  Pallas kernels: 1160 us -> 1210 us
  waiting for transfers between devices: 70.5 us -> 21.8 us
    pallas_call x1, Pallas kernels: 34.5 us -> 87.4 us  [prepare(): pl.pallas_call(prepare_kernel, out_shape=[jax.ShapeDtypeStruct((2, 16, co...]
    ppermute x3 -> x1, waiting for transfers between devices: 53.2 us -> 8.09 us  [swap(): return lax.ppermute(block, 'section', [(0, 1), (1, 0)])]
  transfers between devices with their start and end apart: 15 -> 11, of which waited for: 5 -> 2; matrix products, arithmetic and copies ran while one was open for 8% -> 8% of each run, Pallas kernels for 42% -> 46%
where the time goes in v8:
time: 1480 us; the launch traced here: 1470 us
  Pallas kernels  1210 us (82%)
  matrix products  73.5 us (5%)
  other arithmetic  72.9 us (5%)
  local copies, waits for them, and re-layouts  62.1 us (4%)
  waiting for transfers between devices  21.8 us (1%)
  starting transfers between devices  18.9 us (1%)
  between operations  15.7 us (1%)
    pallas_call x4, Pallas kernels, combine(): pl.pallas_call(kernel, out_shape=[jax.ShapeDtypeStruct((rows, width), jnp...  446 us
    pallas_call x2, Pallas kernels, expert_forward(): pl.pallas_call(kernel, out_shape=shapes, in_specs=[anywhere, near, near,...  170 us
    pallas_call x2, Pallas kernels, expert_backward(): pl.pallas_call(kernel, out_shape=[jax.ShapeDtypeStruct(*result) for resul...  165 us
    pallas_call x2, Pallas kernels, attention_backward_call(): pl.pallas_call(kernel, out_shape=[jax.ShapeDtypeStruct(*result) for resul...  152 us
    pallas_call x2, Pallas kernels, attention_forward_call(): pl.pallas_call(kernel, out_shape=[jax.ShapeDtypeStruct(*result) for resul...  128 us
    pallas_call x1, Pallas kernels, prepare(): pl.pallas_call(prepare_kernel, out_shape=[jax.ShapeDtypeStruct((2, 16, co...  87.4 us
    pallas_call x1, Pallas kernels, last_exchange(): pl.pallas_call(kernel, out_shape=[jax.ShapeDtypeStruct(array.shape, array...  59.7 us
    dot_general x6, matrix products, each_dot(): return jnp.einsum(form, a, b, preferred_element_type=jnp.float32)  53.7 us
  transfers between devices with their start and end apart: 11, of which 2 were waited for; matrix products, arithmetic and copies ran while one was open for 8% of the time, Pallas kernels for 46%

profile of v8, /device:TPU:16, one launch (start us, length us, event | category | flops | bytes accessed | tf_op | source)
XLA Modules:
  0.0 1473.1 jit_solution(13979889118401463843)
XLA Ops:
  10.6 13.6 collective-permute-done
  25.6 8.1 collective-permute-done.1
  37.3 5.9 dynamic-slice_bitcast_fusion.1
  43.4 87.4 %prepare.1 = (bf16[2,16,160,256]{3,2,1,0:T(8,128)(2,1)}, bf16[2,16,256,160]{3,2,1,0:T(8,128)(2,1)}, bf16[2,16,32,256]{3,2,1,0:T(8,128)(2,1)}, bf16[2,48,1536]{2,...) custom-call(bf16[64,256]{1,0:T(8,128)(2,1)} %pad_maximum_fusion.4.x_r, ...), custom_call_target="tpu_custom_call" | custom-call | flops 80000000000 | bytes 100000000 | tf_op jit(solution)/shard_map/prepare/pallas_call | solution.py:501
  137.9 4.1 dynamic-slice_bitcast_fusion.refs_7_
  151.9 72.6 %attention_forward.2 = (f32[256,1536]{1,0:T(8,128)}, bf16[4,256,1536]{2,1,0:T(8,128)(2,1)}, bf16[10,1024,64]{2,1,0:T(8,128)(2,1)}, f32[8,1024]{1,0:T(8,128)}, bf...) custom-call(bf16[256,1536]{1,0:T(8,128)(2,1)} %fusion.4.refs_0_, bf16[1536,640]{1,0:T(8,128)(2,1)} %bitcast.190, ...), custom_call_target="tpu_custom_call" | custom-call | flops 80000000000 | bytes 100000000 | tf_op jit(solution)/shard_map/attention_forward/pallas_call | solution.py:1183
  228.5 86.7 %expert_forward.2 = (bf16[2,1280,1536]{2,1,0:T(8,128)(2,1)}, bf16[2,1280,512]{2,1,0:T(8,128)(2,1)}, bf16[2,1280,512]{2,1,0:T(8,128)(2,1)}, bf16[2,1280,512]{2,1,...) custom-call(bf16[256,1536]{1,0:T(8,128)(2,1)} %multiply_convert_fusion.2.ref, ...), custom_call_target="tpu_custom_call" | custom-call | flops 80000000000 | bytes 100000000 | tf_op jit(solution)/shard_map/expert_forward/pallas_call | solution.py:666
  315.3 99.2 %combine.4 = f32[256,1536]{1,0:T(8,128)} custom-call(bf16[16,256,160]{2,1,0:T(8,128)(2,1)} %get-tuple-element.257.refs_0_, bf16[16,160,1536]{2,1,0:T(8,128)(2,1)} %get-tuple-element.104.refs_1_), custom_call_target="tpu_custom_call" | custom-call | flops 80000000000 | bytes 100000000 | tf_op jit(solution)/shard_map/combine/pallas_call | solution.py:848
  418.3 54.9 %attention_forward.3 = (f32[256,1536]{1,0:T(8,128)}, bf16[4,256,1536]{2,1,0:T(8,128)(2,1)}, bf16[10,1024,64]{2,1,0:T(8,128)(2,1)}, f32[8,1024]{1,0:T(8,128)}, bf...) custom-call(bf16[256,1536]{1,0:T(8,128)(2,1)} %multiply_convert_fusion.1.refs_0_, ...), custom_call_target="tpu_custom_call" | custom-call | flops 80000000000 | bytes 100000000 | tf_op jit(solution)/shard_map/attention_forward/pallas_call | solution.py:1183
  477.7 83.5 %expert_forward.3 = (bf16[2,1280,1536]{2,1,0:T(8,128)(2,1)}, bf16[2,1280,512]{2,1,0:T(8,128)(2,1)}, bf16[2,1280,512]{2,1,0:T(8,128)(2,1)}, bf16[2,1280,512]{2,1,...) custom-call(bf16[256,1536]{1,0:T(8,128)(2,1)} %multiply_convert_fusion.refs_0_, ...), custom_call_target="tpu_custom_call" | custom-call | flops 80000000000 | bytes 100000000 | tf_op jit(solution)/shard_map/expert_forward/pallas_call | solution.py:666
  561.1 85.9 %expert_backward.2 = (bf16[2,1280,1536]{2,1,0:T(8,128)(2,1)}, bf16[2,1280,512]{2,1,0:T(8,128)(2,1)}, bf16[2,1280,512]{2,1,0:T(8,128)(2,1)}, f32[2,1280,128]{2,1,0:T(8,128)}, bf16[16,160,1536]{2,1,0:T(8,128)(2,1)}) custom-call(bf16[256,1536]{1,0:T(8,128)(2,1)} %dynamic-slice_bitcast_fusion.3.refs_0_, bf16[16,160,256]{2,1,0:T(8,128)(2,1)} %get-tuple-element.260.refs_1_, ...), custom_call_target="tpu_custom_call" | custom-call | flops 80000000000 | bytes 100000000 | tf_op jit(solution)/shard_map/expert_backward/pallas_call | solution.py:974
  650.1 6.9 all-to-all-start
  657.5 10.1 convolution_convert_fusion.5.refs_2_
  667.6 7.6 convolution_convert_fusion.4.refs_7_
  675.2 9.0 convolution_convert_fusion.3.refs_11_
  685.2 100.6 %combine.5 = (f32[256,1536]{1,0:T(8,128)}, bf16[2,1536,512]{2,1,0:T(8,128)(2,1)}) custom-call(bf16[16,256,160]{2,1,0:T(8,128)(2,1)} %get-tuple-element.256.refs_0_, bf16[16,160,1536]{2,1,0:T(8,128)(2,1)} %get-tuple-element.119.refs_1_, bf16[2,1536,512]{2,1,0:T(8,128)(2,1)} %convolution_convert_fusion.5.refs_2_), custom_call_target="tpu_custom_call" | custom-call | flops 80000000000 | bytes 100000000 | tf_op jit(solution)/shard_map/combine/pallas_call | solution.py:848
  791.1 72.8 %attention_backward.2 = (f32[256,1536]{1,0:T(8,128)}, bf16[4,256,1536]{2,1,0:T(8,128)(2,1)}, bf16[1024,640]{1,0:T(8,128)(2,1)}, bf16[2,1536,512]{2,1,0:T(8,128)(2,1)}) custom-call(bf16[256,1536]{1,0:T(8,128)(2,1)} %fusion.32.refs_0_, bf16[1536,640]{1,0:T(8,128)(2,1)} %all-gather.6.cloned.1.call-done.refs_1_, ...), custom_call_target="tpu_custom_call" | custom-call | flops 80000000000 | bytes 100000000 | tf_op jit(solution)/shard_map/attention_backward/pallas_call | solution.py:1320
  869.6 79.5 %expert_backward.3 = (bf16[2,1280,1536]{2,1,0:T(8,128)(2,1)}, bf16[2,1280,512]{2,1,0:T(8,128)(2,1)}, bf16[2,1280,512]{2,1,0:T(8,128)(2,1)}, f32[2,1280,128]{2,1,...) custom-call(bf16[256,1536]{1,0:T(8,128)(2,1)} %get-tuple-element.244.refs_0_, ...), custom_call_target="tpu_custom_call" | custom-call | flops 80000000000 | bytes 100000000 | tf_op jit(solution)/shard_map/expert_backward/pallas_call | solution.py:974
  949.1 10.1 convolution_convert_fusion.2.refs_2_
  959.2 7.6 convolution_convert_fusion.1.refs_7_
  966.8 9.4 convolution_convert_fusion.refs_2_
  984.0 98.4 %combine.6 = (f32[256,1536]{1,0:T(8,128)}, bf16[2,1536,512]{2,1,0:T(8,128)(2,1)}, f32[256,1536]{1,0:T(8,128)}) custom-call(bf16[16,256,160]{2,1,0:T(8,128)(2,1)} %get-tuple-element.257.refs_0_, bf16[16,160,1536]{2,1,0:T(8,128)(2,1)} %get-tuple-element.137.refs_1_, bf16[2,1536,512]{2,1,0:T(8,128)(2,1)} %convolution_convert_fusion.2.refs_2_, ...), custom_call_target="tpu_custom_call" | custom-call | flops 80000000000 | bytes 100000000 | tf_op jit(solution)/shard_map/combine/pallas_call | solution.py:848
  1089.0 6.3 all-to-all-start.1
  1095.3 4.6 add_convert_fusion.2
  1106.4 79.2 %attention_backward.3 = (f32[256,1536]{1,0:T(8,128)}, bf16[4,256,1536]{2,1,0:T(8,128)(2,1)}, bf16[1024,640]{1,0:T(8,128)(2,1)}, bf16[2,1536,512]{2,1,0:T(8,128)(2,1)}, bf16[4,2,384,512]{3,2,1,0:T(8,128)(2,1)}) custom-call(bf16[256,1536]{1,0:T(8,128)(2,1)} %get-tuple-element.242.refs_0_, bf16[1536,640]{1,0:T(8,128)(2,1)} %bitcast.191, ...), custom_call_target="tpu_custom_call" | custom-call | flops 80000000000 | bytes 100000000 | tf_op jit(solution)/shard_map/attention_backward/pallas_call | solution.py:1320
  1188.1 3.6 convolution_convert_fusion.6
  1198.5 4.3 copy.110
  1202.8 4.6 add_convert_fusion.1
  1215.7 148.0 %combine.7 = (f32[256,1536]{1,0:T(8,128)}, bf16[2,512,1536]{2,1,0:T(8,128)(2,1)}, bf16[4,2,384,512]{3,2,1,0:T(8,128)(2,1)}) custom-call(bf16[16,256,160]{2,1,0:T(8,128)(2,1)} %get-tuple-element.256.refs_0_, bf16[16,160,1536]{2,1,0:T(8,128)(2,1)} %get-tuple-element.157.refs_1_, bf16[2,512,1536]{2,1,0:T(8,128)(2,1)} %convolution_convert_fusion.refs_2_, ...), custom_call_target="tpu_custom_call" | custom-call | flops 80000000000 | bytes 100000000 | tf_op jit(solution)/shard_map/combine/pallas_call | solution.py:848
  1363.7 4.5 add_convert_fusion
  1382.2 59.7 %last_exchange.1 = (bf16[4,2,128,1536]{3,2,1,0:T(8,128)(2,1)}, bf16[4,96,768]{2,1,0:T(8,128)(2,1)}, bf16[96,1536]{1,0:T(8,128)(2,1)}, f32[256,1536]{1,0:T(8,128)}, f32[256,1536]{1,0:T(8,128)}) custom-call(bf16[4,2,128,1536]{3,2,1,0:T(8,128)(2,1)} %bitcast.166, bf16[4,96,768]{2,1,0:T(8,128)(2,1)} %bitcast.178, bf16[4,96,768]{2,1,0:T(8,128)(2,1)} %bitcast.177, ...), custom_call_target="tpu_custom_call" | custom-call | tf_op jit(solution)/shard_map/last_exchange/pallas_call | solution.py:1412
  1453.5 4.1 bitcast_convert_fusion
  (308 shorter events, 125.0 us)
Async XLA Ops:
  7.2 28.4 %copy-start.52 = (bf16[1,96,512]{2,1,0:T(8,128)(2,1)S(1)}, bf16[1,96,512]{2,1,0:T(8,128)(2,1)}, u32[]{:S(2)}) copy-start(bf16[1,96,512]{2,1,0:T(8,128)(2,1)} %param.19) | copy-start | bytes 294916
  7.2 28.5 %copy-start.41 = (bf16[1,96,1536]{2,1,0:T(8,128)(2,1)S(1)}, bf16[1,96,1536]{2,1,0:T(8,128)(2,1)}, u32[]{:S(2)}) copy-start(bf16[1,96,1536]{2,1,0:T(8,128)(2,1)} %param.17) | copy-start | bytes 884740
  7.2 144.7 %all-gather.4.cloned.1.call-start = ((), (), s32[]{:S(2)}) async-start(), calls=%async_computation.6 | async-start | bytes 1474560 | tf_op jit(solution)/shard_map/all_gather | solution.py:1770
  7.2 16.9 %collective-permute-start = (bf16[96,1536]{1,0:T(8,128)(2,1)}, bf16[96,1536]{1,0:T(8,128)(2,1)S(1)}, u32[]{:S(2)}, u32[]{:S(2)}) collective-permute-start(bf16[96,1536]{1,0:T(8,128)(2,1)} %bitcast.185), channel_id=1, source_target_pairs={{0,0},{1,4},{2,8},{3,12},{4,1},{5,5},{6,9},{7,13},{8,2},{9,6},{10,... | collective-permute-start | bytes 884744 | tf_op jit(solution)/shard_map/ppermute | solution.py:1717
  24.1 9.6 collective-permute-start.1
  25.6 10.2 copy-start.74
  25.6 10.2 copy-start.75
  25.6 10.2 copy-start.60
  34.6 383.7 %all-gather.8.cloned.1.call-start = ((), (), s32[]{:S(2)}) async-start(), calls=%async_computation.8 | async-start | bytes 1474560 | tf_op jit(solution)/shard_map/all_gather | solution.py:1770
  43.3 375.0 %all-gather.6.cloned.1.call-start = ((), (), s32[]{:S(2)}) async-start(), calls=%async_computation.7 | async-start | bytes 2457600 | tf_op jit(solution)/shard_map/all_gather | solution.py:1748
  43.4 91.3 %copy-start.15 = (bf16[2,1,256,1536]{3,2,1,0:T(8,128)(2,1)S(1)}, bf16[2,1,256,1536]{3,2,1,0:T(8,128)(2,1)}, u32[]{:S(2)}) copy-start(bf16[2,1,256,1536]{3,2,1,0:T(8,128)(2,1)} %param.13) | copy-start | bytes 4718596
  132.4 16.5 %copy-start.46 = (f32[1536]{0:T(1024)}, f32[1536]{0:T(1024)S(1)}, u32[]{:S(2)}) copy-start(f32[1536]{0:T(1024)S(1)} %get-tuple-element.239) | copy-start | bytes 18436
  132.4 93.9 %copy-start.48 = (f32[1536]{0:T(1024)}, f32[1536]{0:T(1024)S(1)}, u32[]{:S(2)}) copy-start(f32[1536]{0:T(1024)S(1)} %get-tuple-element.238) | copy-start | bytes 18436
  135.0 13.9 copy-start.61
  226.2 89.0 %copy-start.65 = (f32[256]{0:T(256)}, f32[256]{0:T(256)S(1)}, u32[]{:S(2)}) copy-start(f32[256]{0:T(256)S(1)} %get-tuple-element.250) | copy-start | bytes 3076
  315.3 99.2 %copy-start.7 = (f32[256,1536]{1,0:T(8,128)S(1)}, f32[256,1536]{1,0:T(8,128)}, u32[]{:S(2)}) copy-start(f32[256,1536]{1,0:T(8,128)} %copy-done.6) | copy-start | bytes 4718596
  650.1 135.7 %all-to-all-start = ((f32[16,2,256]{2,1,0:T(2,128)}), f32[16,2,256]{2,1,0:T(2,128)S(1)}, u32[]{:S(2)}, u32[]{:S(2)}) async-start(f32[16,2,256]{2,1,0:T(2,128)} %fusion.1), calls=%async_computation | async-start | bytes 65536 | tf_op jit(solution)/shard_map/all_to_all | solution.py:1635
  657.1 540.0 %reduce-scatter.13.cloned.1.call-start = ((), (), s32[]{:S(2)}) async-start(), calls=%async_computation.11 | async-start | bytes 2949120
  685.2 101.6 %copy-start.4 = (f32[256,1536]{1,0:T(8,128)S(1)}, f32[256,1536]{1,0:T(8,128)}, u32[]{:S(2)}) copy-start(f32[256,1536]{1,0:T(8,128)} %copy-done.3) | copy-start | bytes 4718596
  685.2 101.6 %copy-start.45 = (f32[1536]{0:T(1024)S(1)}, f32[1536]{0:T(1024)}, u32[]{:S(2)}) copy-start(f32[1536]{0:T(1024)} %get-tuple-element.236) | copy-start | bytes 18436
  685.2 101.6 %copy-start.54 = (f32[256]{0:T(256)S(1)}, f32[256]{0:T(256)}, u32[]{:S(2)}) copy-start(f32[256]{0:T(256)} %copy-done.53) | copy-start | bytes 3076
  791.1 72.8 %copy-start.1 = (f32[256,1536]{1,0:T(8,128)S(1)}, f32[256,1536]{1,0:T(8,128)}, u32[]{:S(2)}) copy-start(f32[256,1536]{1,0:T(8,128)} %copy-done) | copy-start | bytes 4718596
  791.1 72.8 %copy-start.51 = (f32[1536]{0:T(1024)S(1)}, f32[1536]{0:T(1024)}, u32[]{:S(2)}) copy-start(f32[1536]{0:T(1024)} %get-tuple-element.237) | copy-start | bytes 18436
  791.1 72.8 %copy-start.59 = (f32[256]{0:T(256)S(1)}, f32[256]{0:T(256)}, u32[]{:S(2)}) copy-start(f32[256]{0:T(256)} %copy-done.58) | copy-start | bytes 3076
  1089.0 13.2 all-to-all-start.1
  1095.2 103.3 %reduce-scatter.9.cloned.1.call-start = ((), (), s32[]{:S(2)}) async-start(), calls=%async_computation.9 | async-start | bytes 1474560 | tf_op jit(solution)/shard_map/reduce_scatter | solution.py:1795
  1101.9 273.0 %reduce-scatter.15.cloned.1.call-start = ((), (), s32[]{:S(2)}) async-start(), calls=%async_computation.12 | async-start | bytes 2949120
  1106.4 79.2 %copy-start.16 = (bf16[2,1,256,1536]{3,2,1,0:T(8,128)(2,1)S(1)}, bf16[2,1,256,1536]{3,2,1,0:T(8,128)(2,1)}, u32[]{:S(2)}) copy-start(bf16[2,1,256,1536]{3,2,1,0:T(8,128)(2,1)} %param.13) | copy-start | bytes 4718596
  1106.4 79.2 %copy-start.47 = (f32[1536]{0:T(1024)S(1)}, f32[1536]{0:T(1024)}, u32[]{:S(2)}) copy-start(f32[1536]{0:T(1024)} %copy-done.46) | copy-start | bytes 18436
  1106.4 79.2 %copy-start.62 = (f32[256]{0:T(256)S(1)}, f32[256]{0:T(256)}, u32[]{:S(2)}) copy-start(f32[256]{0:T(256)} %copy-done.61) | copy-start | bytes 3076
  1202.8 173.5 %reduce-scatter.11.cloned.1.call-start = ((), (), s32[]{:S(2)}) async-start(), calls=%async_computation.10 | async-start | bytes 1474560 | tf_op jit(solution)/shard_map/reduce_scatter | solution.py:1795
  1215.7 148.0 %copy-start.27 = (bf16[2,512,1536]{2,1,0:T(8,128)(2,1)S(1)}, bf16[2,512,1536]{2,1,0:T(8,128)(2,1)}, u32[]{:S(2)}) copy-start(bf16[2,512,1536]{2,1,0:T(8,128)(2,1)} %convolution_convert_fusion.3.refs_11_) | copy-start | bytes 9437188
  (66 other events, 236.1 us)
Sparse Core Ops, SparseCore 0:
  34.7 28.6 all-gather.3
  65.0 33.5 all-gather.7
  130.9 42.0 all-gather.5
  1085.0 50.0 reduce-scatter.12
  1137.3 27.9 reduce-scatter.8
  1202.9 56.4 reduce-scatter.14
  1261.8 39.9 reduce-scatter.10

commit v9 on v8

--- a/solution.py
+++ b/solution.py
@@ -379,7 +379,7 @@
     land = gather[0]
     part = both.at[pl.ds(pl.multiple_of(section * known, known), known)]
     swaps = Carried((None, None), (x_ref, group_ref), (part, groups.at[section]), carry_sem)
-    gates = Carried((None,), (gate_ref,), (gate_out,), carry_sem.at[pl.ds(2, 1)])
+    gates = Carried((None,), (share(gate_ref),), (gate_out,), carry_sem.at[pl.ds(2, 1)])
     spreads = [Spread(groups.at[n], parts.at[n], spread_sem.at[n]) for n in range(2)]
     own_columns = pltpu.make_async_copy(parts.at[0], qkv_out.at[d], lsem.at[2])
 
@@ -507,7 +507,7 @@
             jax.ShapeDtypeStruct((2, known - 16, 16 * depth), bf),
             jax.ShapeDtypeStruct((4,) + group.shape, bf),
             jax.ShapeDtypeStruct(group.shape, bf),
-            jax.ShapeDtypeStruct(gate.shape, bf),
+            jax.ShapeDtypeStruct(share_shape(gate), bf),
         ],
         in_specs=[anywhere] * 3,
         out_specs=[near] * 4 + [anywhere] * 3,
@@ -531,7 +531,17 @@
     )(x, group, gate)
 
 
+def share(ref):
+    count = ref.shape[0] // 4
+    return ref.at[pl.ds(lax.axis_index("seq") * count, count)]
+
+
+def share_shape(array):
+    return (array.shape[0] // 4,) + array.shape[1:]
+
+
 def pick_weights(own_refs, other_refs, held, sems, own_layer):
+    own_refs = [share(ref) for ref in own_refs]
     mine = lax.axis_index("section") == own_layer
 
     @pl.when(mine)
@@ -559,7 +569,7 @@
     count = wg.shape[0]
     carried = None
     if layer == 0:
-        carried = Carried((None,), (wd_own,), (wd_other,), carry_sem)
+        carried = Carried((None,), (share(wd_own),), (wd_other,), carry_sem)
         ready = pick_weights((wg_own, wu_own), (wg_other, wu_other), (wg, wu), wsem, layer)
     else:
         ready = pick_weights(
@@ -638,7 +648,7 @@
 
 
 def expert_forward(layer, x, pick, chosen, router, mine, own, other, collective_id):
-    count, width, units = own[0].shape
+    count, width, units = share_shape(own[0])
     rows = x.shape[0]
     slots = 16 * CAP
     bf = jnp.bfloat16
@@ -660,7 +670,7 @@
 
     shapes = [jax.ShapeDtypeStruct(*result) for result in results]
     if layer == 0:
-        shapes.append(jax.ShapeDtypeStruct(own[2].shape, bf))
+        shapes.append(jax.ShapeDtypeStruct(share_shape(own[2]), bf))
         other = other[:2]
     operands = (x, pick, chosen, router, mine, *own, *other)
     return pl.pallas_call(
@@ -668,7 +678,7 @@
         out_shape=shapes,
         in_specs=[anywhere, near, near, near, near] + [anywhere] * (len(operands) - 5),
         out_specs=[anywhere] * len(shapes),
-        scratch_shapes=[pltpu.VMEM(weight.shape, bf) for weight in own]
+        scratch_shapes=[pltpu.VMEM(share_shape(weight), bf) for weight in own]
         + [pltpu.VMEM(*result) for result in results]
         + [DMA((3,)), DMA((6, 4)), DMA((1, 2))]
         + gather_scratch(rows, width),
@@ -680,14 +690,76 @@
     )(*operands)
 
 
-def combine_kernel(sections, spreads, pick_ref, y_ref, *refs):
+class Products:
+    def __init__(self, pairs, outs, held, sems):
+        self.units = []
+        count = outs[0].shape[0]
+        for j in range(count):
+            at, out_at = 0, 0
+            for left, rights in pairs:
+                first = at
+                loads = [(left, at)] + [(right, at + 1 + k) for k, right in enumerate(rights)]
+                at += len(loads)
+                for k in range(len(rights)):
+                    self.units.append((j, first, first + 1 + k, out_at, loads, k == 0, k + 1 == len(rights)))
+                    out_at += 1
+        self.count, self.pairs, self.outs, self.held, self.sems = count, at, outs, held, sems
+
+    def load(self, j, source, at):
+        return pltpu.make_async_copy(source.at[j], self.held[at], self.sems.at[at])
+
+    def store(self, j, k):
+        at = self.pairs + k
+        return pltpu.make_async_copy(self.held[at], self.outs[k].at[j], self.sems.at[at])
+
+    def start(self):
+        for j, _, _, _, loads, first, _ in self.units:
+            if j == 0 and first:
+                for source, at in loads:
+                    self.load(0, source, at).start()
+
+    def step(self, i):
+        for number, (j, left, right, out, loads, first, last) in enumerate(self.units):
+
+            @pl.when(i == number)
+            def _():
+                if first:
+                    for source, at in loads:
+                        self.load(j, source, at).wait()
+                if j > 0:
+                    self.store(j - 1, out).wait()
+                a, b, c = self.held[left], self.held[right], self.held[self.pairs + out]
+
+                @pl.loop(0, a.shape[1] // 256)
+                def _(m):
+                    columns = pl.ds(pl.multiple_of(m * 256, 256), 256)
+                    c[columns, :] = low(t_dot(a[:, columns], b[...]))
+
+                self.store(j, out).start()
+                if last and j + 1 < self.count:
+                    for source, at in loads:
+                        self.load(j + 1, source, at).start()
+
+    def finish(self):
+        for k in range(len(self.outs)):
+            self.store(self.count - 1, k).wait()
+
+
+def combine_kernel(sections, spreads, pairs, pick_ref, y_ref, *refs):
     kept = len(sections)
     sources, refs = refs[:kept], refs[kept:]
     spread_sources, refs = refs[:spreads], refs[spreads:]
+    factors = []
+    for rights in pairs:
+        factors.append((refs[0], refs[1 : 1 + rights]))
+        refs = refs[1 + rights :]
     out_ref, *refs = refs
     targets, refs = refs[:kept], refs[kept:]
     spread_targets, refs = refs[:spreads], refs[spreads:]
-    y, sent, own, core_in, y_in, z_in, lsem, zs, zr, ys, yr, cs, cr, carry_sem, spread_sem = refs
+    products = sum(pairs)
+    product_outs, refs = refs[:products], refs[products:]
+    y, sent, own, core_in, y_in, z_in, lsem, zs, zr, ys, yr, cs, cr, carry_sem, spread_sem, *refs = refs
+    work = Products(factors, product_outs, refs[:-1], refs[-1]) if pairs else None
     carried = Carried(sections, sources, targets, carry_sem)
     spread = [Spread(a, b, spread_sem) for a, b in zip(spread_sources, spread_targets)]
     d, s = lax.axis_index("dp"), lax.axis_index("seq")
@@ -755,12 +827,17 @@
     start(0)
     for side in spread:
         side.start()
+    if work:
+        work.start()
 
     @pl.loop(0, 8)
     def _(i):
         @pl.when(i < 7)
         def _():
             start(i + 1)
+
+        if work:
+            work.step(i)
 
         z, k = d ^ (3 - i // 2), i % 2
         total = partial_sum(z, k, 0, 0)
@@ -828,9 +905,11 @@
     carried.finish()
     for side in spread:
         side.finish()
-
-
-def combine(pick_t, y, collective_id, carry, spread=()):
+    if work:
+        work.finish()
+
+
+def combine(pick_t, y, collective_id, carry, spread=(), products=()):
     rows, width = pick_t.shape[1], y.shape[2]
     anywhere = pl.BlockSpec(memory_space=pl.ANY)
     near = pl.BlockSpec(memory_space=pltpu.VMEM)
@@ -838,9 +917,18 @@
     arrays = [array for _, array in carry]
 
     arrays = arrays + list(spread)
+    pairs = [len(rights) for _, rights in products]
+    factors = [factor for left, rights in products for factor in (left, *rights)]
+    outs = [
+        jax.ShapeDtypeStruct((left.shape[0], left.shape[2], right.shape[2]), jnp.bfloat16)
+        for left, rights in products
+        for right in rights
+    ]
+    held = [pltpu.VMEM(array.shape[1:], jnp.bfloat16) for array in factors + outs]
+    held = held + [DMA((len(held),))] if held else []
 
     def kernel(*refs):
-        combine_kernel(sections, len(spread), *refs)
+        combine_kernel(sections, len(spread), pairs, *refs)
 
     def blocks(*lead):
         return pltpu.VMEM(lead + (rows, width), jnp.bfloat16)
@@ -848,9 +936,10 @@
     return pl.pallas_call(
         kernel,
         out_shape=[jax.ShapeDtypeStruct((rows, width), jnp.float32)]
-        + [jax.ShapeDtypeStruct(array.shape, array.dtype) for array in arrays],
-        in_specs=[near, anywhere] + [anywhere] * len(arrays),
-        out_specs=[near] + [anywhere] * len(arrays),
+        + [jax.ShapeDtypeStruct(array.shape, array.dtype) for array in arrays]
+        + outs,
+        in_specs=[near, anywhere] + [anywhere] * (len(arrays) + len(factors)),
+        out_specs=[near] + [anywhere] * (len(arrays) + len(outs)),
         scratch_shapes=[
             pltpu.VMEM(y.shape, jnp.bfloat16),
             blocks(4, 2),
@@ -867,13 +956,14 @@
             DMA((4, 2, 2)),
             DMA((max(1, len(arrays)), 2)),
             DMA((4, 2)),
-        ],
+        ]
+        + held,
         compiler_params=pltpu.CompilerParams(
             collective_id=collective_id, has_side_effects=True, vmem_limit_bytes=60 << 20
         ),
         cost_estimate=cost(),
         name="combine",
-    )(pick_t, y, *arrays)
+    )(pick_t, y, *arrays, *factors)
 
 
 def expert_backward_kernel(
@@ -952,7 +1042,7 @@
 
 
 def expert_backward(layer, x, pick, gate, up, slot_gate, own, other, collective_id, carry):
-    count, width, units = own[0].shape
+    count, width, units = share_shape(own[0])
     rows = x.shape[0]
     slots = 16 * CAP
     bf = jnp.bfloat16
@@ -977,7 +1067,7 @@
         + [jax.ShapeDtypeStruct(array.shape, array.dtype) for array in arrays],
         in_specs=[anywhere, near] + [anywhere] * (9 + len(arrays)),
         out_specs=[anywhere] * (5 + len(arrays)),
-        scratch_shapes=[pltpu.VMEM(weight.shape, bf) for weight in own]
+        scratch_shapes=[pltpu.VMEM(share_shape(weight), bf) for weight in own]
         + [pltpu.VMEM(*result) for result in results]
         + [DMA((3,)), DMA((3,)), DMA((5, 4)), DMA((max(1, len(arrays)), 2))]
         + gather_scratch(rows, width),
@@ -1082,6 +1172,7 @@
 def attention_forward_kernel(sections, x_ref, qkv_ref, wo_ref, cos_ref, sin_ref, *refs):
     kept = len(sections)
     sources, refs = refs[:kept], refs[kept:]
+    sources = [share(ref) if to is None else ref for to, ref in zip(sections, sources)]
     out_ref, all_out, heads_out, lse_out, ot_out, *refs = refs
     targets, refs = refs[:kept], refs[kept:]
     wqkv, wo, heads, lse, ot, partial, wsem, osem, carry_sem, *line = refs
@@ -1183,7 +1274,10 @@
     return pl.pallas_call(
         kernel,
         out_shape=[jax.ShapeDtypeStruct(*result) for result in results]
-        + [jax.ShapeDtypeStruct(array.shape, array.dtype) for array in arrays],
+        + [
+            jax.ShapeDtypeStruct(share_shape(array) if to is None else array.shape, array.dtype)
+            for to, array in carry
+        ],
         in_specs=[anywhere] * 3 + [near] * 2 + [anywhere] * len(arrays),
         out_specs=[near] + [anywhere] * (4 + len(arrays)),
         scratch_shapes=[
@@ -1495,7 +1589,7 @@
     attn_scale, ffn_scale, qkv_w, out_w, router_w = weights
     chosen, pick, pick_t, first_expert = picking
     own, other = experts
-    count = own[0].shape[0]
+    count = pick.shape[1] // CAP
     blocks, _, rows = chosen.shape
     received = []
     normed_input = low(rms_norm(layer_in, attn_scale))
@@ -1564,14 +1658,17 @@
     return (after_update, slot_out, saved, (own, other), received)
 
 
-def token_sums(pick_t, slot_out, collective_id, *carry, spread=()):
+def token_sums(pick_t, slot_out, collective_id, *carry, spread=(), products=()):
     if has_kernels():
-        sums, *received = combine(pick_t, slot_out, collective_id, carry, spread)
+        sums, *received = combine(pick_t, slot_out, collective_id, carry, spread, products)
         return sums, received
     sums = give_back(pick_t, slot_out).astype(jnp.float32)
     sums = lax.psum_scatter(sums, TOKENS, scatter_dimension=0, tiled=True)
     received = [pass_to(array, to) for to, array in carry]
-    return sums, received + [spread_rows(array) for array in spread]
+    grads = [
+        low(each_dot("eck,ecn->ekn", left, right)) for left, rights in products for right in rights
+    ]
+    return sums, received + [spread_rows(array) for array in spread] + grads
 
 
 def spread_rows(parts):
@@ -1581,7 +1678,7 @@
 def expert_gradients(number, layer_grad, saved, picking, experts, *carry):
     chosen, pick, pick_t, first_expert = picking
     own, other = experts
-    count = own[0].shape[0]
+    count = pick.shape[1] // CAP
     blocks, _, rows = chosen.shape
     slot_rows, gate_pre, up_pre, scaled, slot_gates = saved[-1]
     if has_kernels():
@@ -1604,17 +1701,17 @@
             each_dot("ecf,edf->ecd", gate_low, gate_w) + each_dot("ecf,edf->ecd", up_low, up_w)
         )
         received = [pass_to(array, to) for to, array in carry]
-    expert_grads = (
-        low(each_dot("ecd,ecf->edf", slot_rows, gate_low)),
-        low(each_dot("ecd,ecf->edf", slot_rows, up_low)),
-        low(each_dot("ecf,ecd->efd", scaled, slot_grads)),
-    )
-    slot_out, *expert_grads = lax.optimization_barrier((slot_out, *expert_grads))
-    return slot_out, gate_term, expert_grads, received
+    by_slot = jnp.transpose(gate_term.reshape(count, blocks, CAP), (1, 0, 2))
+    gate_terms = jnp.sum(
+        pick.reshape(blocks, count, CAP, rows).astype(jnp.float32) * by_slot[..., None], axis=2
+    )
+    gate_terms = lax.all_to_all(gate_terms, TOKENS, split_axis=0, concat_axis=0, tiled=True)
+    products = ((slot_rows, (gate_low, up_low)), (scaled, (slot_grads,)))
+    return slot_out, gate_terms, products, received
 
 
 def backward_layer(
-    number, layer_grad, normed_grad, gate_term, saved, picking, weights, *carry, spread=()
+    number, layer_grad, normed_grad, gate_terms, saved, picking, weights, *carry, spread=()
 ):
     attn_scale, ffn_scale, qkv_w, out_w, router_w = weights
     chosen, pick, _, _ = picking
@@ -1626,13 +1723,7 @@
         own_gates,
         _,
     ) = saved
-    blocks, _, rows = chosen.shape
-    count = gate_term.shape[0]
-    by_slot = jnp.transpose(gate_term.reshape(count, blocks, CAP), (1, 0, 2))
-    gate_terms = jnp.sum(
-        pick.reshape(blocks, count, CAP, rows).astype(jnp.float32) * by_slot[..., None], axis=2
-    )
-    gate_terms = lax.all_to_all(gate_terms, TOKENS, split_axis=0, concat_axis=0, tiled=True)
+    rows = chosen.shape[2]
     gate_terms = jnp.sum(gate_terms.reshape(EXPERTS, -1, rows), axis=1)
     logit_grad = low(
         own_gates * (gate_terms - jnp.sum(own_gates * gate_terms, axis=0, keepdims=True))
@@ -1725,11 +1816,14 @@
         count, units = 1, hidden_units * local // seq
         start, unit_start = seq_index * local // seq, (seq_index % (seq // local)) * units
     first_expert = lax.axis_index("dp") * local + start
-    own_experts = (
-        lax.dynamic_slice(w_gate[0], (start, 0, unit_start), (count, width, units)),
-        lax.dynamic_slice(w_up[0], (start, 0, unit_start), (count, width, units)),
-        lax.dynamic_slice(w_down[0], (start, unit_start, 0), (count, units, width)),
-    )
+    if has_kernels():
+        own_experts = (w_gate[0], w_up[0], w_down[0])
+    else:
+        own_experts = (
+            lax.dynamic_slice(w_gate[0], (start, 0, unit_start), (count, width, units)),
+            lax.dynamic_slice(w_up[0], (start, 0, unit_start), (count, width, units)),
+            lax.dynamic_slice(w_down[0], (start, unit_start, 0), (count, units, width)),
+        )
     small = jnp.concatenate([router_matrix[0].T, attn_gain, ffn_gain], axis=0)
     paths = routes[0, :, 0]
     if has_kernels():
@@ -1829,31 +1923,41 @@
         1, first_out, pickings[1], weights[1], experts, (0, first_out)
     )
     top_grad = top_grad.astype(jnp.float32)
-    slot_out, gate_term, second_experts, _ = expert_gradients(
+    slot_out, gate_terms, products, _ = expert_gradients(
         1, top_grad, second_saved, pickings[1], experts
     )
-    sums, (second_gate,) = token_sums(pickings[1][2], slot_out, 6, (1, second_experts[0]))
-    middle_grad, second_dense, (second_up,) = backward_layer(
-        1, top_grad, sums, gate_term, second_saved, pickings[1], weights[1], (1, second_experts[1])
-    )
-    slot_out, gate_term, first_experts, (second_down,) = expert_gradients(
-        0, middle_grad, first_saved, pickings[0], experts, (1, second_experts[2])
-    )
-    sums, (first_gate, other_middle) = token_sums(
-        pickings[0][2], slot_out, 7, (0, first_experts[0]), (1, middle_grad)
-    )
+    sums, second_experts = token_sums(pickings[1][2], slot_out, 6, products=products)
+    middle_grad, second_dense, (second_gate,) = backward_layer(
+        1, top_grad, sums, gate_terms, second_saved, pickings[1], weights[1], (1, second_experts[0])
+    )
+    slot_out, gate_terms, products, (second_up,) = expert_gradients(
+        0, middle_grad, first_saved, pickings[0], experts, (1, second_experts[1])
+    )
+    (rows_in, (gate_low, up_low)), down_product = products
+    gate_grad = low(each_dot("ecd,ecf->edf", rows_in, gate_low))
+    slot_out, gate_grad, gate_terms = lax.optimization_barrier((slot_out, gate_grad, gate_terms))
+    sums, (first_gate, second_down, *first_experts) = token_sums(
+        pickings[0][2],
+        slot_out,
+        7,
+        (0, gate_grad),
+        (1, second_experts[2]),
+        products=((rows_in, (up_low,)), down_product),
+    )
+    first_experts = [gate_grad, *first_experts]
     sums, *second_dense = lax.optimization_barrier((sums, *second_dense))
     second_dense = dp_sums(second_dense)
     gate_sum = low(summed((first_experts[0], second_experts[0]), (first_gate, second_gate)))
-    bottom_grad, first_dense, (first_up, gate_rows) = backward_layer(
+    bottom_grad, first_dense, (first_up, other_middle, gate_rows) = backward_layer(
         0,
         middle_grad,
         sums,
-        gate_term,
+        gate_terms,
         first_saved,
         pickings[0],
         weights[0],
         (0, first_experts[1]),
+        (1, middle_grad),
         spread=(row_parts(gate_sum, 0),),
     )
     up_sum = low(summed((first_experts[1], second_experts[1]), (first_up, second_up)))

time: 1480 us -> 1450 us (0.980)
  matrix products: 73.5 us -> 32.4 us
    dot_general x6 -> x1, matrix products: 53.7 us -> 10.1 us  [each_dot(): return jnp.einsum(form, a, b, preferred_element_type=jnp.float32)]
  transfers between devices with their start and end apart: 11 -> 11, of which waited for: 2 -> 2; matrix products, arithmetic and copies ran while one was open for 8% -> 7% of each run, Pallas kernels for 46% -> 47%
where the time goes in v9:
time: 1450 us; the launch traced here: 1430 us
  Pallas kernels  1210 us (83%)
  other arithmetic  77 us (5%)
  local copies, waits for them, and re-layouts  52 us (4%)
  matrix products  32.4 us (2%)
  waiting for transfers between devices  21.8 us (2%)
  starting transfers between devices  18.9 us (1%)
  between operations  15.4 us (1%)
    pallas_call x4, Pallas kernels, combine(): pl.pallas_call(kernel, out_shape=[jax.ShapeDtypeStruct((rows, width), jnp...  450 us
    pallas_call x2, Pallas kernels, expert_forward(): pl.pallas_call(kernel, out_shape=shapes, in_specs=[anywhere, near, near,...  173 us
    pallas_call x2, Pallas kernels, expert_backward(): pl.pallas_call(kernel, out_shape=[jax.ShapeDtypeStruct(*result) for resul...  166 us
    pallas_call x2, Pallas kernels, attention_backward_call(): pl.pallas_call(kernel, out_shape=[jax.ShapeDtypeStruct(*result) for resul...  151 us
    pallas_call x2, Pallas kernels, attention_forward_call(): pl.pallas_call(kernel, out_shape=[jax.ShapeDtypeStruct(*result) for resul...  128 us
    pallas_call x1, Pallas kernels, prepare(): pl.pallas_call(prepare_kernel, out_shape=[jax.ShapeDtypeStruct((2, 16, co...  87.4 us
    pallas_call x1, Pallas kernels, last_exchange(): pl.pallas_call(kernel, out_shape=[jax.ShapeDtypeStruct(array.shape, array...  59.6 us
  transfers between devices with their start and end apart: 11, of which 2 were waited for; matrix products, arithmetic and copies ran while one was open for 7% of the time, Pallas kernels for 47%

profile of v9, /device:TPU:16, one launch (start us, length us, event | category | flops | bytes accessed | tf_op | source)
XLA Modules:
  0.0 1432.1 jit_solution(12536212588113635967)
XLA Ops:
  7.3 3.3 collective-permute-start
  10.6 13.6 collective-permute-done
  25.7 8.1 collective-permute-done.1
  36.6 87.4 %prepare.1 = (bf16[2,16,160,256]{3,2,1,0:T(8,128)(2,1)}, bf16[2,16,256,160]{3,2,1,0:T(8,128)(2,1)}, bf16[2,16,32,256]{3,2,1,0:T(8,128)(2,1)}, bf16[2,48,1536]{2,...) custom-call(bf16[64,256]{1,0:T(8,128)(2,1)} %pad_maximum_fusion.4.x_r, ...), custom_call_target="tpu_custom_call" | custom-call | flops 80000000000 | bytes 100000000 | tf_op jit(solution)/shard_map/prepare/pallas_call | solution.py:501
  135.9 4.8 slice_bitcast_fusion
  144.6 73.7 %attention_forward.2 = (f32[256,1536]{1,0:T(8,128)}, bf16[4,256,1536]{2,1,0:T(8,128)(2,1)}, bf16[10,1024,64]{2,1,0:T(8,128)(2,1)}, f32[8,1024]{1,0:T(8,128)}, bf...) custom-call(bf16[256,1536]{1,0:T(8,128)(2,1)} %fusion.4.refs_0_, bf16[1536,640]{1,0:T(8,128)(2,1)} %bitcast.190, ...), custom_call_target="tpu_custom_call" | custom-call | flops 80000000000 | bytes 100000000 | tf_op jit(solution)/shard_map/attention_forward/pallas_call | solution.py:1274
  222.3 91.2 %expert_forward.2 = (bf16[2,1280,1536]{2,1,0:T(8,128)(2,1)}, bf16[2,1280,512]{2,1,0:T(8,128)(2,1)}, bf16[2,1280,512]{2,1,0:T(8,128)(2,1)}, bf16[2,1280,512]{2,1,...) custom-call(bf16[256,1536]{1,0:T(8,128)(2,1)} %multiply_convert_fusion.2.ref, ...), custom_call_target="tpu_custom_call" | custom-call | flops 80000000000 | bytes 100000000 | tf_op jit(solution)/shard_map/expert_forward/pallas_call | solution.py:676
  313.5 98.1 %combine.4 = f32[256,1536]{1,0:T(8,128)} custom-call(bf16[16,256,160]{2,1,0:T(8,128)(2,1)} %get-tuple-element.257.refs_0_, bf16[16,160,1536]{2,1,0:T(8,128)(2,1)} %get-tuple-element.104.refs_1_), custom_call_target="tpu_custom_call" | custom-call | flops 80000000000 | bytes 100000000 | tf_op jit(solution)/shard_map/combine/pallas_call | solution.py:936
  415.5 54.7 %attention_forward.3 = (f32[256,1536]{1,0:T(8,128)}, bf16[4,256,1536]{2,1,0:T(8,128)(2,1)}, bf16[10,1024,64]{2,1,0:T(8,128)(2,1)}, f32[8,1024]{1,0:T(8,128)}, bf...) custom-call(bf16[256,1536]{1,0:T(8,128)(2,1)} %multiply_convert_fusion.1.refs_0_, ...), custom_call_target="tpu_custom_call" | custom-call | flops 80000000000 | bytes 100000000 | tf_op jit(solution)/shard_map/attention_forward/pallas_call | solution.py:1274
  474.7 82.1 %expert_forward.3 = (bf16[2,1280,1536]{2,1,0:T(8,128)(2,1)}, bf16[2,1280,512]{2,1,0:T(8,128)(2,1)}, bf16[2,1280,512]{2,1,0:T(8,128)(2,1)}, bf16[2,1280,512]{2,1,...) custom-call(bf16[256,1536]{1,0:T(8,128)(2,1)} %multiply_convert_fusion.refs_0_, ...), custom_call_target="tpu_custom_call" | custom-call | flops 80000000000 | bytes 100000000 | tf_op jit(solution)/shard_map/expert_forward/pallas_call | solution.py:676
  556.8 85.4 %expert_backward.2 = (bf16[2,1280,1536]{2,1,0:T(8,128)(2,1)}, bf16[2,1280,512]{2,1,0:T(8,128)(2,1)}, bf16[2,1280,512]{2,1,0:T(8,128)(2,1)}, f32[2,1280,128]{2,1,0:T(8,128)}, bf16[16,160,1536]{2,1,0:T(8,128)(2,1)}) custom-call(bf16[256,1536]{1,0:T(8,128)(2,1)} %dynamic-slice_bitcast_fusion.refs_0_, bf16[16,160,256]{2,1,0:T(8,128)(2,1)} %get-tuple-element.260.refs_1_, ...), custom_call_target="tpu_custom_call" | custom-call | flops 80000000000 | bytes 100000000 | tf_op jit(solution)/shard_map/expert_backward/pallas_call | solution.py:1064
  645.3 7.2 all-to-all-start
  653.6 100.6 %combine.5 = (f32[256,1536]{1,0:T(8,128)}, bf16[2,1536,512]{2,1,0:T(8,128)(2,1)}, bf16[2,1536,512]{2,1,0:T(8,128)(2,1)}, bf16[2,512,1536]{2,1,0:T(8,128)(2,1)}) custom-call(bf16[16,256,160]{2,1,0:T(8,128)(2,1)} %get-tuple-element.256.refs_0_, bf16[16,160,1536]{2,1,0:T(8,128)(2,1)} %get-tuple-element.113.refs_1_, ...), custom_call_target="tpu_custom_call" | custom-call | flops 80000000000 | bytes 100000000 | tf_op jit(solution)/shard_map/combine/pallas_call | solution.py:936
  759.5 71.6 %attention_backward.2 = (f32[256,1536]{1,0:T(8,128)}, bf16[4,256,1536]{2,1,0:T(8,128)(2,1)}, bf16[1024,640]{1,0:T(8,128)(2,1)}, bf16[2,1536,512]{2,1,0:T(8,128)(2,1)}) custom-call(bf16[256,1536]{1,0:T(8,128)(2,1)} %fusion.32.refs_0_, bf16[1536,640]{1,0:T(8,128)(2,1)} %all-gather.6.cloned.1.call-done.refs_1_, ...), custom_call_target="tpu_custom_call" | custom-call | flops 80000000000 | bytes 100000000 | tf_op jit(solution)/shard_map/attention_backward/pallas_call | solution.py:1414
  833.4 3.4 fusion.35
  836.8 80.2 %expert_backward.3 = (bf16[2,1280,1536]{2,1,0:T(8,128)(2,1)}, bf16[2,1280,512]{2,1,0:T(8,128)(2,1)}, bf16[2,1280,512]{2,1,0:T(8,128)(2,1)}, f32[2,1280,128]{2,1,...) custom-call(bf16[256,1536]{1,0:T(8,128)(2,1)} %get-tuple-element.244.refs_0_, ...), custom_call_target="tpu_custom_call" | custom-call | flops 80000000000 | bytes 100000000 | tf_op jit(solution)/shard_map/expert_backward/pallas_call | solution.py:1064
  920.1 6.5 all-to-all-start.1
  926.9 10.1 convolution_convert_fusion.refs_2_
  939.3 4.2 convolution_convert_fusion.2
  943.8 101.5 %combine.6 = (f32[256,1536]{1,0:T(8,128)}, bf16[2,1536,512]{2,1,0:T(8,128)(2,1)}, bf16[2,512,1536]{2,1,0:T(8,128)(2,1)}, bf16[2,1536,512]{2,1,0:T(8,128)(2,1)}, bf16[2,512,1536]{2,1,0:T(8,128)(2,1)}) custom-call(bf16[16,256,160]{2,1,0:T(8,128)(2,1)} %get-tuple-element.257.refs_0_, bf16[16,160,1536]{2,1,0:T(8,128)(2,1)} %get-tuple-element.133.refs_1_, ...), custom_call_target="tpu_custom_call" | custom-call | flops 80000000000 | bytes 100000000 | tf_op jit(solution)/shard_map/combine/pallas_call | solution.py:936
  1050.1 4.6 add_convert_fusion.2
  1060.1 3.2 fusion.33
  1063.4 79.1 %attention_backward.3 = (f32[256,1536]{1,0:T(8,128)}, bf16[4,256,1536]{2,1,0:T(8,128)(2,1)}, bf16[1024,640]{1,0:T(8,128)(2,1)}, bf16[2,1536,512]{2,1,0:T(8,128)(...) custom-call(bf16[256,1536]{1,0:T(8,128)(2,1)} %get-tuple-element.242.refs_0_, bf16[1536,640]{1,0:T(8,128)(2,1)} %bitcast.191, ...), custom_call_target="tpu_custom_call" | custom-call | flops 80000000000 | bytes 100000000 | tf_op jit(solution)/shard_map/attention_backward/pallas_call | solution.py:1414
  1145.0 4.1 convolution_convert_fusion.1
  1156.0 4.3 copy.85
  1160.3 4.6 add_convert_fusion.1
  1169.8 149.3 %combine.7 = (f32[256,1536]{1,0:T(8,128)}, bf16[2,512,1536]{2,1,0:T(8,128)(2,1)}, bf16[4,2,384,512]{3,2,1,0:T(8,128)(2,1)}) custom-call(bf16[16,256,160]{2,1,0:T(8,128)(2,1)} %get-tuple-element.256.refs_0_, bf16[16,160,1536]{2,1,0:T(8,128)(2,1)} %get-tuple-element.157.refs_1_, bf16[2,512,1536]{2,1,0:T(8,128)(2,1)} %get-tuple-element.158.refs_2_, ...), custom_call_target="tpu_custom_call" | custom-call | flops 80000000000 | bytes 100000000 | tf_op jit(solution)/shard_map/combine/pallas_call | solution.py:936
  1319.1 4.5 add_convert_fusion
  1327.6 6.5 bitcast_convert_fusion.1
  1341.4 59.6 %last_exchange.1 = (bf16[4,2,128,1536]{3,2,1,0:T(8,128)(2,1)}, bf16[4,96,768]{2,1,0:T(8,128)(2,1)}, bf16[96,1536]{1,0:T(8,128)(2,1)}, f32[256,1536]{1,0:T(8,128)}, f32[256,1536]{1,0:T(8,128)}) custom-call(bf16[4,2,128,1536]{3,2,1,0:T(8,128)(2,1)} %bitcast.152, bf16[4,96,768]{2,1,0:T(8,128)(2,1)} %bitcast.163, bf16[4,96,768]{2,1,0:T(8,128)(2,1)} %bitcast.164, ...), custom_call_target="tpu_custom_call" | custom-call | tf_op jit(solution)/shard_map/last_exchange/pallas_call | solution.py:1506
  1404.5 3.6 bitcast_convert_fusion
  1417.5 3.8 select_bitcast_fusion.1
  (282 shorter events, 102.0 us)
Async XLA Ops:
  7.2 27.5 %copy-start.36 = (bf16[1,96,1536]{2,1,0:T(8,128)(2,1)S(1)}, bf16[1,96,1536]{2,1,0:T(8,128)(2,1)}, u32[]{:S(2)}) copy-start(bf16[1,96,1536]{2,1,0:T(8,128)(2,1)} %param.17) | copy-start | bytes 884740
  7.2 27.7 %copy-start.47 = (bf16[1,96,512]{2,1,0:T(8,128)(2,1)S(1)}, bf16[1,96,512]{2,1,0:T(8,128)(2,1)}, u32[]{:S(2)}) copy-start(bf16[1,96,512]{2,1,0:T(8,128)(2,1)} %param.18) | copy-start | bytes 294916
  7.2 27.7 %copy-start.48 = (bf16[1,96,512]{2,1,0:T(8,128)(2,1)S(1)}, bf16[1,96,512]{2,1,0:T(8,128)(2,1)}, u32[]{:S(2)}) copy-start(bf16[1,96,512]{2,1,0:T(8,128)(2,1)} %param.19) | copy-start | bytes 294916
  7.2 137.4 %all-gather.4.cloned.1.call-start = ((), (), s32[]{:S(2)}) async-start(), calls=%async_computation.6 | async-start | bytes 1474560 | tf_op jit(solution)/shard_map/all_gather | solution.py:1864
  7.3 16.9 %collective-permute-start = (bf16[96,1536]{1,0:T(8,128)(2,1)}, bf16[96,1536]{1,0:T(8,128)(2,1)S(1)}, u32[]{:S(2)}, u32[]{:S(2)}) collective-permute-start(bf16[96,1536]{1,0:T(8,128)(2,1)} %bitcast.185), channel_id=1, source_target_pairs={{0,0},{1,4},{2,8},{3,12},{4,1},{5,5},{6,9},{7,13},{8,2},{9,6},{10,... | collective-permute-start | bytes 884744 | tf_op jit(solution)/shard_map/ppermute | solution.py:1808
  24.1 9.6 collective-permute-start.1
  34.7 380.9 %all-gather.8.cloned.1.call-start = ((), (), s32[]{:S(2)}) async-start(), calls=%async_computation.8 | async-start | bytes 1474560 | tf_op jit(solution)/shard_map/all_gather | solution.py:1864
  36.5 379.0 %all-gather.6.cloned.1.call-start = ((), (), s32[]{:S(2)}) async-start(), calls=%async_computation.7 | async-start | bytes 2457600 | tf_op jit(solution)/shard_map/all_gather | solution.py:1842
  36.6 90.5 %copy-start.13 = (bf16[2,1,256,1536]{3,2,1,0:T(8,128)(2,1)S(1)}, bf16[2,1,256,1536]{3,2,1,0:T(8,128)(2,1)}, u32[]{:S(2)}) copy-start(bf16[2,1,256,1536]{3,2,1,0:T(8,128)(2,1)} %param.13) | copy-start | bytes 4718596
  125.5 16.2 %copy-start.41 = (f32[1536]{0:T(1024)}, f32[1536]{0:T(1024)S(1)}, u32[]{:S(2)}) copy-start(f32[1536]{0:T(1024)S(1)} %get-tuple-element.239) | copy-start | bytes 18436
  125.5 94.6 %copy-start.43 = (f32[1536]{0:T(1024)}, f32[1536]{0:T(1024)S(1)}, u32[]{:S(2)}) copy-start(f32[1536]{0:T(1024)S(1)} %get-tuple-element.238) | copy-start | bytes 18436
  127.4 14.3 copy-start.57
  220.0 93.4 %copy-start.61 = (f32[256]{0:T(256)}, f32[256]{0:T(256)S(1)}, u32[]{:S(2)}) copy-start(f32[256]{0:T(256)S(1)} %get-tuple-element.250) | copy-start | bytes 3076
  313.5 98.1 %copy-start.7 = (f32[256,1536]{1,0:T(8,128)S(1)}, f32[256,1536]{1,0:T(8,128)}, u32[]{:S(2)}) copy-start(f32[256,1536]{1,0:T(8,128)} %copy-done.6) | copy-start | bytes 4718596
  556.8 87.4 %copy-start.22 = (bf16[1,16,160,256]{3,2,1,0:T(8,128)(2,1)S(1)}, bf16[1,16,160,256]{3,2,1,0:T(8,128)(2,1)}, u32[]{:S(2)}) copy-start(bf16[1,16,160,256]{3,2,1,0:T(8,128)(2,1)} %get-tuple-element.261) | copy-start | bytes 3932164
  642.2 10.3 copy-start.17
  645.3 109.0 %all-to-all-start = ((f32[16,2,256]{2,1,0:T(2,128)}), f32[16,2,256]{2,1,0:T(2,128)S(1)}, u32[]{:S(2)}, u32[]{:S(2)}) async-start(f32[16,2,256]{2,1,0:T(2,128)} %fusion.1), calls=%async_computation | async-start | bytes 65536 | tf_op jit(solution)/shard_map/all_to_all | solution.py:1708
  653.5 101.7 %copy-start.1 = (f32[256,1536]{1,0:T(8,128)S(1)}, f32[256,1536]{1,0:T(8,128)}, u32[]{:S(2)}) copy-start(f32[256,1536]{1,0:T(8,128)} %copy-done) | copy-start | bytes 4718596
  653.6 101.7 %copy-start.40 = (f32[1536]{0:T(1024)S(1)}, f32[1536]{0:T(1024)}, u32[]{:S(2)}) copy-start(f32[1536]{0:T(1024)} %get-tuple-element.236) | copy-start | bytes 18436
  653.6 101.7 %copy-start.50 = (f32[256]{0:T(256)S(1)}, f32[256]{0:T(256)}, u32[]{:S(2)}) copy-start(f32[256]{0:T(256)} %copy-done.49) | copy-start | bytes 3076
  759.5 71.6 %copy-start.4 = (f32[256,1536]{1,0:T(8,128)S(1)}, f32[256,1536]{1,0:T(8,128)}, u32[]{:S(2)}) copy-start(f32[256,1536]{1,0:T(8,128)} %copy-done.3) | copy-start | bytes 4718596
  759.5 71.6 %copy-start.46 = (f32[1536]{0:T(1024)S(1)}, f32[1536]{0:T(1024)}, u32[]{:S(2)}) copy-start(f32[1536]{0:T(1024)} %get-tuple-element.237) | copy-start | bytes 18436
  759.5 71.6 %copy-start.54 = (f32[256]{0:T(256)S(1)}, f32[256]{0:T(256)}, u32[]{:S(2)}) copy-start(f32[256]{0:T(256)} %copy-done.53) | copy-start | bytes 3076
  920.1 23.7 %all-to-all-start.1 = ((f32[16,2,256]{2,1,0:T(2,128)}), f32[16,2,256]{2,1,0:T(2,128)S(1)}, u32[]{:S(2)}, u32[]{:S(2)}) async-start(f32[16,2,256]{2,1,0:T(2,128)} %fusion), calls=%async_computation.1 | async-start | bytes 65536 | tf_op jit(solution)/shard_map/all_to_all | solution.py:1708
  926.6 228.0 %reduce-scatter.13.cloned.1.call-start = ((), (), s32[]{:S(2)}) async-start(), calls=%async_computation.11 | async-start | bytes 2949120
  1047.8 108.2 %reduce-scatter.9.cloned.1.call-start = ((), (), s32[]{:S(2)}) async-start(), calls=%async_computation.9 | async-start | bytes 1474560 | tf_op jit(solution)/shard_map/reduce_scatter | solution.py:1889
  1060.1 274.0 %reduce-scatter.15.cloned.1.call-start = ((), (), s32[]{:S(2)}) async-start(), calls=%async_computation.12 | async-start | bytes 2949120
  1063.4 79.2 %copy-start.14 = (bf16[2,1,256,1536]{3,2,1,0:T(8,128)(2,1)S(1)}, bf16[2,1,256,1536]{3,2,1,0:T(8,128)(2,1)}, u32[]{:S(2)}) copy-start(bf16[2,1,256,1536]{3,2,1,0:T(8,128)(2,1)} %param.13) | copy-start | bytes 4718596
  1063.4 79.2 %copy-start.42 = (f32[1536]{0:T(1024)S(1)}, f32[1536]{0:T(1024)}, u32[]{:S(2)}) copy-start(f32[1536]{0:T(1024)} %copy-done.41) | copy-start | bytes 18436
  1063.4 79.2 %copy-start.58 = (f32[256]{0:T(256)S(1)}, f32[256]{0:T(256)}, u32[]{:S(2)}) copy-start(f32[256]{0:T(256)} %copy-done.57) | copy-start | bytes 3076
  1160.2 175.2 %reduce-scatter.11.cloned.1.call-start = ((), (), s32[]{:S(2)}) async-start(), calls=%async_computation.10 | async-start | bytes 1474560 | tf_op jit(solution)/shard_map/reduce_scatter | solution.py:1889
  1169.8 149.3 %copy-start.27 = (bf16[2,512,1536]{2,1,0:T(8,128)(2,1)S(1)}, bf16[2,512,1536]{2,1,0:T(8,128)(2,1)}, u32[]{:S(2)}) copy-start(bf16[2,512,1536]{2,1,0:T(8,128)(2,1)} %get-tuple-element.135.refs_3_) | copy-start | bytes 9437188
  (57 other events, 219.6 us)
Sparse Core Ops, SparseCore 0:
  34.8 33.8 all-gather.3
  70.3 34.2 all-gather.7
  124.1 45.3 all-gather.5
  1047.9 46.6 reduce-scatter.12
  1097.4 27.8 reduce-scatter.8
  1160.4 54.4 reduce-scatter.14
  1217.2 43.3 reduce-scatter.10

commit v10 on v9

--- a/solution.py
+++ b/solution.py
@@ -1,5 +1,6 @@
 import jax
 import jax.numpy as jnp
+import numpy as np
 from jax import lax
 from jax.experimental import pallas as pl
 from jax.experimental.pallas import tpu as pltpu
@@ -13,6 +14,7 @@
 CAP = 80
 GROUP = HEADS // KV_HEADS
 TOKENS = ("dp", "seq")
+PIECES = 4
 MESH = pl.DeviceIdType.MESH
 DMA = pltpu.SemaphoreType.DMA
 
@@ -261,6 +263,71 @@
         self.local.wait()
         for copy in self.copies:
             copy.wait()
+
+
+class SumSpread:
+    def __init__(self, refs, target, held):
+        self.refs, self.target = refs, target
+        self.a, self.b, self.parts, self.loads, self.sems = held
+
+    def copies(self, own, received):
+        return [
+            pltpu.make_async_copy(own, self.a, self.loads.at[0]),
+            pltpu.make_async_copy(received, self.b, self.loads.at[1]),
+        ]
+
+    def load(self):
+        own_0, own_1, in_0, in_1 = self.refs
+
+        @pl.when(lax.axis_index("section") == 0)
+        def _():
+            for copy in self.copies(own_0, in_0):
+                copy.start()
+
+        @pl.when(lax.axis_index("section") == 1)
+        def _():
+            for copy in self.copies(own_1, in_1):
+                copy.start()
+
+    def start(self):
+        for copy in self.copies(self.refs[0], self.refs[2]):
+            copy.wait()
+        group, count, rows, width = self.parts.shape
+        chunk = 24576 // width
+        for g in range(group):
+            for j in range(count):
+
+                @pl.loop(0, rows // chunk)
+                def _(m):
+                    here = pl.ds(pl.multiple_of(m * chunk, chunk), chunk)
+                    there = pl.ds(pl.multiple_of(g * rows + m * chunk, chunk), chunk)
+                    total = self.a[j, there, :].astype(jnp.float32)
+                    total = total + self.b[j, there, :].astype(jnp.float32)
+                    self.parts[g, j, here, :] = low(total)
+
+        self.spread = Spread(self.parts, self.target, self.sems)
+        self.spread.start()
+
+    def finish(self):
+        self.spread.finish()
+
+
+def parts_shape(array):
+    count, rows, width = array.shape
+    return (4, count, rows // 4, width)
+
+
+def sum_scratch(arrays):
+    if not arrays:
+        return []
+    shape, bf = arrays[0].shape, jnp.bfloat16
+    return [
+        pltpu.VMEM(shape, bf),
+        pltpu.VMEM(shape, bf),
+        pltpu.VMEM(parts_shape(arrays[0]), bf),
+        DMA((2,)),
+        DMA((4, 2)),
+    ]
 
 
 def cost():
@@ -721,7 +788,7 @@
     def step(self, i):
         for number, (j, left, right, out, loads, first, last) in enumerate(self.units):
 
-            @pl.when(i == number)
+            @pl.when(i == number * (PIECES // 2))
             def _():
                 if first:
                     for source, at in loads:
@@ -749,6 +816,7 @@
     kept = len(sections)
     sources, refs = refs[:kept], refs[kept:]
     spread_sources, refs = refs[:spreads], refs[spreads:]
+    spreads = spreads // 4
     factors = []
     for rights in pairs:
         factors.append((refs[0], refs[1 : 1 + rights]))
@@ -758,12 +826,15 @@
     spread_targets, refs = refs[:spreads], refs[spreads:]
     products = sum(pairs)
     product_outs, refs = refs[:products], refs[products:]
-    y, sent, own, core_in, y_in, z_in, lsem, zs, zr, ys, yr, cs, cr, carry_sem, spread_sem, *refs = refs
+    y, sent, own, core_in, y_in, z_in, lsem, zs, zr, ys, yr, cs, cr, carry_sem, *refs = refs
+    held, refs = refs[: 5 * spreads], refs[5 * spreads :]
     work = Products(factors, product_outs, refs[:-1], refs[-1]) if pairs else None
     carried = Carried(sections, sources, targets, carry_sem)
-    spread = [Spread(a, b, spread_sem) for a, b in zip(spread_sources, spread_targets)]
+    spread = [SumSpread(spread_sources, spread_targets[0], held)] if spreads else []
+    for side in spread:
+        side.load()
     d, s = lax.axis_index("dp"), lax.axis_index("seq")
-    half = out_ref.shape[0] // 2
+    piece = out_ref.shape[0] // PIECES
 
     def loaded(b):
         return pltpu.make_async_copy(y_ref.at[b], y.at[b], lsem.at[b])
@@ -780,7 +851,7 @@
     carried.start()
 
     def rows(k):
-        return pl.ds(pl.multiple_of(k * half, half), half)
+        return pl.ds(pl.multiple_of(k * piece, piece), piece)
 
     def partial_sum(z, k, across, other_core):
         b = z * 4 + column(across, other_core)
@@ -814,7 +885,7 @@
         )
 
     def start(i):
-        z, k = d ^ (3 - i // 2), i % 2
+        z, k = d ^ (3 - i // PIECES), i % PIECES
         sent[z, 1, rows(k), :] = low(partial_sum(z, k, 1, 1))
         core_copy(z, k, 1).start()
         total = partial_sum(z, k, 1, 0)
@@ -830,16 +901,16 @@
     if work:
         work.start()
 
-    @pl.loop(0, 8)
+    @pl.loop(0, 4 * PIECES)
     def _(i):
-        @pl.when(i < 7)
+        @pl.when(i < 4 * PIECES - 1)
         def _():
             start(i + 1)
 
         if work:
             work.step(i)
 
-        z, k = d ^ (3 - i // 2), i % 2
+        z, k = d ^ (3 - i // PIECES), i % PIECES
         total = partial_sum(z, k, 0, 0)
         core_copy(z, k, 0).wait_recv()
         total = total + core_in[z, 0, rows(k), :].astype(jnp.float32)
@@ -876,7 +947,7 @@
         def _():
             out_ref[rows(k), :] = total
 
-    for k in range(2):
+    for k in range(PIECES):
 
         @pl.when(d < 3)
         def _():
@@ -889,7 +960,7 @@
             out_ref[rows(k), :] += z_in[1, d, rows(k), :].astype(jnp.float32)
 
     for z in range(4):
-        for k in range(2):
+        for k in range(PIECES):
             core_copy(z, k, 0).wait_send()
             core_copy(z, k, 1).wait_send()
             y_copy(z, k).wait_send()
@@ -916,6 +987,9 @@
     sections = tuple(to for to, _ in carry)
     arrays = [array for _, array in carry]
 
+    carries = [jax.ShapeDtypeStruct(array.shape, array.dtype) for array in arrays]
+    if spread:
+        carries.append(jax.ShapeDtypeStruct(parts_shape(spread[0]), jnp.bfloat16))
     arrays = arrays + list(spread)
     pairs = [len(rights) for _, rights in products]
     factors = [factor for left, rights in products for factor in (left, *rights)]
@@ -936,10 +1010,10 @@
     return pl.pallas_call(
         kernel,
         out_shape=[jax.ShapeDtypeStruct((rows, width), jnp.float32)]
-        + [jax.ShapeDtypeStruct(array.shape, array.dtype) for array in arrays]
+        + carries
         + outs,
         in_specs=[near, anywhere] + [anywhere] * (len(arrays) + len(factors)),
-        out_specs=[near] + [anywhere] * (len(arrays) + len(outs)),
+        out_specs=[near] + [anywhere] * (len(carries) + len(outs)),
         scratch_shapes=[
             pltpu.VMEM(y.shape, jnp.bfloat16),
             blocks(4, 2),
@@ -948,15 +1022,15 @@
             blocks(4),
             blocks(2, 4),
             DMA((16,)),
-            DMA((4, 2)),
-            DMA((2, 4, 2)),
-            DMA((4, 2)),
-            DMA((4, 2)),
-            DMA((4, 2, 2)),
-            DMA((4, 2, 2)),
-            DMA((max(1, len(arrays)), 2)),
-            DMA((4, 2)),
+            DMA((4, PIECES)),
+            DMA((2, 4, PIECES)),
+            DMA((4, PIECES)),
+            DMA((4, PIECES)),
+            DMA((4, PIECES, 2)),
+            DMA((4, PIECES, 2)),
+            DMA((max(1, len(carry)), 2)),
         ]
+        + sum_scratch(spread)
         + held,
         compiler_params=pltpu.CompilerParams(
             collective_id=collective_id, has_side_effects=True, vmem_limit_bytes=60 << 20
@@ -1306,11 +1380,15 @@
     kept = len(sections)
     sources, refs = refs[:kept], refs[kept:]
     spread_sources, refs = refs[:spreads], refs[spreads:]
+    spreads = spreads // 4
     out_ref, all_out, grads_out, *refs = refs
     targets, refs = refs[:kept], refs[kept:]
     spread_targets, refs = refs[:spreads], refs[spreads:]
-    wqkv, wo, heads, douts, dk, dv, dqt, grads, partial, wsem, osem, carry_sem, spread_sem, *line = refs
-    spread = [Spread(a, b, spread_sem) for a, b in zip(spread_sources, spread_targets)]
+    held, refs = refs[: 5 * spreads], refs[5 * spreads :]
+    wqkv, wo, heads, douts, dk, dv, dqt, grads, partial, wsem, osem, carry_sem, *line = refs
+    spread = [SumSpread(spread_sources, spread_targets[0], held)] if spreads else []
+    for side in spread:
+        side.load()
     line = Line(line)
     carried = Carried(sections, sources, targets, carry_sem)
     s = line.s
@@ -1406,6 +1484,9 @@
     kv = heads.shape[0] // (GROUP + 2)
     queries = GROUP * kv
 
+    carries = [jax.ShapeDtypeStruct(array.shape, array.dtype) for array in arrays]
+    if spread:
+        carries.append(jax.ShapeDtypeStruct(parts_shape(spread[0]), bf))
     arrays = arrays + list(spread)
 
     def kernel(*refs):
@@ -1414,10 +1495,11 @@
     return pl.pallas_call(
         kernel,
         out_shape=[jax.ShapeDtypeStruct(*result) for result in results]
-        + [jax.ShapeDtypeStruct(array.shape, array.dtype) for array in arrays],
+        + carries,
         in_specs=[anywhere] * 3 + [near] * 2 + [anywhere, near] + [anywhere] * len(arrays),
-        out_specs=[near] + [anywhere] * (2 + len(arrays)),
-        scratch_shapes=[
+        out_specs=[near] + [anywhere] * (2 + len(carries)),
+        scratch_shapes=sum_scratch(spread)
+        + [
             pltpu.VMEM(qkv_w.shape, bf),
             pltpu.VMEM(out_w.shape, bf),
             pltpu.VMEM(heads.shape, bf),
@@ -1429,8 +1511,7 @@
             pltpu.VMEM((rows, width), f32),
             DMA((3,)),
             DMA((2,)),
-            DMA((max(1, len(arrays)), 2)),
-            DMA((4, 2)),
+            DMA((max(1, len(carry)), 2)),
         ]
         + seq_scratch(rows, width),
         compiler_params=pltpu.CompilerParams(
@@ -1441,12 +1522,14 @@
     )(x, qkv_w, out_w, *tables, heads, lse, *arrays)
 
 
-def last_kernel(sections, down_ref, cols_ref, cols_other, out_ref, out_other, *refs):
+def last_kernel(sections, own_0, own_1, in_0, in_1, cols_ref, cols_other, out_ref, out_other, *refs):
     kept = len(sections)
     sources, refs = refs[:kept], refs[kept:]
     down_out, cols_out, rows_out, *refs = refs
     targets, refs = refs[:kept], refs[kept:]
-    cols_in, cols, out_in, out_sum, down_sem, cols_sem, row_sem, swap_sem, carry_sem = refs
+    cols_in, cols, out_in, out_sum, cols_sem, row_sem, swap_sem, carry_sem, *held = refs
+    down = SumSpread((own_0, own_1, in_0, in_1), down_out, held)
+    down.load()
     d, s, section = lax.axis_index("dp"), lax.axis_index("seq"), lax.axis_index("section")
     barrier = pltpu.get_barrier_semaphore()
 
@@ -1468,7 +1551,6 @@
 
     swaps = Carried((None, None), (cols_other, out_other), (cols_in, out_in), swap_sem)
     carried = Carried(sections, sources, targets, carry_sem)
-    down = Spread(down_ref, down_out, down_sem)
     swaps.start()
     down.start()
     swaps.finish()
@@ -1493,7 +1575,7 @@
     carried.finish()
 
 
-def last_exchange(down, cols, cols_other, out, out_other, collective_id, carry):
+def last_exchange(downs, cols, cols_other, out, out_other, collective_id, carry):
     bf = jnp.bfloat16
     anywhere = pl.BlockSpec(memory_space=pl.ANY)
     near = pl.BlockSpec(memory_space=pltpu.VMEM)
@@ -1506,9 +1588,10 @@
     return pl.pallas_call(
         kernel,
         out_shape=[
-            jax.ShapeDtypeStruct(array.shape, array.dtype) for array in (down, cols, out, *arrays)
+            jax.ShapeDtypeStruct(parts_shape(downs[0]), bf),
+            *[jax.ShapeDtypeStruct(array.shape, array.dtype) for array in (cols, out, *arrays)],
         ],
-        in_specs=[anywhere, near, anywhere, near, anywhere] + [anywhere] * len(arrays),
+        in_specs=[anywhere] * 4 + [near, anywhere, near, anywhere] + [anywhere] * len(arrays),
         out_specs=[anywhere, near, near] + [anywhere] * len(arrays),
         scratch_shapes=[
             pltpu.VMEM(cols.shape, bf),
@@ -1516,24 +1599,26 @@
             pltpu.VMEM(out.shape, bf),
             pltpu.VMEM(out.shape, bf),
             DMA((4, 2)),
-            DMA((4, 2)),
             DMA((2,)),
             DMA((2, 2)),
             DMA((max(1, len(arrays)), 2)),
-        ],
+        ]
+        + sum_scratch(downs),
         compiler_params=pltpu.CompilerParams(
             collective_id=collective_id, has_side_effects=True, vmem_limit_bytes=60 << 20
         ),
         name="last_exchange",
-    )(down, cols, cols_other, out, out_other, *arrays)
+    )(*downs, cols, cols_other, out, out_other, *arrays)
 
 
 def wide_tables(length):
-    cos_table, sin_table = rotary_tables(length)
-    cos_table, sin_table = cos_table[:, 0], sin_table[:, 0]
+    half_dim = HEAD_DIM // 2
+    frequency = 10000.0 ** (-np.arange(half_dim, dtype=np.float32) * 2.0 / HEAD_DIM)
+    angles = np.arange(length, dtype=np.float32)[:, None] * frequency.astype(np.float32)[None, :]
+    cos_table, sin_table = np.cos(angles), np.sin(angles)
     return (
-        jnp.concatenate([cos_table] * 4, axis=1),
-        jnp.concatenate([-sin_table, sin_table] * 2, axis=1),
+        jnp.asarray(np.concatenate([cos_table] * 4, axis=1), jnp.float32),
+        jnp.asarray(np.concatenate([-sin_table, sin_table] * 2, axis=1), jnp.float32),
     )
 
 
@@ -1668,7 +1753,7 @@
     grads = [
         low(each_dot("eck,ecn->ekn", left, right)) for left, rights in products for right in rights
     ]
-    return sums, received + [spread_rows(array) for array in spread] + grads
+    return sums, received + list(spread) + grads
 
 
 def spread_rows(parts):
@@ -1752,7 +1837,7 @@
         normed_attn = low(dot_t(qkv_grad, qkv_w))
         normed_attn = lax.psum_scatter(normed_attn, "seq", scatter_dimension=0, tiled=True)
         received = [pass_to(array, to) for to, array in carry]
-        received = received + [spread_rows(array) for array in spread]
+        received = received + list(spread)
     out_grad = dot(mixed_t, branch_all)
     qkv_weight_grad = t_dot(normed_all, qkv_grad)
     input_part, attn_gain_grad = jax.vjp(rms_norm, layer_in, attn_scale)[1](
@@ -1947,7 +2032,13 @@
     first_experts = [gate_grad, *first_experts]
     sums, *second_dense = lax.optimization_barrier((sums, *second_dense))
     second_dense = dp_sums(second_dense)
-    gate_sum = low(summed((first_experts[0], second_experts[0]), (first_gate, second_gate)))
+
+    def handed(kind, *received):
+        own = (first_experts[kind], second_experts[kind])
+        if has_kernels():
+            return (*own, *received)
+        return [spread_rows(row_parts(low(summed(own, received)), kind))]
+
     bottom_grad, first_dense, (first_up, other_middle, gate_rows) = backward_layer(
         0,
         middle_grad,
@@ -1958,9 +2049,8 @@
         weights[0],
         (0, first_experts[1]),
         (1, middle_grad),
-        spread=(row_parts(gate_sum, 0),),
-    )
-    up_sum = low(summed((first_experts[1], second_experts[1]), (first_up, second_up)))
+        spread=handed(0, first_gate, second_gate),
+    )
     second_slots, *first_dense, second_dense[0], second_dense[1] = lax.optimization_barrier(
         (second_slots, *first_dense, *second_dense)
     )
@@ -1970,16 +2060,15 @@
         second_slots,
         8,
         (0, first_experts[2]),
-        spread=(row_parts(up_sum, 1),),
+        spread=handed(1, first_up, second_up),
     )
     sums, *first_dense = lax.optimization_barrier((sums, *first_dense))
     second_out = second_updated + sums
-    down_sum = low(summed((first_experts[2], second_experts[2]), (first_down, second_down)))
     own_cols, own_rows = [own_layer((first_dense[k], second_dense[k])) for k in range(2)]
     other_cols, other_rows = [own_layer((second_dense[k], first_dense[k])) for k in range(2)]
     if has_kernels():
         down_rows, cols_sum, out_sum, other_second, other_bottom = last_exchange(
-            row_parts(down_sum, 2),
+            handed(2, first_down, second_down),
             own_cols.reshape(seq, depth, -1),
             other_cols.reshape(seq, depth, -1),
             own_rows,
@@ -1988,7 +2077,7 @@
             ((1, second_out), (0, bottom_grad)),
         )
     else:
-        down_rows = spread_rows(row_parts(down_sum, 2))
+        (down_rows,) = handed(2, first_down, second_down)
         cols_sum = low(own_cols.astype(jnp.float32) + swap(other_cols).astype(jnp.float32))
         cols_sum = spread_rows(cols_sum.reshape(seq, depth, -1))
         out_sum = low(own_rows.astype(jnp.float32) + swap(other_rows).astype(jnp.float32))

time: 1450 us -> 1440 us (level)
  Pallas kernels: 1210 us -> 1240 us
  other arithmetic: 77 us -> 61.8 us
  transfers between devices with their start and end apart: 11 -> 11, of which waited for: 2 -> 2; matrix products, arithmetic and copies ran while one was open for 7% -> 5% of each run, Pallas kernels for 47% -> 49%
where the time goes in v10:
time: 1440 us; the launch traced here: 1430 us
  Pallas kernels  1240 us (86%)
  other arithmetic  61.8 us (4%)
  local copies, waits for them, and re-layouts  46.4 us (3%)
  matrix products  32.4 us (2%)
  waiting for transfers between devices  21.8 us (2%)
  starting transfers between devices  19.4 us (1%)
  between operations  15.4 us (1%)
    pallas_call x4, Pallas kernels, combine(): pl.pallas_call(kernel, out_shape=[jax.ShapeDtypeStruct((rows, width), jnp...  461 us
    pallas_call x2, Pallas kernels, expert_forward(): pl.pallas_call(kernel, out_shape=shapes, in_specs=[anywhere, near, near,...  185 us
    pallas_call x2, Pallas kernels, expert_backward(): pl.pallas_call(kernel, out_shape=[jax.ShapeDtypeStruct(*result) for resul...  166 us
    pallas_call x2, Pallas kernels, attention_backward_call(): pl.pallas_call(kernel, out_shape=[jax.ShapeDtypeStruct(*result) for resul...  151 us
    pallas_call x2, Pallas kernels, attention_forward_call(): pl.pallas_call(kernel, out_shape=[jax.ShapeDtypeStruct(*result) for resul...  127 us
    pallas_call x1, Pallas kernels, prepare(): pl.pallas_call(prepare_kernel, out_shape=[jax.ShapeDtypeStruct((2, 16, co...  88 us
    pallas_call x1, Pallas kernels, last_exchange(): pl.pallas_call(kernel, out_shape=[jax.ShapeDtypeStruct(parts_shape(downs[...  59.7 us
  transfers between devices with their start and end apart: 11, of which 2 were waited for; matrix products, arithmetic and copies ran while one was open for 5% of the time, Pallas kernels for 49%

profile of v10, /device:TPU:16, one launch (start us, length us, event | category | flops | bytes accessed | tf_op | source)
XLA Modules:
  0.0 1434.8 jit_solution(12046328574211577806)
XLA Ops:
  7.3 3.3 collective-permute-start
  10.6 13.6 collective-permute-done
  25.7 8.1 collective-permute-done.1
  36.5 88.0 %prepare.1 = (bf16[2,16,160,256]{3,2,1,0:T(8,128)(2,1)}, bf16[2,16,256,160]{3,2,1,0:T(8,128)(2,1)}, bf16[2,16,32,256]{3,2,1,0:T(8,128)(2,1)}, bf16[2,48,1536]{2,...) custom-call(bf16[64,256]{1,0:T(8,128)(2,1)} %pad_maximum_fusion.2.x_r, ...), custom_call_target="tpu_custom_call" | custom-call | flops 80000000000 | bytes 100000000 | tf_op jit(solution)/shard_map/prepare/pallas_call | solution.py:568
  128.0 4.5 fusion.34
  134.1 5.0 slice_bitcast_fusion
  141.8 73.5 %attention_forward.2 = (f32[256,1536]{1,0:T(8,128)}, bf16[4,256,1536]{2,1,0:T(8,128)(2,1)}, bf16[10,1024,64]{2,1,0:T(8,128)(2,1)}, f32[8,1024]{1,0:T(8,128)}, bf...) custom-call(bf16[256,1536]{1,0:T(8,128)(2,1)} %fusion.4.refs_0_, bf16[1536,640]{1,0:T(8,128)(2,1)} %bitcast.172, ...), custom_call_target="tpu_custom_call" | custom-call | flops 80000000000 | bytes 100000000 | tf_op jit(solution)/shard_map/attention_forward/pallas_call | solution.py:1348
  219.2 101.9 %expert_forward.2 = (bf16[2,1280,1536]{2,1,0:T(8,128)(2,1)}, bf16[2,1280,512]{2,1,0:T(8,128)(2,1)}, bf16[2,1280,512]{2,1,0:T(8,128)(2,1)}, bf16[2,1280,512]{2,1,...) custom-call(bf16[256,1536]{1,0:T(8,128)(2,1)} %multiply_convert_fusion.2.ref, ...), custom_call_target="tpu_custom_call" | custom-call | flops 80000000000 | bytes 100000000 | tf_op jit(solution)/shard_map/expert_forward/pallas_call | solution.py:743
  321.1 101.1 %combine.4 = f32[256,1536]{1,0:T(8,128)} custom-call(bf16[16,256,160]{2,1,0:T(8,128)(2,1)} %get-tuple-element.257.refs_0_, bf16[16,160,1536]{2,1,0:T(8,128)(2,1)} %get-tuple-element.104.refs_1_), custom_call_target="tpu_custom_call" | custom-call | flops 80000000000 | bytes 100000000 | tf_op jit(solution)/shard_map/combine/pallas_call | solution.py:1010
  426.1 53.2 %attention_forward.3 = (f32[256,1536]{1,0:T(8,128)}, bf16[4,256,1536]{2,1,0:T(8,128)(2,1)}, bf16[10,1024,64]{2,1,0:T(8,128)(2,1)}, f32[8,1024]{1,0:T(8,128)}, bf...) custom-call(bf16[256,1536]{1,0:T(8,128)(2,1)} %multiply_convert_fusion.1.refs_0_, ...), custom_call_target="tpu_custom_call" | custom-call | flops 80000000000 | bytes 100000000 | tf_op jit(solution)/shard_map/attention_forward/pallas_call | solution.py:1348
  483.8 83.0 %expert_forward.3 = (bf16[2,1280,1536]{2,1,0:T(8,128)(2,1)}, bf16[2,1280,512]{2,1,0:T(8,128)(2,1)}, bf16[2,1280,512]{2,1,0:T(8,128)(2,1)}, bf16[2,1280,512]{2,1,...) custom-call(bf16[256,1536]{1,0:T(8,128)(2,1)} %multiply_convert_fusion.refs_0_, ...), custom_call_target="tpu_custom_call" | custom-call | flops 80000000000 | bytes 100000000 | tf_op jit(solution)/shard_map/expert_forward/pallas_call | solution.py:743
  566.8 85.5 %expert_backward.2 = (bf16[2,1280,1536]{2,1,0:T(8,128)(2,1)}, bf16[2,1280,512]{2,1,0:T(8,128)(2,1)}, bf16[2,1280,512]{2,1,0:T(8,128)(2,1)}, f32[2,1280,128]{2,1,0:T(8,128)}, bf16[16,160,1536]{2,1,0:T(8,128)(2,1)}) custom-call(bf16[256,1536]{1,0:T(8,128)(2,1)} %dynamic-slice_bitcast_fusion.refs_0_, bf16[16,160,256]{2,1,0:T(8,128)(2,1)} %get-tuple-element.260.refs_1_, ...), custom_call_target="tpu_custom_call" | custom-call | flops 80000000000 | bytes 100000000 | tf_op jit(solution)/shard_map/expert_backward/pallas_call | solution.py:1138
  655.4 7.4 all-to-all-start
  663.9 104.2 %combine.5 = (f32[256,1536]{1,0:T(8,128)}, bf16[2,1536,512]{2,1,0:T(8,128)(2,1)}, bf16[2,1536,512]{2,1,0:T(8,128)(2,1)}, bf16[2,512,1536]{2,1,0:T(8,128)(2,1)}) custom-call(bf16[16,256,160]{2,1,0:T(8,128)(2,1)} %get-tuple-element.256.refs_0_, bf16[16,160,1536]{2,1,0:T(8,128)(2,1)} %get-tuple-element.113.refs_1_, ...), custom_call_target="tpu_custom_call" | custom-call | flops 80000000000 | bytes 100000000 | tf_op jit(solution)/shard_map/combine/pallas_call | solution.py:1010
  773.3 71.3 %attention_backward.2 = (f32[256,1536]{1,0:T(8,128)}, bf16[4,256,1536]{2,1,0:T(8,128)(2,1)}, bf16[1024,640]{1,0:T(8,128)(2,1)}, bf16[2,1536,512]{2,1,0:T(8,128)(2,1)}) custom-call(bf16[256,1536]{1,0:T(8,128)(2,1)} %fusion.29.refs_0_, bf16[1536,640]{1,0:T(8,128)(2,1)} %all-gather.6.cloned.1.call-done.refs_1_, ...), custom_call_target="tpu_custom_call" | custom-call | flops 80000000000 | bytes 100000000 | tf_op jit(solution)/shard_map/attention_backward/pallas_call | solution.py:1495
  847.0 3.4 fusion.32
  850.4 80.6 %expert_backward.3 = (bf16[2,1280,1536]{2,1,0:T(8,128)(2,1)}, bf16[2,1280,512]{2,1,0:T(8,128)(2,1)}, bf16[2,1280,512]{2,1,0:T(8,128)(2,1)}, f32[2,1280,128]{2,1,...) custom-call(bf16[256,1536]{1,0:T(8,128)(2,1)} %get-tuple-element.244.refs_0_, ...), custom_call_target="tpu_custom_call" | custom-call | flops 80000000000 | bytes 100000000 | tf_op jit(solution)/shard_map/expert_backward/pallas_call | solution.py:1138
  934.2 6.5 all-to-all-start.1
  940.8 10.1 convolution_convert_fusion.refs_2_.refs_9_
  953.3 4.2 convolution_convert_fusion.2
  957.8 103.9 %combine.6 = (f32[256,1536]{1,0:T(8,128)}, bf16[2,1536,512]{2,1,0:T(8,128)(2,1)}, bf16[2,512,1536]{2,1,0:T(8,128)(2,1)}, bf16[2,1536,512]{2,1,0:T(8,128)(2,1)}, bf16[2,512,1536]{2,1,0:T(8,128)(2,1)}) custom-call(bf16[16,256,160]{2,1,0:T(8,128)(2,1)} %get-tuple-element.257.refs_0_, bf16[16,160,1536]{2,1,0:T(8,128)(2,1)} %get-tuple-element.133.refs_1_, ...), custom_call_target="tpu_custom_call" | custom-call | flops 80000000000 | bytes 100000000 | tf_op jit(solution)/shard_map/combine/pallas_call | solution.py:1010
  1066.5 3.2 multiply_reduce_fusion.1
  1069.8 3.3 fusion.30
  1073.1 79.6 %attention_backward.3 = (f32[256,1536]{1,0:T(8,128)}, bf16[4,256,1536]{2,1,0:T(8,128)(2,1)}, bf16[1024,640]{1,0:T(8,128)(2,1)}, bf16[2,1536,512]{2,1,0:T(8,128)(...) custom-call(bf16[256,1536]{1,0:T(8,128)(2,1)} %get-tuple-element.242.refs_0_, bf16[1536,640]{1,0:T(8,128)(2,1)} %bitcast.173, ...), custom_call_target="tpu_custom_call" | custom-call | flops 80000000000 | bytes 100000000 | tf_op jit(solution)/shard_map/attention_backward/pallas_call | solution.py:1495
  1155.2 4.1 convolution_convert_fusion.1
  1166.8 4.3 copy.84
  1172.5 3.0 fusion.9.refs_9_
  1175.5 152.2 %combine.7 = (f32[256,1536]{1,0:T(8,128)}, bf16[2,512,1536]{2,1,0:T(8,128)(2,1)}, bf16[4,2,384,512]{3,2,1,0:T(8,128)(2,1)}) custom-call(bf16[16,256,160]{2,1,0:T(8,128)(2,1)} %get-tuple-element.256.refs_0_, bf16[16,160,1536]{2,1,0:T(8,128)(2,1)} %get-tuple-element.157.refs_1_, bf16[2,512,1536]{2,1,0:T(8,128)(2,1)} %get-tuple-element.158.refs_2_.refs_0_, ...), custom_call_target="tpu_custom_call" | custom-call | flops 80000000000 | bytes 100000000 | tf_op jit(solution)/shard_map/combine/pallas_call | solution.py:1010
  1327.7 9.5 bitcast_convert_fusion.1
  1344.5 59.7 %last_exchange.1 = (bf16[4,2,128,1536]{3,2,1,0:T(8,128)(2,1)}, bf16[4,96,768]{2,1,0:T(8,128)(2,1)}, bf16[96,1536]{1,0:T(8,128)(2,1)}, f32[256,1536]{1,0:T(8,128)}, f32[256,1536]{1,0:T(8,128)}) custom-call(bf16[2,512,1536]{2,1,0:T(8,128)(2,1)} %get-tuple-element.158.refs_2_.refs_0_, bf16[2,512,1536]{2,1,0:T(8,128)(2,1)} %get-tuple-element.135.refs_3_.refs_1_, ...), custom_call_target="tpu_custom_call" | custom-call | tf_op jit(solution)/shard_map/last_exchange/pallas_call | solution.py:1588
  1407.6 3.6 bitcast_convert_fusion
  1420.7 3.3 select_bitcast_fusion.1
  (260 shorter events, 81.7 us)
Async XLA Ops:
  7.2 27.5 %copy-start.30 = (bf16[1,96,1536]{2,1,0:T(8,128)(2,1)S(1)}, bf16[1,96,1536]{2,1,0:T(8,128)(2,1)}, u32[]{:S(2)}) copy-start(bf16[1,96,1536]{2,1,0:T(8,128)(2,1)} %param.25) | copy-start | bytes 884740
  7.2 27.6 %copy-start.41 = (bf16[1,96,512]{2,1,0:T(8,128)(2,1)S(1)}, bf16[1,96,512]{2,1,0:T(8,128)(2,1)}, u32[]{:S(2)}) copy-start(bf16[1,96,512]{2,1,0:T(8,128)(2,1)} %param.26) | copy-start | bytes 294916
  7.2 27.7 %copy-start.42 = (bf16[1,96,512]{2,1,0:T(8,128)(2,1)S(1)}, bf16[1,96,512]{2,1,0:T(8,128)(2,1)}, u32[]{:S(2)}) copy-start(bf16[1,96,512]{2,1,0:T(8,128)(2,1)} %param.27) | copy-start | bytes 294916
  7.2 134.5 %all-gather.4.cloned.1.call-start = ((), (), s32[]{:S(2)}) async-start(), calls=%async_computation.6 | async-start | bytes 1474560 | tf_op jit(solution)/shard_map/all_gather | solution.py:1949
  7.3 16.9 %collective-permute-start = (bf16[96,1536]{1,0:T(8,128)(2,1)}, bf16[96,1536]{1,0:T(8,128)(2,1)S(1)}, u32[]{:S(2)}, u32[]{:S(2)}) collective-permute-start(bf16[96,1536]{1,0:T(8,128)(2,1)} %bitcast.167), channel_id=1, source_target_pairs={{0,0},{1,4},{2,8},{3,12},{4,1},{5,5},{6,9},{7,13},{8,2},{9,6},{10,... | collective-permute-start | bytes 884744 | tf_op jit(solution)/shard_map/ppermute | solution.py:1893
  24.1 9.6 collective-permute-start.1
  34.6 391.5 %all-gather.8.cloned.1.call-start = ((), (), s32[]{:S(2)}) async-start(), calls=%async_computation.8 | async-start | bytes 1474560 | tf_op jit(solution)/shard_map/all_gather | solution.py:1949
  36.5 389.6 %all-gather.6.cloned.1.call-start = ((), (), s32[]{:S(2)}) async-start(), calls=%async_computation.7 | async-start | bytes 2457600 | tf_op jit(solution)/shard_map/all_gather | solution.py:1927
  36.5 91.2 %copy-start.13 = (bf16[2,1,256,1536]{3,2,1,0:T(8,128)(2,1)S(1)}, bf16[2,1,256,1536]{3,2,1,0:T(8,128)(2,1)}, u32[]{:S(2)}) copy-start(bf16[2,1,256,1536]{3,2,1,0:T(8,128)(2,1)} %param.21) | copy-start | bytes 4718596
  126.1 14.0 copy-start.35
  126.1 90.9 %copy-start.37 = (f32[1536]{0:T(1024)}, f32[1536]{0:T(1024)S(1)}, u32[]{:S(2)}) copy-start(f32[1536]{0:T(1024)S(1)} %get-tuple-element.238) | copy-start | bytes 18436
  127.9 12.1 copy-start.51
  217.0 104.1 %copy-start.55 = (f32[256]{0:T(256)}, f32[256]{0:T(256)S(1)}, u32[]{:S(2)}) copy-start(f32[256]{0:T(256)S(1)} %get-tuple-element.250) | copy-start | bytes 3076
  321.1 101.1 %copy-start.7 = (f32[256,1536]{1,0:T(8,128)S(1)}, f32[256,1536]{1,0:T(8,128)}, u32[]{:S(2)}) copy-start(f32[256,1536]{1,0:T(8,128)} %copy-done.6) | copy-start | bytes 4718596
  566.8 87.5 %copy-start.21 = (bf16[1,16,160,256]{3,2,1,0:T(8,128)(2,1)S(1)}, bf16[1,16,160,256]{3,2,1,0:T(8,128)(2,1)}, u32[]{:S(2)}) copy-start(bf16[1,16,160,256]{3,2,1,0:T(8,128)(2,1)} %get-tuple-element.261) | copy-start | bytes 3932164
  652.3 10.5 copy-start.17
  655.4 112.7 %all-to-all-start = ((f32[16,2,256]{2,1,0:T(2,128)}), f32[16,2,256]{2,1,0:T(2,128)S(1)}, u32[]{:S(2)}, u32[]{:S(2)}) async-start(f32[16,2,256]{2,1,0:T(2,128)} %fusion.1), calls=%async_computation | async-start | bytes 65536 | tf_op jit(solution)/shard_map/all_to_all | solution.py:1793
  663.8 105.3 %copy-start.1 = (f32[256,1536]{1,0:T(8,128)S(1)}, f32[256,1536]{1,0:T(8,128)}, u32[]{:S(2)}) copy-start(f32[256,1536]{1,0:T(8,128)} %copy-done) | copy-start | bytes 4718596
  663.8 105.2 %copy-start.34 = (f32[1536]{0:T(1024)S(1)}, f32[1536]{0:T(1024)}, u32[]{:S(2)}) copy-start(f32[1536]{0:T(1024)} %get-tuple-element.236) | copy-start | bytes 18436
  663.8 105.2 %copy-start.44 = (f32[256]{0:T(256)S(1)}, f32[256]{0:T(256)}, u32[]{:S(2)}) copy-start(f32[256]{0:T(256)} %copy-done.43) | copy-start | bytes 3076
  773.3 71.3 %copy-start.4 = (f32[256,1536]{1,0:T(8,128)S(1)}, f32[256,1536]{1,0:T(8,128)}, u32[]{:S(2)}) copy-start(f32[256,1536]{1,0:T(8,128)} %copy-done.3) | copy-start | bytes 4718596
  773.3 71.3 %copy-start.40 = (f32[1536]{0:T(1024)S(1)}, f32[1536]{0:T(1024)}, u32[]{:S(2)}) copy-start(f32[1536]{0:T(1024)} %get-tuple-element.237) | copy-start | bytes 18436
  773.3 71.4 %copy-start.48 = (f32[256]{0:T(256)S(1)}, f32[256]{0:T(256)}, u32[]{:S(2)}) copy-start(f32[256]{0:T(256)} %copy-done.47) | copy-start | bytes 3076
  934.2 23.6 %all-to-all-start.1 = ((f32[16,2,256]{2,1,0:T(2,128)}), f32[16,2,256]{2,1,0:T(2,128)S(1)}, u32[]{:S(2)}, u32[]{:S(2)}) async-start(f32[16,2,256]{2,1,0:T(2,128)} %fusion), calls=%async_computation.1 | async-start | bytes 65536 | tf_op jit(solution)/shard_map/all_to_all | solution.py:1793
  940.7 224.0 %reduce-scatter.13.cloned.1.call-start = ((), (), s32[]{:S(2)}) async-start(), calls=%async_computation.11 | async-start | bytes 2949120
  1064.1 102.7 %reduce-scatter.9.cloned.1.call-start = ((), (), s32[]{:S(2)}) async-start(), calls=%async_computation.9 | async-start | bytes 1474560 | tf_op jit(solution)/shard_map/reduce_scatter | solution.py:1974
  1069.8 267.3 %reduce-scatter.15.cloned.1.call-start = ((), (), s32[]{:S(2)}) async-start(), calls=%async_computation.12 | async-start | bytes 2949120
  1073.1 79.6 %copy-start.14 = (bf16[2,1,256,1536]{3,2,1,0:T(8,128)(2,1)S(1)}, bf16[2,1,256,1536]{3,2,1,0:T(8,128)(2,1)}, u32[]{:S(2)}) copy-start(bf16[2,1,256,1536]{3,2,1,0:T(8,128)(2,1)} %param.21) | copy-start | bytes 4718596
  1073.1 79.6 %copy-start.36 = (f32[1536]{0:T(1024)S(1)}, f32[1536]{0:T(1024)}, u32[]{:S(2)}) copy-start(f32[1536]{0:T(1024)} %copy-done.35) | copy-start | bytes 18436
  1073.1 79.6 %copy-start.52 = (f32[256]{0:T(256)S(1)}, f32[256]{0:T(256)}, u32[]{:S(2)}) copy-start(f32[256]{0:T(256)} %copy-done.51) | copy-start | bytes 3076
  1171.1 167.4 %reduce-scatter.11.cloned.1.call-start = ((), (), s32[]{:S(2)}) async-start(), calls=%async_computation.10 | async-start | bytes 1474560 | tf_op jit(solution)/shard_map/reduce_scatter | solution.py:1974
  1327.7 10.9 copy-start.2
  (51 other events, 193.8 us)
Sparse Core Ops, SparseCore 0:
  34.7 33.8 all-gather.3
  70.8 34.6 all-gather.7
  124.7 45.2 all-gather.5
  1064.2 46.6 reduce-scatter.12
  1113.7 27.8 reduce-scatter.8
  1171.2 50.4 reduce-scatter.14
  1224.0 46.9 reduce-scatter.10

commit v11 on v10

--- a/solution.py
+++ b/solution.py
@@ -385,10 +385,23 @@
     core_copy(x_ref, d, 0).start()
     own.wait()
 
+    inner = (d > 0) & (d < 3)
+
+    def send_on(q):
+        following = near_first(d, q)
+        y_copy(place(following, s), following).start()
+        core_copy(place(following, s), following, 0).start()
+
     @pl.loop(0, 4)
     def _(i):
         @pl.when(i < 3)
         def _():
+            early = inner & (i > 0)
+
+            @pl.when(early)
+            def _():
+                send_on(i + 1)
+
             left, right = d - (i + 1), d + (i + 1)
 
             @pl.when(left >= 0)
@@ -407,11 +420,11 @@
                 def _():
                     z_copy(place(right, s), right, False).start()
 
-            following = d ^ (i + 1)
-            y_copy(place(following, s), following).start()
-            core_copy(place(following, s), following, 0).start()
-
-        z = d ^ i
+            @pl.when(jnp.logical_not(early))
+            def _():
+                send_on(i + 1)
+
+        z = near_first(d, i)
         y_copy(place(z, s ^ 2), z).wait_recv()
         core_copy(place(z, s ^ 2), z, 1).start()
         core_copy(place(z, s ^ 1), z, 0).wait_recv()
@@ -436,13 +449,13 @@
 
 def prepare_kernel(
     x_ref, group_ref, gate_ref,
-    pick_out, pick_t_out, chosen_out, small_out, qkv_out, parts_out, gate_out,
+    pick_0, pick_1, pick_t_0, pick_t_1, chosen_0, chosen_1, small_out, qkv_out, parts_out, gate_out,
     both, places, groups, parts, lsem, carry_sem, spread_sem, qs, qr, *gather
 ):
     d, s, section = lax.axis_index("dp"), lax.axis_index("seq"), lax.axis_index("section")
     known = x_ref.shape[0]
-    count = pick_out.shape[2] // CAP
-    rows = pick_out.shape[3]
+    count = pick_0.shape[1] // CAP
+    rows = pick_0.shape[2]
     land = gather[0]
     part = both.at[pl.ds(pl.multiple_of(section * known, known), known)]
     swaps = Carried((None, None), (x_ref, group_ref), (part, groups.at[section]), carry_sem)
@@ -505,16 +518,15 @@
     expert = lax.broadcasted_iota(jnp.int32, (EXPERTS, rows), 0)
     lane = lax.broadcasted_iota(jnp.int32, (rows, count * CAP), 1)
 
-    @pl.loop(0, 2)
-    def _(layer):
+    def tables(layer, pick_out, pick_t_out, chosen_out):
         @pl.loop(0, 16)
         def _(b):
-            paths = land[b, pl.ds(pl.multiple_of(layer * known, 16), 16), :].astype(jnp.float32)
+            paths = land[b, layer * known : layer * known + 16, :].astype(jnp.float32)
             paths = jnp.where(section == 0, paths[:TOP_K], paths[TOP_K:]).astype(jnp.int32)
             chosen = expert == paths[0:1]
             for k in range(1, TOP_K):
                 chosen = chosen | (expert == paths[k : k + 1])
-            chosen_out[layer, b] = low(chosen)
+            chosen_out[b] = low(chosen)
             mine = [
                 jnp.max((paths == first_expert + j).astype(jnp.float32), axis=0, keepdims=True)
                 for j in range(count)
@@ -523,24 +535,23 @@
             place = jnp.where(mine > 0.5, dot(low(mine), before), -10000.0)
             places[...] = place
             for j in range(count):
-                pick_out[layer, b, j * CAP : (j + 1) * CAP, :] = low(
+                pick_out[b, j * CAP : (j + 1) * CAP, :] = low(
                     slot == place[j : j + 1].astype(jnp.int32)
                 )
             turned = places[...].T.astype(jnp.int32)
             pick_t = turned[:, 0:1] == lane
             for j in range(1, count):
                 pick_t = pick_t & (lane < j * CAP) | (turned[:, j : j + 1] == lane - j * CAP)
-            pick_t_out[layer, b] = low(pick_t)
+            pick_t_out[b] = low(pick_t)
 
         depth = small_out.shape[2] // 16
         for b in range(16):
-            small = land[b, pl.ds(pl.multiple_of(layer * known + 16, 16), known - 16), :]
+            small = land[b, layer * known + 16 : (layer + 1) * known, :]
             small_out[layer, :, b * depth : (b + 1) * depth] = small[:, :depth]
 
-        @pl.when(layer == 0)
-        def _():
-            hop(2)
-
+    tables(0, pick_0, pick_t_0, chosen_0)
+    hop(2)
+    tables(1, pick_1, pick_t_1, chosen_1)
     hop(3)
     spreads[1].finish()
     layer_1 = pltpu.make_async_copy(parts.at[1], parts_out, lsem.at[0])
@@ -568,16 +579,19 @@
     return pl.pallas_call(
         prepare_kernel,
         out_shape=[
-            jax.ShapeDtypeStruct((2, 16, count * CAP, rows), bf),
-            jax.ShapeDtypeStruct((2, 16, rows, count * CAP), bf),
-            jax.ShapeDtypeStruct((2, 16, EXPERTS, rows), bf),
+            jax.ShapeDtypeStruct((16, count * CAP, rows), bf),
+            jax.ShapeDtypeStruct((16, count * CAP, rows), bf),
+            jax.ShapeDtypeStruct((16, rows, count * CAP), bf),
+            jax.ShapeDtypeStruct((16, rows, count * CAP), bf),
+            jax.ShapeDtypeStruct((16, EXPERTS, rows), bf),
+            jax.ShapeDtypeStruct((16, EXPERTS, rows), bf),
             jax.ShapeDtypeStruct((2, known - 16, 16 * depth), bf),
             jax.ShapeDtypeStruct((4,) + group.shape, bf),
             jax.ShapeDtypeStruct(group.shape, bf),
             jax.ShapeDtypeStruct(share_shape(gate), bf),
         ],
         in_specs=[anywhere] * 3,
-        out_specs=[near] * 4 + [anywhere] * 3,
+        out_specs=[near] * 7 + [anywhere] * 3,
         scratch_shapes=[
             pltpu.VMEM((2 * known, width), bf),
             pltpu.VMEM((8, rows), jnp.float32),
@@ -810,6 +824,20 @@
     def finish(self):
         for k in range(len(self.outs)):
             self.store(self.count - 1, k).wait()
+
+
+def far_first(d, q):
+    inner = (d % 3 + 2) // 3
+    base = 3 - q + inner * (q // 2) * (2 * q - 5)
+    mirrored = d // 2
+    return base * (1 - 2 * mirrored) + 3 * mirrored
+
+
+def near_first(d, q):
+    inner = (d % 3 + 2) // 3
+    base = q + inner * (1 - q // 2) * (1 - 2 * q)
+    mirrored = d // 2
+    return base * (1 - 2 * mirrored) + 3 * mirrored
 
 
 def combine_kernel(sections, spreads, pairs, pick_ref, y_ref, *refs):
@@ -843,7 +871,7 @@
         return s ^ (2 * across) ^ other_core
 
     for i in range(4):
-        z = d ^ (3 - i)
+        z = far_first(d, i)
         for across in (1, 0):
             for other_core in (1, 0):
                 loaded(z * 4 + column(across, other_core)).start()
@@ -885,7 +913,7 @@
         )
 
     def start(i):
-        z, k = d ^ (3 - i // PIECES), i % PIECES
+        z, k = far_first(d, i // PIECES), i % PIECES
         sent[z, 1, rows(k), :] = low(partial_sum(z, k, 1, 1))
         core_copy(z, k, 1).start()
         total = partial_sum(z, k, 1, 0)
@@ -910,7 +938,7 @@
         if work:
             work.step(i)
 
-        z, k = d ^ (3 - i // PIECES), i % PIECES
+        z, k = far_first(d, i // PIECES), i % PIECES
         total = partial_sum(z, k, 0, 0)
         core_copy(z, k, 0).wait_recv()
         total = total + core_in[z, 0, rows(k), :].astype(jnp.float32)
@@ -1914,7 +1942,7 @@
     if has_kernels():
         small = jnp.pad(small, ((0, -small.shape[0] % 16), (0, 256 - depth)))
         paths = low(jnp.transpose(paths, (0, 2, 1)).reshape(2 * TOP_K, -1))
-        picks, picks_t, chosens, small, qkv_first, qkv_second, other_gate = prepare(
+        *tables, small, qkv_first, qkv_second, other_gate = prepare(
             jnp.concatenate([paths, small], axis=0),
             own_group,
             own_experts[0],
@@ -1923,7 +1951,7 @@
             depth,
             13,
         )
-        pickings = [(chosens[n], picks[n], picks_t[n], first_expert) for n in range(2)]
+        pickings = [(tables[4 + n], tables[n], tables[2 + n], first_expert) for n in range(2)]
         qkv_second = lax.all_gather(
             qkv_second.reshape(seq * depth, -1), "dp", axis=0, tiled=True
         )
@@ -2051,9 +2079,7 @@
         (1, middle_grad),
         spread=handed(0, first_gate, second_gate),
     )
-    second_slots, *first_dense, second_dense[0], second_dense[1] = lax.optimization_barrier(
-        (second_slots, *first_dense, *second_dense)
-    )
+    second_slots, *first_dense = lax.optimization_barrier((second_slots, *first_dense))
     first_dense = dp_sums(first_dense)
     sums, (first_down, up_rows) = token_sums(
         pickings[1][2],

time: 1440 us -> 1400 us (0.972)
  Pallas kernels: 1240 us -> 1190 us
  waiting for transfers between devices: 21.8 us -> 36.3 us
    pallas_call x4, Pallas kernels: 461 us -> 419 us  [combine(): pl.pallas_call(kernel, out_shape=[jax.ShapeDtypeStruct((rows, width), jnp...]
  transfers between devices with their start and end apart: 11 -> 11, of which waited for: 2 -> 3; matrix products, arithmetic and copies ran while one was open for 5% -> 4% of each run, Pallas kernels for 49% -> 43%
where the time goes in v11:
time: 1400 us; the launch traced here: 1390 us
  Pallas kernels  1190 us (85%)
  other arithmetic  61.7 us (4%)
  waiting for transfers between devices  36.3 us (3%)
  matrix products  34.3 us (2%)
  local copies, waits for them, and re-layouts  33.2 us (2%)
  starting transfers between devices  21.2 us (2%)
  between operations  15.5 us (1%)
    pallas_call x4, Pallas kernels, combine(): pl.pallas_call(kernel, out_shape=[jax.ShapeDtypeStruct((rows, width), jnp...  419 us
    pallas_call x2, Pallas kernels, expert_forward(): pl.pallas_call(kernel, out_shape=shapes, in_specs=[anywhere, near, near,...  184 us
    pallas_call x2, Pallas kernels, expert_backward(): pl.pallas_call(kernel, out_shape=[jax.ShapeDtypeStruct(*result) for resul...  163 us
    pallas_call x2, Pallas kernels, attention_backward_call(): pl.pallas_call(kernel, out_shape=[jax.ShapeDtypeStruct(*result) for resul...  151 us
    pallas_call x2, Pallas kernels, attention_forward_call(): pl.pallas_call(kernel, out_shape=[jax.ShapeDtypeStruct(*result) for resul...  127 us
    pallas_call x1, Pallas kernels, prepare(): pl.pallas_call(prepare_kernel, out_shape=[jax.ShapeDtypeStruct((16, count...  87.9 us
    pallas_call x1, Pallas kernels, last_exchange(): pl.pallas_call(kernel, out_shape=[jax.ShapeDtypeStruct(parts_shape(downs[...  59.2 us
  transfers between devices with their start and end apart: 11, of which 3 were waited for; matrix products, arithmetic and copies ran while one was open for 4% of the time, Pallas kernels for 43%

profile of v11, /device:TPU:16, one launch (start us, length us, event | category | flops | bytes accessed | tf_op | source)
XLA Modules:
  0.0 1393.4 jit_solution(5408247841001630598)
XLA Ops:
  7.3 3.3 collective-permute-start
  10.6 13.6 collective-permute-done
  25.7 8.1 collective-permute-done.1
  36.5 87.9 %prepare.1 = (bf16[16,160,256]{2,1,0:T(8,128)(2,1)}, bf16[16,160,256]{2,1,0:T(8,128)(2,1)}, bf16[16,256,160]{2,1,0:T(8,128)(2,1)}, bf16[16,256,160]{2,1,0:T(8,12...) custom-call(bf16[64,256]{1,0:T(8,128)(2,1)} %pad_maximum_fusion.2.x_, ...), custom_call_target="tpu_custom_call" | custom-call | flops 80000000000 | bytes 100000000 | tf_op jit(solution)/shard_map/prepare/pallas_call | solution.py:579
  131.8 73.7 %attention_forward.2 = (f32[256,1536]{1,0:T(8,128)}, bf16[4,256,1536]{2,1,0:T(8,128)(2,1)}, bf16[10,1024,64]{2,1,0:T(8,128)(2,1)}, f32[8,1024]{1,0:T(8,128)}, bf...) custom-call(bf16[256,1536]{1,0:T(8,128)(2,1)} %fusion.4.refs_0_, bf16[1536,640]{1,0:T(8,128)(2,1)} %bitcast.160, ...), custom_call_target="tpu_custom_call" | custom-call | flops 80000000000 | bytes 100000000 | tf_op jit(solution)/shard_map/attention_forward/pallas_call | solution.py:1376
  209.4 101.3 %expert_forward.2 = (bf16[2,1280,1536]{2,1,0:T(8,128)(2,1)}, bf16[2,1280,512]{2,1,0:T(8,128)(2,1)}, bf16[2,1280,512]{2,1,0:T(8,128)(2,1)}, bf16[2,1280,512]{2,1,...) custom-call(bf16[256,1536]{1,0:T(8,128)(2,1)} %multiply_convert_fusion.2.ref, ...), custom_call_target="tpu_custom_call" | custom-call | flops 80000000000 | bytes 100000000 | tf_op jit(solution)/shard_map/expert_forward/pallas_call | solution.py:757
  310.8 85.7 %combine.4 = f32[256,1536]{1,0:T(8,128)} custom-call(bf16[16,256,160]{2,1,0:T(8,128)(2,1)} %get-tuple-element.100.refs_0_, bf16[16,160,1536]{2,1,0:T(8,128)(2,1)} %get-tuple-element.105.refs_1_), custom_call_target="tpu_custom_call" | custom-call | flops 80000000000 | bytes 100000000 | tf_op jit(solution)/shard_map/combine/pallas_call | solution.py:1038
  402.1 53.4 %attention_forward.3 = (f32[256,1536]{1,0:T(8,128)}, bf16[4,256,1536]{2,1,0:T(8,128)(2,1)}, bf16[10,1024,64]{2,1,0:T(8,128)(2,1)}, f32[8,1024]{1,0:T(8,128)}, bf...) custom-call(bf16[256,1536]{1,0:T(8,128)(2,1)} %multiply_convert_fusion.1.refs_0_, ...), custom_call_target="tpu_custom_call" | custom-call | flops 80000000000 | bytes 100000000 | tf_op jit(solution)/shard_map/attention_forward/pallas_call | solution.py:1376
  460.2 83.0 %expert_forward.3 = (bf16[2,1280,1536]{2,1,0:T(8,128)(2,1)}, bf16[2,1280,512]{2,1,0:T(8,128)(2,1)}, bf16[2,1280,512]{2,1,0:T(8,128)(2,1)}, bf16[2,1280,512]{2,1,...) custom-call(bf16[256,1536]{1,0:T(8,128)(2,1)} %copy-done.17, ...), custom_call_target="tpu_custom_call" | custom-call | flops 80000000000 | bytes 100000000 | tf_op jit(solution)/shard_map/expert_forward/pallas_call | solution.py:757
  543.3 84.0 %expert_backward.2 = (bf16[2,1280,1536]{2,1,0:T(8,128)(2,1)}, bf16[2,1280,512]{2,1,0:T(8,128)(2,1)}, bf16[2,1280,512]{2,1,0:T(8,128)(2,1)}, f32[2,1280,128]{2,1,0:T(8,128)}, bf16[16,160,1536]{2,1,0:T(8,128)(2,1)}) custom-call(bf16[256,1536]{1,0:T(8,128)(2,1)} %dynamic-slice_bitcast_fusion.refs_0_, bf16[16,160,256]{2,1,0:T(8,128)(2,1)} %get-tuple-element.109.refs_1_, ...), custom_call_target="tpu_custom_call" | custom-call | flops 80000000000 | bytes 100000000 | tf_op jit(solution)/shard_map/expert_backward/pallas_call | solution.py:1166
  630.4 8.6 all-to-all-start
  639.1 87.1 %combine.5 = (f32[256,1536]{1,0:T(8,128)}, bf16[2,1536,512]{2,1,0:T(8,128)(2,1)}, bf16[2,1536,512]{2,1,0:T(8,128)(2,1)}, bf16[2,512,1536]{2,1,0:T(8,128)(2,1)}) custom-call(bf16[16,256,160]{2,1,0:T(8,128)(2,1)} %get-tuple-element.108.refs_0_, bf16[16,160,1536]{2,1,0:T(8,128)(2,1)} %get-tuple-element.117.refs_1_, ...), custom_call_target="tpu_custom_call" | custom-call | flops 80000000000 | bytes 100000000 | tf_op jit(solution)/shard_map/combine/pallas_call | solution.py:1038
  727.3 2.8 multiply_reduce_fusion.2
  731.6 71.7 %attention_backward.2 = (f32[256,1536]{1,0:T(8,128)}, bf16[4,256,1536]{2,1,0:T(8,128)(2,1)}, bf16[1024,640]{1,0:T(8,128)(2,1)}, bf16[2,1536,512]{2,1,0:T(8,128)(2,1)}) custom-call(bf16[256,1536]{1,0:T(8,128)(2,1)} %fusion.29.refs_0_, bf16[1536,640]{1,0:T(8,128)(2,1)} %all-gather.6.cloned.1.call-done.refs_1_, ...), custom_call_target="tpu_custom_call" | custom-call | flops 80000000000 | bytes 100000000 | tf_op jit(solution)/shard_map/attention_backward/pallas_call | solution.py:1523
  805.8 3.4 fusion.32
  809.1 79.3 %expert_backward.3 = (bf16[2,1280,1536]{2,1,0:T(8,128)(2,1)}, bf16[2,1280,512]{2,1,0:T(8,128)(2,1)}, bf16[2,1280,512]{2,1,0:T(8,128)(2,1)}, f32[2,1280,128]{2,1,...) custom-call(bf16[256,1536]{1,0:T(8,128)(2,1)} %get-tuple-element.246.refs_0_, ...), custom_call_target="tpu_custom_call" | custom-call | flops 80000000000 | bytes 100000000 | tf_op jit(solution)/shard_map/expert_backward/pallas_call | solution.py:1166
  891.5 7.4 all-to-all-start.1
  899.0 10.1 convolution_convert_fusion.refs_2_.refs_9_
  911.5 3.6 convolution_convert_fusion.2
  917.0 87.2 %combine.6 = (f32[256,1536]{1,0:T(8,128)}, bf16[2,1536,512]{2,1,0:T(8,128)(2,1)}, bf16[2,512,1536]{2,1,0:T(8,128)(2,1)}, bf16[2,1536,512]{2,1,0:T(8,128)(2,1)}, bf16[2,512,1536]{2,1,0:T(8,128)(2,1)}) custom-call(bf16[16,256,160]{2,1,0:T(8,128)(2,1)} %get-tuple-element.100.refs_0_, bf16[16,160,1536]{2,1,0:T(8,128)(2,1)} %get-tuple-element.137.refs_1_, ...), custom_call_target="tpu_custom_call" | custom-call | flops 80000000000 | bytes 100000000 | tf_op jit(solution)/shard_map/combine/pallas_call | solution.py:1038
  1008.6 79.1 %attention_backward.3 = (f32[256,1536]{1,0:T(8,128)}, bf16[4,256,1536]{2,1,0:T(8,128)(2,1)}, bf16[1024,640]{1,0:T(8,128)(2,1)}, bf16[2,1536,512]{2,1,0:T(8,128)(...) custom-call(bf16[256,1536]{1,0:T(8,128)(2,1)} %get-tuple-element.244.refs_0_, bf16[1536,640]{1,0:T(8,128)(2,1)} %bitcast.161, ...), custom_call_target="tpu_custom_call" | custom-call | flops 80000000000 | bytes 100000000 | tf_op jit(solution)/shard_map/attention_backward/pallas_call | solution.py:1523
  1089.7 4.3 convolution_convert_fusion.3
  1094.0 4.5 convolution_convert_fusion.1
  1100.2 4.3 copy.82
  1105.1 4.3 copy.84
  1110.2 158.5 %combine.7 = (f32[256,1536]{1,0:T(8,128)}, bf16[2,512,1536]{2,1,0:T(8,128)(2,1)}, bf16[4,2,384,512]{3,2,1,0:T(8,128)(2,1)}) custom-call(bf16[16,256,160]{2,1,0:T(8,128)(2,1)} %get-tuple-element.108.refs_0_, bf16[16,160,1536]{2,1,0:T(8,128)(2,1)} %get-tuple-element.159.refs_1_, bf16[2,512,1536]{2,1,0:T(8,128)(2,1)} %get-tuple-element.160.refs_2_.refs_0_, ...), custom_call_target="tpu_custom_call" | custom-call | flops 80000000000 | bytes 100000000 | tf_op jit(solution)/shard_map/combine/pallas_call | solution.py:1038
  1268.8 3.2 fusion.9.refs_9_
  1271.9 8.6 bitcast_convert_fusion.1
  1288.4 13.4 reduce-scatter.11.cloned.1.call-done
  1303.5 59.2 %last_exchange.1 = (bf16[4,2,128,1536]{3,2,1,0:T(8,128)(2,1)}, bf16[4,96,768]{2,1,0:T(8,128)(2,1)}, bf16[96,1536]{1,0:T(8,128)(2,1)}, f32[256,1536]{1,0:T(8,128)}, f32[256,1536]{1,0:T(8,128)}) custom-call(bf16[2,512,1536]{2,1,0:T(8,128)(2,1)} %get-tuple-element.160.refs_2_.refs_0_, bf16[2,512,1536]{2,1,0:T(8,128)(2,1)} %get-tuple-element.139.refs_3_.refs_1_, ...), custom_call_target="tpu_custom_call" | custom-call | tf_op jit(solution)/shard_map/last_exchange/pallas_call | solution.py:1616
  1366.2 3.6 bitcast_convert_fusion
  1379.2 3.3 select_bitcast_fusion.1
  (263 shorter events, 76.5 us)
Async XLA Ops:
  7.2 124.6 %all-gather.4.cloned.1.call-start = ((), (), s32[]{:S(2)}) async-start(), calls=%async_computation.6 | async-start | bytes 1474560 | tf_op jit(solution)/shard_map/all_gather | solution.py:1977
  7.3 16.9 %collective-permute-start = (bf16[96,1536]{1,0:T(8,128)(2,1)}, bf16[96,1536]{1,0:T(8,128)(2,1)S(1)}, u32[]{:S(2)}, u32[]{:S(2)}) collective-permute-start(bf16[96,1536]{1,0:T(8,128)(2,1)} %bitcast.155), channel_id=1, source_target_pairs={{0,0},{1,4},{2,8},{3,12},{4,1},{5,5},{6,9},{7,13},{8,2},{9,6},{10,... | collective-permute-start | bytes 884744 | tf_op jit(solution)/shard_map/ppermute | solution.py:1921
  24.1 9.6 collective-permute-start.1
  34.6 367.5 %all-gather.8.cloned.1.call-start = ((), (), s32[]{:S(2)}) async-start(), calls=%async_computation.8 | async-start | bytes 1474560 | tf_op jit(solution)/shard_map/all_gather | solution.py:1977
  36.5 365.7 %all-gather.6.cloned.1.call-start = ((), (), s32[]{:S(2)}) async-start(), calls=%async_computation.7 | async-start | bytes 2457600 | tf_op jit(solution)/shard_map/all_gather | solution.py:1955
  36.5 91.1 %copy-start.13 = (bf16[2,1,256,1536]{3,2,1,0:T(8,128)(2,1)S(1)}, bf16[2,1,256,1536]{3,2,1,0:T(8,128)(2,1)}, u32[]{:S(2)}) copy-start(bf16[2,1,256,1536]{3,2,1,0:T(8,128)(2,1)} %param.21) | copy-start | bytes 4718596
  126.0 81.2 %copy-start.38 = (f32[1536]{0:T(1024)}, f32[1536]{0:T(1024)S(1)}, u32[]{:S(2)}) copy-start(f32[1536]{0:T(1024)S(1)} %get-tuple-element.240) | copy-start | bytes 18436
  207.2 103.5 %copy-start.60 = (f32[256]{0:T(256)}, f32[256]{0:T(256)S(1)}, u32[]{:S(2)}) copy-start(f32[256]{0:T(256)S(1)} %get-tuple-element.252) | copy-start | bytes 3076
  310.7 85.8 %copy-start.15 = (bf16[256,1536]{1,0:T(8,128)(2,1)S(1)}, bf16[256,1536]{1,0:T(8,128)(2,1)}, u32[]{:S(2)}) copy-start(bf16[256,1536]{1,0:T(8,128)(2,1)} %multiply_convert_fusion.2.refs_0_) | copy-start | bytes 2359300
  310.7 85.8 %copy-start.27 = (bf16[2,48,1536]{2,1,0:T(8,128)(2,1)S(1)}, bf16[2,48,1536]{2,1,0:T(8,128)(2,1)}, u32[]{:S(2)}) copy-start(bf16[2,48,1536]{2,1,0:T(8,128)(2,1)} %get-tuple-element.97) | copy-start | bytes 884740
  310.8 88.0 %copy-start.7 = (f32[256,1536]{1,0:T(8,128)S(1)}, f32[256,1536]{1,0:T(8,128)}, u32[]{:S(2)}) copy-start(f32[256,1536]{1,0:T(8,128)} %copy-done.6) | copy-start | bytes 4718596
  630.4 95.9 %all-to-all-start = ((f32[16,2,256]{2,1,0:T(2,128)}), f32[16,2,256]{2,1,0:T(2,128)S(1)}, u32[]{:S(2)}, u32[]{:S(2)}) async-start(f32[16,2,256]{2,1,0:T(2,128)} %fusion.1), calls=%async_computation | async-start | bytes 65536 | tf_op jit(solution)/shard_map/all_to_all | solution.py:1821
  639.1 87.2 %copy-start.30 = (f32[32,256]{1,0:T(8,128)S(1)}, f32[32,256]{1,0:T(8,128)}, u32[]{:S(2)}) copy-start(f32[32,256]{1,0:T(8,128)} %get-tuple-element.270) | copy-start | bytes 98308
  639.1 87.2 %copy-start.54 = (f32[256]{0:T(256)S(1)}, f32[256]{0:T(256)}, u32[]{:S(2)}) copy-start(f32[256]{0:T(256)} %get-tuple-element.269) | copy-start | bytes 3076
  639.1 87.3 %copy-start.18 = (bf16[256,1536]{1,0:T(8,128)(2,1)S(1)}, bf16[256,1536]{1,0:T(8,128)(2,1)}, u32[]{:S(2)}) copy-start(bf16[256,1536]{1,0:T(8,128)(2,1)} %copy-done.17) | copy-start | bytes 2359300
  639.1 88.2 %copy-start.1 = (f32[256,1536]{1,0:T(8,128)S(1)}, f32[256,1536]{1,0:T(8,128)}, u32[]{:S(2)}) copy-start(f32[256,1536]{1,0:T(8,128)} %copy-done) | copy-start | bytes 4718596
  639.1 88.2 %copy-start.35 = (f32[1536]{0:T(1024)S(1)}, f32[1536]{0:T(1024)}, u32[]{:S(2)}) copy-start(f32[1536]{0:T(1024)} %get-tuple-element.238) | copy-start | bytes 18436
  639.1 88.2 %copy-start.45 = (f32[256]{0:T(256)S(1)}, f32[256]{0:T(256)}, u32[]{:S(2)}) copy-start(f32[256]{0:T(256)} %copy-done.44) | copy-start | bytes 3076
  891.5 25.3 %all-to-all-start.1 = ((f32[16,2,256]{2,1,0:T(2,128)}), f32[16,2,256]{2,1,0:T(2,128)S(1)}, u32[]{:S(2)}, u32[]{:S(2)}) async-start(f32[16,2,256]{2,1,0:T(2,128)} %fusion), calls=%async_computation.1 | async-start | bytes 65536 | tf_op jit(solution)/shard_map/all_to_all | solution.py:1821
  898.9 381.6 %reduce-scatter.13.cloned.1.call-start = ((), (), s32[]{:S(2)}) async-start(), calls=%async_computation.11 | async-start | bytes 2949120
  917.0 87.3 %copy-start.16 = (bf16[256,1536]{1,0:T(8,128)(2,1)S(1)}, bf16[256,1536]{1,0:T(8,128)(2,1)}, u32[]{:S(2)}) copy-start(bf16[256,1536]{1,0:T(8,128)(2,1)} %multiply_convert_fusion.2.refs_0_) | copy-start | bytes 2359300
  917.0 87.5 %copy-start.8 = (f32[256,1536]{1,0:T(8,128)S(1)}, f32[256,1536]{1,0:T(8,128)}, u32[]{:S(2)}) copy-start(f32[256,1536]{1,0:T(8,128)} %copy-done.6) | copy-start | bytes 4718596
  917.0 87.5 %copy-start.39 = (f32[1536]{0:T(1024)S(1)}, f32[1536]{0:T(1024)}, u32[]{:S(2)}) copy-start(f32[1536]{0:T(1024)} %copy-done.38) | copy-start | bytes 18436
  917.0 87.5 %copy-start.47 = (f32[256]{0:T(256)S(1)}, f32[256]{0:T(256)}, u32[]{:S(2)}) copy-start(f32[256]{0:T(256)} %copy-done.46) | copy-start | bytes 3076
  1008.6 79.1 %copy-start.14 = (bf16[2,1,256,1536]{3,2,1,0:T(8,128)(2,1)S(1)}, bf16[2,1,256,1536]{3,2,1,0:T(8,128)(2,1)}, u32[]{:S(2)}) copy-start(bf16[2,1,256,1536]{3,2,1,0:T(8,128)(2,1)} %param.21) | copy-start | bytes 4718596
  1008.6 79.1 %copy-start.37 = (f32[1536]{0:T(1024)S(1)}, f32[1536]{0:T(1024)}, u32[]{:S(2)}) copy-start(f32[1536]{0:T(1024)} %copy-done.36) | copy-start | bytes 18436
  1008.6 79.1 %copy-start.56 = (f32[256]{0:T(256)S(1)}, f32[256]{0:T(256)}, u32[]{:S(2)}) copy-start(f32[256]{0:T(256)} %copy-done.55) | copy-start | bytes 3076
  1104.5 177.4 %reduce-scatter.9.cloned.1.call-start = ((), (), s32[]{:S(2)}) async-start(), calls=%async_computation.9 | async-start | bytes 1474560 | tf_op jit(solution)/shard_map/reduce_scatter | solution.py:2002
  1105.1 179.6 %reduce-scatter.15.cloned.1.call-start = ((), (), s32[]{:S(2)}) async-start(), calls=%async_computation.12 | async-start | bytes 2949120
  1109.4 192.3 %reduce-scatter.11.cloned.1.call-start = ((), (), s32[]{:S(2)}) async-start(), calls=%async_computation.10 | async-start | bytes 1474560 | tf_op jit(solution)/shard_map/reduce_scatter | solution.py:2002
  1110.2 158.6 %copy-start.59 = (f32[256]{0:T(256)S(1)}, f32[256]{0:T(256)}, u32[]{:S(2)}) copy-start(f32[256]{0:T(256)} %copy-done.58) | copy-start | bytes 3076
  1110.2 158.6 %copy-start.19 = (f32[256,1536]{1,0:T(8,128)S(1)}, f32[256,1536]{1,0:T(8,128)}, u32[]{:S(2)}) copy-start(f32[256,1536]{1,0:T(8,128)} %get-tuple-element.156) | copy-start | bytes 4718596
  (54 other events, 546.5 us)
Sparse Core Ops, SparseCore 0:
  34.7 33.8 all-gather.3
  70.8 34.6 all-gather.7
  124.6 45.4 all-gather.5
  1104.6 51.5 reduce-scatter.12
  1158.4 46.7 reduce-scatter.8
  1207.9 61.7 reduce-scatter.14
  1272.0 29.6 reduce-scatter.10

commit v12 on v11

--- a/solution.py
+++ b/solution.py
@@ -347,112 +347,128 @@
     ]
 
 
-def gather_blocks(x_ref, scratch, compute, carried=None, first=None, spread=False):
-    land, lsem, zs, zr, ys, yr, cs, cr = scratch
-    d, s = lax.axis_index("dp"), lax.axis_index("seq")
-
-    def place(z, column):
-        return land.at[z * 4 + column]
-
-    def z_copy(src, z, right):
-        target = d + 1 if right else d - 1
-        return remote(src, place(z, s), zs.at[int(right), z], zr.at[z], dp=target)
-
-    def y_copy(src, z):
-        return remote(src, place(z, s), ys.at[z], yr.at[z], seq=s ^ 2)
-
-    def core_copy(src, z, across):
-        column = s ^ 2 if across else s
-        return remote(src, place(z, column), cs.at[z, across], cr.at[z, across], seq=s ^ 1)
-
-    greet(d, s, None if carried is None else carried.section, spread)
-    if first is not None:
-        first()
-    own = pltpu.make_async_copy(x_ref, place(d, s), lsem)
-    own.start()
-    if carried is not None and first is None:
+class Gather:
+    def __init__(self, scratch):
+        self.land, self.lsem, self.zs, self.zr, self.ys, self.yr, self.cs, self.cr = scratch
+        self.d, self.s = lax.axis_index("dp"), lax.axis_index("seq")
+
+    def place(self, z, column):
+        return self.land.at[z * 4 + column]
+
+    def z_copy(self, src, z, right):
+        target = self.d + 1 if right else self.d - 1
+        return remote(src, self.place(z, self.s), self.zs.at[int(right), z], self.zr.at[z], dp=target)
+
+    def y_copy(self, src, z):
+        return remote(src, self.place(z, self.s), self.ys.at[z], self.yr.at[z], seq=self.s ^ 2)
+
+    def core_copy(self, src, z, across):
+        column = self.s ^ 2 if across else self.s
+        return remote(
+            src, self.place(z, column), self.cs.at[z, across], self.cr.at[z, across], seq=self.s ^ 1
+        )
+
+    def begin(self, x_ref):
+        d = self.d
+        own = pltpu.make_async_copy(x_ref, self.place(d, self.s), self.lsem)
+        own.start()
+
+        @pl.when(d < 3)
+        def _():
+            self.z_copy(x_ref, d, True).start()
+
+        @pl.when(d > 0)
+        def _():
+            self.z_copy(x_ref, d, False).start()
+
+        self.y_copy(x_ref, d).start()
+        self.core_copy(x_ref, d, 0).start()
+        own.wait()
+
+    def send_on(self, q):
+        following = near_first(self.d, q)
+        here = self.place(following, self.s)
+        self.y_copy(here, following).start()
+        self.core_copy(here, following, 0).start()
+
+    def step(self, i):
+        d, s, place = self.d, self.s, self.place
+
+        @pl.when(i < 3)
+        def _():
+            early = (d > 0) & (d < 3) & (i > 0)
+
+            @pl.when(early)
+            def _():
+                self.send_on(i + 1)
+
+            left, right = d - (i + 1), d + (i + 1)
+
+            @pl.when(left >= 0)
+            def _():
+                self.z_copy(place(left, s), left, True).wait_recv()
+
+                @pl.when(d < 3)
+                def _():
+                    self.z_copy(place(left, s), left, True).start()
+
+            @pl.when(right <= 3)
+            def _():
+                self.z_copy(place(right, s), right, False).wait_recv()
+
+                @pl.when(d > 0)
+                def _():
+                    self.z_copy(place(right, s), right, False).start()
+
+            @pl.when(jnp.logical_not(early))
+            def _():
+                self.send_on(i + 1)
+
+        z = near_first(d, i)
+        self.y_copy(place(z, s ^ 2), z).wait_recv()
+        self.core_copy(place(z, s ^ 2), z, 1).start()
+        self.core_copy(place(z, s ^ 1), z, 0).wait_recv()
+        self.core_copy(place(z, s ^ 3), z, 1).wait_recv()
+        return z
+
+    def finish(self):
+        d, s, place = self.d, self.s, self.place
+        for z in range(4):
+
+            @pl.when((z <= d) & (d < 3))
+            def _():
+                self.z_copy(place(z, s), z, True).wait_send()
+
+            @pl.when((z >= d) & (d > 0))
+            def _():
+                self.z_copy(place(z, s), z, False).wait_send()
+
+            self.y_copy(place(z, s), z).wait_send()
+            self.core_copy(place(z, s), z, 0).wait_send()
+            self.core_copy(place(z, s), z, 1).wait_send()
+
+
+def gather_blocks(x_ref, scratch, compute, carried=None):
+    gather = Gather(scratch)
+    greet(gather.d, gather.s, None if carried is None else carried.section)
+    gather.begin(x_ref)
+    if carried is not None:
         carried.start()
-
-    @pl.when(d < 3)
-    def _():
-        z_copy(x_ref, d, True).start()
-
-    @pl.when(d > 0)
-    def _():
-        z_copy(x_ref, d, False).start()
-
-    y_copy(x_ref, d).start()
-    core_copy(x_ref, d, 0).start()
-    own.wait()
-
-    inner = (d > 0) & (d < 3)
-
-    def send_on(q):
-        following = near_first(d, q)
-        y_copy(place(following, s), following).start()
-        core_copy(place(following, s), following, 0).start()
 
     @pl.loop(0, 4)
     def _(i):
-        @pl.when(i < 3)
-        def _():
-            early = inner & (i > 0)
-
-            @pl.when(early)
-            def _():
-                send_on(i + 1)
-
-            left, right = d - (i + 1), d + (i + 1)
-
-            @pl.when(left >= 0)
-            def _():
-                z_copy(place(left, s), left, True).wait_recv()
-
-                @pl.when(d < 3)
-                def _():
-                    z_copy(place(left, s), left, True).start()
-
-            @pl.when(right <= 3)
-            def _():
-                z_copy(place(right, s), right, False).wait_recv()
-
-                @pl.when(d > 0)
-                def _():
-                    z_copy(place(right, s), right, False).start()
-
-            @pl.when(jnp.logical_not(early))
-            def _():
-                send_on(i + 1)
-
-        z = near_first(d, i)
-        y_copy(place(z, s ^ 2), z).wait_recv()
-        core_copy(place(z, s ^ 2), z, 1).start()
-        core_copy(place(z, s ^ 1), z, 0).wait_recv()
-        core_copy(place(z, s ^ 3), z, 1).wait_recv()
-        compute(z)
-
-    for z in range(4):
-
-        @pl.when((z <= d) & (d < 3))
-        def _():
-            z_copy(place(z, s), z, True).wait_send()
-
-        @pl.when((z >= d) & (d > 0))
-        def _():
-            z_copy(place(z, s), z, False).wait_send()
-
-        y_copy(place(z, s), z).wait_send()
-        core_copy(place(z, s), z, 0).wait_send()
-        core_copy(place(z, s), z, 1).wait_send()
-    return land
+        compute(gather.step(i))
+
+    gather.finish()
 
 
 def prepare_kernel(
-    x_ref, group_ref, gate_ref,
-    pick_0, pick_1, pick_t_0, pick_t_1, chosen_0, chosen_1, small_out, qkv_out, parts_out, gate_out,
+    x_ref, group_ref, gate_ref, grad_ref,
+    pick_0, pick_1, pick_t_0, pick_t_1, chosen_0, chosen_1, small_out, qkv_out, parts_out, gate_out, grad_out,
     both, places, groups, parts, lsem, carry_sem, spread_sem, qs, qr, *gather
 ):
     d, s, section = lax.axis_index("dp"), lax.axis_index("seq"), lax.axis_index("section")
+    small_gather, grad_gather = Gather(gather[:8]), Gather([grad_out] + list(gather[8:]))
     known = x_ref.shape[0]
     count = pick_0.shape[1] // CAP
     rows = pick_0.shape[2]
@@ -509,8 +525,18 @@
             def _():
                 along(qkv_out.at[d + h], d + h, False).start()
 
-    gather_blocks(both, gather, lambda z: None, gates, first, True)
+    greet(d, s, section, True)
+    first()
+    small_gather.begin(both)
+    grad_gather.begin(grad_ref)
+
+    @pl.loop(0, 4)
+    def _(i):
+        small_gather.step(i)
+
+    small_gather.finish()
     hop(1)
+    grad_gather.step(0)
     first_expert = (d * 4 + s) * count
     before = lax.broadcasted_iota(jnp.int32, (rows, rows), 0)
     before = low(before < lax.broadcasted_iota(jnp.int32, (rows, rows), 1))
@@ -551,8 +577,12 @@
 
     tables(0, pick_0, pick_t_0, chosen_0)
     hop(2)
+    grad_gather.step(1)
     tables(1, pick_1, pick_t_1, chosen_1)
     hop(3)
+    grad_gather.step(2)
+    grad_gather.step(3)
+    grad_gather.finish()
     spreads[1].finish()
     layer_1 = pltpu.make_async_copy(parts.at[1], parts_out, lsem.at[0])
     layer_1.start()
@@ -571,8 +601,9 @@
     gates.finish()
 
 
-def prepare(x, group, gate, count, rows, depth, collective_id):
+def prepare(x, group, gate, grad, count, depth, collective_id):
     known, width = x.shape
+    rows = grad.shape[0]
     bf = jnp.bfloat16
     anywhere = pl.BlockSpec(memory_space=pl.ANY)
     near = pl.BlockSpec(memory_space=pltpu.VMEM)
@@ -589,9 +620,10 @@
             jax.ShapeDtypeStruct((4,) + group.shape, bf),
             jax.ShapeDtypeStruct(group.shape, bf),
             jax.ShapeDtypeStruct(share_shape(gate), bf),
+            jax.ShapeDtypeStruct((16,) + grad.shape, bf),
         ],
-        in_specs=[anywhere] * 3,
-        out_specs=[near] * 7 + [anywhere] * 3,
+        in_specs=[anywhere] * 4,
+        out_specs=[near] * 7 + [anywhere] * 4,
         scratch_shapes=[
             pltpu.VMEM((2 * known, width), bf),
             pltpu.VMEM((8, rows), jnp.float32),
@@ -603,13 +635,14 @@
             DMA((2, 4)),
             DMA((4,)),
         ]
-        + gather_scratch(2 * known, width),
+        + gather_scratch(2 * known, width)
+        + gather_scratch(*grad.shape)[1:],
         compiler_params=pltpu.CompilerParams(
             collective_id=collective_id, has_side_effects=True, vmem_limit_bytes=60 << 20
         ),
         cost_estimate=cost(),
         name="prepare",
-    )(x, group, gate)
+    )(x, group, gate, grad)
 
 
 def share(ref):
@@ -1077,6 +1110,7 @@
     rows_out, gate_out, up_out, term_out, y_out, *refs = refs
     targets, refs = refs[:kept], refs[kept:]
     wg, wu, wd, rows, gate, up, slot_gate, y, wsem, isem, osem, carry_sem, *gather = refs
+    gathered = len(x_ref.shape) == 3
     carried = Carried(sections, sources, targets, carry_sem)
     count = wg.shape[0]
     ready = pick_weights(
@@ -1101,7 +1135,7 @@
         ] + [pltpu.make_async_copy(y.at[pl.ds(z * 4, 4)], y_out.at[pl.ds(z * 4, 4)], osem.at[4, z])]
 
     def compute(z):
-        @pl.when(z == d)
+        @pl.when(z == (0 if gathered else d))
         def _():
             for k in range(3):
                 ready(k)
@@ -1136,8 +1170,23 @@
         for copy in outs(z):
             copy.start()
 
-    gather_blocks(x_ref, gather, compute, carried)
-    carried.finish()
+    if gathered:
+
+        def arriving(z):
+            part = pl.ds(z * 4, 4)
+            return pltpu.make_async_copy(x_ref.at[part], land.at[part], gather[1].at[z])
+
+        for z in range(4):
+            arriving(z).start()
+
+        @pl.loop(0, 4)
+        def _(z):
+            arriving(z).wait()
+            compute(z)
+
+    else:
+        gather_blocks(x_ref, gather, compute, carried)
+        carried.finish()
     for z in range(4):
         for copy in outs(z):
             copy.wait()
@@ -1145,7 +1194,8 @@
 
 def expert_backward(layer, x, pick, gate, up, slot_gate, own, other, collective_id, carry):
     count, width, units = share_shape(own[0])
-    rows = x.shape[0]
+    rows = x.shape[-2]
+    gathered = x.ndim == 3
     slots = 16 * CAP
     bf = jnp.bfloat16
     anywhere = pl.BlockSpec(memory_space=pl.ANY)
@@ -1172,9 +1222,11 @@
         scratch_shapes=[pltpu.VMEM(share_shape(weight), bf) for weight in own]
         + [pltpu.VMEM(*result) for result in results]
         + [DMA((3,)), DMA((3,)), DMA((5, 4)), DMA((max(1, len(arrays)), 2))]
-        + gather_scratch(rows, width),
+        + ([pltpu.VMEM(x.shape, bf), DMA((4,))] if gathered else gather_scratch(rows, width)),
         compiler_params=pltpu.CompilerParams(
-            collective_id=collective_id, has_side_effects=True, vmem_limit_bytes=60 << 20
+            collective_id=None if gathered else collective_id,
+            has_side_effects=not gathered,
+            vmem_limit_bytes=60 << 20,
         ),
         cost_estimate=cost(),
         name="expert_backward",
@@ -1788,7 +1840,7 @@
     return lax.all_to_all(parts, "seq", split_axis=0, concat_axis=0, tiled=True)
 
 
-def expert_gradients(number, layer_grad, saved, picking, experts, *carry):
+def expert_gradients(number, layer_grad, saved, picking, experts, *carry, grad_all=None):
     chosen, pick, pick_t, first_expert = picking
     own, other = experts
     count = pick.shape[1] // CAP
@@ -1796,7 +1848,7 @@
     slot_rows, gate_pre, up_pre, scaled, slot_gates = saved[-1]
     if has_kernels():
         slot_grads, gate_low, up_low, gate_term, slot_out, *received = expert_backward(
-            number, low(layer_grad), pick, gate_pre, up_pre, slot_gates, own, other, 4 + number, carry
+            number, low(layer_grad) if grad_all is None else grad_all, pick, gate_pre, up_pre, slot_gates, own, other, 4 + number, carry
         )
         gate_term = gate_term[:, :, :1]
     else:
@@ -1942,12 +1994,12 @@
     if has_kernels():
         small = jnp.pad(small, ((0, -small.shape[0] % 16), (0, 256 - depth)))
         paths = low(jnp.transpose(paths, (0, 2, 1)).reshape(2 * TOP_K, -1))
-        *tables, small, qkv_first, qkv_second, other_gate = prepare(
+        *tables, small, qkv_first, qkv_second, other_gate, top_all = prepare(
             jnp.concatenate([paths, small], axis=0),
             own_group,
             own_experts[0],
+            top_grad,
             count,
-            hidden_in.shape[2],
             depth,
             13,
         )
@@ -1965,6 +2017,7 @@
         paths = paths.reshape(2, dp * seq, -1, TOP_K)
         pickings = [routing(paths[n], first_expert, count) + (first_expert,) for n in range(2)]
         other_gate = swap(own_experts[0])
+        top_all = None
         other_group = swap(own_group)
         qkv_layers = []
         for number in range(2):
@@ -2037,24 +2090,24 @@
     )
     top_grad = top_grad.astype(jnp.float32)
     slot_out, gate_terms, products, _ = expert_gradients(
-        1, top_grad, second_saved, pickings[1], experts
+        1, top_grad, second_saved, pickings[1], experts, grad_all=top_all
     )
     sums, second_experts = token_sums(pickings[1][2], slot_out, 6, products=products)
-    middle_grad, second_dense, (second_gate,) = backward_layer(
-        1, top_grad, sums, gate_terms, second_saved, pickings[1], weights[1], (1, second_experts[0])
-    )
-    slot_out, gate_terms, products, (second_up,) = expert_gradients(
-        0, middle_grad, first_saved, pickings[0], experts, (1, second_experts[1])
+    middle_grad, second_dense, _ = backward_layer(
+        1, top_grad, sums, gate_terms, second_saved, pickings[1], weights[1]
+    )
+    slot_out, gate_terms, products, (second_gate,) = expert_gradients(
+        0, middle_grad, first_saved, pickings[0], experts, (1, second_experts[0])
     )
     (rows_in, (gate_low, up_low)), down_product = products
     gate_grad = low(each_dot("ecd,ecf->edf", rows_in, gate_low))
     slot_out, gate_grad, gate_terms = lax.optimization_barrier((slot_out, gate_grad, gate_terms))
-    sums, (first_gate, second_down, *first_experts) = token_sums(
+    sums, (first_gate, second_up, *first_experts) = token_sums(
         pickings[0][2],
         slot_out,
         7,
         (0, gate_grad),
-        (1, second_experts[2]),
+        (1, second_experts[1]),
         products=((rows_in, (up_low,)), down_product),
     )
     first_experts = [gate_grad, *first_experts]
@@ -2067,7 +2120,7 @@
             return (*own, *received)
         return [spread_rows(row_parts(low(summed(own, received)), kind))]
 
-    bottom_grad, first_dense, (first_up, other_middle, gate_rows) = backward_layer(
+    bottom_grad, first_dense, (first_up, second_down, gate_rows) = backward_layer(
         0,
         middle_grad,
         sums,
@@ -2076,16 +2129,18 @@
         pickings[0],
         weights[0],
         (0, first_experts[1]),
-        (1, middle_grad),
+        (1, second_experts[2]),
         spread=handed(0, first_gate, second_gate),
     )
-    second_slots, *first_dense = lax.optimization_barrier((second_slots, *first_dense))
+    second_slots, *dense = lax.optimization_barrier((second_slots, *first_dense, *second_dense))
+    first_dense, second_dense = dense[:2], dense[2:]
     first_dense = dp_sums(first_dense)
-    sums, (first_down, up_rows) = token_sums(
+    sums, (first_down, other_middle, up_rows) = token_sums(
         pickings[1][2],
         second_slots,
         8,
         (0, first_experts[2]),
+        (1, middle_grad),
         spread=handed(1, first_up, second_up),
     )
     sums, *first_dense = lax.optimization_barrier((sums, *first_dense))

time: 1400 us -> 1370 us (0.979)
  Pallas kernels: 1190 us -> 1170 us
  waiting for transfers between devices: 36.3 us -> 21.8 us
    pallas_call x1, Pallas kernels: 87.9 us -> 145 us  [prepare(): pl.pallas_call(prepare_kernel, out_shape=[jax.ShapeDtypeStruct((16, count...]
    pallas_call x2, Pallas kernels: 163 us -> 108 us  [expert_backward(): pl.pallas_call(kernel, out_shape=[jax.ShapeDtypeStruct(*result) for resul...]
    pallas_call x4, Pallas kernels: 419 us -> 395 us  [combine(): pl.pallas_call(kernel, out_shape=[jax.ShapeDtypeStruct((rows, width), jnp...]
  transfers between devices with their start and end apart: 11 -> 11, of which waited for: 3 -> 2; matrix products, arithmetic and copies ran while one was open for 4% -> 5% of each run, Pallas kernels for 43% -> 52%
where the time goes in v12:
time: 1370 us; the launch traced here: 1360 us
  Pallas kernels  1170 us (85%)
  other arithmetic  61 us (4%)
  local copies, waits for them, and re-layouts  35.9 us (3%)
  matrix products  33.9 us (2%)
  waiting for transfers between devices  21.8 us (2%)
  starting transfers between devices  20.9 us (2%)
  between operations  15.7 us (1%)
    pallas_call x4, Pallas kernels, combine(): pl.pallas_call(kernel, out_shape=[jax.ShapeDtypeStruct((rows, width), jnp...  395 us
    pallas_call x2, Pallas kernels, expert_forward(): pl.pallas_call(kernel, out_shape=shapes, in_specs=[anywhere, near, near,...  188 us
    pallas_call x2, Pallas kernels, attention_backward_call(): pl.pallas_call(kernel, out_shape=[jax.ShapeDtypeStruct(*result) for resul...  145 us
    pallas_call x1, Pallas kernels, prepare(): pl.pallas_call(prepare_kernel, out_shape=[jax.ShapeDtypeStruct((16, count...  145 us
    pallas_call x2, Pallas kernels, attention_forward_call(): pl.pallas_call(kernel, out_shape=[jax.ShapeDtypeStruct(*result) for resul...  127 us
    pallas_call x2, Pallas kernels, expert_backward(): pl.pallas_call(kernel, out_shape=[jax.ShapeDtypeStruct(*result) for resul...  108 us
    pallas_call x1, Pallas kernels, last_exchange(): pl.pallas_call(kernel, out_shape=[jax.ShapeDtypeStruct(parts_shape(downs[...  60.2 us
  transfers between devices with their start and end apart: 11, of which 2 were waited for; matrix products, arithmetic and copies ran while one was open for 5% of the time, Pallas kernels for 52%

profile of v12, /device:TPU:16, one launch (start us, length us, event | category | flops | bytes accessed | tf_op | source)
XLA Modules:
  0.0 1357.6 jit_solution(973670161500039781)
XLA Ops:
  7.3 3.3 collective-permute-start
  10.6 13.6 collective-permute-done
  25.7 8.1 collective-permute-done.1
  37.5 145.2 %prepare.1 = (bf16[16,160,256]{2,1,0:T(8,128)(2,1)}, bf16[16,160,256]{2,1,0:T(8,128)(2,1)}, bf16[16,256,160]{2,1,0:T(8,128)(2,1)}, bf16[16,256,160]{2,1,0:T(8,12...) custom-call(bf16[64,256]{1,0:T(8,128)(2,1)} %pad_maximum_fusion.2.x_, ...), custom_call_target="tpu_custom_call" | custom-call | flops 80000000000 | bytes 100000000 | tf_op jit(solution)/shard_map/prepare/pallas_call | solution.py:610
  189.1 74.4 %attention_forward.2 = (f32[256,1536]{1,0:T(8,128)}, bf16[4,256,1536]{2,1,0:T(8,128)(2,1)}, bf16[10,1024,64]{2,1,0:T(8,128)(2,1)}, f32[8,1024]{1,0:T(8,128)}, bf...) custom-call(bf16[256,1536]{1,0:T(8,128)(2,1)} %fusion.4.refs_0_, bf16[1536,640]{1,0:T(8,128)(2,1)} %bitcast.160, ...), custom_call_target="tpu_custom_call" | custom-call | flops 80000000000 | bytes 100000000 | tf_op jit(solution)/shard_map/attention_forward/pallas_call | solution.py:1428
  267.5 103.4 %expert_forward.2 = (bf16[2,1280,1536]{2,1,0:T(8,128)(2,1)}, bf16[2,1280,512]{2,1,0:T(8,128)(2,1)}, bf16[2,1280,512]{2,1,0:T(8,128)(2,1)}, bf16[2,1280,512]{2,1,...) custom-call(bf16[256,1536]{1,0:T(8,128)(2,1)} %multiply_convert_fusion.2.ref, ...), custom_call_target="tpu_custom_call" | custom-call | flops 80000000000 | bytes 100000000 | tf_op jit(solution)/shard_map/expert_forward/pallas_call | solution.py:790
  370.9 86.2 %combine.4 = f32[256,1536]{1,0:T(8,128)} custom-call(bf16[16,256,160]{2,1,0:T(8,128)(2,1)} %get-tuple-element.103.refs_0_, bf16[16,160,1536]{2,1,0:T(8,128)(2,1)} %get-tuple-element.108.refs_1_), custom_call_target="tpu_custom_call" | custom-call | flops 80000000000 | bytes 100000000 | tf_op jit(solution)/shard_map/combine/pallas_call | solution.py:1071
  461.0 52.5 %attention_forward.3 = (f32[256,1536]{1,0:T(8,128)}, bf16[4,256,1536]{2,1,0:T(8,128)(2,1)}, bf16[10,1024,64]{2,1,0:T(8,128)(2,1)}, f32[8,1024]{1,0:T(8,128)}, bf...) custom-call(bf16[256,1536]{1,0:T(8,128)(2,1)} %multiply_convert_fusion.1.refs_0_, ...), custom_call_target="tpu_custom_call" | custom-call | flops 80000000000 | bytes 100000000 | tf_op jit(solution)/shard_map/attention_forward/pallas_call | solution.py:1428
  518.6 84.2 %expert_forward.3 = (bf16[2,1280,1536]{2,1,0:T(8,128)(2,1)}, bf16[2,1280,512]{2,1,0:T(8,128)(2,1)}, bf16[2,1280,512]{2,1,0:T(8,128)(2,1)}, bf16[2,1280,512]{2,1,...) custom-call(bf16[256,1536]{1,0:T(8,128)(2,1)} %copy-done.17, ...), custom_call_target="tpu_custom_call" | custom-call | flops 80000000000 | bytes 100000000 | tf_op jit(solution)/shard_map/expert_forward/pallas_call | solution.py:790
  602.8 31.2 %expert_backward.2 = (bf16[2,1280,1536]{2,1,0:T(8,128)(2,1)}, bf16[2,1280,512]{2,1,0:T(8,128)(2,1)}, bf16[2,1280,512]{2,1,0:T(8,128)(2,1)}, f32[2,1280,128]{2,1,0:T(8,128)}, bf16[16,160,1536]{2,1,0:T(8,128)(2,1)}) custom-call(bf16[16,256,1536]{2,1,0:T(8,128)(2,1)} %get-tuple-element.117.refs_0_, bf16[16,160,256]{2,1,0:T(8,128)(2,1)} %get-tuple-element.112.refs_1_, ...), custom_call_target="tpu_custom_call" | custom-call | flops 80000000000 | bytes 100000000 | tf_op jit(solution)/shard_map/expert_backward/pallas_call | solution.py:1216
  637.1 6.8 all-to-all-start
  644.0 87.0 %combine.5 = (f32[256,1536]{1,0:T(8,128)}, bf16[2,1536,512]{2,1,0:T(8,128)(2,1)}, bf16[2,1536,512]{2,1,0:T(8,128)(2,1)}, bf16[2,512,1536]{2,1,0:T(8,128)(2,1)}) custom-call(bf16[16,256,160]{2,1,0:T(8,128)(2,1)} %get-tuple-element.111.refs_0_, bf16[16,160,1536]{2,1,0:T(8,128)(2,1)} %get-tuple-element.121.refs_1_, ...), custom_call_target="tpu_custom_call" | custom-call | flops 80000000000 | bytes 100000000 | tf_op jit(solution)/shard_map/combine/pallas_call | solution.py:1071
  732.0 2.8 multiply_reduce_fusion.2
  736.3 66.1 %attention_backward.2 = (f32[256,1536]{1,0:T(8,128)}, bf16[4,256,1536]{2,1,0:T(8,128)(2,1)}, bf16[1024,640]{1,0:T(8,128)(2,1)}) custom-call(bf16[256,1536]{1,0:T(8,128)(2,1)} %fusion.29.refs_0_, bf16[1536,640]{1,0:T(8,128)(2,1)} %all-gather.6.cloned.1.call-done.refs_1_, bf16[384,1536]{1,0:T(8,128)(2,1)} %all-gather.8.cloned.1.call-done.refs_2_, ...), custom_call_target="tpu_custom_call" | custom-call | flops 80000000000 | bytes 100000000 | tf_op jit(solution)/shard_map/attention_backward/pallas_call | solution.py:1575
  804.8 3.4 fusion.32
  808.2 77.1 %expert_backward.3 = (bf16[2,1280,1536]{2,1,0:T(8,128)(2,1)}, bf16[2,1280,512]{2,1,0:T(8,128)(2,1)}, bf16[2,1280,512]{2,1,0:T(8,128)(2,1)}, f32[2,1280,128]{2,1,...) custom-call(bf16[256,1536]{1,0:T(8,128)(2,1)} %get-tuple-element.252.refs_0_, ...), custom_call_target="tpu_custom_call" | custom-call | flops 80000000000 | bytes 100000000 | tf_op jit(solution)/shard_map/expert_backward/pallas_call | solution.py:1216
  888.4 9.1 all-to-all-start.1
  897.6 10.1 convolution_convert_fusion.refs_2_.refs_9_
  910.1 4.2 convolution_convert_fusion.2
  914.6 86.0 %combine.6 = (f32[256,1536]{1,0:T(8,128)}, bf16[2,1536,512]{2,1,0:T(8,128)(2,1)}, bf16[2,1536,512]{2,1,0:T(8,128)(2,1)}, bf16[2,1536,512]{2,1,0:T(8,128)(2,1)}, bf16[2,512,1536]{2,1,0:T(8,128)(2,1)}) custom-call(bf16[16,256,160]{2,1,0:T(8,128)(2,1)} %get-tuple-element.103.refs_0_, bf16[16,160,1536]{2,1,0:T(8,128)(2,1)} %get-tuple-element.140.refs_1_, ...), custom_call_target="tpu_custom_call" | custom-call | flops 80000000000 | bytes 100000000 | tf_op jit(solution)/shard_map/combine/pallas_call | solution.py:1071
  1005.5 3.2 multiply_reduce_fusion.1
  1008.8 3.3 fusion.30
  1012.2 79.2 %attention_backward.3 = (f32[256,1536]{1,0:T(8,128)}, bf16[4,256,1536]{2,1,0:T(8,128)(2,1)}, bf16[1024,640]{1,0:T(8,128)(2,1)}, bf16[2,1536,512]{2,1,0:T(8,128)(...) custom-call(bf16[256,1536]{1,0:T(8,128)(2,1)} %get-tuple-element.250.refs_0_, ...), custom_call_target="tpu_custom_call" | custom-call | flops 80000000000 | bytes 100000000 | tf_op jit(solution)/shard_map/attention_backward/pallas_call | solution.py:1575
  1093.9 4.1 convolution_convert_fusion.1
  1105.5 4.3 copy.84
  1111.2 3.0 fusion.9.refs_9_
  1114.1 135.6 %combine.7 = (f32[256,1536]{1,0:T(8,128)}, bf16[2,512,1536]{2,1,0:T(8,128)(2,1)}, f32[256,1536]{1,0:T(8,128)}, bf16[4,2,384,512]{3,2,1,0:T(8,128)(2,1)}) custom-call(bf16[16,256,160]{2,1,0:T(8,128)(2,1)} %get-tuple-element.111.refs_0_, bf16[16,160,1536]{2,1,0:T(8,128)(2,1)} %get-tuple-element.165.refs_1_, ...), custom_call_target="tpu_custom_call" | custom-call | flops 80000000000 | bytes 100000000 | tf_op jit(solution)/shard_map/combine/pallas_call | solution.py:1071
  1249.7 9.5 bitcast_convert_fusion.1
  1260.6 2.8 add.132.refs_8_
  1266.6 60.2 %last_exchange.1 = (bf16[4,2,128,1536]{3,2,1,0:T(8,128)(2,1)}, bf16[4,96,768]{2,1,0:T(8,128)(2,1)}, bf16[96,1536]{1,0:T(8,128)(2,1)}, f32[256,1536]{1,0:T(8,128)}, f32[256,1536]{1,0:T(8,128)}) custom-call(bf16[2,512,1536]{2,1,0:T(8,128)(2,1)} %get-tuple-element.166.refs_2_.refs_0_, bf16[2,512,1536]{2,1,0:T(8,128)(2,1)} %get-tuple-element.156.refs_8_.refs_1_, ...), custom_call_target="tpu_custom_call" | custom-call | tf_op jit(solution)/shard_map/last_exchange/pallas_call | solution.py:1668
  1330.2 3.6 bitcast_convert_fusion
  1343.2 3.3 select_bitcast_fusion.1
  (259 shorter events, 75.2 us)
Async XLA Ops:
  7.2 27.5 %copy-start.30 = (bf16[1,96,1536]{2,1,0:T(8,128)(2,1)S(1)}, bf16[1,96,1536]{2,1,0:T(8,128)(2,1)}, u32[]{:S(2)}) copy-start(bf16[1,96,1536]{2,1,0:T(8,128)(2,1)} %param.25) | copy-start | bytes 884740
  7.2 27.6 %copy-start.41 = (bf16[1,96,512]{2,1,0:T(8,128)(2,1)S(1)}, bf16[1,96,512]{2,1,0:T(8,128)(2,1)}, u32[]{:S(2)}) copy-start(bf16[1,96,512]{2,1,0:T(8,128)(2,1)} %param.26) | copy-start | bytes 294916
  7.2 27.7 %copy-start.42 = (bf16[1,96,512]{2,1,0:T(8,128)(2,1)S(1)}, bf16[1,96,512]{2,1,0:T(8,128)(2,1)}, u32[]{:S(2)}) copy-start(bf16[1,96,512]{2,1,0:T(8,128)(2,1)} %param.27) | copy-start | bytes 294916
  7.2 181.9 %all-gather.4.cloned.1.call-start = ((), (), s32[]{:S(2)}) async-start(), calls=%async_computation.6 | async-start | bytes 1474560 | tf_op jit(solution)/shard_map/all_gather | solution.py:2030
  7.3 16.9 %collective-permute-start = (bf16[96,1536]{1,0:T(8,128)(2,1)}, bf16[96,1536]{1,0:T(8,128)(2,1)S(1)}, u32[]{:S(2)}, u32[]{:S(2)}) collective-permute-start(bf16[96,1536]{1,0:T(8,128)(2,1)} %bitcast.155), channel_id=1, source_target_pairs={{0,0},{1,4},{2,8},{3,12},{4,1},{5,5},{6,9},{7,13},{8,2},{9,6},{10,... | collective-permute-start | bytes 884744 | tf_op jit(solution)/shard_map/ppermute | solution.py:1973
  24.1 9.6 collective-permute-start.1
  34.6 426.4 %all-gather.8.cloned.1.call-start = ((), (), s32[]{:S(2)}) async-start(), calls=%async_computation.8 | async-start | bytes 1474560 | tf_op jit(solution)/shard_map/all_gather | solution.py:2030
  37.4 423.6 %all-gather.6.cloned.1.call-start = ((), (), s32[]{:S(2)}) async-start(), calls=%async_computation.7 | async-start | bytes 2457600 | tf_op jit(solution)/shard_map/all_gather | solution.py:2007
  37.5 148.4 %copy-start.13 = (bf16[2,1,256,1536]{3,2,1,0:T(8,128)(2,1)S(1)}, bf16[2,1,256,1536]{3,2,1,0:T(8,128)(2,1)}, u32[]{:S(2)}) copy-start(bf16[2,1,256,1536]{3,2,1,0:T(8,128)(2,1)} %param.21) | copy-start | bytes 4718596
  184.2 79.3 %copy-start.35 = (f32[1536]{0:T(1024)}, f32[1536]{0:T(1024)S(1)}, u32[]{:S(2)}) copy-start(f32[1536]{0:T(1024)S(1)} %get-tuple-element.247) | copy-start | bytes 18436
  184.2 81.0 %copy-start.37 = (f32[1536]{0:T(1024)}, f32[1536]{0:T(1024)S(1)}, u32[]{:S(2)}) copy-start(f32[1536]{0:T(1024)S(1)} %get-tuple-element.246) | copy-start | bytes 18436
  186.7 76.8 %copy-start.52 = (f32[256]{0:T(256)}, f32[256]{0:T(256)S(1)}, u32[]{:S(2)}) copy-start(f32[256]{0:T(256)S(1)} %fusion.25) | copy-start | bytes 3076
  265.3 105.6 %copy-start.56 = (f32[256]{0:T(256)}, f32[256]{0:T(256)S(1)}, u32[]{:S(2)}) copy-start(f32[256]{0:T(256)S(1)} %get-tuple-element.258) | copy-start | bytes 3076
  370.9 86.2 %copy-start.7 = (f32[256,1536]{1,0:T(8,128)S(1)}, f32[256,1536]{1,0:T(8,128)}, u32[]{:S(2)}) copy-start(f32[256,1536]{1,0:T(8,128)} %copy-done.6) | copy-start | bytes 4718596
  637.1 93.9 %all-to-all-start = ((f32[16,2,256]{2,1,0:T(2,128)}), f32[16,2,256]{2,1,0:T(2,128)S(1)}, u32[]{:S(2)}, u32[]{:S(2)}) async-start(f32[16,2,256]{2,1,0:T(2,128)} %fusion.1), calls=%async_computation | async-start | bytes 65536 | tf_op jit(solution)/shard_map/all_to_all | solution.py:1873
  643.9 87.0 %copy-start.28 = (f32[32,256]{1,0:T(8,128)S(1)}, f32[32,256]{1,0:T(8,128)}, u32[]{:S(2)}) copy-start(f32[32,256]{1,0:T(8,128)} %get-tuple-element.276) | copy-start | bytes 98308
  643.9 87.1 %copy-start.51 = (f32[256]{0:T(256)S(1)}, f32[256]{0:T(256)}, u32[]{:S(2)}) copy-start(f32[256]{0:T(256)} %get-tuple-element.275) | copy-start | bytes 3076
  643.9 87.2 %copy-start.18 = (bf16[256,1536]{1,0:T(8,128)(2,1)S(1)}, bf16[256,1536]{1,0:T(8,128)(2,1)}, u32[]{:S(2)}) copy-start(bf16[256,1536]{1,0:T(8,128)(2,1)} %copy-done.17) | copy-start | bytes 2359300
  643.9 88.1 %copy-start.1 = (f32[256,1536]{1,0:T(8,128)S(1)}, f32[256,1536]{1,0:T(8,128)}, u32[]{:S(2)}) copy-start(f32[256,1536]{1,0:T(8,128)} %copy-done) | copy-start | bytes 4718596
  643.9 88.1 %copy-start.34 = (f32[1536]{0:T(1024)S(1)}, f32[1536]{0:T(1024)}, u32[]{:S(2)}) copy-start(f32[1536]{0:T(1024)} %get-tuple-element.244) | copy-start | bytes 18436
  643.9 88.1 %copy-start.44 = (f32[256]{0:T(256)S(1)}, f32[256]{0:T(256)}, u32[]{:S(2)}) copy-start(f32[256]{0:T(256)} %copy-done.43) | copy-start | bytes 3076
  736.3 66.2 %copy-start.4 = (f32[256,1536]{1,0:T(8,128)S(1)}, f32[256,1536]{1,0:T(8,128)}, u32[]{:S(2)}) copy-start(f32[256,1536]{1,0:T(8,128)} %copy-done.3) | copy-start | bytes 4718596
  736.3 66.2 %copy-start.40 = (f32[1536]{0:T(1024)S(1)}, f32[1536]{0:T(1024)}, u32[]{:S(2)}) copy-start(f32[1536]{0:T(1024)} %get-tuple-element.245) | copy-start | bytes 18436
  736.3 66.2 %copy-start.48 = (f32[256]{0:T(256)S(1)}, f32[256]{0:T(256)}, u32[]{:S(2)}) copy-start(f32[256]{0:T(256)} %copy-done.47) | copy-start | bytes 3076
  888.4 26.1 %all-to-all-start.1 = ((f32[16,2,256]{2,1,0:T(2,128)}), f32[16,2,256]{2,1,0:T(2,128)S(1)}, u32[]{:S(2)}, u32[]{:S(2)}) async-start(f32[16,2,256]{2,1,0:T(2,128)} %fusion), calls=%async_computation.1 | async-start | bytes 65536 | tf_op jit(solution)/shard_map/all_to_all | solution.py:1873
  897.5 205.8 %reduce-scatter.13.cloned.1.call-start = ((), (), s32[]{:S(2)}) async-start(), calls=%async_computation.11 | async-start | bytes 2949120
  1003.1 102.4 %reduce-scatter.9.cloned.1.call-start = ((), (), s32[]{:S(2)}) async-start(), calls=%async_computation.9 | async-start | bytes 1474560 | tf_op jit(solution)/shard_map/reduce_scatter | solution.py:2055
  1008.7 250.4 %reduce-scatter.15.cloned.1.call-start = ((), (), s32[]{:S(2)}) async-start(), calls=%async_computation.12 | async-start | bytes 2949120
  1012.2 79.2 %copy-start.14 = (bf16[2,1,256,1536]{3,2,1,0:T(8,128)(2,1)S(1)}, bf16[2,1,256,1536]{3,2,1,0:T(8,128)(2,1)}, u32[]{:S(2)}) copy-start(bf16[2,1,256,1536]{3,2,1,0:T(8,128)(2,1)} %param.21) | copy-start | bytes 4718596
  1012.2 79.2 %copy-start.36 = (f32[1536]{0:T(1024)S(1)}, f32[1536]{0:T(1024)}, u32[]{:S(2)}) copy-start(f32[1536]{0:T(1024)} %copy-done.35) | copy-start | bytes 18436
  1012.2 79.2 %copy-start.53 = (f32[256]{0:T(256)S(1)}, f32[256]{0:T(256)}, u32[]{:S(2)}) copy-start(f32[256]{0:T(256)} %copy-done.52) | copy-start | bytes 3076
  1109.8 150.8 %reduce-scatter.11.cloned.1.call-start = ((), (), s32[]{:S(2)}) async-start(), calls=%async_computation.10 | async-start | bytes 1474560 | tf_op jit(solution)/shard_map/reduce_scatter | solution.py:2055
  (52 other events, 191.7 us)
Sparse Core Ops, SparseCore 0:
  34.7 32.9 all-gather.3
  69.8 41.3 all-gather.7
  182.9 59.6 all-gather.5
  1003.2 47.0 reduce-scatter.12
  1053.0 27.8 reduce-scatter.8
  1109.9 51.4 reduce-scatter.14
  1163.7 46.9 reduce-scatter.10

commit v13 on v12

--- a/solution.py
+++ b/solution.py
@@ -465,19 +465,20 @@
 def prepare_kernel(
     x_ref, group_ref, gate_ref, grad_ref,
     pick_0, pick_1, pick_t_0, pick_t_1, chosen_0, chosen_1, small_out, qkv_out, parts_out, gate_out, grad_out,
-    both, places, groups, parts, lsem, carry_sem, spread_sem, qs, qr, *gather
+    both, places, block, groups, parts, lsem, osem, carry_sem, spread_sem, qs, qr, *gather
 ):
     d, s, section = lax.axis_index("dp"), lax.axis_index("seq"), lax.axis_index("section")
-    small_gather, grad_gather = Gather(gather[:8]), Gather([grad_out] + list(gather[8:]))
+    gather = Gather(gather)
+    land = gather.land
     known = x_ref.shape[0]
     count = pick_0.shape[1] // CAP
     rows = pick_0.shape[2]
-    land = gather[0]
+    width = x_ref.shape[1]
     part = both.at[pl.ds(pl.multiple_of(section * known, known), known)]
     swaps = Carried((None, None), (x_ref, group_ref), (part, groups.at[section]), carry_sem)
     gates = Carried((None,), (share(gate_ref),), (gate_out,), carry_sem.at[pl.ds(2, 1)])
     spreads = [Spread(groups.at[n], parts.at[n], spread_sem.at[n]) for n in range(2)]
-    own_columns = pltpu.make_async_copy(parts.at[0], qkv_out.at[d], lsem.at[2])
+    own_columns = pltpu.make_async_copy(parts.at[0], qkv_out.at[d], lsem.at[3])
 
     def along(src, z, right):
         target = d + 1 if right else d - 1
@@ -488,6 +489,7 @@
         own = [
             pltpu.make_async_copy(x_ref, part, lsem.at[0]),
             pltpu.make_async_copy(group_ref, groups.at[section], lsem.at[1]),
+            pltpu.make_async_copy(grad_ref, block.at[pl.ds(0, rows)], lsem.at[2]),
         ]
         for copy in own:
             copy.start()
@@ -525,18 +527,6 @@
             def _():
                 along(qkv_out.at[d + h], d + h, False).start()
 
-    greet(d, s, section, True)
-    first()
-    small_gather.begin(both)
-    grad_gather.begin(grad_ref)
-
-    @pl.loop(0, 4)
-    def _(i):
-        small_gather.step(i)
-
-    small_gather.finish()
-    hop(1)
-    grad_gather.step(0)
     first_expert = (d * 4 + s) * count
     before = lax.broadcasted_iota(jnp.int32, (rows, rows), 0)
     before = low(before < lax.broadcasted_iota(jnp.int32, (rows, rows), 1))
@@ -544,10 +534,11 @@
     expert = lax.broadcasted_iota(jnp.int32, (EXPERTS, rows), 0)
     lane = lax.broadcasted_iota(jnp.int32, (rows, count * CAP), 1)
 
-    def tables(layer, pick_out, pick_t_out, chosen_out):
-        @pl.loop(0, 16)
+    def tables(z, layer, pick_out, pick_t_out, chosen_out):
+        @pl.loop(z * 4, z * 4 + 4)
         def _(b):
-            paths = land[b, layer * known : layer * known + 16, :].astype(jnp.float32)
+            lanes = slice(2 * layer * width, (2 * layer + 1) * width)
+            paths = land[b, rows : rows + 16, lanes].astype(jnp.float32)
             paths = jnp.where(section == 0, paths[:TOP_K], paths[TOP_K:]).astype(jnp.int32)
             chosen = expert == paths[0:1]
             for k in range(1, TOP_K):
@@ -570,19 +561,43 @@
                 pick_t = pick_t & (lane < j * CAP) | (turned[:, j : j + 1] == lane - j * CAP)
             pick_t_out[b] = low(pick_t)
 
-        depth = small_out.shape[2] // 16
+    greet(d, s, section, True)
+    first()
+    for part_of in range(4):
+        lanes = slice(part_of * width, (part_of + 1) * width)
+        block[rows:, lanes] = both[part_of * known // 2 : (part_of + 1) * known // 2, :]
+    block[rows:, 4 * width :] = jnp.zeros((known // 2, block.shape[1] - 4 * width), block.dtype)
+    gather.begin(block)
+
+    def grad_copy(z):
+        four = pl.ds(z * 4, 4)
+        return pltpu.make_async_copy(land.at[four, pl.ds(0, rows)], grad_out.at[four], osem.at[z])
+
+    @pl.loop(0, 4)
+    def _(i):
+        z = gather.step(i)
+        grad_copy(z).start()
+        for h in (1, 2, 3):
+
+            @pl.when(i == h - 1)
+            def _():
+                hop(h)
+
+        tables(z, 0, pick_0, pick_t_0, chosen_0)
+        tables(z, 1, pick_1, pick_t_1, chosen_1)
+
+    depth = small_out.shape[2] // 16
+    rest = known // 2 - 16
+    for layer in range(2):
         for b in range(16):
-            small = land[b, layer * known + 16 : (layer + 1) * known, :]
-            small_out[layer, :, b * depth : (b + 1) * depth] = small[:, :depth]
-
-    tables(0, pick_0, pick_t_0, chosen_0)
-    hop(2)
-    grad_gather.step(1)
-    tables(1, pick_1, pick_t_1, chosen_1)
-    hop(3)
-    grad_gather.step(2)
-    grad_gather.step(3)
-    grad_gather.finish()
+            columns = slice(b * depth, (b + 1) * depth)
+            begin = 2 * layer * width
+            small_out[layer, :rest, columns] = land[b, rows + 16 :, begin : begin + depth]
+            begin = begin + width
+            small_out[layer, rest:, columns] = land[b, rows:, begin : begin + depth]
+    gather.finish()
+    for z in range(4):
+        grad_copy(z).wait()
     spreads[1].finish()
     layer_1 = pltpu.make_async_copy(parts.at[1], parts_out, lsem.at[0])
     layer_1.start()
@@ -627,16 +642,17 @@
         scratch_shapes=[
             pltpu.VMEM((2 * known, width), bf),
             pltpu.VMEM((8, rows), jnp.float32),
+            pltpu.VMEM((rows + known // 2, grad.shape[1]), bf),
             pltpu.VMEM((2,) + group.shape, bf),
             pltpu.VMEM((2,) + group.shape, bf),
-            DMA((3,)),
+            DMA((4,)),
+            DMA((4,)),
             DMA((3, 2)),
             DMA((2, 4, 2)),
             DMA((2, 4)),
             DMA((4,)),
         ]
-        + gather_scratch(2 * known, width)
-        + gather_scratch(*grad.shape)[1:],
+        + gather_scratch(rows + known // 2, grad.shape[1]),
         compiler_params=pltpu.CompilerParams(
             collective_id=collective_id, has_side_effects=True, vmem_limit_bytes=60 << 20
         ),

time: 1370 us -> 1360 us (level)
  no operation moved by 1% of the time
where the time goes in v13:
time: 1360 us; the launch traced here: 1350 us
  Pallas kernels  1160 us (85%)
  other arithmetic  60.9 us (4%)
  local copies, waits for them, and re-layouts  35.9 us (3%)
  matrix products  33.9 us (2%)
  waiting for transfers between devices  21.8 us (2%)
  starting transfers between devices  20.8 us (2%)
  between operations  15.7 us (1%)
    pallas_call x4, Pallas kernels, combine(): pl.pallas_call(kernel, out_shape=[jax.ShapeDtypeStruct((rows, width), jnp...  392 us
    pallas_call x2, Pallas kernels, expert_forward(): pl.pallas_call(kernel, out_shape=shapes, in_specs=[anywhere, near, near,...  187 us
    pallas_call x2, Pallas kernels, attention_backward_call(): pl.pallas_call(kernel, out_shape=[jax.ShapeDtypeStruct(*result) for resul...  145 us
    pallas_call x1, Pallas kernels, prepare(): pl.pallas_call(prepare_kernel, out_shape=[jax.ShapeDtypeStruct((16, count...  141 us
    pallas_call x2, Pallas kernels, attention_forward_call(): pl.pallas_call(kernel, out_shape=[jax.ShapeDtypeStruct(*result) for resul...  127 us
    pallas_call x2, Pallas kernels, expert_backward(): pl.pallas_call(kernel, out_shape=[jax.ShapeDtypeStruct(*result) for resul...  108 us
    pallas_call x1, Pallas kernels, last_exchange(): pl.pallas_call(kernel, out_shape=[jax.ShapeDtypeStruct(parts_shape(downs[...  60.2 us
  transfers between devices with their start and end apart: 11, of which 2 were waited for; matrix products, arithmetic and copies ran while one was open for 5% of the time, Pallas kernels for 52%

profile of v13, /device:TPU:16, one launch (start us, length us, event | category | flops | bytes accessed | tf_op | source)
XLA Modules:
  0.0 1349.3 jit_solution(1229378221179808893)
XLA Ops:
  7.3 3.3 collective-permute-start
  10.6 13.6 %collective-permute-done = bf16[96,1536]{1,0:T(8,128)(2,1)S(1)} collective-permute-done((bf16[96,1536]{1,0:T(8,128)(2,1)}, bf16[96,1536]{1,0:T(8,128)(2,1)S(1)}, u32[]{:S(2)}, u32[]{:S(2)}) %collective-permute-start) | collective-permute-done | bytes 294944 | tf_op jit(solution)/shard_map/ppermute | solution.py:1989
  25.7 8.1 collective-permute-done.1
  37.5 140.8 %prepare.1 = (bf16[16,160,256]{2,1,0:T(8,128)(2,1)}, bf16[16,160,256]{2,1,0:T(8,128)(2,1)}, bf16[16,256,160]{2,1,0:T(8,128)(2,1)}, bf16[16,256,160]{2,1,0:T(8,12...) custom-call(bf16[64,256]{1,0:T(8,128)(2,1)} %pad_maximum_fusion.2.x_, ...), custom_call_target="tpu_custom_call" | custom-call | flops 80000000000 | bytes 100000000 | tf_op jit(solution)/shard_map/prepare/pallas_call | solution.py:625
  184.6 73.9 %attention_forward.2 = (f32[256,1536]{1,0:T(8,128)}, bf16[4,256,1536]{2,1,0:T(8,128)(2,1)}, bf16[10,1024,64]{2,1,0:T(8,128)(2,1)}, f32[8,1024]{1,0:T(8,128)}, bf...) custom-call(bf16[256,1536]{1,0:T(8,128)(2,1)} %fusion.4.refs_0_, bf16[1536,640]{1,0:T(8,128)(2,1)} %bitcast.160, ...), custom_call_target="tpu_custom_call" | custom-call | flops 80000000000 | bytes 100000000 | tf_op jit(solution)/shard_map/attention_forward/pallas_call | solution.py:1444
  262.5 99.4 %expert_forward.2 = (bf16[2,1280,1536]{2,1,0:T(8,128)(2,1)}, bf16[2,1280,512]{2,1,0:T(8,128)(2,1)}, bf16[2,1280,512]{2,1,0:T(8,128)(2,1)}, bf16[2,1280,512]{2,1,...) custom-call(bf16[256,1536]{1,0:T(8,128)(2,1)} %multiply_convert_fusion.2.ref, ...), custom_call_target="tpu_custom_call" | custom-call | flops 80000000000 | bytes 100000000 | tf_op jit(solution)/shard_map/expert_forward/pallas_call | solution.py:806
  362.0 83.4 %combine.4 = f32[256,1536]{1,0:T(8,128)} custom-call(bf16[16,256,160]{2,1,0:T(8,128)(2,1)} %get-tuple-element.103.refs_0_, bf16[16,160,1536]{2,1,0:T(8,128)(2,1)} %get-tuple-element.108.refs_1_), custom_call_target="tpu_custom_call" | custom-call | flops 80000000000 | bytes 100000000 | tf_op jit(solution)/shard_map/combine/pallas_call | solution.py:1087
  449.3 53.2 %attention_forward.3 = (f32[256,1536]{1,0:T(8,128)}, bf16[4,256,1536]{2,1,0:T(8,128)(2,1)}, bf16[10,1024,64]{2,1,0:T(8,128)(2,1)}, f32[8,1024]{1,0:T(8,128)}, bf...) custom-call(bf16[256,1536]{1,0:T(8,128)(2,1)} %multiply_convert_fusion.1.refs_0_, ...), custom_call_target="tpu_custom_call" | custom-call | flops 80000000000 | bytes 100000000 | tf_op jit(solution)/shard_map/attention_forward/pallas_call | solution.py:1444
  507.5 87.1 %expert_forward.3 = (bf16[2,1280,1536]{2,1,0:T(8,128)(2,1)}, bf16[2,1280,512]{2,1,0:T(8,128)(2,1)}, bf16[2,1280,512]{2,1,0:T(8,128)(2,1)}, bf16[2,1280,512]{2,1,...) custom-call(bf16[256,1536]{1,0:T(8,128)(2,1)} %copy-done.17, ...), custom_call_target="tpu_custom_call" | custom-call | flops 80000000000 | bytes 100000000 | tf_op jit(solution)/shard_map/expert_forward/pallas_call | solution.py:806
  594.6 31.3 %expert_backward.2 = (bf16[2,1280,1536]{2,1,0:T(8,128)(2,1)}, bf16[2,1280,512]{2,1,0:T(8,128)(2,1)}, bf16[2,1280,512]{2,1,0:T(8,128)(2,1)}, f32[2,1280,128]{2,1,0:T(8,128)}, bf16[16,160,1536]{2,1,0:T(8,128)(2,1)}) custom-call(bf16[16,256,1536]{2,1,0:T(8,128)(2,1)} %get-tuple-element.117.refs_0_, bf16[16,160,256]{2,1,0:T(8,128)(2,1)} %get-tuple-element.112.refs_1_, ...), custom_call_target="tpu_custom_call" | custom-call | flops 80000000000 | bytes 100000000 | tf_op jit(solution)/shard_map/expert_backward/pallas_call | solution.py:1232
  629.0 6.6 all-to-all-start
  635.7 87.0 %combine.5 = (f32[256,1536]{1,0:T(8,128)}, bf16[2,1536,512]{2,1,0:T(8,128)(2,1)}, bf16[2,1536,512]{2,1,0:T(8,128)(2,1)}, bf16[2,512,1536]{2,1,0:T(8,128)(2,1)}) custom-call(bf16[16,256,160]{2,1,0:T(8,128)(2,1)} %get-tuple-element.111.refs_0_, bf16[16,160,1536]{2,1,0:T(8,128)(2,1)} %get-tuple-element.121.refs_1_, ...), custom_call_target="tpu_custom_call" | custom-call | flops 80000000000 | bytes 100000000 | tf_op jit(solution)/shard_map/combine/pallas_call | solution.py:1087
  723.7 2.8 multiply_reduce_fusion.2
  728.0 66.1 %attention_backward.2 = (f32[256,1536]{1,0:T(8,128)}, bf16[4,256,1536]{2,1,0:T(8,128)(2,1)}, bf16[1024,640]{1,0:T(8,128)(2,1)}) custom-call(bf16[256,1536]{1,0:T(8,128)(2,1)} %fusion.29.refs_0_, bf16[1536,640]{1,0:T(8,128)(2,1)} %all-gather.6.cloned.1.call-done.refs_1_, bf16[384,1536]{1,0:T(8,128)(2,1)} %all-gather.8.cloned.1.call-done.refs_2_, ...), custom_call_target="tpu_custom_call" | custom-call | flops 80000000000 | bytes 100000000 | tf_op jit(solution)/shard_map/attention_backward/pallas_call | solution.py:1591
  796.6 3.4 fusion.32
  799.9 77.1 %expert_backward.3 = (bf16[2,1280,1536]{2,1,0:T(8,128)(2,1)}, bf16[2,1280,512]{2,1,0:T(8,128)(2,1)}, bf16[2,1280,512]{2,1,0:T(8,128)(2,1)}, f32[2,1280,128]{2,1,...) custom-call(bf16[256,1536]{1,0:T(8,128)(2,1)} %get-tuple-element.252.refs_0_, ...), custom_call_target="tpu_custom_call" | custom-call | flops 80000000000 | bytes 100000000 | tf_op jit(solution)/shard_map/expert_backward/pallas_call | solution.py:1232
  880.2 9.1 all-to-all-start.1
  889.4 10.1 convolution_convert_fusion.refs_2_.refs_9_
  901.9 4.2 convolution_convert_fusion.2
  906.3 86.0 %combine.6 = (f32[256,1536]{1,0:T(8,128)}, bf16[2,1536,512]{2,1,0:T(8,128)(2,1)}, bf16[2,1536,512]{2,1,0:T(8,128)(2,1)}, bf16[2,1536,512]{2,1,0:T(8,128)(2,1)}, bf16[2,512,1536]{2,1,0:T(8,128)(2,1)}) custom-call(bf16[16,256,160]{2,1,0:T(8,128)(2,1)} %get-tuple-element.103.refs_0_, bf16[16,160,1536]{2,1,0:T(8,128)(2,1)} %get-tuple-element.140.refs_1_, ...), custom_call_target="tpu_custom_call" | custom-call | flops 80000000000 | bytes 100000000 | tf_op jit(solution)/shard_map/combine/pallas_call | solution.py:1087
  997.2 3.2 multiply_reduce_fusion.1
  1000.5 3.3 fusion.30
  1003.9 79.2 %attention_backward.3 = (f32[256,1536]{1,0:T(8,128)}, bf16[4,256,1536]{2,1,0:T(8,128)(2,1)}, bf16[1024,640]{1,0:T(8,128)(2,1)}, bf16[2,1536,512]{2,1,0:T(8,128)(...) custom-call(bf16[256,1536]{1,0:T(8,128)(2,1)} %get-tuple-element.250.refs_0_, ...), custom_call_target="tpu_custom_call" | custom-call | flops 80000000000 | bytes 100000000 | tf_op jit(solution)/shard_map/attention_backward/pallas_call | solution.py:1591
  1085.6 4.1 convolution_convert_fusion.1
  1097.2 4.3 copy.84
  1102.9 3.0 fusion.9.refs_9_
  1105.9 135.6 %combine.7 = (f32[256,1536]{1,0:T(8,128)}, bf16[2,512,1536]{2,1,0:T(8,128)(2,1)}, f32[256,1536]{1,0:T(8,128)}, bf16[4,2,384,512]{3,2,1,0:T(8,128)(2,1)}) custom-call(bf16[16,256,160]{2,1,0:T(8,128)(2,1)} %get-tuple-element.111.refs_0_, bf16[16,160,1536]{2,1,0:T(8,128)(2,1)} %get-tuple-element.165.refs_1_, ...), custom_call_target="tpu_custom_call" | custom-call | flops 80000000000 | bytes 100000000 | tf_op jit(solution)/shard_map/combine/pallas_call | solution.py:1087
  1241.4 9.5 bitcast_convert_fusion.1
  1252.3 2.8 add.132.refs_8_
  1258.3 60.2 %last_exchange.1 = (bf16[4,2,128,1536]{3,2,1,0:T(8,128)(2,1)}, bf16[4,96,768]{2,1,0:T(8,128)(2,1)}, bf16[96,1536]{1,0:T(8,128)(2,1)}, f32[256,1536]{1,0:T(8,128)}, f32[256,1536]{1,0:T(8,128)}) custom-call(bf16[2,512,1536]{2,1,0:T(8,128)(2,1)} %get-tuple-element.166.refs_2_.refs_0_, bf16[2,512,1536]{2,1,0:T(8,128)(2,1)} %get-tuple-element.156.refs_8_.refs_1_, ...), custom_call_target="tpu_custom_call" | custom-call | tf_op jit(solution)/shard_map/last_exchange/pallas_call | solution.py:1684
  1321.9 3.6 bitcast_convert_fusion
  1334.9 3.3 select_bitcast_fusion.1
  (259 shorter events, 75.2 us)
Async XLA Ops:
  7.2 27.5 %copy-start.30 = (bf16[1,96,1536]{2,1,0:T(8,128)(2,1)S(1)}, bf16[1,96,1536]{2,1,0:T(8,128)(2,1)}, u32[]{:S(2)}) copy-start(bf16[1,96,1536]{2,1,0:T(8,128)(2,1)} %param.25) | copy-start | bytes 884740
  7.2 27.6 %copy-start.41 = (bf16[1,96,512]{2,1,0:T(8,128)(2,1)S(1)}, bf16[1,96,512]{2,1,0:T(8,128)(2,1)}, u32[]{:S(2)}) copy-start(bf16[1,96,512]{2,1,0:T(8,128)(2,1)} %param.26) | copy-start | bytes 294916
  7.2 27.7 %copy-start.42 = (bf16[1,96,512]{2,1,0:T(8,128)(2,1)S(1)}, bf16[1,96,512]{2,1,0:T(8,128)(2,1)}, u32[]{:S(2)}) copy-start(bf16[1,96,512]{2,1,0:T(8,128)(2,1)} %param.27) | copy-start | bytes 294916
  7.2 177.4 %all-gather.4.cloned.1.call-start = ((), (), s32[]{:S(2)}) async-start(), calls=%async_computation.6 | async-start | bytes 1474560 | tf_op jit(solution)/shard_map/all_gather | solution.py:2046
  7.3 16.9 %collective-permute-start = (bf16[96,1536]{1,0:T(8,128)(2,1)}, bf16[96,1536]{1,0:T(8,128)(2,1)S(1)}, u32[]{:S(2)}, u32[]{:S(2)}) collective-permute-start(bf16[96,1536]{1,0:T(8,128)(2,1)} %bitcast.155), channel_id=1, source_target_pairs={{0,0},{1,4},{2,8},{3,12},{4,1},{5,5},{6,9},{7,13},{8,2},{9,6},{10,... | collective-permute-start | bytes 884744 | tf_op jit(solution)/shard_map/ppermute | solution.py:1989
  24.1 9.6 collective-permute-start.1
  34.6 414.7 %all-gather.8.cloned.1.call-start = ((), (), s32[]{:S(2)}) async-start(), calls=%async_computation.8 | async-start | bytes 1474560 | tf_op jit(solution)/shard_map/all_gather | solution.py:2046
  37.4 411.9 %all-gather.6.cloned.1.call-start = ((), (), s32[]{:S(2)}) async-start(), calls=%async_computation.7 | async-start | bytes 2457600 | tf_op jit(solution)/shard_map/all_gather | solution.py:2023
  37.5 144.0 %copy-start.13 = (bf16[2,1,256,1536]{3,2,1,0:T(8,128)(2,1)S(1)}, bf16[2,1,256,1536]{3,2,1,0:T(8,128)(2,1)}, u32[]{:S(2)}) copy-start(bf16[2,1,256,1536]{3,2,1,0:T(8,128)(2,1)} %param.21) | copy-start | bytes 4718596
  179.8 78.7 %copy-start.35 = (f32[1536]{0:T(1024)}, f32[1536]{0:T(1024)S(1)}, u32[]{:S(2)}) copy-start(f32[1536]{0:T(1024)S(1)} %get-tuple-element.247) | copy-start | bytes 18436
  179.8 80.5 %copy-start.37 = (f32[1536]{0:T(1024)}, f32[1536]{0:T(1024)S(1)}, u32[]{:S(2)}) copy-start(f32[1536]{0:T(1024)S(1)} %get-tuple-element.246) | copy-start | bytes 18436
  182.3 76.3 %copy-start.52 = (f32[256]{0:T(256)}, f32[256]{0:T(256)S(1)}, u32[]{:S(2)}) copy-start(f32[256]{0:T(256)S(1)} %fusion.25) | copy-start | bytes 3076
  260.3 101.7 %copy-start.56 = (f32[256]{0:T(256)}, f32[256]{0:T(256)S(1)}, u32[]{:S(2)}) copy-start(f32[256]{0:T(256)S(1)} %get-tuple-element.258) | copy-start | bytes 3076
  361.9 83.4 %copy-start.7 = (f32[256,1536]{1,0:T(8,128)S(1)}, f32[256,1536]{1,0:T(8,128)}, u32[]{:S(2)}) copy-start(f32[256,1536]{1,0:T(8,128)} %copy-done.6) | copy-start | bytes 4718596
  629.0 93.7 %all-to-all-start = ((f32[16,2,256]{2,1,0:T(2,128)}), f32[16,2,256]{2,1,0:T(2,128)S(1)}, u32[]{:S(2)}, u32[]{:S(2)}) async-start(f32[16,2,256]{2,1,0:T(2,128)} %fusion.1), calls=%async_computation | async-start | bytes 65536 | tf_op jit(solution)/shard_map/all_to_all | solution.py:1889
  635.6 87.0 %copy-start.28 = (f32[32,256]{1,0:T(8,128)S(1)}, f32[32,256]{1,0:T(8,128)}, u32[]{:S(2)}) copy-start(f32[32,256]{1,0:T(8,128)} %get-tuple-element.276) | copy-start | bytes 98308
  635.6 87.0 %copy-start.51 = (f32[256]{0:T(256)S(1)}, f32[256]{0:T(256)}, u32[]{:S(2)}) copy-start(f32[256]{0:T(256)} %get-tuple-element.275) | copy-start | bytes 3076
  635.7 87.2 %copy-start.18 = (bf16[256,1536]{1,0:T(8,128)(2,1)S(1)}, bf16[256,1536]{1,0:T(8,128)(2,1)}, u32[]{:S(2)}) copy-start(bf16[256,1536]{1,0:T(8,128)(2,1)} %copy-done.17) | copy-start | bytes 2359300
  635.7 88.1 %copy-start.1 = (f32[256,1536]{1,0:T(8,128)S(1)}, f32[256,1536]{1,0:T(8,128)}, u32[]{:S(2)}) copy-start(f32[256,1536]{1,0:T(8,128)} %copy-done) | copy-start | bytes 4718596
  635.7 88.0 %copy-start.34 = (f32[1536]{0:T(1024)S(1)}, f32[1536]{0:T(1024)}, u32[]{:S(2)}) copy-start(f32[1536]{0:T(1024)} %get-tuple-element.244) | copy-start | bytes 18436
  635.7 88.0 %copy-start.44 = (f32[256]{0:T(256)S(1)}, f32[256]{0:T(256)}, u32[]{:S(2)}) copy-start(f32[256]{0:T(256)} %copy-done.43) | copy-start | bytes 3076
  728.0 66.2 %copy-start.4 = (f32[256,1536]{1,0:T(8,128)S(1)}, f32[256,1536]{1,0:T(8,128)}, u32[]{:S(2)}) copy-start(f32[256,1536]{1,0:T(8,128)} %copy-done.3) | copy-start | bytes 4718596
  728.0 66.2 %copy-start.40 = (f32[1536]{0:T(1024)S(1)}, f32[1536]{0:T(1024)}, u32[]{:S(2)}) copy-start(f32[1536]{0:T(1024)} %get-tuple-element.245) | copy-start | bytes 18436
  728.0 66.2 %copy-start.48 = (f32[256]{0:T(256)S(1)}, f32[256]{0:T(256)}, u32[]{:S(2)}) copy-start(f32[256]{0:T(256)} %copy-done.47) | copy-start | bytes 3076
  880.2 26.1 %all-to-all-start.1 = ((f32[16,2,256]{2,1,0:T(2,128)}), f32[16,2,256]{2,1,0:T(2,128)S(1)}, u32[]{:S(2)}, u32[]{:S(2)}) async-start(f32[16,2,256]{2,1,0:T(2,128)} %fusion), calls=%async_computation.1 | async-start | bytes 65536 | tf_op jit(solution)/shard_map/all_to_all | solution.py:1889
  889.3 205.8 %reduce-scatter.13.cloned.1.call-start = ((), (), s32[]{:S(2)}) async-start(), calls=%async_computation.11 | async-start | bytes 2949120
  994.8 102.4 %reduce-scatter.9.cloned.1.call-start = ((), (), s32[]{:S(2)}) async-start(), calls=%async_computation.9 | async-start | bytes 1474560 | tf_op jit(solution)/shard_map/reduce_scatter | solution.py:2071
  1000.5 250.4 %reduce-scatter.15.cloned.1.call-start = ((), (), s32[]{:S(2)}) async-start(), calls=%async_computation.12 | async-start | bytes 2949120
  1003.9 79.2 %copy-start.14 = (bf16[2,1,256,1536]{3,2,1,0:T(8,128)(2,1)S(1)}, bf16[2,1,256,1536]{3,2,1,0:T(8,128)(2,1)}, u32[]{:S(2)}) copy-start(bf16[2,1,256,1536]{3,2,1,0:T(8,128)(2,1)} %param.21) | copy-start | bytes 4718596
  1003.9 79.2 %copy-start.36 = (f32[1536]{0:T(1024)S(1)}, f32[1536]{0:T(1024)}, u32[]{:S(2)}) copy-start(f32[1536]{0:T(1024)} %copy-done.35) | copy-start | bytes 18436
  1003.9 79.2 %copy-start.53 = (f32[256]{0:T(256)S(1)}, f32[256]{0:T(256)}, u32[]{:S(2)}) copy-start(f32[256]{0:T(256)} %copy-done.52) | copy-start | bytes 3076
  1101.5 150.8 %reduce-scatter.11.cloned.1.call-start = ((), (), s32[]{:S(2)}) async-start(), calls=%async_computation.10 | async-start | bytes 1474560 | tf_op jit(solution)/shard_map/reduce_scatter | solution.py:2071
  (52 other events, 191.8 us)
Sparse Core Ops, SparseCore 0:
  34.7 32.9 all-gather.3
  69.8 42.0 all-gather.7
  178.4 53.5 all-gather.5
  994.9 46.9 reduce-scatter.12
  1044.7 27.8 reduce-scatter.8
  1101.6 51.4 reduce-scatter.14
  1155.4 46.9 reduce-scatter.10
